TPU v7x, 32 devices: a whole 2x2x4 slice. The times are simulated.
32 devices in a mesh: gz: 4 (over x, core), gy: 8 (over z, y).
Axes of the slice: x: 2, y: 2, z: 4, core: 2. Of those that a mesh axis runs over, the one named last changes fastest.
Arguments:
- flow_state: float32 [5, 8, 512, 512], P(None, None, 'gy', 'gz'), may hold values from -6 to 6
- velocity: float32 [8, 512, 512], P(None, 'gy', 'gz'), may hold values from -6 to 6
- metric_y: float32 [512], replicated, may hold values from 2000 to 4000
- metric_z: float32 [512], replicated, may hold values from 32000 to 64000
Outputs:
- correction: float32 [5, 8, 512, 512], P(None, None, 'gy', 'gz')
All inputs are finite; a program needn't handle non-finite values.
Results may differ from a plain program's by a relative error of at most 0.0009.
Values sent between devices are 32-bit elements; how exact they have to be, the bound alone decides.
No kernel may reach another device: no remote copies, remote signals or barrier semaphores. Data moves between devices by JAX's collectives and lax.ppermute only.
A program may use at most 64 MiB of HBM per device.

v0:
```python
import functools

import jax
import jax.numpy as jnp
from jax import lax
from jax.experimental import pallas as pl
from jax.experimental.pallas import tpu as pltpu
from jax.sharding import PartitionSpec as P

viscous = 0.25
explicit_fourth = 0.04
implicit_fourth = 0.05
time_step = 1048576.0
LANES = 128
EXTRA = 8
SWEEPS = 3
HIGHEST = lax.Precision.HIGHEST


def mm(a, b):
    return (
        a[0] * b[0] + a[1] * b[2],
        a[0] * b[1] + a[1] * b[3],
        a[2] * b[0] + a[3] * b[2],
        a[2] * b[1] + a[3] * b[3],
    )


def inverse_of_one_minus(a):
    p, q, r, s = 1.0 - a[0], -a[1], -a[2], 1.0 - a[3]
    d = 1.0 / (p * s - q * r)
    return (s * d, -q * d, -r * d, p * d)


def pick(condition, a, b):
    return tuple(jnp.where(condition, x, y) for x, y in zip(a, b))


def lane_roll(x, by):
    return pltpu.roll(x, by % LANES, 1)


def row_roll(x, by):
    by = by % x.shape[0]
    return jnp.concatenate([x[x.shape[0] - by :], x[: x.shape[0] - by]], axis=0)


def factor(metric, ny, nz, wy):
    rows = ny + nz
    lane = lax.broadcasted_iota(jnp.int32, (rows, LANES), 1)
    row = lax.broadcasted_iota(jnp.int32, (rows, LANES), 0)
    block = jnp.where(row < ny, row, row - ny)
    to_end = jnp.where(row < ny, ny, nz) - 1 - block
    even = (lane & 1) == 0

    def before(x, by):
        rolled = lane_roll(x, by)
        value = jnp.where(lane < by, row_roll(rolled, 1), rolled)
        return jnp.where((lane < by) & (block == 0), 0.0, value)

    def after(x, by):
        rolled = lane_roll(x, -by)
        value = jnp.where(lane >= LANES - by, row_roll(rolled, -1), rolled)
        return jnp.where((lane >= LANES - by) & (to_end == 0), 0.0, value)

    first = (lane == 0) & (block == 0)
    last = (lane == LANES - 1) & (to_end == 0)
    face_low = 0.5 * (jnp.where(first, metric, before(metric, 1)) + metric)
    face_high = 0.5 * (metric + jnp.where(last, metric, after(metric, 1)))
    ones = jnp.ones_like(metric)
    zeros = jnp.zeros_like(metric)

    def eliminate(sign):
        back = before if sign > 0 else after
        face_in, face_out = (face_low, face_high) if sign > 0 else (face_high, face_low)
        place = block if sign > 0 else to_end
        ratio, far = ones, zeros
        for _ in range(SWEEPS):
            eps = 4.0 * implicit_fourth - implicit_fourth * back(ratio, 1)
            mass = (1.0 + 6.0 * implicit_fourth) - implicit_fourth * back(far, 2) - 2.0 * eps
            eps_in = back(eps, 1)
            scale = 1.0 / (face_in + 2.0 * eps_in)
            m = ((mass + face_in) * scale, mass - eps_in * eps_in * scale, scale, ones)
            step = 1
            while step < LANES:
                inside = (lane >= step) if sign > 0 else (lane < LANES - step)
                m = pick(inside, mm(m, tuple(lane_roll(x, sign * step) for x in m)), m)
                step *= 2
            edge = LANES - 1 if sign > 0 else 0
            total = tuple(jnp.broadcast_to(x[:, edge : edge + 1], (rows, LANES)) for x in m)
            step = 1
            while step < max(ny, nz):
                total = pick(
                    place >= step, mm(total, tuple(row_roll(x, sign * step) for x in total)), total
                )
                step *= 2
            top = jnp.where(place >= 1, row_roll(total[0], sign), 1.0)
            low = jnp.where(place >= 1, row_roll(total[2], sign), 0.0)
            eta = (m[0] * top + m[1] * low) / (m[2] * top + m[3] * low)
            one_over = 1.0 / (face_out + (eta + 2.0 * eps))
            ratio = (face_out + eps) * one_over
            far = implicit_fourth * one_over
        return ratio, far, one_over

    near_l, far_l, pivot_l = eliminate(1)
    near_r, far_r, _ = eliminate(-1)
    near_l = jnp.where((to_end == 0) & (lane >= LANES - 1), 0.0, near_l)
    far_l = jnp.where((to_end == 0) & (lane >= LANES - 2), 0.0, far_l)
    near_r = jnp.where((block == 0) & (lane < 1), 0.0, near_r)
    far_r = jnp.where((block == 0) & (lane < 2), 0.0, far_r)

    def of_even(x):
        return jnp.where(even, x, lane_roll(x, 1))

    def of_odd(x):
        return jnp.where(even, lane_roll(x, -1), x)

    t0, t1, r0, r1 = of_even(near_l), of_odd(near_l), of_even(far_l), of_odd(far_l)
    from_right = (t0 * t1 - r0, -t0 * r1, t1, -r1)
    p1 = of_odd(pivot_l)
    left_inverse = (of_even(pivot_l) + t0 * t0 * p1, t0 * p1, t0 * p1, p1)
    s0, s1, q0, q1 = of_even(near_r), of_odd(near_r), of_even(far_r), of_odd(far_r)
    from_left = (-q0, s0, -s1 * q0, s1 * s0 - q1)
    from_left_after = tuple(after(x, 2) for x in from_left)
    from_right_before = tuple(before(x, 2) for x in from_right)
    diagonal = mm(inverse_of_one_minus(mm(from_right, from_left_after)), left_inverse)
    width = jnp.where(row < ny, wy, LANES)
    place = lane & (width - 1)
    to_right, to_left = from_right, from_left
    step = 2
    while step < LANES:
        to_right = pick(
            place + step < width, mm(to_right, tuple(lane_roll(x, -step) for x in to_right)), to_right
        )
        to_left = pick(place >= step, mm(to_left, tuple(lane_roll(x, step) for x in to_left)), to_left)
        step *= 2
    return from_right, from_left, diagonal, to_right, to_left, from_right_before, from_left_after


def cell_weights(chain, column, even):
    return jnp.where(even, chain[column], chain[2 + column])


def first_kernel(ny, nz, partners, flow, speed, metric_y, metric_z, *refs):
    sources, factors, chains = refs[:3]
    messages = refs[3 : 3 + partners]
    spread = refs[3 + partners]
    fields, planes_x, wy, _ = flow.shape
    rows = ny + nz
    core_rows = fields * planes_x * wy

    lane = lax.broadcasted_iota(jnp.int32, (wy, LANES), 1)
    extra_row = lax.broadcasted_iota(jnp.int32, (EXTRA, LANES), 0)
    for part in range(3):
        spread[part, 0:8, :] = jnp.zeros((8, LANES), jnp.float32)
        spread[part, wy + 8 : wy + 16, :] = jnp.zeros((8, LANES), jnp.float32)
    side = time_step * (viscous + 4.0 * explicit_fourth)
    half = time_step * 0.5
    centre = time_step * (-6.0 * viscous - 12.0 * explicit_fourth)
    fourth = -time_step * explicit_fourth

    def plane(index, carry):
        field, x = index // planes_x, index % planes_x
        u = flow[field, x]
        flux = u * speed[x]
        high, low = jnp.minimum(x + 1, planes_x - 1), jnp.maximum(x - 1, 0)
        has_high = jnp.where(x + 1 < planes_x, 1.0, 0.0)
        has_low = jnp.where(x > 0, 1.0, 0.0)
        u_high, u_low = flow[field, high] * has_high, flow[field, low] * has_low
        total = (
            centre * u
            + (time_step * viscous) * (u_high + u_low)
            - half * (u_high * speed[high] - u_low * speed[low])
        )
        onward = side * u + half * flux
        backward = side * u - half * flux
        far = fourth * u
        spread[0, 8 : wy + 8, :] = onward
        spread[1, 8 : wy + 8, :] = backward
        spread[2, 8 : wy + 8, :] = far
        total = total + (spread[0, 7 : wy + 7, :] + spread[1, 9 : wy + 9, :])
        total = total + (spread[2, 6 : wy + 6, :] + spread[2, 10 : wy + 10, :])
        a, b = lane_roll(onward, 1), lane_roll(backward, -1)
        c, d = lane_roll(far, 2), lane_roll(far, -2)
        ends = jnp.where(lane < 1, a, 0.0) + jnp.where(lane >= LANES - 1, b, 0.0)
        ends = ends + jnp.where(lane < 2, c, 0.0) + jnp.where(lane >= LANES - 2, d, 0.0)
        inner = jnp.where(lane < 1, 0.0, a) + jnp.where(lane >= LANES - 1, 0.0, b)
        inner = inner + jnp.where(lane < 2, 0.0, c) + jnp.where(lane >= LANES - 2, 0.0, d)
        start = pl.multiple_of(index * wy, 8)
        sources[pl.ds(start, wy), 0:LANES] = total + inner
        sources[pl.ds(start, wy), LANES : 2 * LANES] = ends
        above = spread[1, 7:15, :] + spread[2, 8:16, :]
        below = spread[0, wy + 5 : wy + 13, :] + spread[2, wy + 4 : wy + 12, :]
        extra = jnp.where(extra_row < 2, above, jnp.where(extra_row < 4, below, 0.0))
        start = pl.multiple_of(core_rows + index * EXTRA, 8)
        sources[pl.ds(start, EXTRA), 0:LANES] = extra
        sources[pl.ds(start, EXTRA), LANES : 2 * LANES] = jnp.zeros((EXTRA, LANES), jnp.float32)
        return carry

    lax.fori_loop(0, fields * planes_x, plane, 0)

    metric = jnp.concatenate([metric_y[...], metric_z[...]], axis=0)
    parts = factor(metric, ny, nz, wy)
    from_right, from_left, diagonal, to_right, to_left, before, after = parts
    for number, value in enumerate(v for part in parts for v in part):
        factors[number] = value
    for number, value in enumerate(to_right + to_left):
        chains[number] = value

    me = lax.axis_index("gz")
    mine = lax.broadcasted_iota(jnp.int32, (rows, LANES), 0) == ny + me
    even = (lax.broadcasted_iota(jnp.int32, (1, LANES), 1) & 1) == 0
    lane = lax.broadcasted_iota(jnp.int32, (1, LANES), 1)

    def own(values):
        return tuple(jnp.sum(jnp.where(mine, v, 0.0), axis=0, keepdims=True) for v in values)

    up, down = own(to_right), own(to_left)
    up_past, down_past = own(mm(before, to_right)), own(mm(after, to_left))
    unit = (1.0, 0.0, 0.0, 1.0)
    weights = []
    for column in range(2):
        same = jnp.where(even, unit[column], unit[2 + column])
        inside_up = cell_weights(up, column, even)
        inside_down = cell_weights(down, column, even)
        past_up = lane_roll(cell_weights(up_past, column, even), -2)
        past_down = lane_roll(cell_weights(down_past, column, even), 2)
        ends_up = jnp.where(lane < 2, same, jnp.where(lane >= LANES - 2, past_up, 0.0))
        ends_down = jnp.where(lane < 2, past_down, jnp.where(lane >= LANES - 2, same, 0.0))
        weights.append(
            (
                jnp.concatenate([inside_up, ends_up], axis=1),
                jnp.concatenate([inside_down, ends_down], axis=1),
            )
        )
    stack = []
    for k in range(1, partners + 1):
        upward = jnp.bitwise_xor(me, k) > me
        stack += [jnp.where(upward, w[0], w[1]) for w in weights]
    while len(stack) % 8:
        stack.append(jnp.zeros((1, 2 * LANES), jnp.float32))
    moments = lax.dot_general(
        jnp.concatenate(stack, axis=0),
        sources[...],
        (((1,), (1,)), ((), ())),
        precision=HIGHEST,
        preferred_element_type=jnp.float32,
    )
    for k in range(partners):
        messages[k][...] = moments[2 * k : 2 * k + 2]


def dense_inverse(columns, start, width, low_ref, high_ref):
    lane = lax.broadcasted_iota(jnp.int32, (1, LANES), 1)
    pairs = width // 2
    fits = width + 4 <= LANES

    def at(pair, number):
        return columns[pl.ds(start + 2 * pair, 1), number : number + 1]

    def two_by_two(pair, number):
        return tuple(at(pair, number + k) for k in range(4))

    def inject(pair, values, block, extra, extra_lane):
        top, bottom = values
        top = jnp.where(lane == 2 * pair, block[0], jnp.where(lane == 2 * pair + 1, block[1], top))
        bottom = jnp.where(lane == 2 * pair, block[2], jnp.where(lane == 2 * pair + 1, block[3], bottom))
        if extra is not None and fits:
            top = jnp.where(lane == extra_lane, extra[0], jnp.where(lane == extra_lane + 1, extra[1], top))
            bottom = jnp.where(
                lane == extra_lane, extra[2], jnp.where(lane == extra_lane + 1, extra[3], bottom)
            )
        return top, bottom

    zero = jnp.zeros((1, LANES), jnp.float32)
    low = high = (zero, zero)
    for step in range(pairs):
        i, j = step, pairs - 1 - step
        t = two_by_two(i, 4)
        low = (t[0] * low[0] + t[1] * low[1], t[2] * low[0] + t[3] * low[1])
        block = two_by_two(i, 8)
        extra = None
        if i == 0:
            b = two_by_two(0, 12)
            extra = mm(block, (b[0], b[2], b[1], b[3]))
        low = inject(i, low, block, extra, width)
        t = two_by_two(j, 0)
        high = (t[0] * high[0] + t[1] * high[1], t[2] * high[0] + t[3] * high[1])
        block = two_by_two(j, 8)
        extra = None
        if step == 0:
            b = two_by_two(pairs - 1, 16)
            extra = mm(block, (b[0], b[2], b[1], b[3]))
        high = inject(j, high, block, extra, width + 2)
        low_ref[2 * i : 2 * i + 1, :] = low[0]
        low_ref[2 * i + 1 : 2 * i + 2, :] = low[1]
        high_ref[2 * j : 2 * j + 1, :] = high[0]
        high_ref[2 * j + 1 : 2 * j + 2, :] = high[1]
    row = lax.broadcasted_iota(jnp.int32, (width, LANES), 0)
    column = lax.broadcasted_iota(jnp.int32, (width, LANES), 1)
    lower = (column <= row) | ((column >= width) & (column < width + 2))
    return jnp.where(lower, low_ref[0:width, :], high_ref[0:width, :])


def chain_product(chains, number, place, begin, end, reverse):
    def step(index, product):
        block = begin + end - 1 - index if reverse else index
        row, lane = place(block)
        return mm(product, tuple(chains[number + k, row, lane] for k in range(4)))

    one, zero = jnp.float32(1.0), jnp.float32(0.0)
    return lax.fori_loop(begin, end, step, (one, zero, zero, one))


def stage_plan(count):
    plan, stride = [], 1
    while stride < count:
        radix = 4 if count // stride >= 4 else 2
        plan.append((stride, radix))
        stride *= radix
    return plan


def second_kernel(
    ny, nz, count_y, wy, partners, chains, sources, factors, local, entering, inverse_y, weights_y, coefs, *scratch
):
    columns, low_ref, high_ref, spread = scratch
    me_z, me_y = lax.axis_index("gz"), lax.axis_index("gy")

    def transposed(row):
        rows = [factors[number, pl.ds(row, 1), :] for number in range(12)]
        rows += [factors[20 + number, pl.ds(row, 1), :] for number in range(8)]
        rows += [factors[12 + number, pl.ds(row, 1), :] for number in range(8)]
        rows.append(jnp.zeros((4, LANES), jnp.float32))
        return jnp.concatenate(rows, axis=0).T

    columns[...] = transposed(ny + me_z)
    inverse = dense_inverse(columns, 0, LANES, low_ref, high_ref)
    spread[0:LANES, :] = inverse
    spread[LANES : 2 * LANES, :] = jnp.zeros((LANES, LANES), jnp.float32)
    past = tuple(columns[LANES - 1 : LANES, 16 + k : 17 + k] for k in range(4))
    ahead = tuple(columns[0:1, 12 + k : 13 + k] for k in range(4))
    head0, head1 = spread[0:1, :], spread[1:2, :]
    tail0, tail1 = spread[LANES - 2 : LANES - 1, :], spread[LANES - 1 : LANES, :]
    for q in range(2):
        spread[LANES + q : LANES + q + 1, :] = past[2 * q] * tail0 + past[2 * q + 1] * tail1
        spread[2 * LANES - 2 + q : 2 * LANES - 1 + q, :] = ahead[2 * q] * head0 + ahead[2 * q + 1] * head1
    local[...] = jnp.dot(
        sources[...], spread[...], precision=HIGHEST, preferred_element_type=jnp.float32
    )

    entering[...] = jnp.zeros(entering.shape, jnp.float32)

    def place_z(block):
        return ny + block, 0

    def place_z_end(block):
        return ny + block, LANES - 1

    for k in range(1, partners + 1):
        other = jnp.bitwise_xor(me_z, k)
        lower = other < me_z
        up = chain_product(chains, 0, place_z, other + 1, me_z, False)
        down = chain_product(chains, 4, place_z_end, me_z + 1, other, True)
        for p in range(2):
            from_low = up[2 * p] * head0 + up[2 * p + 1] * head1
            from_high = down[2 * p] * tail0 + down[2 * p + 1] * tail1
            row = 2 * (k - 1) + p
            entering[row : row + 1, :] = jnp.where(lower, from_low, from_high)

    cell = me_y * wy
    columns[...] = transposed(cell // LANES)
    start = lax.rem(cell, LANES)
    inverse_y[...] = dense_inverse(columns, start, wy, low_ref, high_ref)
    row = lax.broadcasted_iota(jnp.int32, (wy, LANES), 0)
    extra_row = lax.broadcasted_iota(jnp.int32, (EXTRA, LANES), 0)
    unit = (1.0, 0.0, 0.0, 1.0)

    def head(number):
        return tuple(columns[pl.ds(start, 1), number + k : number + k + 1] for k in range(4))

    def tail(number):
        return tuple(columns[pl.ds(start + wy - 1, 1), number + k : number + k + 1] for k in range(4))

    past_up, past_down = mm(head(12), head(20)), mm(tail(16), tail(24))
    for column in range(2):
        for output, number in ((column, 20), (2 + column, 24)):
            even = columns[pl.ds(start, wy), number + column : number + column + 1]
            odd = columns[pl.ds(start, wy), number + 2 + column : number + 3 + column]
            weights_y[output, 0:wy, :] = jnp.where((row & 1) == 0, even, odd)
        for output, early, late in (
            (column, (past_up[column], past_up[2 + column]), (unit[column], unit[2 + column])),
            (2 + column, (unit[column], unit[2 + column]), (past_down[column], past_down[2 + column])),
        ):
            value = jnp.zeros((EXTRA, LANES), jnp.float32)
            for r, v in enumerate(early + late):
                value = jnp.where(extra_row == r, v, value)
            weights_y[output, wy : wy + EXTRA, :] = value

    def place_y(block):
        c = block * wy
        return c // LANES, lax.rem(c, LANES)

    def place_y_end(block):
        c = block * wy + wy - 1
        return c // LANES, lax.rem(c, LANES)

    base = 0
    for stride, radix in stage_plan(count_y):
        group = me_y // stride
        first = (group // radix) * radix
        for k in range(radix):
            other = first + jnp.bitwise_xor(group - first, k)
            entries = []
            if k > 0:
                up = chain_product(chains, 0, place_y, (other + 1) * stride, me_y, False)
                down = chain_product(chains, 4, place_y_end, me_y + 1, other * stride, True)
                is_low, is_high = other < group, other > group
                entries += [jnp.where(is_low, v, 0.0) for v in up]
                entries += [jnp.where(is_high, v, 0.0) for v in down]
            else:
                entries += [jnp.float32(0.0)] * 8
            entries += chain_product(
                chains, 0, place_y, (other + 1) * stride, (first + radix) * stride, False
            )
            entries += chain_product(chains, 4, place_y_end, first * stride, other * stride, True)
            for offset, value in enumerate(entries):
                coefs[base + offset] = value
            base += 16


def third_kernel(partners, wy, weights_y, local, entering, *refs):
    messages, (solved, carried) = refs[:partners], refs[partners:]
    planes = carried.shape[1]
    received = [m[...] for m in messages]
    padding = entering.shape[0] - 2 * partners
    if padding:
        received.append(jnp.zeros((padding, received[0].shape[1]), jnp.float32))
    received = jnp.concatenate(received, axis=0)
    solved[...] = local[...] + jnp.dot(
        received.T, entering[...], precision=HIGHEST, preferred_element_type=jnp.float32
    )

    def plane(index, carry):
        start = pl.multiple_of(index * wy, 8)
        core = solved[pl.ds(start, wy), :]
        start = pl.multiple_of(planes * wy + index * EXTRA, 8)
        extra = solved[pl.ds(start, EXTRA), :]
        for number in range(4):
            value = jnp.sum(core * weights_y[number, 0:wy, :], axis=0, keepdims=True)
            value = value + jnp.sum(extra * weights_y[number, wy : wy + EXTRA, :], axis=0, keepdims=True)
            carried[number, pl.ds(index, 1), :] = value
        return carry

    lax.fori_loop(0, planes, plane, 0)


def local_y_kernel(wy, solved, inverse_y, out):
    planes = out.shape[0]
    matrix = inverse_y[:, 0 : wy + EXTRA]

    def plane(index, carry):
        start = pl.multiple_of(index * wy, 8)
        core = solved[pl.ds(start, wy), :]
        start = pl.multiple_of(planes * wy + index * EXTRA, 8)
        both = jnp.concatenate([core, solved[pl.ds(start, EXTRA), :]], axis=0)
        out[index] = jnp.dot(matrix, both, precision=HIGHEST, preferred_element_type=jnp.float32)
        return carry

    lax.fori_loop(0, planes, plane, 0)


def combine(coefs, base, values, number):
    first = 0 if number in (0, 8) else 2
    out = [None, None]
    for k, value in values:
        for q in range(2):
            for p in range(2):
                term = coefs[base + 16 * k + number + 2 * p + q] * value[first + p]
                out[q] = term if out[q] is None else out[q] + term
    return out


def stage_kernel(base, stride, radix, narrow, has_entered, coefs, *refs):
    values = [(k, refs[k]) for k in range(radix)]
    position = radix
    entered = None
    if has_entered:
        entered = refs[position]
        position += 1
    message, entering = refs[position : position + 2]
    below = combine(coefs, base, values[1:], 0)
    above = combine(coefs, base, values[1:], 4)
    for row, value in enumerate(below + above):
        entering[row] = value if entered is None else value + entered[row]
    upward = combine(coefs, base, values, 8)
    downward = combine(coefs, base, values, 12)
    if narrow:
        group = lax.axis_index("gy") // (stride * radix)
        sends_up = lax.rem(group, 2) == 0
        for row in range(2):
            message[row] = jnp.where(sends_up, upward[row], downward[row])
    else:
        for row, value in enumerate(upward + downward):
            message[row] = value


def last_kernel(base, radix, narrow, wy, coefs, local, inverse_y, entered, *refs):
    messages, (out, st) = refs[: radix - 1], refs[radix - 1 :]
    values = [(k + 1, m) for k, m in enumerate(messages)]
    if narrow:
        values = [(k, (m[0], m[1], m[0], m[1])) for k, m in values]
    below = combine(coefs, base, values, 0)
    above = combine(coefs, base, values, 4)
    for row, value in enumerate(below + above):
        st[row] = value + entered[row]
    sides = [
        jnp.broadcast_to(inverse_y[:, c : c + 1], (wy, LANES)) for c in (0, 1, wy - 2, wy - 1)
    ]
    fields, planes_x = out.shape[:2]
    for field in range(fields):

        def plane(x, carry):
            index = field * planes_x + x
            value = local[index]
            for number in range(4):
                value = value + sides[number] * st[number, pl.ds(index, 1), :]
            out[field, x] = value
            return carry

        lax.fori_loop(0, planes_x, plane, 0)


VMEM = pl.BlockSpec(memory_space=pltpu.VMEM)
SMEM = pl.BlockSpec(memory_space=pltpu.SMEM)
PARAMS = pltpu.CompilerParams(vmem_limit_bytes=40 * 1024 * 1024)


def array(*shape):
    return jax.ShapeDtypeStruct(shape, jnp.float32)


def cost(flops, data):
    return pl.CostEstimate(flops=flops, bytes_accessed=data, transcendentals=0)


def on_device(mesh, flow, speed, metric_y, metric_z):
    fields, planes_x, wy, wz = flow.shape
    count_y, count_z = mesh.shape["gy"], mesh.shape["gz"]
    assert wz == LANES
    ny, nz = metric_y.shape[0] // LANES, metric_z.shape[0] // LANES
    planes = fields * planes_x
    rows = planes * (wy + EXTRA)
    partners = count_z - 1
    entering_rows = -(-2 * partners // 8) * 8
    outputs = pl.pallas_call(
        functools.partial(first_kernel, ny, nz, partners),
        out_shape=[array(rows, 2 * LANES), array(28, ny + nz, LANES), array(8, ny + nz, LANES)]
        + [array(2, rows)] * partners,
        in_specs=[VMEM] * 4,
        out_specs=[VMEM] * (3 + partners),
        scratch_shapes=[pltpu.VMEM((3, wy + 16, LANES), jnp.float32)],
        compiler_params=PARAMS,
        name="forcing_and_factor",
    )(flow, speed, metric_y.reshape(ny, LANES), metric_z.reshape(nz, LANES))
    sources, factors, chains = outputs[:3]

    def exchange(values, axis, count, stride, radix):
        received = []
        for k, value in zip(range(1, radix), values):
            pairs = [(i, i ^ (k * stride)) for i in range(count)]
            received.append(lax.ppermute(value, axis, pairs))
        return received

    received = exchange(outputs[3:], "gz", count_z, 1, count_z)
    plan = stage_plan(count_y)
    local, entering, inverse_y, weights_y, coefs = pl.pallas_call(
        functools.partial(second_kernel, ny, nz, count_y, wy, partners),
        out_shape=[
            array(rows, LANES),
            array(entering_rows, LANES),
            array(wy, LANES),
            array(4, wy + EXTRA, LANES),
            array(16 * sum(radix for _, radix in plan)),
        ],
        in_specs=[SMEM, VMEM, VMEM],
        out_specs=[VMEM] * 4 + [SMEM],
        scratch_shapes=[
            pltpu.VMEM((LANES, 32), jnp.float32),
            pltpu.VMEM((LANES, LANES), jnp.float32),
            pltpu.VMEM((LANES, LANES), jnp.float32),
            pltpu.VMEM((2 * LANES, LANES), jnp.float32),
        ],
        compiler_params=PARAMS,
        cost_estimate=cost(2 * rows * 256 * 128 * 6, 4 * rows * 384),
        name="local_z",
    )(chains, sources, factors)
    solved, carried = pl.pallas_call(
        functools.partial(third_kernel, partners, wy),
        out_shape=[array(rows, LANES), array(4, planes, LANES)],
        in_specs=[VMEM] * (3 + partners),
        out_specs=[VMEM] * 2,
        compiler_params=PARAMS,
        name="finish_z",
    )(weights_y, local, entering, *received)

    narrow = plan[-1][1] == 2 and len(plan) > 1
    base, entered, result = 0, None, None
    for number, (stride, radix) in enumerate(plan):
        received = exchange([carried] * (radix - 1), "gy", count_y, stride, radix)
        if number == 0:
            result = pl.pallas_call(
                functools.partial(local_y_kernel, wy),
                out_shape=array(planes, wy, LANES),
                in_specs=[VMEM] * 2,
                out_specs=VMEM,
                compiler_params=PARAMS,
                cost_estimate=cost(2 * rows * 128 * 128 * 6, 4 * rows * 256),
                name="local_y",
            )(solved, inverse_y)
        if number + 1 < len(plan):
            slim = narrow and number + 2 == len(plan)
            inputs = [carried] + received + ([entered] if entered is not None else [])
            carried, entered = pl.pallas_call(
                functools.partial(stage_kernel, base, stride, radix, slim, entered is not None),
                out_shape=[array(2 if slim else 4, planes, LANES), array(4, planes, LANES)],
                in_specs=[SMEM] + [VMEM] * len(inputs),
                out_specs=[VMEM] * 2,
                compiler_params=PARAMS,
                name="join_groups",
            )(coefs, *inputs)
            base += 16 * radix
        else:
            if entered is None:
                entered = jnp.zeros((4, planes, LANES), jnp.float32)
            return pl.pallas_call(
                functools.partial(last_kernel, base, radix, narrow, wy),
                out_shape=array(fields, planes_x, wy, wz),
                in_specs=[SMEM] + [VMEM] * (3 + len(received)),
                out_specs=VMEM,
                scratch_shapes=[pltpu.VMEM((4, planes, LANES), jnp.float32)],
                compiler_params=PARAMS,
                name="finish_y",
            )(coefs, result, inverse_y, entered, *received)


def solution(mesh):
    placed = (P(None, None, "gy", "gz"), P(None, "gy", "gz"), P(), P())
    return jax.shard_map(
        functools.partial(on_device, mesh),
        mesh=mesh,
        in_specs=placed,
        out_specs=P(None, None, "gy", "gz"),
        check_vma=False,
    )
```

profile of v0, /device:TPU:0, one launch (start us, length us, event | category | flops | bytes accessed | tf_op | source)
XLA Modules:
  0.0 47.4 jit_solution(7718447954329589006)
XLA Ops:
  0.0 1.3 %copy-done = f32[5,8,64,128]{3,2,1,0:T(8,128)S(1)} copy-done((f32[5,8,64,128]{3,2,1,0:T(8,128)S(1)}, f32[5,8,64,128]{3,2,1,0:T(8,128)}, u32[]{:S(2)}) %copy-start) | copy-done | bytes 1310744
  1.3 0.9 %copy-done.1 = f32[8,64,128]{2,1,0:T(8,128)S(1)} copy-done((f32[8,64,128]{2,1,0:T(8,128)S(1)}, f32[8,64,128]{2,1,0:T(8,128)}, u32[]{:S(2)}) %copy-start.1) | copy-done | bytes 262168
  2.3 0.7 %copy-done.2 = f32[512]{0:T(512)S(1)} copy-done((f32[512]{0:T(512)S(1)}, f32[512]{0:T(512)}, u32[]{:S(2)}) %copy-start.2) | copy-done | bytes 2072
  3.0 0.7 %copy-done.3 = f32[512]{0:T(512)S(1)} copy-done((f32[512]{0:T(512)S(1)}, f32[512]{0:T(512)}, u32[]{:S(2)}) %copy-start.3) | copy-done | bytes 2072
  3.6 9.7 %forcing_and_factor.1 = (f32[2880,256]{1,0:T(8,128)S(1)}, f32[28,8,128]{2,1,0:T(8,128)S(1)}, f32[8,8,128]{2,1,0:T(8,128)S(1)}, f32[2,2880]{1,0:T(2,128)S(1)}, f3...) custom-call(f32[5,8,64,128]{3,2,1,0:T(8,128)S(1)} %copy-done, f32[8,64,128]{2,1,0:T(8,128)S(1)} %copy-done.1, ...), custom_call_target="tpu_custom_call" | custom-call | tf_op jit(solution)/shard_map/forcing_and_factor/pallas_call | solution.py:556
  13.3 0.5 %collective-permute-start = (f32[2,2880]{1,0:T(2,128)S(1)}, f32[2,2880]{1,0:T(2,128)S(1)}, u32[]{:S(2)}, u32[]{:S(2)}) collective-permute-start(f32[2,2880]{1,0:T(2,128)S(1)} %get-tuple-element.27), channel_id=1, source_target_pairs={{0,8},{8,0},{16,24},{24,16},{1,9},{9,1},{17,25},{25,17},{2,10},{10... | collective-permute-start | bytes 69128 | tf_op jit(solution)/shard_map/ppermute | solution.py:572
  13.8 2.5 %collective-permute-start.1 = (f32[2,2880]{1,0:T(2,128)S(1)}, f32[2,2880]{1,0:T(2,128)S(1)}, u32[]{:S(2)}, u32[]{:S(2)}) collective-permute-start(f32[2,2880]{1,0:T(2,128)S(1)} %get-tuple-element.28), channel_id=1, source_target_pairs={{0,16},{8,24},{16,0},{24,8},{1,17},{9,25},{17,1},{25,9},{2,18},{10... | collective-permute-start | bytes 69128 | tf_op jit(solution)/shard_map/ppermute | solution.py:572
  16.3 0.1 collective-permute-start.2
  16.5 8.5 %local_z.1 = (f32[2880,128]{1,0:T(8,128)S(1)}, f32[8,128]{1,0:T(8,128)S(1)}, f32[64,128]{1,0:T(8,128)S(1)}, f32[4,72,128]{2,1,0:T(8,128)S(1)}, f32[96]{0:T(128)S(1)}) custom-call(f32[8,8,128]{2,1,0:T(8,128)S(1)} %get-tuple-element.20.chains, f32[2880,256]{1,0:T(8,128)S(1)} %get-tuple-element.21.sources, f32[28,8,128]{2,1,0:T(8,128)S(1)} %get-tuple-element.22.factors), custom_call_target="tpu_custom_call" | custom-call | flops 1132462080 | bytes 4423680 | tf_op jit(solution)/shard_map/local_z/pallas_call | solution.py:577
  25.0 0.0 collective-permute-done.refs_0_
  25.0 0.0 collective-permute-done.1.refs_1_
  25.0 0.0 collective-permute-done.2.refs_2_
  25.0 2.5 %finish_z.1 = (f32[2880,128]{1,0:T(8,128)S(1)}, f32[4,40,128]{2,1,0:T(8,128)S(1)}) custom-call(f32[4,72,128]{2,1,0:T(8,128)S(1)} %get-tuple-element.24.weights_y, f32[2880,128]{1,0:T(8,128)S(1)} %get-tuple-element.25.local, f32[8,128]{1,0:T(8,128)S(1)} %get-tuple-element.26.entering, f32[2,2880]{1,0:T(2,128)S(1)} %collective-permute-done.refs_0_, ...), custom_call_target="tpu_custom_call" | custom-call | tf_op jit(solution)/shard_map/finish_z/pallas_call | solution.py:598
  27.5 2.7 %collective-permute-start.5 = (f32[4,40,128]{2,1,0:T(8,128)S(1)}, f32[4,40,128]{2,1,0:T(8,128)S(1)}, u32[]{:S(2)}, u32[]{:S(2)}) collective-permute-start(f32[4,40,128]{2,1,0:T(8,128)S(1)} %get-tuple-element.32.refs_0_), channel_id=1, source_target_pairs={{0,3},{1,2},{2,1},{3,0},{4,7},{5,6},{6,5},{7,4},{8,11},{9,10},{10,... | collective-permute-start | bytes 245768 | tf_op jit(solution)/shard_map/ppermute | solution.py:572
  30.3 0.5 collective-permute-start.4
  30.7 0.4 collective-permute-start.3
  31.1 2.5 %collective-permute-done.5.refs_3_ = f32[4,40,128]{2,1,0:T(8,128)S(1)} collective-permute-done((f32[4,40,128]{2,1,0:T(8,128)S(1)}, f32[4,40,128]{2,1,0:T(8,128)S(1)}, u32[]{:S(2)}, u32[]{:S(2)}) %collective-permute-start.5) | collective-permute-done | bytes 81952 | tf_op jit(solution)/shard_map/ppermute | solution.py:572
  33.6 1.5 %collective-permute-done.4.refs_2_ = f32[4,40,128]{2,1,0:T(8,128)S(1)} collective-permute-done((f32[4,40,128]{2,1,0:T(8,128)S(1)}, f32[4,40,128]{2,1,0:T(8,128)S(1)}, u32[]{:S(2)}, u32[]{:S(2)}) %collective-permute-start.4) | collective-permute-done | bytes 81952 | tf_op jit(solution)/shard_map/ppermute | solution.py:572
  35.1 0.1 collective-permute-done.3.refs_1_
  35.2 0.6 %join_groups.1 = (f32[2,40,128]{2,1,0:T(8,128)S(1)}, f32[4,40,128]{2,1,0:T(8,128)S(1)}) custom-call(f32[96]{0:T(128)S(1)} %get-tuple-element.23.coefs, f32[4,40,128]{2,1,0:T(8,128)S(1)} %get-tuple-element.32.refs_0_, f32[4,40,128]{2,1,0:T(8,128)S(1)} %collective-permute-done.3.refs_1_, f32[4,40,128]{2,1,0:T(8,128)S(1)} %collective-permute-done.4.refs_2_, ...), custom_call_target="tpu_custom_call" | custom-call | tf_op jit(solution)/shard_map/join_groups/pallas_call | solution.py:624
  35.8 2.6 %collective-permute-start.6 = (f32[2,40,128]{2,1,0:T(8,128)S(1)}, f32[2,40,128]{2,1,0:T(8,128)S(1)}, u32[]{:S(2)}, u32[]{:S(2)}) collective-permute-start(f32[2,40,128]{2,1,0:T(8,128)S(1)} %get-tuple-element.34), channel_id=1, source_target_pairs={{0,4},{1,5},{2,6},{3,7},{4,0},{5,1},{6,2},{7,3},{8,12},{9,13},{10,... | collective-permute-start | bytes 122888 | tf_op jit(solution)/shard_map/ppermute | solution.py:572
  38.4 6.7 %local_y.1.local = f32[40,64,128]{2,1,0:T(8,128)S(1)} custom-call(f32[2880,128]{1,0:T(8,128)S(1)} %get-tuple-element.30.solved, f32[64,128]{1,0:T(8,128)S(1)} %get-tuple-element.31.inverse_y), custom_call_target="tpu_custom_call" | custom-call | flops 566231040 | bytes 2949120 | tf_op jit(solution)/shard_map/local_y/pallas_call | solution.py:612
  45.1 0.0 collective-permute-done.6.refs_0_
  45.1 2.2 %finish_y.1 = f32[5,8,64,128]{3,2,1,0:T(8,128)} custom-call(f32[96]{0:T(128)S(1)} %get-tuple-element.23.coefs, f32[40,64,128]{2,1,0:T(8,128)S(1)} %local_y.1.local, f32[64,128]{1,0:T(8,128)S(1)} %get-tuple-element.31.inverse_y, f32[4,40,128]{2,1,0:T(8,128)S(1)} %get-tuple-element.33.entered, f32[2,40,128]{2,1,0:T(8,128)S(1)} %collective-permute-done.6.refs_0_), custom_call_target="tpu_custom_call" | custom-call | tf_op jit(solution)/shard_map/finish_y/pallas_call | solution.py:636
  (4 shorter events, 0.0 us)
Async XLA Ops:
  0.0 1.3 %copy-start = (f32[5,8,64,128]{3,2,1,0:T(8,128)S(1)}, f32[5,8,64,128]{3,2,1,0:T(8,128)}, u32[]{:S(2)}) copy-start(f32[5,8,64,128]{3,2,1,0:T(8,128)} %flow.1) | copy-start | bytes 3932164
  1.3 0.9 %copy-start.1 = (f32[8,64,128]{2,1,0:T(8,128)S(1)}, f32[8,64,128]{2,1,0:T(8,128)}, u32[]{:S(2)}) copy-start(f32[8,64,128]{2,1,0:T(8,128)} %speed.1) | copy-start | bytes 786436
  2.3 0.7 %copy-start.2 = (f32[512]{0:T(512)S(1)}, f32[512]{0:T(512)}, u32[]{:S(2)}) copy-start(f32[512]{0:T(512)} %param.6) | copy-start | bytes 6148
  3.0 0.7 %copy-start.3 = (f32[512]{0:T(512)S(1)}, f32[512]{0:T(512)}, u32[]{:S(2)}) copy-start(f32[512]{0:T(512)} %param.7) | copy-start | bytes 6148
  13.3 11.7 %collective-permute-start = (f32[2,2880]{1,0:T(2,128)S(1)}, f32[2,2880]{1,0:T(2,128)S(1)}, u32[]{:S(2)}, u32[]{:S(2)}) collective-permute-start(f32[2,2880]{1,0:T(2,128)S(1)} %get-tuple-element.27), channel_id=1, source_target_pairs={{0,8},{8,0},{16,24},{24,16},{1,9},{9,1},{17,25},{25,17},{2,10},{10... | collective-permute-start | bytes 69128 | tf_op jit(solution)/shard_map/ppermute | solution.py:572
  13.8 11.2 %collective-permute-start.1 = (f32[2,2880]{1,0:T(2,128)S(1)}, f32[2,2880]{1,0:T(2,128)S(1)}, u32[]{:S(2)}, u32[]{:S(2)}) collective-permute-start(f32[2,2880]{1,0:T(2,128)S(1)} %get-tuple-element.28), channel_id=1, source_target_pairs={{0,16},{8,24},{16,0},{24,8},{1,17},{9,25},{17,1},{25,9},{2,18},{10... | collective-permute-start | bytes 69128 | tf_op jit(solution)/shard_map/ppermute | solution.py:572
  16.3 8.7 %collective-permute-start.2 = (f32[2,2880]{1,0:T(2,128)S(1)}, f32[2,2880]{1,0:T(2,128)S(1)}, u32[]{:S(2)}, u32[]{:S(2)}) collective-permute-start(f32[2,2880]{1,0:T(2,128)S(1)} %get-tuple-element.29), channel_id=1, source_target_pairs={{0,24},{8,16},{16,8},{24,0},{1,25},{9,17},{17,9},{25,1},{2,26},{10... | collective-permute-start | bytes 69128 | tf_op jit(solution)/shard_map/ppermute | solution.py:572
  27.5 6.0 %collective-permute-start.5 = (f32[4,40,128]{2,1,0:T(8,128)S(1)}, f32[4,40,128]{2,1,0:T(8,128)S(1)}, u32[]{:S(2)}, u32[]{:S(2)}) collective-permute-start(f32[4,40,128]{2,1,0:T(8,128)S(1)} %get-tuple-element.32.refs_0_), channel_id=1, source_target_pairs={{0,3},{1,2},{2,1},{3,0},{4,7},{5,6},{6,5},{7,4},{8,11},{9,10},{10,... | collective-permute-start | bytes 245768 | tf_op jit(solution)/shard_map/ppermute | solution.py:572
  30.3 4.8 %collective-permute-start.4 = (f32[4,40,128]{2,1,0:T(8,128)S(1)}, f32[4,40,128]{2,1,0:T(8,128)S(1)}, u32[]{:S(2)}, u32[]{:S(2)}) collective-permute-start(f32[4,40,128]{2,1,0:T(8,128)S(1)} %get-tuple-element.32.refs_0_), channel_id=1, source_target_pairs={{0,2},{1,3},{2,0},{3,1},{4,6},{5,7},{6,4},{7,5},{8,10},{9,11},{10,... | collective-permute-start | bytes 245768 | tf_op jit(solution)/shard_map/ppermute | solution.py:572
  30.7 4.4 %collective-permute-start.3 = (f32[4,40,128]{2,1,0:T(8,128)S(1)}, f32[4,40,128]{2,1,0:T(8,128)S(1)}, u32[]{:S(2)}, u32[]{:S(2)}) collective-permute-start(f32[4,40,128]{2,1,0:T(8,128)S(1)} %get-tuple-element.32.refs_0_), channel_id=1, source_target_pairs={{0,1},{1,0},{2,3},{3,2},{4,5},{5,4},{6,7},{7,6},{8,9},{9,8},{10,11... | collective-permute-start | bytes 245768 | tf_op jit(solution)/shard_map/ppermute | solution.py:572
  35.8 9.3 %collective-permute-start.6 = (f32[2,40,128]{2,1,0:T(8,128)S(1)}, f32[2,40,128]{2,1,0:T(8,128)S(1)}, u32[]{:S(2)}, u32[]{:S(2)}) collective-permute-start(f32[2,40,128]{2,1,0:T(8,128)S(1)} %get-tuple-element.34), channel_id=1, source_target_pairs={{0,4},{1,5},{2,6},{3,7},{4,0},{5,1},{6,2},{7,3},{8,12},{9,13},{10,... | collective-permute-start | bytes 122888 | tf_op jit(solution)/shard_map/ppermute | solution.py:572
where the time goes:
time: 47.6 us; the launch traced here: 47.4 us
  Pallas kernels  30.3 us (64%)
  starting transfers between devices  9.32 us (20%)
  waiting for transfers between devices  4.09 us (9%)
  local copies, waits for them, and re-layouts  3.63 us (8%)
    pallas_call x1, Pallas kernels, on_device(): pl.pallas_call(functools.partial(first_kernel, ny, nz, partners), out_sha...  9.71 us
    ppermute x7, starting transfers between devices, exchange(): received.append(lax.ppermute(value, axis, pairs))  9.32 us
    pallas_call x1, Pallas kernels, on_device(): pl.pallas_call(functools.partial(second_kernel, ny, nz, count_y, wy, part...  8.53 us
    pallas_call x1, Pallas kernels, on_device(): pl.pallas_call(functools.partial(local_y_kernel, wy), out_shape=array(pla...  6.65 us
    ppermute x7, waiting for transfers between devices, exchange(): received.append(lax.ppermute(value, axis, pairs))  4.09 us
    unnamed x8, local copies, waits for them, and re-layouts  3.63 us
    pallas_call x1, Pallas kernels, on_device(): pl.pallas_call(functools.partial(third_kernel, partners, wy), out_shape=[...  2.49 us
    pallas_call x1, Pallas kernels, on_device(): pl.pallas_call(functools.partial(last_kernel, base, radix, narrow, wy), o...  2.24 us
  transfers between devices with their start and end apart: 7, of which 3 were waited for; matrix products, arithmetic and copies ran while one was open for 0% of the time, Pallas kernels for 32%

commit v1 on v0

v1 whole, which is shorter than its diff:
```python
import functools

import jax
import jax.numpy as jnp
from jax import lax
from jax.experimental import pallas as pl
from jax.experimental.pallas import tpu as pltpu
from jax.sharding import PartitionSpec as P

viscous = 0.25
explicit_fourth = 0.04
implicit_fourth = 0.05
time_step = 1048576.0
LANES = 128
EXTRA = 8


def mm(a, b):
    return (
        a[0] * b[0] + a[1] * b[2],
        a[0] * b[1] + a[1] * b[3],
        a[2] * b[0] + a[3] * b[2],
        a[2] * b[1] + a[3] * b[3],
    )


def inverse_of_one_minus(a):
    p, q, r, s = 1.0 - a[0], -a[1], -a[2], 1.0 - a[3]
    d = 1.0 / (p * s - q * r)
    return (s * d, -q * d, -r * d, p * d)


def pick(condition, a, b):
    return tuple(jnp.where(condition, x, y) for x, y in zip(a, b))


def halves(x):
    high = x.astype(jnp.bfloat16)
    return high, (x - high.astype(jnp.float32)).astype(jnp.bfloat16)


def matmul(a, b, dims=(((1,), (0,)), ((), ()))):
    return lax.dot_general(a, b, dims, preferred_element_type=jnp.float32)


def lane_roll(x, by):
    return pltpu.roll(x, by % LANES, 1)


def row_roll(x, by):
    by = by % x.shape[0]
    return jnp.concatenate([x[x.shape[0] - by :], x[: x.shape[0] - by]], axis=0)


class Factor:
    def __init__(self, metric, ny, nz, wy):
        self.ny, self.nz, self.wy, self.rows = ny, nz, wy, ny + nz
        self.lane = lax.broadcasted_iota(jnp.int32, (self.rows, LANES), 1)
        self.row = lax.broadcasted_iota(jnp.int32, (self.rows, LANES), 0)
        self.block = jnp.where(self.row < ny, self.row, self.row - ny)
        self.to_end = jnp.where(self.row < ny, ny, nz) - 1 - self.block
        first = (self.lane == 0) & (self.block == 0)
        last = (self.lane == LANES - 1) & (self.to_end == 0)
        self.face_low = 0.5 * (jnp.where(first, metric, self.before(metric, 1)) + metric)
        self.face_high = 0.5 * (metric + jnp.where(last, metric, self.after(metric, 1)))

    def before(self, x, by):
        rolled = lane_roll(x, by)
        value = jnp.where(self.lane < by, row_roll(rolled, 1), rolled)
        return jnp.where((self.lane < by) & (self.block == 0), 0.0, value)

    def after(self, x, by):
        rolled = lane_roll(x, -by)
        value = jnp.where(self.lane >= LANES - by, row_roll(rolled, -1), rolled)
        return jnp.where((self.lane >= LANES - by) & (self.to_end == 0), 0.0, value)

    def sweep(self, sign, ratio, far):
        rows = self.rows
        back = self.before if sign > 0 else self.after
        if sign > 0:
            face_in, face_out, place = self.face_low, self.face_high, self.block
        else:
            face_in, face_out, place = self.face_high, self.face_low, self.to_end
        eps = 4.0 * implicit_fourth - implicit_fourth * back(ratio, 1)
        mass = (1.0 + 6.0 * implicit_fourth) - implicit_fourth * back(far, 2) - 2.0 * eps
        eps_in = back(eps, 1)
        scale = 1.0 / (face_in + 2.0 * eps_in)
        m = ((mass + face_in) * scale, mass - eps_in * eps_in * scale, scale, jnp.ones_like(scale))
        step = 1
        while step < LANES:
            inside = (self.lane >= step) if sign > 0 else (self.lane < LANES - step)
            m = pick(inside, mm(m, tuple(lane_roll(x, sign * step) for x in m)), m)
            step *= 2
        edge = LANES - 1 if sign > 0 else 0
        total = tuple(jnp.broadcast_to(x[:, edge : edge + 1], (rows, LANES)) for x in m)
        step = 1
        while step < max(self.ny, self.nz):
            total = pick(
                place >= step, mm(total, tuple(row_roll(x, sign * step) for x in total)), total
            )
            step *= 2
        top = jnp.where(place >= 1, row_roll(total[0], sign), 1.0)
        low = jnp.where(place >= 1, row_roll(total[2], sign), 0.0)
        eta = (m[0] * top + m[1] * low) / (m[2] * top + m[3] * low)
        one_over = 1.0 / (face_out + (eta + 2.0 * eps))
        return (face_out + eps) * one_over, implicit_fourth * one_over, one_over

    def finish(self, near_l, far_l, pivot_l, near_r, far_r):
        lane, block, to_end = self.lane, self.block, self.to_end
        even = (lane & 1) == 0
        near_l = jnp.where((to_end == 0) & (lane >= LANES - 1), 0.0, near_l)
        far_l = jnp.where((to_end == 0) & (lane >= LANES - 2), 0.0, far_l)
        near_r = jnp.where((block == 0) & (lane < 1), 0.0, near_r)
        far_r = jnp.where((block == 0) & (lane < 2), 0.0, far_r)

        def of_even(x):
            return jnp.where(even, x, lane_roll(x, 1))

        def of_odd(x):
            return jnp.where(even, lane_roll(x, -1), x)

        t0, t1, r0, r1 = of_even(near_l), of_odd(near_l), of_even(far_l), of_odd(far_l)
        from_right = (t0 * t1 - r0, -t0 * r1, t1, -r1)
        p1 = of_odd(pivot_l)
        left_inverse = (of_even(pivot_l) + t0 * t0 * p1, t0 * p1, t0 * p1, p1)
        s0, s1, q0, q1 = of_even(near_r), of_odd(near_r), of_even(far_r), of_odd(far_r)
        from_left = (-q0, s0, -s1 * q0, s1 * s0 - q1)
        from_left_after = tuple(self.after(x, 2) for x in from_left)
        from_right_before = tuple(self.before(x, 2) for x in from_right)
        diagonal = mm(inverse_of_one_minus(mm(from_right, from_left_after)), left_inverse)
        width = jnp.where(self.row < self.ny, self.wy, LANES)
        place = lane & (width - 1)
        right, left = from_right, from_left
        step = 2
        while step < LANES:
            right = pick(place + step < width, mm(right, tuple(lane_roll(x, -step) for x in right)), right)
            left = pick(place >= step, mm(left, tuple(lane_roll(x, step) for x in left)), left)
            step *= 2
        return from_right, from_left, diagonal, right, left, from_right_before, from_left_after


def cell_weights(chain, column, even):
    return jnp.where(even, chain[column], chain[2 + column])


def first_kernel(ny, nz, partners, flow_hbm, speed_hbm, metric_y, metric_z, *refs):
    high, low, factors, chains = refs[:4]
    messages = refs[4 : 4 + partners]
    flow, speed, metric, spread, arrived = refs[4 + partners :]
    fields, planes_x, wy, _ = flow.shape
    rows = ny + nz
    core_rows = fields * planes_x * wy

    copies = [
        pltpu.make_async_copy(metric_y, metric.at[0:ny], arrived.at[fields]),
        pltpu.make_async_copy(metric_z, metric.at[ny:rows], arrived.at[fields + 1]),
        pltpu.make_async_copy(speed_hbm, speed, arrived.at[fields + 2]),
    ]
    for copy in copies:
        copy.start()
    for field in range(fields):
        pltpu.make_async_copy(flow_hbm.at[field], flow.at[field], arrived.at[field]).start()

    lane = lax.broadcasted_iota(jnp.int32, (wy, LANES), 1)
    extra_row = lax.broadcasted_iota(jnp.int32, (EXTRA, LANES), 0)
    for slot in range(2):
        for part in range(3):
            spread[slot, part, 0:8, :] = jnp.zeros((8, LANES), jnp.float32)
            spread[slot, part, wy + 8 : wy + 16, :] = jnp.zeros((8, LANES), jnp.float32)
    side = time_step * (viscous + 4.0 * explicit_fourth)
    half = time_step * 0.5
    centre = time_step * (-6.0 * viscous - 12.0 * explicit_fourth)
    fourth = -time_step * explicit_fourth

    def store(start, column, value):
        first, second = halves(value)
        high[pl.ds(start, value.shape[0]), column : column + LANES] = first
        low[pl.ds(start, value.shape[0]), column : column + LANES] = second

    def one_field(field):
        values = [flow[field, x] for x in range(planes_x)]
        fluxes = [half * (values[x] * speed[x]) for x in range(planes_x)]
        extras = []
        for x in range(planes_x):
            u, flux, slot = values[x], fluxes[x], x % 2
            total = centre * u
            for other, sign in ((x + 1, -1), (x - 1, 1)):
                if 0 <= other < planes_x:
                    total = total + (time_step * viscous) * values[other]
                    total = total + fluxes[other] if sign > 0 else total - fluxes[other]
            scaled = side * u
            onward, backward, far = scaled + flux, scaled - flux, fourth * u
            spread[slot, 0, 8 : wy + 8, :] = onward
            spread[slot, 1, 8 : wy + 8, :] = backward
            spread[slot, 2, 8 : wy + 8, :] = far
            total = total + (spread[slot, 0, 7 : wy + 7, :] + spread[slot, 1, 9 : wy + 9, :])
            total = total + (spread[slot, 2, 6 : wy + 6, :] + spread[slot, 2, 10 : wy + 10, :])
            a, b = lane_roll(onward, 1), lane_roll(backward, -1)
            c, d = lane_roll(far, 2), lane_roll(far, -2)
            ends = jnp.where(lane < 2, c + jnp.where(lane < 1, a, 0.0), 0.0)
            ends = jnp.where(lane >= LANES - 2, d + jnp.where(lane >= LANES - 1, b, 0.0), ends)
            index = field * planes_x + x
            start = pl.multiple_of(index * wy, 16)
            store(start, 0, total + ((a + b) + (c + d) - ends))
            store(start, LANES, ends)
            above = spread[slot, 1, 7:15, :] + spread[slot, 2, 8:16, :]
            below = spread[slot, 0, wy + 5 : wy + 13, :] + spread[slot, 2, wy + 4 : wy + 12, :]
            extras.append(jnp.where(extra_row < 2, above, jnp.where(extra_row < 4, below, 0.0)))
            if len(extras) == 2:
                start = pl.multiple_of(core_rows + (index - 1) * EXTRA, 16)
                store(start, 0, jnp.concatenate(extras, axis=0))
                for ref in (high, low):
                    ref[pl.ds(start, 2 * EXTRA), LANES : 2 * LANES] = jnp.zeros(
                        (2 * EXTRA, LANES), jnp.bfloat16
                    )
                extras = []

    copies[0].wait()
    copies[1].wait()
    factor = Factor(metric[...], ny, nz, wy)
    copies[2].wait()

    def step(field, carry):
        pltpu.make_async_copy(flow_hbm.at[field], flow.at[field], arrived.at[field]).wait()
        left, right = carry
        left = factor.sweep(1, left[0], left[1])
        right = factor.sweep(-1, right[0], right[1])
        one_field(field)
        return left, right

    guess = (jnp.ones((rows, LANES), jnp.float32),) + (jnp.zeros((rows, LANES), jnp.float32),) * 2
    left, right = lax.fori_loop(0, fields, step, (guess, guess))

    parts = factor.finish(left[0], left[1], left[2], right[0], right[1])
    from_right, from_left, diagonal, to_right, to_left, before, after = parts
    for number, value in enumerate(v for part in parts for v in part):
        factors[number] = value
    for number, value in enumerate(to_right + to_left):
        chains[number] = value

    me = lax.axis_index("gz")
    mine = lax.broadcasted_iota(jnp.int32, (rows, LANES), 0) == ny + me
    even = (lax.broadcasted_iota(jnp.int32, (1, LANES), 1) & 1) == 0
    lane = lax.broadcasted_iota(jnp.int32, (1, LANES), 1)

    def own(values):
        return tuple(jnp.sum(jnp.where(mine, v, 0.0), axis=0, keepdims=True) for v in values)

    up, down = own(to_right), own(to_left)
    up_past, down_past = own(mm(before, to_right)), own(mm(after, to_left))
    unit = (1.0, 0.0, 0.0, 1.0)
    weights = []
    for column in range(2):
        same = jnp.where(even, unit[column], unit[2 + column])
        inside_up = cell_weights(up, column, even)
        inside_down = cell_weights(down, column, even)
        past_up = lane_roll(cell_weights(up_past, column, even), -2)
        past_down = lane_roll(cell_weights(down_past, column, even), 2)
        ends_up = jnp.where(lane < 2, same, jnp.where(lane >= LANES - 2, past_up, 0.0))
        ends_down = jnp.where(lane < 2, past_down, jnp.where(lane >= LANES - 2, same, 0.0))
        weights.append(
            (
                jnp.concatenate([inside_up, ends_up], axis=1),
                jnp.concatenate([inside_down, ends_down], axis=1),
            )
        )
    stack = []
    for k in range(1, partners + 1):
        upward = jnp.bitwise_xor(me, k) > me
        stack += [jnp.where(upward, w[0], w[1]) for w in weights]
    while len(stack) % 8:
        stack.append(jnp.zeros((1, 2 * LANES), jnp.float32))
    count = len(stack)
    stack = jnp.concatenate(stack, axis=0)
    first = stack.astype(jnp.bfloat16).astype(jnp.float32)
    both = jnp.concatenate([first, stack - first], axis=0).astype(jnp.bfloat16)
    across = (((1,), (1,)), ((), ()))
    on_high = matmul(both, high[...], across)
    on_low = matmul(both, low[...], across)
    moments = (on_high[:count] + on_high[count:]) + on_low[:count]
    for k in range(partners):
        messages[k][...] = moments[2 * k : 2 * k + 2]


def dense_inverse(columns, start, width, low_ref, high_ref):
    lane = lax.broadcasted_iota(jnp.int32, (1, LANES), 1)
    pairs = width // 2
    fits = width + 4 <= LANES

    def at(pair, number):
        return columns[pl.ds(start + 2 * pair, 1), number : number + 1]

    def two_by_two(pair, number):
        return tuple(at(pair, number + k) for k in range(4))

    def inject(pair, values, block, extra, extra_lane):
        top, bottom = values
        top = jnp.where(lane == 2 * pair, block[0], jnp.where(lane == 2 * pair + 1, block[1], top))
        bottom = jnp.where(lane == 2 * pair, block[2], jnp.where(lane == 2 * pair + 1, block[3], bottom))
        if extra is not None and fits:
            top = jnp.where(lane == extra_lane, extra[0], jnp.where(lane == extra_lane + 1, extra[1], top))
            bottom = jnp.where(
                lane == extra_lane, extra[2], jnp.where(lane == extra_lane + 1, extra[3], bottom)
            )
        return top, bottom

    zero = jnp.zeros((1, LANES), jnp.float32)
    low = high = (zero, zero)
    for step in range(pairs):
        i, j = step, pairs - 1 - step
        t = two_by_two(i, 4)
        low = (t[0] * low[0] + t[1] * low[1], t[2] * low[0] + t[3] * low[1])
        block = two_by_two(i, 8)
        extra = None
        if i == 0:
            b = two_by_two(0, 12)
            extra = mm(block, (b[0], b[2], b[1], b[3]))
        low = inject(i, low, block, extra, width)
        t = two_by_two(j, 0)
        high = (t[0] * high[0] + t[1] * high[1], t[2] * high[0] + t[3] * high[1])
        block = two_by_two(j, 8)
        extra = None
        if step == 0:
            b = two_by_two(pairs - 1, 16)
            extra = mm(block, (b[0], b[2], b[1], b[3]))
        high = inject(j, high, block, extra, width + 2)
        low_ref[2 * i : 2 * i + 1, :] = low[0]
        low_ref[2 * i + 1 : 2 * i + 2, :] = low[1]
        high_ref[2 * j : 2 * j + 1, :] = high[0]
        high_ref[2 * j + 1 : 2 * j + 2, :] = high[1]
    row = lax.broadcasted_iota(jnp.int32, (width, LANES), 0)
    column = lax.broadcasted_iota(jnp.int32, (width, LANES), 1)
    lower = (column <= row) | ((column >= width) & (column < width + 2))
    return jnp.where(lower, low_ref[0:width, :], high_ref[0:width, :])


def stage_plan(count):
    plan, stride = [], 1
    while stride < count:
        radix = 4 if count // stride >= 4 else 2
        plan.append((stride, radix))
        stride *= radix
    return plan


def transposed(factors, row):
    rows = [factors[number, pl.ds(row, 1), :] for number in range(12)]
    rows += [factors[20 + number, pl.ds(row, 1), :] for number in range(8)]
    rows += [factors[12 + number, pl.ds(row, 1), :] for number in range(8)]
    rows.append(jnp.zeros((4, LANES), jnp.float32))
    return jnp.concatenate(rows, axis=0).T


def chain_products(chains, number, place, blocks, begins, ends, masks, reverse):
    count = -(-len(begins) // 8) * 8
    row = lax.broadcasted_iota(jnp.int32, (count, LANES), 0)
    begin = jnp.zeros((count, LANES), jnp.int32)
    end, mask = begin, jnp.zeros((count, LANES), jnp.float32)
    for r, (b, e, m) in enumerate(zip(begins, ends, masks)):
        begin, end = jnp.where(row == r, b, begin), jnp.where(row == r, e, end)
        mask = jnp.where(row == r, m, mask)
    one, zero = jnp.ones((count, LANES), jnp.float32), jnp.zeros((count, LANES), jnp.float32)
    product = (one, zero, zero, one)
    for block in range(blocks - 1, -1, -1) if reverse else range(blocks):
        where = place(block)
        value = tuple(chains[number + k, where[0], where[1]] for k in range(4))
        product = pick((begin <= block) & (block < end), mm(product, value), product)
    return tuple(x * mask for x in product)


def truth(condition):
    return jnp.where(condition, 1.0, 0.0)


def second_kernel(ny, nz, count_z, wy, partners, chains, factors, matrix, entering, weights_y, *scratch):
    columns, low_ref, high_ref, rows_ref = scratch
    me_z, me_y = lax.axis_index("gz"), lax.axis_index("gy")

    columns[...] = transposed(factors, ny + me_z)
    inverse = dense_inverse(columns, 0, LANES, low_ref, high_ref)
    rows_ref[0:LANES, :] = inverse
    rows_ref[LANES : 2 * LANES, :] = jnp.zeros((LANES, LANES), jnp.float32)
    past = tuple(columns[LANES - 1 : LANES, 16 + k : 17 + k] for k in range(4))
    ahead = tuple(columns[0:1, 12 + k : 13 + k] for k in range(4))
    head0, head1 = rows_ref[0:1, :], rows_ref[1:2, :]
    tail0, tail1 = rows_ref[LANES - 2 : LANES - 1, :], rows_ref[LANES - 1 : LANES, :]
    for q in range(2):
        rows_ref[LANES + q : LANES + q + 1, :] = past[2 * q] * tail0 + past[2 * q + 1] * tail1
        rows_ref[2 * LANES - 2 + q : 2 * LANES - 1 + q, :] = ahead[2 * q] * head0 + ahead[2 * q + 1] * head1
    first, second = halves(rows_ref[...])
    matrix[0 : 2 * LANES, :] = first
    matrix[2 * LANES : 4 * LANES, :] = second
    matrix[4 * LANES : 6 * LANES, :] = first

    others = [jnp.bitwise_xor(me_z, k) for k in range(1, partners + 1)]
    always = [1.0] * partners
    up = chain_products(
        chains, 0, lambda b: (ny + b, 0), count_z, [o + 1 for o in others], [me_z] * partners, always, False
    )
    down = chain_products(
        chains, 4, lambda b: (ny + b, LANES - 1), count_z, [me_z + 1] * partners, others, always, True
    )
    stack = []
    for k, other in enumerate(others):
        for p in range(2):
            from_low = up[2 * p][k : k + 1] * head0 + up[2 * p + 1][k : k + 1] * head1
            from_high = down[2 * p][k : k + 1] * tail0 + down[2 * p + 1][k : k + 1] * tail1
            stack.append(jnp.where(other < me_z, from_low, from_high))
    while len(stack) % 8:
        stack.append(jnp.zeros((1, LANES), jnp.float32))
    stack = jnp.concatenate(stack, axis=0)
    first = stack.astype(jnp.bfloat16).astype(jnp.float32)
    entering[...] = jnp.concatenate([first, stack - first, first], axis=0)

    cell = me_y * wy
    columns[...] = transposed(factors, cell // LANES)
    start = lax.rem(cell, LANES)
    row = lax.broadcasted_iota(jnp.int32, (wy, LANES), 0)
    extra_row = lax.broadcasted_iota(jnp.int32, (EXTRA, LANES), 0)
    unit = (1.0, 0.0, 0.0, 1.0)

    def head(number):
        return tuple(columns[pl.ds(start, 1), number + k : number + k + 1] for k in range(4))

    def tail(number):
        return tuple(columns[pl.ds(start + wy - 1, 1), number + k : number + k + 1] for k in range(4))

    past_up, past_down = mm(head(12), head(20)), mm(tail(16), tail(24))
    for column in range(2):
        for output, number in ((column, 20), (2 + column, 24)):
            even = columns[pl.ds(start, wy), number + column : number + column + 1]
            odd = columns[pl.ds(start, wy), number + 2 + column : number + 3 + column]
            weights_y[output, 0:wy, :] = jnp.where((row & 1) == 0, even, odd)
        for output, early, late in (
            (column, (past_up[column], past_up[2 + column]), (unit[column], unit[2 + column])),
            (2 + column, (unit[column], unit[2 + column]), (past_down[column], past_down[2 + column])),
        ):
            value = jnp.zeros((EXTRA, LANES), jnp.float32)
            for r, v in enumerate(early + late):
                value = jnp.where(extra_row == r, v, value)
            weights_y[output, wy : wy + EXTRA, :] = value


def y_kernel(count_y, wy, chains, factors, unused, inverse_y, coefs, columns, low_ref, high_ref):
    me_y = lax.axis_index("gy")
    cell = me_y * wy
    columns[...] = transposed(factors, cell // LANES)
    start = lax.rem(cell, LANES)
    inverse_y[...] = dense_inverse(columns, start, wy, low_ref, high_ref)

    up, down = ([], [], []), ([], [], [])
    plan = stage_plan(count_y)
    for number, (stride, radix) in enumerate(plan):
        group = me_y // stride
        first = (group // radix) * radix
        others = [first + jnp.bitwise_xor(group - first, k) for k in range(radix)]
        for other in others[1:]:
            for lists, values in (
                (up, ((other + 1) * stride, me_y, truth(other < group))),
                (down, (me_y + 1, other * stride, truth(other > group))),
            ):
                for one, value in zip(lists, values):
                    one.append(value)
        if number + 1 < len(plan):
            for other in others:
                for lists, values in (
                    (up, ((other + 1) * stride, (first + radix) * stride, 1.0)),
                    (down, (first * stride, other * stride, 1.0)),
                ):
                    for one, value in zip(lists, values):
                        one.append(value)

    def place(block):
        return block * wy // LANES, block * wy % LANES

    def place_end(block):
        return place(block)[0], place(block)[1] + wy - 1

    for base, value in (
        (0, chain_products(chains, 0, place, count_y, *up, False)),
        (4, chain_products(chains, 4, place_end, count_y, *down, True)),
    ):
        for k in range(4):
            coefs[base + k] = value[k]


def third_kernel(partners, wy, weights_y, high, low, matrix, entering, *refs):
    messages, (solved, carried) = refs[:partners], refs[partners:]
    planes = carried.shape[1]
    received = [m[...] for m in messages]
    padding = entering.shape[0] // 3 - 2 * partners
    if padding:
        received.append(jnp.zeros((padding, received[0].shape[1]), jnp.float32))
    received = jnp.concatenate(received, axis=0)
    first = received.astype(jnp.bfloat16).astype(jnp.float32)
    received = jnp.concatenate([first, first, received - first], axis=0).T.astype(jnp.bfloat16)
    entered = entering[...].astype(jnp.bfloat16)
    parts = planes // 8
    total = planes * (wy + EXTRA)

    def solve(begin, size):
        rows = slice(begin, begin + size)
        left = jnp.concatenate([high[rows, :], high[rows, :], low[rows, :]], axis=1)
        return matmul(left, matrix[...]) + matmul(received[rows], entered)

    extra = solve(planes * wy, planes * EXTRA)
    solved[planes * wy : total, :] = extra
    for part in range(parts):
        core = solve(part * 8 * wy, 8 * wy)
        solved[part * 8 * wy : (part + 1) * 8 * wy, :] = core
        for number in range(4):
            lines = []
            for k in range(8):
                index = part * 8 + k
                value = jnp.sum(core[k * wy : (k + 1) * wy] * weights_y[number, 0:wy, :], axis=0, keepdims=True)
                past = extra[index * EXTRA : (index + 1) * EXTRA] * weights_y[number, wy : wy + EXTRA, :]
                lines.append(value + jnp.sum(past, axis=0, keepdims=True))
            carried[number, part * 8 : (part + 1) * 8, :] = jnp.concatenate(lines, axis=0)


def local_y_kernel(wy, solved, inverse_y, out):
    planes = out.shape[0]
    first, second = halves(inverse_y[:, 0 : wy + EXTRA])
    left = jnp.concatenate([first, second, first], axis=1)

    def part(index, carry):
        for k in range(8):
            number = index * 8 + k
            start = pl.multiple_of(number * wy, 8)
            core = solved[pl.ds(start, wy), :]
            start = pl.multiple_of(planes * wy + number * EXTRA, 8)
            both = jnp.concatenate([core, solved[pl.ds(start, EXTRA), :]], axis=0)
            top, rest = halves(both)
            out[number] = matmul(left, jnp.concatenate([top, top, rest], axis=0))
        return carry

    lax.fori_loop(0, planes // 8, part, 0)


def combine(coefs, side, row, values):
    first = 0 if side == 0 else 2
    out = [None, None]
    for k, value in enumerate(values):
        for q in range(2):
            for p in range(2):
                term = coefs[side + 2 * p + q, row + k : row + k + 1, :] * value[first + p]
                out[q] = term if out[q] is None else out[q] + term
    return out


def stage_kernel(base, stride, radix, narrow, has_entered, coefs, *refs):
    values = refs[:radix]
    position = radix
    entered = None
    if has_entered:
        entered = refs[position]
        position += 1
    message, entering = refs[position : position + 2]
    below = combine(coefs, 0, base, values[1:])
    above = combine(coefs, 4, base, values[1:])
    for row, value in enumerate(below + above):
        entering[row] = value if entered is None else value + entered[row]
    upward = combine(coefs, 0, base + radix - 1, values)
    downward = combine(coefs, 4, base + radix - 1, values)
    if narrow:
        group = lax.axis_index("gy") // (stride * radix)
        sends_up = lax.rem(group, 2) == 0
        for row in range(2):
            message[row] = jnp.where(sends_up, upward[row], downward[row])
    else:
        for row, value in enumerate(upward + downward):
            message[row] = value


def last_kernel(base, radix, narrow, wy, coefs, local, inverse_y, entered, *refs):
    messages, (out_hbm, out, sent) = refs[: radix - 1], refs[radix - 1 :]
    values = list(messages)
    if narrow:
        values = [(m[0], m[1], m[0], m[1]) for m in values]
    below = combine(coefs, 0, base, values)
    above = combine(coefs, 4, base, values)
    st = [value + entered[row] for row, value in enumerate(below + above)]
    sides = [
        jnp.broadcast_to(inverse_y[:, c : c + 1], (wy, LANES)) for c in (0, 1, wy - 2, wy - 1)
    ]
    fields, planes_x = out.shape[:2]
    copies = []
    for field in range(fields):
        for x in range(planes_x):
            index = field * planes_x + x
            value = local[index]
            for number in range(4):
                value = value + sides[number] * st[number][index : index + 1]
            out[field, x] = value
        copy = pltpu.make_async_copy(out.at[field], out_hbm.at[field], sent.at[field])
        copy.start()
        copies.append(copy)
    for copy in copies:
        copy.wait()


VMEM = pl.BlockSpec(memory_space=pltpu.VMEM)
HBM = pl.BlockSpec(memory_space=pltpu.HBM)
SMEM = pl.BlockSpec(memory_space=pltpu.SMEM)
PARAMS = pltpu.CompilerParams(vmem_limit_bytes=40 * 1024 * 1024)


def array(*shape):
    return jax.ShapeDtypeStruct(shape, jnp.float32)


def cost(flops, data):
    return pl.CostEstimate(flops=flops, bytes_accessed=data, transcendentals=0)


def on_device(mesh, flow, speed, metric_y, metric_z):
    fields, planes_x, wy, wz = flow.shape
    count_y, count_z = mesh.shape["gy"], mesh.shape["gz"]
    assert wz == LANES
    ny, nz = metric_y.shape[0] // LANES, metric_z.shape[0] // LANES
    planes = fields * planes_x
    rows = planes * (wy + EXTRA)
    partners = count_z - 1
    entering_rows = -(-2 * partners // 8) * 8
    half = jax.ShapeDtypeStruct((rows, 2 * LANES), jnp.bfloat16)
    outputs = pl.pallas_call(
        functools.partial(first_kernel, ny, nz, partners),
        out_shape=[half, half, array(28, ny + nz, LANES), array(8, ny + nz, LANES)]
        + [array(2, rows)] * partners,
        in_specs=[HBM] * 4,
        out_specs=[VMEM] * (4 + partners),
        scratch_shapes=[
            pltpu.VMEM(flow.shape, jnp.float32),
            pltpu.VMEM(speed.shape, jnp.float32),
            pltpu.VMEM((ny + nz, LANES), jnp.float32),
            pltpu.VMEM((2, 3, wy + 16, LANES), jnp.float32),
            pltpu.SemaphoreType.DMA((fields + 3,)),
        ],
        compiler_params=PARAMS,
        name="forcing_and_factor",
    )(flow, speed, metric_y.reshape(ny, LANES), metric_z.reshape(nz, LANES))
    high, low, factors, chains = outputs[:4]

    def exchange(values, axis, count, stride, radix):
        received = []
        for k, value in zip(range(1, radix), values):
            pairs = [(i, i ^ (k * stride)) for i in range(count)]
            received.append(lax.ppermute(value, axis, pairs))
        return received

    received = exchange(outputs[4:], "gz", count_z, 1, count_z)
    plan = stage_plan(count_y)
    work = [pltpu.VMEM((LANES, 32), jnp.float32)] + [pltpu.VMEM((LANES, LANES), jnp.float32)] * 2
    matrix, entering, weights_y = pl.pallas_call(
        functools.partial(second_kernel, ny, nz, count_z, wy, partners),
        out_shape=[
            jax.ShapeDtypeStruct((6 * LANES, LANES), jnp.bfloat16),
            array(3 * entering_rows, LANES),
            array(4, wy + EXTRA, LANES),
        ],
        in_specs=[SMEM, VMEM],
        out_specs=[VMEM] * 3,
        scratch_shapes=work + [pltpu.VMEM((2 * LANES, LANES), jnp.float32)],
        compiler_params=PARAMS,
        cost_estimate=cost(2 * rows * 256 * 128 * 6, 4 * rows * 384),
        name="inverse_z",
    )(chains, factors)
    solved, carried = pl.pallas_call(
        functools.partial(third_kernel, partners, wy),
        out_shape=[array(rows, LANES), array(4, planes, LANES)],
        in_specs=[VMEM] * (5 + partners),
        out_specs=[VMEM] * 2,
        compiler_params=PARAMS,
        name="finish_z",
    )(weights_y, high, low, matrix, entering, *received)

    narrow = plan[-1][1] == 2 and len(plan) > 1
    base, entered, result = 0, None, None
    for number, (stride, radix) in enumerate(plan):
        received = exchange([carried] * (radix - 1), "gy", count_y, stride, radix)
        if number == 0:
            entries = sum(2 * radix - 1 for _, radix in plan[:-1]) + plan[-1][1] - 1
            inverse_y, coefs = pl.pallas_call(
                functools.partial(y_kernel, count_y, wy),
                out_shape=[array(wy, LANES), array(8, -(-entries // 8) * 8, LANES)],
                in_specs=[SMEM, VMEM, HBM],
                out_specs=[VMEM] * 2,
                scratch_shapes=work,
                compiler_params=PARAMS,
                cost_estimate=cost(2 * rows * 128 * 128 * 6, 4 * rows * 256),
                name="inverse_y",
            )(chains, factors, carried)
            result = pl.pallas_call(
                functools.partial(local_y_kernel, wy),
                out_shape=array(planes, wy, LANES),
                in_specs=[VMEM] * 2,
                out_specs=VMEM,
                compiler_params=PARAMS,
                cost_estimate=cost(2 * rows * 128 * 128 * 6, 4 * rows * 256),
                name="local_y",
            )(solved, inverse_y)
        if number + 1 < len(plan):
            slim = narrow and number + 2 == len(plan)
            inputs = [carried] + received + ([entered] if entered is not None else [])
            carried, entered = pl.pallas_call(
                functools.partial(stage_kernel, base, stride, radix, slim, entered is not None),
                out_shape=[array(2 if slim else 4, planes, LANES), array(4, planes, LANES)],
                in_specs=[VMEM] * (1 + len(inputs)),
                out_specs=[VMEM] * 2,
                compiler_params=PARAMS,
                name="join_groups",
            )(coefs, *inputs)
            base += 2 * radix - 1
        else:
            if entered is None:
                entered = jnp.zeros((4, planes, LANES), jnp.float32)
            return pl.pallas_call(
                functools.partial(last_kernel, base, radix, narrow, wy),
                out_shape=array(fields, planes_x, wy, wz),
                in_specs=[VMEM] * (4 + len(received)),
                out_specs=HBM,
                scratch_shapes=[
                    pltpu.VMEM(flow.shape, jnp.float32),
                    pltpu.SemaphoreType.DMA((fields,)),
                ],
                compiler_params=PARAMS,
                name="finish_y",
            )(coefs, result, inverse_y, entered, *received)


def solution(mesh):
    placed = (P(None, None, "gy", "gz"), P(None, "gy", "gz"), P(), P())
    return jax.shard_map(
        functools.partial(on_device, mesh),
        mesh=mesh,
        in_specs=placed,
        out_specs=P(None, None, "gy", "gz"),
        check_vma=False,
    )
```

time: 47.6 us -> 32.4 us (0.68)
  Pallas kernels: 30.3 us -> 16.4 us
  waiting for transfers between devices: 4.09 us -> 2.68 us
    pallas_call x1, Pallas kernels: 6.65 us -> 1.54 us  [on_device(): pl.pallas_call(functools.partial(local_y_kernel, wy), out_shape=array(pla...]
    pallas_call x1, Pallas kernels: 9.71 us -> 5.55 us  [on_device(): pl.pallas_call(functools.partial(first_kernel, ny, nz, partners), out_sha...]
    pallas_call x1 -> x2, Pallas kernels: 8.53 us -> 5.82 us  [the longest x1 3.61 us: on_device(): pl.pallas_call(functools.partial(second_kernel, ny, nz, count_z, wy, part...]
    ppermute x7, waiting for transfers between devices: 4.09 us -> 2.68 us  [exchange(): received.append(lax.ppermute(value, axis, pairs))]
    pallas_call x1, Pallas kernels: 2.49 us -> 1.82 us  [on_device(): pl.pallas_call(functools.partial(third_kernel, partners, wy), out_shape=[...]
    pallas_call x1, Pallas kernels: 2.24 us -> 1.59 us  [on_device(): pl.pallas_call(functools.partial(last_kernel, base, radix, narrow, wy), o...]
    pallas_call x1, Pallas kernels: 0.63 us -> 0.08 us  [on_device(): pl.pallas_call(functools.partial(stage_kernel, base, stride, radix, slim,...]
  transfers between devices with their start and end apart: 7 -> 7, of which waited for: 3 -> 3; matrix products, arithmetic and copies ran while one was open for 0% -> 0% of each run, Pallas kernels for 32% -> 23%
where the time goes in v1:
time: 32.4 us; the launch traced here: 32.2 us
  Pallas kernels  16.4 us (51%)
  starting transfers between devices  9.42 us (29%)
  local copies, waits for them, and re-layouts  3.63 us (11%)
  waiting for transfers between devices  2.68 us (8%)
    ppermute x7, starting transfers between devices, exchange(): received.append(lax.ppermute(value, axis, pairs))  9.42 us
    pallas_call x1, Pallas kernels, on_device(): pl.pallas_call(functools.partial(first_kernel, ny, nz, partners), out_sha...  5.55 us
    unnamed x8, local copies, waits for them, and re-layouts  3.63 us
    pallas_call x1, Pallas kernels, on_device(): pl.pallas_call(functools.partial(second_kernel, ny, nz, count_z, wy, part...  3.61 us
    ppermute x7, waiting for transfers between devices, exchange(): received.append(lax.ppermute(value, axis, pairs))  2.68 us
    pallas_call x1, Pallas kernels, on_device(): pl.pallas_call(functools.partial(y_kernel, count_y, wy), out_shape=[array...  2.21 us
    pallas_call x1, Pallas kernels, on_device(): pl.pallas_call(functools.partial(third_kernel, partners, wy), out_shape=[...  1.82 us
    pallas_call x1, Pallas kernels, on_device(): pl.pallas_call(functools.partial(last_kernel, base, radix, narrow, wy), o...  1.59 us
  transfers between devices with their start and end apart: 7, of which 3 were waited for; matrix products, arithmetic and copies ran while one was open for 0% of the time, Pallas kernels for 23%

profile of v1, /device:TPU:0, one launch (start us, length us, event | category | flops | bytes accessed | tf_op | source)
XLA Modules:
  0.0 32.2 jit_solution(780208902963525718)
XLA Ops:
  0.0 1.3 %copy-done = f32[5,8,64,128]{3,2,1,0:T(8,128)S(1)} copy-done((f32[5,8,64,128]{3,2,1,0:T(8,128)S(1)}, f32[5,8,64,128]{3,2,1,0:T(8,128)}, u32[]{:S(2)}) %copy-start) | copy-done | bytes 1310744
  1.3 0.9 %copy-done.1 = f32[8,64,128]{2,1,0:T(8,128)S(1)} copy-done((f32[8,64,128]{2,1,0:T(8,128)S(1)}, f32[8,64,128]{2,1,0:T(8,128)}, u32[]{:S(2)}) %copy-start.1) | copy-done | bytes 262168
  2.3 0.7 %copy-done.2 = f32[512]{0:T(512)S(1)} copy-done((f32[512]{0:T(512)S(1)}, f32[512]{0:T(512)}, u32[]{:S(2)}) %copy-start.2) | copy-done | bytes 2072
  3.0 0.7 %copy-done.3 = f32[512]{0:T(512)S(1)} copy-done((f32[512]{0:T(512)S(1)}, f32[512]{0:T(512)}, u32[]{:S(2)}) %copy-start.3) | copy-done | bytes 2072
  3.6 5.5 %forcing_and_factor.1 = (bf16[2880,256]{1,0:T(8,128)(2,1)S(1)}, bf16[2880,256]{1,0:T(8,128)(2,1)S(1)}, f32[28,8,128]{2,1,0:T(8,128)S(1)}, f32[8,8,128]{2,1,0:T(8...) custom-call(f32[5,8,64,128]{3,2,1,0:T(8,128)S(1)} %copy-done, ...), custom_call_target="tpu_custom_call" | custom-call | tf_op jit(solution)/shard_map/forcing_and_factor/pallas_call | solution.py:626
  9.2 0.5 %collective-permute-start = (f32[2,2880]{1,0:T(2,128)S(1)}, f32[2,2880]{1,0:T(2,128)S(1)}, u32[]{:S(2)}, u32[]{:S(2)}) collective-permute-start(f32[2,2880]{1,0:T(2,128)S(1)} %get-tuple-element.28), channel_id=1, source_target_pairs={{0,8},{8,0},{16,24},{24,16},{1,9},{9,1},{17,25},{25,17},{2,10},{10... | collective-permute-start | bytes 69128 | tf_op jit(solution)/shard_map/ppermute | solution.py:648
  9.7 2.6 %collective-permute-start.1 = (f32[2,2880]{1,0:T(2,128)S(1)}, f32[2,2880]{1,0:T(2,128)S(1)}, u32[]{:S(2)}, u32[]{:S(2)}) collective-permute-start(f32[2,2880]{1,0:T(2,128)S(1)} %get-tuple-element.29), channel_id=1, source_target_pairs={{0,16},{8,24},{16,0},{24,8},{1,17},{9,25},{17,1},{25,9},{2,18},{10... | collective-permute-start | bytes 69128 | tf_op jit(solution)/shard_map/ppermute | solution.py:648
  12.3 0.1 collective-permute-start.2
  12.3 3.6 %inverse_z.1 = (bf16[768,128]{1,0:T(8,128)(2,1)S(1)}, f32[24,128]{1,0:T(8,128)S(1)}, f32[4,72,128]{2,1,0:T(8,128)S(1)}) custom-call(f32[8,8,128]{2,1,0:T(8,128)S(1)} %get-tuple-element.21.chains, f32[28,8,128]{2,1,0:T(8,128)S(1)} %get-tuple-element.22.factors), custom_call_target="tpu_custom_call" | custom-call | flops 1132462080 | bytes 4423680 | tf_op jit(solution)/shard_map/inverse_z/pallas_call | solution.py:654
  16.0 0.0 collective-permute-done.refs_0_
  16.0 0.0 collective-permute-done.1.refs_1_
  16.0 1.8 %finish_z.1 = (f32[2880,128]{1,0:T(8,128)S(1)}, f32[4,40,128]{2,1,0:T(8,128)S(1)}) custom-call(f32[4,72,128]{2,1,0:T(8,128)S(1)} %get-tuple-element.23.weights_y, bf16[2880,256]{1,0:T(8,128)(2,1)S(1)} %get-tuple-element.24.high, bf16[2880,256]{1,0:T(8,128)(2,1)S(1)} %get-tuple-element.25.low, bf16[768,128]{1,0:T(8,128)(2,1)S(1)} %get-tuple-element.26.matrix, ...), custom_call_target="tpu_custom_call" | custom-call | tf_op jit(solution)/shard_map/finish_z/pallas_call | solution.py:668
  17.8 2.8 %collective-permute-start.5 = (f32[4,40,128]{2,1,0:T(8,128)S(1)}, f32[4,40,128]{2,1,0:T(8,128)S(1)}, u32[]{:S(2)}, u32[]{:S(2)}) collective-permute-start(f32[4,40,128]{2,1,0:T(8,128)S(1)} %get-tuple-element.31.unused.refs_0_), channel_id=1, source_target_pairs={{0,3},{1,2},{2,1},{3,0},{4,7},{5,6},{6,5},{7,4},{8,11},{9,10},{10,... | collective-permute-start | bytes 245768 | tf_op jit(solution)/shard_map/ppermute | solution.py:648
  20.6 0.4 %collective-permute-start.4 = (f32[4,40,128]{2,1,0:T(8,128)S(1)}, f32[4,40,128]{2,1,0:T(8,128)S(1)}, u32[]{:S(2)}, u32[]{:S(2)}) collective-permute-start(f32[4,40,128]{2,1,0:T(8,128)S(1)} %get-tuple-element.31.unused.refs_0_), channel_id=1, source_target_pairs={{0,2},{1,3},{2,0},{3,1},{4,6},{5,7},{6,4},{7,5},{8,10},{9,11},{10,... | collective-permute-start | bytes 245768 | tf_op jit(solution)/shard_map/ppermute | solution.py:648
  21.1 0.3 collective-permute-start.3
  21.4 2.2 %inverse_y.1 = (f32[64,128]{1,0:T(8,128)S(1)}, f32[8,8,128]{2,1,0:T(8,128)S(1)}) custom-call(f32[8,8,128]{2,1,0:T(8,128)S(1)} %get-tuple-element.21.chains, f32[28,8,128]{2,1,0:T(8,128)S(1)} %get-tuple-element.22.factors, f32[4,40,128]{2,1,0:T(8,128)S(1)} %get-tuple-element.31.unused.refs_0_), custom_call_target="tpu_custom_call" | custom-call | flops 566231040 | bytes 2949120 | tf_op jit(solution)/shard_map/inverse_y/pallas_call | solution.py:683
  23.6 0.4 %collective-permute-done.5.refs_3_ = f32[4,40,128]{2,1,0:T(8,128)S(1)} collective-permute-done((f32[4,40,128]{2,1,0:T(8,128)S(1)}, f32[4,40,128]{2,1,0:T(8,128)S(1)}, u32[]{:S(2)}, u32[]{:S(2)}) %collective-permute-start.5) | collective-permute-done | bytes 81952 | tf_op jit(solution)/shard_map/ppermute | solution.py:648
  24.0 1.6 %collective-permute-done.4.refs_2_ = f32[4,40,128]{2,1,0:T(8,128)S(1)} collective-permute-done((f32[4,40,128]{2,1,0:T(8,128)S(1)}, f32[4,40,128]{2,1,0:T(8,128)S(1)}, u32[]{:S(2)}, u32[]{:S(2)}) %collective-permute-start.4) | collective-permute-done | bytes 81952 | tf_op jit(solution)/shard_map/ppermute | solution.py:648
  25.5 0.0 collective-permute-done.3.refs_1_
  25.5 0.1 join_groups.1
  25.6 2.7 %collective-permute-start.6 = (f32[2,40,128]{2,1,0:T(8,128)S(1)}, f32[2,40,128]{2,1,0:T(8,128)S(1)}, u32[]{:S(2)}, u32[]{:S(2)}) collective-permute-start(f32[2,40,128]{2,1,0:T(8,128)S(1)} %get-tuple-element.36), channel_id=1, source_target_pairs={{0,4},{1,5},{2,6},{3,7},{4,0},{5,1},{6,2},{7,3},{8,12},{9,13},{10,... | collective-permute-start | bytes 122888 | tf_op jit(solution)/shard_map/ppermute | solution.py:648
  28.3 1.5 %local_y.1.local = f32[40,64,128]{2,1,0:T(8,128)S(1)} custom-call(f32[2880,128]{1,0:T(8,128)S(1)} %get-tuple-element.33.solved, f32[64,128]{1,0:T(8,128)S(1)} %get-tuple-element.34.inverse_y), custom_call_target="tpu_custom_call" | custom-call | flops 566231040 | bytes 2949120 | tf_op jit(solution)/shard_map/local_y/pallas_call | solution.py:693
  29.9 0.7 %collective-permute-done.6.refs_0_ = f32[2,40,128]{2,1,0:T(8,128)S(1)} collective-permute-done((f32[2,40,128]{2,1,0:T(8,128)S(1)}, f32[2,40,128]{2,1,0:T(8,128)S(1)}, u32[]{:S(2)}, u32[]{:S(2)}) %collective-permute-start.6) | collective-permute-done | bytes 40992 | tf_op jit(solution)/shard_map/ppermute | solution.py:648
  30.6 1.6 %finish_y.1 = f32[5,8,64,128]{3,2,1,0:T(8,128)} custom-call(f32[8,8,128]{2,1,0:T(8,128)S(1)} %get-tuple-element.32.coefs, f32[40,64,128]{2,1,0:T(8,128)S(1)} %local_y.1.local, f32[64,128]{1,0:T(8,128)S(1)} %get-tuple-element.34.inverse_y, f32[4,40,128]{2,1,0:T(8,128)S(1)} %get-tuple-element.35.entered, f32[2,40,128]{2,1,0:T(8,128)S(1)} %collective-permute-done.6.refs_0_), custom_call_target="tpu_custom_call" | custom-call | tf_op jit(solution)/shard_map/finish_y/pallas_call | solution.py:717
  (5 shorter events, 0.0 us)
Async XLA Ops:
  0.0 1.3 %copy-start = (f32[5,8,64,128]{3,2,1,0:T(8,128)S(1)}, f32[5,8,64,128]{3,2,1,0:T(8,128)}, u32[]{:S(2)}) copy-start(f32[5,8,64,128]{3,2,1,0:T(8,128)} %flow_hbm.1) | copy-start | bytes 3932164
  1.3 0.9 %copy-start.1 = (f32[8,64,128]{2,1,0:T(8,128)S(1)}, f32[8,64,128]{2,1,0:T(8,128)}, u32[]{:S(2)}) copy-start(f32[8,64,128]{2,1,0:T(8,128)} %speed_hbm.1) | copy-start | bytes 786436
  2.3 0.7 %copy-start.2 = (f32[512]{0:T(512)S(1)}, f32[512]{0:T(512)}, u32[]{:S(2)}) copy-start(f32[512]{0:T(512)} %param.6) | copy-start | bytes 6148
  3.0 0.7 %copy-start.3 = (f32[512]{0:T(512)S(1)}, f32[512]{0:T(512)}, u32[]{:S(2)}) copy-start(f32[512]{0:T(512)} %param.7) | copy-start | bytes 6148
  9.2 6.8 %collective-permute-start = (f32[2,2880]{1,0:T(2,128)S(1)}, f32[2,2880]{1,0:T(2,128)S(1)}, u32[]{:S(2)}, u32[]{:S(2)}) collective-permute-start(f32[2,2880]{1,0:T(2,128)S(1)} %get-tuple-element.28), channel_id=1, source_target_pairs={{0,8},{8,0},{16,24},{24,16},{1,9},{9,1},{17,25},{25,17},{2,10},{10... | collective-permute-start | bytes 69128 | tf_op jit(solution)/shard_map/ppermute | solution.py:648
  9.7 6.3 %collective-permute-start.1 = (f32[2,2880]{1,0:T(2,128)S(1)}, f32[2,2880]{1,0:T(2,128)S(1)}, u32[]{:S(2)}, u32[]{:S(2)}) collective-permute-start(f32[2,2880]{1,0:T(2,128)S(1)} %get-tuple-element.29), channel_id=1, source_target_pairs={{0,16},{8,24},{16,0},{24,8},{1,17},{9,25},{17,1},{25,9},{2,18},{10... | collective-permute-start | bytes 69128 | tf_op jit(solution)/shard_map/ppermute | solution.py:648
  12.3 3.7 %collective-permute-start.2 = (f32[2,2880]{1,0:T(2,128)S(1)}, f32[2,2880]{1,0:T(2,128)S(1)}, u32[]{:S(2)}, u32[]{:S(2)}) collective-permute-start(f32[2,2880]{1,0:T(2,128)S(1)} %get-tuple-element.30), channel_id=1, source_target_pairs={{0,24},{8,16},{16,8},{24,0},{1,25},{9,17},{17,9},{25,1},{2,26},{10... | collective-permute-start | bytes 69128 | tf_op jit(solution)/shard_map/ppermute | solution.py:648
  17.8 6.2 %collective-permute-start.5 = (f32[4,40,128]{2,1,0:T(8,128)S(1)}, f32[4,40,128]{2,1,0:T(8,128)S(1)}, u32[]{:S(2)}, u32[]{:S(2)}) collective-permute-start(f32[4,40,128]{2,1,0:T(8,128)S(1)} %get-tuple-element.31.unused.refs_0_), channel_id=1, source_target_pairs={{0,3},{1,2},{2,1},{3,0},{4,7},{5,6},{6,5},{7,4},{8,11},{9,10},{10,... | collective-permute-start | bytes 245768 | tf_op jit(solution)/shard_map/ppermute | solution.py:648
  20.6 4.9 %collective-permute-start.4 = (f32[4,40,128]{2,1,0:T(8,128)S(1)}, f32[4,40,128]{2,1,0:T(8,128)S(1)}, u32[]{:S(2)}, u32[]{:S(2)}) collective-permute-start(f32[4,40,128]{2,1,0:T(8,128)S(1)} %get-tuple-element.31.unused.refs_0_), channel_id=1, source_target_pairs={{0,2},{1,3},{2,0},{3,1},{4,6},{5,7},{6,4},{7,5},{8,10},{9,11},{10,... | collective-permute-start | bytes 245768 | tf_op jit(solution)/shard_map/ppermute | solution.py:648
  21.1 4.4 %collective-permute-start.3 = (f32[4,40,128]{2,1,0:T(8,128)S(1)}, f32[4,40,128]{2,1,0:T(8,128)S(1)}, u32[]{:S(2)}, u32[]{:S(2)}) collective-permute-start(f32[4,40,128]{2,1,0:T(8,128)S(1)} %get-tuple-element.31.unused.refs_0_), channel_id=1, source_target_pairs={{0,1},{1,0},{2,3},{3,2},{4,5},{5,4},{6,7},{7,6},{8,9},{9,8},{10,11... | collective-permute-start | bytes 245768 | tf_op jit(solution)/shard_map/ppermute | solution.py:648
  25.6 5.0 %collective-permute-start.6 = (f32[2,40,128]{2,1,0:T(8,128)S(1)}, f32[2,40,128]{2,1,0:T(8,128)S(1)}, u32[]{:S(2)}, u32[]{:S(2)}) collective-permute-start(f32[2,40,128]{2,1,0:T(8,128)S(1)} %get-tuple-element.36), channel_id=1, source_target_pairs={{0,4},{1,5},{2,6},{3,7},{4,0},{5,1},{6,2},{7,3},{8,12},{9,13},{10,... | collective-permute-start | bytes 122888 | tf_op jit(solution)/shard_map/ppermute | solution.py:648

commit v2 on v1

--- a/solution.py
+++ b/solution.py
@@ -73,6 +73,16 @@
         rolled = lane_roll(x, -by)
         value = jnp.where(self.lane >= LANES - by, row_roll(rolled, -1), rolled)
         return jnp.where((self.lane >= LANES - by) & (self.to_end == 0), 0.0, value)
+
+    def guess(self, sign):
+        face = self.face_high if sign > 0 else self.face_low
+        if sign > 0:
+            cell = self.lane + LANES * self.block
+        else:
+            cell = LANES - 1 - self.lane + LANES * self.to_end
+        near = face / (cell + 1).astype(jnp.float32)
+        one_over = 1.0 / (face + jnp.sqrt(face + near * near))
+        return face * one_over, implicit_fourth * one_over, one_over
 
     def sweep(self, sign, ratio, far):
         rows = self.rows
@@ -200,14 +210,15 @@
             ends = jnp.where(lane < 2, c + jnp.where(lane < 1, a, 0.0), 0.0)
             ends = jnp.where(lane >= LANES - 2, d + jnp.where(lane >= LANES - 1, b, 0.0), ends)
             index = field * planes_x + x
-            start = pl.multiple_of(index * wy, 16)
+            start = index * wy if isinstance(index, int) else pl.multiple_of(index * wy, 16)
             store(start, 0, total + ((a + b) + (c + d) - ends))
             store(start, LANES, ends)
             above = spread[slot, 1, 7:15, :] + spread[slot, 2, 8:16, :]
             below = spread[slot, 0, wy + 5 : wy + 13, :] + spread[slot, 2, wy + 4 : wy + 12, :]
             extras.append(jnp.where(extra_row < 2, above, jnp.where(extra_row < 4, below, 0.0)))
             if len(extras) == 2:
-                start = pl.multiple_of(core_rows + (index - 1) * EXTRA, 16)
+                start = core_rows + (index - 1) * EXTRA
+                start = start if isinstance(index, int) else pl.multiple_of(start, 16)
                 store(start, 0, jnp.concatenate(extras, axis=0))
                 for ref in (high, low):
                     ref[pl.ds(start, 2 * EXTRA), LANES : 2 * LANES] = jnp.zeros(
@@ -220,16 +231,23 @@
     factor = Factor(metric[...], ny, nz, wy)
     copies[2].wait()
 
-    def step(field, carry):
+    def arrive(field):
         pltpu.make_async_copy(flow_hbm.at[field], flow.at[field], arrived.at[field]).wait()
+
+    def step(index, carry):
         left, right = carry
         left = factor.sweep(1, left[0], left[1])
         right = factor.sweep(-1, right[0], right[1])
+        for k in range(2):
+            arrive(2 * index + k)
+            one_field(2 * index + k)
+        return left, right
+
+    assert fields // 2 >= 2
+    left, right = lax.fori_loop(0, fields // 2, step, (factor.guess(1), factor.guess(-1)))
+    for field in range(fields // 2 * 2, fields):
+        arrive(field)
         one_field(field)
-        return left, right
-
-    guess = (jnp.ones((rows, LANES), jnp.float32),) + (jnp.zeros((rows, LANES), jnp.float32),) * 2
-    left, right = lax.fori_loop(0, fields, step, (guess, guess))
 
     parts = factor.finish(left[0], left[1], left[2], right[0], right[1])
     from_right, from_left, diagonal, to_right, to_left, before, after = parts
@@ -282,56 +300,73 @@
         messages[k][...] = moments[2 * k : 2 * k + 2]
 
 
-def dense_inverse(columns, start, width, low_ref, high_ref):
-    lane = lax.broadcasted_iota(jnp.int32, (1, LANES), 1)
-    pairs = width // 2
+def dense_inverse(columns, start, width, stack):
+    parts = 8
+    steps = width // (2 * parts)
+    lane = lax.broadcasted_iota(jnp.int32, (parts, LANES), 1)
+    part = lax.broadcasted_iota(jnp.int32, (parts, LANES), 0)
     fits = width + 4 <= LANES
-
-    def at(pair, number):
-        return columns[pl.ds(start + 2 * pair, 1), number : number + 1]
-
-    def two_by_two(pair, number):
-        return tuple(at(pair, number + k) for k in range(4))
-
-    def inject(pair, values, block, extra, extra_lane):
-        top, bottom = values
-        top = jnp.where(lane == 2 * pair, block[0], jnp.where(lane == 2 * pair + 1, block[1], top))
-        bottom = jnp.where(lane == 2 * pair, block[2], jnp.where(lane == 2 * pair + 1, block[3], bottom))
-        if extra is not None and fits:
-            top = jnp.where(lane == extra_lane, extra[0], jnp.where(lane == extra_lane + 1, extra[1], top))
-            bottom = jnp.where(
-                lane == extra_lane, extra[2], jnp.where(lane == extra_lane + 1, extra[3], bottom)
+    values = [columns[pl.ds(start + 2 * i, parts, stride=2 * steps), :] for i in range(steps)]
+
+    def wide(i, number):
+        return tuple(
+            jnp.broadcast_to(values[i][:, number + k : number + k + 1], (parts, LANES)) for k in range(4)
+        )
+
+    blocks = [wide(i, 8) for i in range(steps)]
+    zero, one = jnp.zeros((parts, LANES), jnp.float32), jnp.ones((parts, LANES), jnp.float32)
+
+    def put(rows, i, extra, extra_lane, owner):
+        first = 2 * (part * steps + i)
+        out = []
+        for r in range(2):
+            row = jnp.where(lane == first, blocks[i][2 * r], rows[r])
+            row = jnp.where(lane == first + 1, blocks[i][2 * r + 1], row)
+            if extra is not None and fits:
+                row = jnp.where((part == owner) & (lane == extra_lane), extra[2 * r], row)
+                row = jnp.where((part == owner) & (lane == extra_lane + 1), extra[2 * r + 1], row)
+            out.append(row)
+        return tuple(out)
+
+    def run(order, number, ends, extra_lane, owner):
+        rows, product, out = (zero, zero), (one, zero, zero, one), {}
+        for i in order:
+            t = wide(i, number)
+            rows = (t[0] * rows[0] + t[1] * rows[1], t[2] * rows[0] + t[3] * rows[1])
+            extra = None
+            if i == order[0]:
+                e = wide(i, ends)
+                extra = mm(blocks[i], (e[0], e[2], e[1], e[3]))
+            rows = put(rows, i, extra, extra_lane, owner)
+            product = mm(t, product)
+            out[i] = rows, product
+        rows, product = out[order[-1]]
+        entering, last = [None] * parts, (jnp.zeros((1, LANES), jnp.float32),) * 2
+        sequence = range(parts) if number == 4 else range(parts - 1, -1, -1)
+        for p in sequence:
+            entering[p] = last
+            own, across = [r[p : p + 1] for r in rows], [x[p : p + 1] for x in product]
+            last = (
+                own[0] + across[0] * last[0] + across[1] * last[1],
+                own[1] + across[2] * last[0] + across[3] * last[1],
             )
-        return top, bottom
-
-    zero = jnp.zeros((1, LANES), jnp.float32)
-    low = high = (zero, zero)
-    for step in range(pairs):
-        i, j = step, pairs - 1 - step
-        t = two_by_two(i, 4)
-        low = (t[0] * low[0] + t[1] * low[1], t[2] * low[0] + t[3] * low[1])
-        block = two_by_two(i, 8)
-        extra = None
-        if i == 0:
-            b = two_by_two(0, 12)
-            extra = mm(block, (b[0], b[2], b[1], b[3]))
-        low = inject(i, low, block, extra, width)
-        t = two_by_two(j, 0)
-        high = (t[0] * high[0] + t[1] * high[1], t[2] * high[0] + t[3] * high[1])
-        block = two_by_two(j, 8)
-        extra = None
-        if step == 0:
-            b = two_by_two(pairs - 1, 16)
-            extra = mm(block, (b[0], b[2], b[1], b[3]))
-        high = inject(j, high, block, extra, width + 2)
-        low_ref[2 * i : 2 * i + 1, :] = low[0]
-        low_ref[2 * i + 1 : 2 * i + 2, :] = low[1]
-        high_ref[2 * j : 2 * j + 1, :] = high[0]
-        high_ref[2 * j + 1 : 2 * j + 2, :] = high[1]
-    row = lax.broadcasted_iota(jnp.int32, (width, LANES), 0)
-    column = lax.broadcasted_iota(jnp.int32, (width, LANES), 1)
-    lower = (column <= row) | ((column >= width) & (column < width + 2))
-    return jnp.where(lower, low_ref[0:width, :], high_ref[0:width, :])
+        entering = [jnp.concatenate([e[r] for e in entering], axis=0) for r in range(2)]
+        result = []
+        for i in range(steps):
+            rows, product = out[i]
+            for r in range(2):
+                result.append(rows[r] + product[2 * r] * entering[0] + product[2 * r + 1] * entering[1])
+        return result
+
+    low = run(list(range(steps)), 4, 12, width, 0)
+    high = run(list(range(steps - 1, -1, -1)), 0, 16, width + 2, parts - 1)
+    for k in range(2 * steps):
+        lower = lane <= 2 * (part * steps + k // 2) + 1
+        if fits:
+            lower = lower & (lane < width) | ((lane >= width) & (lane < width + 2))
+        stack[parts * k : parts * (k + 1), :] = jnp.where(lower, low[k], high[k])
+    rows = [stack[pl.ds(p, 2 * steps, stride=parts), :] for p in range(parts)]
+    return jnp.concatenate(rows, axis=0)
 
 
 def stage_plan(count):
@@ -373,11 +408,11 @@
 
 
 def second_kernel(ny, nz, count_z, wy, partners, chains, factors, matrix, entering, weights_y, *scratch):
-    columns, low_ref, high_ref, rows_ref = scratch
+    columns, stacked, rows_ref = scratch
     me_z, me_y = lax.axis_index("gz"), lax.axis_index("gy")
 
-    columns[...] = transposed(factors, ny + me_z)
-    inverse = dense_inverse(columns, 0, LANES, low_ref, high_ref)
+    columns[0:LANES, 0:32] = transposed(factors, ny + me_z)
+    inverse = dense_inverse(columns, 0, LANES, stacked)
     rows_ref[0:LANES, :] = inverse
     rows_ref[LANES : 2 * LANES, :] = jnp.zeros((LANES, LANES), jnp.float32)
     past = tuple(columns[LANES - 1 : LANES, 16 + k : 17 + k] for k in range(4))
@@ -413,7 +448,7 @@
     entering[...] = jnp.concatenate([first, stack - first, first], axis=0)
 
     cell = me_y * wy
-    columns[...] = transposed(factors, cell // LANES)
+    columns[0:LANES, 0:32] = transposed(factors, cell // LANES)
     start = lax.rem(cell, LANES)
     row = lax.broadcasted_iota(jnp.int32, (wy, LANES), 0)
     extra_row = lax.broadcasted_iota(jnp.int32, (EXTRA, LANES), 0)
@@ -441,12 +476,12 @@
             weights_y[output, wy : wy + EXTRA, :] = value
 
 
-def y_kernel(count_y, wy, chains, factors, unused, inverse_y, coefs, columns, low_ref, high_ref):
+def y_kernel(count_y, wy, chains, factors, unused, inverse_y, coefs, columns, stacked):
     me_y = lax.axis_index("gy")
     cell = me_y * wy
-    columns[...] = transposed(factors, cell // LANES)
+    columns[0:LANES, 0:32] = transposed(factors, cell // LANES)
     start = lax.rem(cell, LANES)
-    inverse_y[...] = dense_inverse(columns, start, wy, low_ref, high_ref)
+    inverse_y[...] = dense_inverse(columns, start, wy, stacked)
 
     up, down = ([], [], []), ([], [], [])
     plan = stage_plan(count_y)
@@ -609,6 +644,10 @@
     return jax.ShapeDtypeStruct(shape, jnp.float32)
 
 
+def in_hbm(x):
+    return pltpu.with_memory_space_constraint(x, pltpu.HBM)
+
+
 def cost(flops, data):
     return pl.CostEstimate(flops=flops, bytes_accessed=data, transcendentals=0)
 
@@ -638,7 +677,7 @@
         ],
         compiler_params=PARAMS,
         name="forcing_and_factor",
-    )(flow, speed, metric_y.reshape(ny, LANES), metric_z.reshape(nz, LANES))
+    )(*(in_hbm(x) for x in (flow, speed, metric_y.reshape(ny, LANES), metric_z.reshape(nz, LANES))))
     high, low, factors, chains = outputs[:4]
 
     def exchange(values, axis, count, stride, radix):
@@ -650,7 +689,7 @@
 
     received = exchange(outputs[4:], "gz", count_z, 1, count_z)
     plan = stage_plan(count_y)
-    work = [pltpu.VMEM((LANES, 32), jnp.float32)] + [pltpu.VMEM((LANES, LANES), jnp.float32)] * 2
+    work = [pltpu.VMEM((LANES + 16, LANES), jnp.float32)] * 2
     matrix, entering, weights_y = pl.pallas_call(
         functools.partial(second_kernel, ny, nz, count_z, wy, partners),
         out_shape=[

time: 32.4 us -> 28.3 us (0.87)
  local copies, waits for them, and re-layouts: 3.63 us -> 0 us
  Pallas kernels: 16.4 us -> 14.2 us
  waiting for transfers between devices: 2.68 us -> 4.56 us
    unnamed x8 -> x0, local copies, waits for them, and re-layouts: 3.63 us -> none
    ppermute x7, waiting for transfers between devices: 2.68 us -> 4.56 us  [exchange(): received.append(lax.ppermute(value, axis, pairs))]
    pallas_call x1, Pallas kernels: 3.61 us -> 1.87 us  [on_device(): pl.pallas_call(functools.partial(second_kernel, ny, nz, count_z, wy, part...]
    pallas_call x1, Pallas kernels: 2.21 us -> 1.42 us  [on_device(): pl.pallas_call(functools.partial(y_kernel, count_y, wy), out_shape=[array...]
  transfers between devices with their start and end apart: 7 -> 7, of which waited for: 3 -> 5; matrix products, arithmetic and copies ran while one was open for 0% -> 0% of each run, Pallas kernels for 23% -> 17%
where the time goes in v2:
time: 28.3 us; the launch traced here: 28.2 us
  Pallas kernels  14.2 us (50%)
  starting transfers between devices  9.36 us (33%)
  waiting for transfers between devices  4.56 us (16%)
    ppermute x7, starting transfers between devices, exchange(): received.append(lax.ppermute(value, axis, pairs))  9.36 us
    pallas_call x1, Pallas kernels, on_device(): pl.pallas_call(functools.partial(first_kernel, ny, nz, partners), out_sha...  5.86 us
    ppermute x7, waiting for transfers between devices, exchange(): received.append(lax.ppermute(value, axis, pairs))  4.56 us
    pallas_call x1, Pallas kernels, on_device(): pl.pallas_call(functools.partial(second_kernel, ny, nz, count_z, wy, part...  1.87 us
    pallas_call x1, Pallas kernels, on_device(): pl.pallas_call(functools.partial(third_kernel, partners, wy), out_shape=[...  1.82 us
    pallas_call x1, Pallas kernels, on_device(): pl.pallas_call(functools.partial(last_kernel, base, radix, narrow, wy), o...  1.59 us
    pallas_call x1, Pallas kernels, on_device(): pl.pallas_call(functools.partial(local_y_kernel, wy), out_shape=array(pla...  1.53 us
    pallas_call x1, Pallas kernels, on_device(): pl.pallas_call(functools.partial(y_kernel, count_y, wy), out_shape=[array...  1.42 us
  transfers between devices with their start and end apart: 7, of which 5 were waited for; matrix products, arithmetic and copies ran while one was open for 0% of the time, Pallas kernels for 17%

profile of v2, /device:TPU:0, one launch (start us, length us, event | category | flops | bytes accessed | tf_op | source)
XLA Modules:
  0.0 28.2 jit_solution(10414523461657421632)
XLA Ops:
  0.0 5.9 %forcing_and_factor.1 = (bf16[2880,256]{1,0:T(8,128)(2,1)S(1)}, bf16[2880,256]{1,0:T(8,128)(2,1)S(1)}, f32[28,8,128]{2,1,0:T(8,128)S(1)}, f32[8,8,128]{2,1,0:T(8...) custom-call(f32[5,8,64,128]{3,2,1,0:T(8,128)} %flow_hbm.1, ...), custom_call_target="tpu_custom_call" | custom-call | tf_op jit(solution)/shard_map/forcing_and_factor/pallas_call | solution.py:665
  5.9 0.5 %collective-permute-start = (f32[2,2880]{1,0:T(2,128)S(1)}, f32[2,2880]{1,0:T(2,128)S(1)}, u32[]{:S(2)}, u32[]{:S(2)}) collective-permute-start(f32[2,2880]{1,0:T(2,128)S(1)} %get-tuple-element.28), channel_id=1, source_target_pairs={{0,8},{8,0},{16,24},{24,16},{1,9},{9,1},{17,25},{25,17},{2,10},{10... | collective-permute-start | bytes 69128 | tf_op jit(solution)/shard_map/ppermute | solution.py:687
  6.4 2.6 %collective-permute-start.1 = (f32[2,2880]{1,0:T(2,128)S(1)}, f32[2,2880]{1,0:T(2,128)S(1)}, u32[]{:S(2)}, u32[]{:S(2)}) collective-permute-start(f32[2,2880]{1,0:T(2,128)S(1)} %get-tuple-element.29), channel_id=1, source_target_pairs={{0,16},{8,24},{16,0},{24,8},{1,17},{9,25},{17,1},{25,9},{2,18},{10... | collective-permute-start | bytes 69128 | tf_op jit(solution)/shard_map/ppermute | solution.py:687
  9.0 0.1 collective-permute-start.2
  9.0 1.9 %inverse_z.1 = (bf16[768,128]{1,0:T(8,128)(2,1)S(1)}, f32[24,128]{1,0:T(8,128)S(1)}, f32[4,72,128]{2,1,0:T(8,128)S(1)}) custom-call(f32[8,8,128]{2,1,0:T(8,128)S(1)} %get-tuple-element.21.chains, f32[28,8,128]{2,1,0:T(8,128)S(1)} %get-tuple-element.22.factors), custom_call_target="tpu_custom_call" | custom-call | flops 1132462080 | bytes 4423680 | tf_op jit(solution)/shard_map/inverse_z/pallas_call | solution.py:693
  10.9 0.0 collective-permute-done.refs_0_
  10.9 0.0 collective-permute-done.1.refs_1_
  10.9 1.3 %collective-permute-done.2.refs_2_ = f32[2,2880]{1,0:T(2,128)S(1)} collective-permute-done((f32[2,2880]{1,0:T(2,128)S(1)}, f32[2,2880]{1,0:T(2,128)S(1)}, u32[]{:S(2)}, u32[]{:S(2)}) %collective-permute-start.2) | collective-permute-done | bytes 23072 | tf_op jit(solution)/shard_map/ppermute | solution.py:687
  12.2 1.8 %finish_z.1 = (f32[2880,128]{1,0:T(8,128)S(1)}, f32[4,40,128]{2,1,0:T(8,128)S(1)}) custom-call(f32[4,72,128]{2,1,0:T(8,128)S(1)} %get-tuple-element.23.weights_y, bf16[2880,256]{1,0:T(8,128)(2,1)S(1)} %get-tuple-element.24.high, bf16[2880,256]{1,0:T(8,128)(2,1)S(1)} %get-tuple-element.25.low, bf16[768,128]{1,0:T(8,128)(2,1)S(1)} %get-tuple-element.26.matrix, ...), custom_call_target="tpu_custom_call" | custom-call | tf_op jit(solution)/shard_map/finish_z/pallas_call | solution.py:707
  14.0 2.6 %collective-permute-start.5 = (f32[4,40,128]{2,1,0:T(8,128)S(1)}, f32[4,40,128]{2,1,0:T(8,128)S(1)}, u32[]{:S(2)}, u32[]{:S(2)}) collective-permute-start(f32[4,40,128]{2,1,0:T(8,128)S(1)} %get-tuple-element.31.unused.refs_0_), channel_id=1, source_target_pairs={{0,3},{1,2},{2,1},{3,0},{4,7},{5,6},{6,5},{7,4},{8,11},{9,10},{10,... | collective-permute-start | bytes 245768 | tf_op jit(solution)/shard_map/ppermute | solution.py:687
  16.6 0.4 %collective-permute-start.4 = (f32[4,40,128]{2,1,0:T(8,128)S(1)}, f32[4,40,128]{2,1,0:T(8,128)S(1)}, u32[]{:S(2)}, u32[]{:S(2)}) collective-permute-start(f32[4,40,128]{2,1,0:T(8,128)S(1)} %get-tuple-element.31.unused.refs_0_), channel_id=1, source_target_pairs={{0,2},{1,3},{2,0},{3,1},{4,6},{5,7},{6,4},{7,5},{8,10},{9,11},{10,... | collective-permute-start | bytes 245768 | tf_op jit(solution)/shard_map/ppermute | solution.py:687
  17.1 0.5 %collective-permute-start.3 = (f32[4,40,128]{2,1,0:T(8,128)S(1)}, f32[4,40,128]{2,1,0:T(8,128)S(1)}, u32[]{:S(2)}, u32[]{:S(2)}) collective-permute-start(f32[4,40,128]{2,1,0:T(8,128)S(1)} %get-tuple-element.31.unused.refs_0_), channel_id=1, source_target_pairs={{0,1},{1,0},{2,3},{3,2},{4,5},{5,4},{6,7},{7,6},{8,9},{9,8},{10,11... | collective-permute-start | bytes 245768 | tf_op jit(solution)/shard_map/ppermute | solution.py:687
  17.6 1.4 %inverse_y.1 = (f32[64,128]{1,0:T(8,128)S(1)}, f32[8,8,128]{2,1,0:T(8,128)S(1)}) custom-call(f32[8,8,128]{2,1,0:T(8,128)S(1)} %get-tuple-element.21.chains, f32[28,8,128]{2,1,0:T(8,128)S(1)} %get-tuple-element.22.factors, f32[4,40,128]{2,1,0:T(8,128)S(1)} %get-tuple-element.31.unused.refs_0_), custom_call_target="tpu_custom_call" | custom-call | flops 566231040 | bytes 2949120 | tf_op jit(solution)/shard_map/inverse_y/pallas_call | solution.py:722
  19.0 1.0 %collective-permute-done.5.refs_3_ = f32[4,40,128]{2,1,0:T(8,128)S(1)} collective-permute-done((f32[4,40,128]{2,1,0:T(8,128)S(1)}, f32[4,40,128]{2,1,0:T(8,128)S(1)}, u32[]{:S(2)}, u32[]{:S(2)}) %collective-permute-start.5) | collective-permute-done | bytes 81952 | tf_op jit(solution)/shard_map/ppermute | solution.py:687
  20.0 1.3 %collective-permute-done.4.refs_2_ = f32[4,40,128]{2,1,0:T(8,128)S(1)} collective-permute-done((f32[4,40,128]{2,1,0:T(8,128)S(1)}, f32[4,40,128]{2,1,0:T(8,128)S(1)}, u32[]{:S(2)}, u32[]{:S(2)}) %collective-permute-start.4) | collective-permute-done | bytes 81952 | tf_op jit(solution)/shard_map/ppermute | solution.py:687
  21.3 0.2 collective-permute-done.3.refs_1_
  21.5 0.1 join_groups.1
  21.6 2.7 %collective-permute-start.6 = (f32[2,40,128]{2,1,0:T(8,128)S(1)}, f32[2,40,128]{2,1,0:T(8,128)S(1)}, u32[]{:S(2)}, u32[]{:S(2)}) collective-permute-start(f32[2,40,128]{2,1,0:T(8,128)S(1)} %get-tuple-element.36), channel_id=1, source_target_pairs={{0,4},{1,5},{2,6},{3,7},{4,0},{5,1},{6,2},{7,3},{8,12},{9,13},{10,... | collective-permute-start | bytes 122888 | tf_op jit(solution)/shard_map/ppermute | solution.py:687
  24.3 1.5 %local_y.1.local = f32[40,64,128]{2,1,0:T(8,128)S(1)} custom-call(f32[2880,128]{1,0:T(8,128)S(1)} %get-tuple-element.33.solved, f32[64,128]{1,0:T(8,128)S(1)} %get-tuple-element.34.inverse_y), custom_call_target="tpu_custom_call" | custom-call | flops 566231040 | bytes 2949120 | tf_op jit(solution)/shard_map/local_y/pallas_call | solution.py:732
  25.8 0.8 %collective-permute-done.6.refs_0_ = f32[2,40,128]{2,1,0:T(8,128)S(1)} collective-permute-done((f32[2,40,128]{2,1,0:T(8,128)S(1)}, f32[2,40,128]{2,1,0:T(8,128)S(1)}, u32[]{:S(2)}, u32[]{:S(2)}) %collective-permute-start.6) | collective-permute-done | bytes 40992 | tf_op jit(solution)/shard_map/ppermute | solution.py:687
  26.6 1.6 %finish_y.1 = f32[5,8,64,128]{3,2,1,0:T(8,128)} custom-call(f32[8,8,128]{2,1,0:T(8,128)S(1)} %get-tuple-element.32.coefs, f32[40,64,128]{2,1,0:T(8,128)S(1)} %local_y.1.local, f32[64,128]{1,0:T(8,128)S(1)} %get-tuple-element.34.inverse_y, f32[4,40,128]{2,1,0:T(8,128)S(1)} %get-tuple-element.35.entered, f32[2,40,128]{2,1,0:T(8,128)S(1)} %collective-permute-done.6.refs_0_), custom_call_target="tpu_custom_call" | custom-call | tf_op jit(solution)/shard_map/finish_y/pallas_call | solution.py:756
Async XLA Ops:
  5.9 5.0 %collective-permute-start = (f32[2,2880]{1,0:T(2,128)S(1)}, f32[2,2880]{1,0:T(2,128)S(1)}, u32[]{:S(2)}, u32[]{:S(2)}) collective-permute-start(f32[2,2880]{1,0:T(2,128)S(1)} %get-tuple-element.28), channel_id=1, source_target_pairs={{0,8},{8,0},{16,24},{24,16},{1,9},{9,1},{17,25},{25,17},{2,10},{10... | collective-permute-start | bytes 69128 | tf_op jit(solution)/shard_map/ppermute | solution.py:687
  6.4 4.5 %collective-permute-start.1 = (f32[2,2880]{1,0:T(2,128)S(1)}, f32[2,2880]{1,0:T(2,128)S(1)}, u32[]{:S(2)}, u32[]{:S(2)}) collective-permute-start(f32[2,2880]{1,0:T(2,128)S(1)} %get-tuple-element.29), channel_id=1, source_target_pairs={{0,16},{8,24},{16,0},{24,8},{1,17},{9,25},{17,1},{25,9},{2,18},{10... | collective-permute-start | bytes 69128 | tf_op jit(solution)/shard_map/ppermute | solution.py:687
  9.0 3.2 %collective-permute-start.2 = (f32[2,2880]{1,0:T(2,128)S(1)}, f32[2,2880]{1,0:T(2,128)S(1)}, u32[]{:S(2)}, u32[]{:S(2)}) collective-permute-start(f32[2,2880]{1,0:T(2,128)S(1)} %get-tuple-element.30), channel_id=1, source_target_pairs={{0,24},{8,16},{16,8},{24,0},{1,25},{9,17},{17,9},{25,1},{2,26},{10... | collective-permute-start | bytes 69128 | tf_op jit(solution)/shard_map/ppermute | solution.py:687
  14.0 6.0 %collective-permute-start.5 = (f32[4,40,128]{2,1,0:T(8,128)S(1)}, f32[4,40,128]{2,1,0:T(8,128)S(1)}, u32[]{:S(2)}, u32[]{:S(2)}) collective-permute-start(f32[4,40,128]{2,1,0:T(8,128)S(1)} %get-tuple-element.31.unused.refs_0_), channel_id=1, source_target_pairs={{0,3},{1,2},{2,1},{3,0},{4,7},{5,6},{6,5},{7,4},{8,11},{9,10},{10,... | collective-permute-start | bytes 245768 | tf_op jit(solution)/shard_map/ppermute | solution.py:687
  16.6 4.7 %collective-permute-start.4 = (f32[4,40,128]{2,1,0:T(8,128)S(1)}, f32[4,40,128]{2,1,0:T(8,128)S(1)}, u32[]{:S(2)}, u32[]{:S(2)}) collective-permute-start(f32[4,40,128]{2,1,0:T(8,128)S(1)} %get-tuple-element.31.unused.refs_0_), channel_id=1, source_target_pairs={{0,2},{1,3},{2,0},{3,1},{4,6},{5,7},{6,4},{7,5},{8,10},{9,11},{10,... | collective-permute-start | bytes 245768 | tf_op jit(solution)/shard_map/ppermute | solution.py:687
  17.1 4.4 %collective-permute-start.3 = (f32[4,40,128]{2,1,0:T(8,128)S(1)}, f32[4,40,128]{2,1,0:T(8,128)S(1)}, u32[]{:S(2)}, u32[]{:S(2)}) collective-permute-start(f32[4,40,128]{2,1,0:T(8,128)S(1)} %get-tuple-element.31.unused.refs_0_), channel_id=1, source_target_pairs={{0,1},{1,0},{2,3},{3,2},{4,5},{5,4},{6,7},{7,6},{8,9},{9,8},{10,11... | collective-permute-start | bytes 245768 | tf_op jit(solution)/shard_map/ppermute | solution.py:687
  21.6 5.0 %collective-permute-start.6 = (f32[2,40,128]{2,1,0:T(8,128)S(1)}, f32[2,40,128]{2,1,0:T(8,128)S(1)}, u32[]{:S(2)}, u32[]{:S(2)}) collective-permute-start(f32[2,40,128]{2,1,0:T(8,128)S(1)} %get-tuple-element.36), channel_id=1, source_target_pairs={{0,4},{1,5},{2,6},{3,7},{4,0},{5,1},{6,2},{7,3},{8,12},{9,13},{10,... | collective-permute-start | bytes 122888 | tf_op jit(solution)/shard_map/ppermute | solution.py:687

commit v3 on v2

--- a/solution.py
+++ b/solution.py
@@ -153,10 +153,11 @@
     return jnp.where(even, chain[column], chain[2 + column])
 
 
-def first_kernel(ny, nz, partners, flow_hbm, speed_hbm, metric_y, metric_z, *refs):
+def first_kernel(ny, nz, partners, paired, flow_hbm, speed_hbm, metric_y, metric_z, *refs):
     high, low, factors, chains = refs[:4]
-    messages = refs[4 : 4 + partners]
-    flow, speed, metric, spread, arrived = refs[4 + partners :]
+    count = 1 if paired else partners
+    messages = refs[4 : 4 + count]
+    flow, speed, metric, spread, arrived = refs[4 + count :]
     fields, planes_x, wy, _ = flow.shape
     rows = ny + nz
     core_rows = fields * planes_x * wy
@@ -210,7 +211,7 @@
             ends = jnp.where(lane < 2, c + jnp.where(lane < 1, a, 0.0), 0.0)
             ends = jnp.where(lane >= LANES - 2, d + jnp.where(lane >= LANES - 1, b, 0.0), ends)
             index = field * planes_x + x
-            start = index * wy if isinstance(index, int) else pl.multiple_of(index * wy, 16)
+            start = index * wy
             store(start, 0, total + ((a + b) + (c + d) - ends))
             store(start, LANES, ends)
             above = spread[slot, 1, 7:15, :] + spread[slot, 2, 8:16, :]
@@ -218,7 +219,6 @@
             extras.append(jnp.where(extra_row < 2, above, jnp.where(extra_row < 4, below, 0.0)))
             if len(extras) == 2:
                 start = core_rows + (index - 1) * EXTRA
-                start = start if isinstance(index, int) else pl.multiple_of(start, 16)
                 store(start, 0, jnp.concatenate(extras, axis=0))
                 for ref in (high, low):
                     ref[pl.ds(start, 2 * EXTRA), LANES : 2 * LANES] = jnp.zeros(
@@ -229,32 +229,23 @@
     copies[0].wait()
     copies[1].wait()
     factor = Factor(metric[...], ny, nz, wy)
+
+    guess_l, guess_r = factor.guess(1), factor.guess(-1)
+    left, right = factor.sweep(1, *guess_l[:2]), factor.sweep(-1, *guess_r[:2])
     copies[2].wait()
-
-    def arrive(field):
+    for field in range(fields):
         pltpu.make_async_copy(flow_hbm.at[field], flow.at[field], arrived.at[field]).wait()
-
-    def step(index, carry):
-        left, right = carry
-        left = factor.sweep(1, left[0], left[1])
-        right = factor.sweep(-1, right[0], right[1])
-        for k in range(2):
-            arrive(2 * index + k)
-            one_field(2 * index + k)
-        return left, right
-
-    assert fields // 2 >= 2
-    left, right = lax.fori_loop(0, fields // 2, step, (factor.guess(1), factor.guess(-1)))
-    for field in range(fields // 2 * 2, fields):
-        arrive(field)
+    left, right = factor.sweep(1, *left[:2]), factor.sweep(-1, *right[:2])
+    for field in range(fields // 2):
         one_field(field)
-
-    parts = factor.finish(left[0], left[1], left[2], right[0], right[1])
+    parts = factor.finish(*left, *right[:2])
     from_right, from_left, diagonal, to_right, to_left, before, after = parts
     for number, value in enumerate(v for part in parts for v in part):
         factors[number] = value
     for number, value in enumerate(to_right + to_left):
         chains[number] = value
+    for field in range(fields // 2, fields):
+        one_field(field)
 
     me = lax.axis_index("gz")
     mine = lax.broadcasted_iota(jnp.int32, (rows, LANES), 0) == ny + me
@@ -282,10 +273,26 @@
                 jnp.concatenate([inside_down, ends_down], axis=1),
             )
         )
-    stack = []
-    for k in range(1, partners + 1):
-        upward = jnp.bitwise_xor(me, k) > me
-        stack += [jnp.where(upward, w[0], w[1]) for w in weights]
+    if paired:
+        lower = (me & 1) == 0
+        stack = [jnp.where(lower, w[0], w[1]) for w in weights]
+        peer = lax.broadcasted_iota(jnp.int32, (rows, LANES), 0) == ny + jnp.bitwise_xor(me, 1)
+
+        def of_peer(values, place):
+            chosen = tuple(jnp.sum(jnp.where(peer, v, 0.0), axis=0, keepdims=True) for v in values)
+            return tuple(jnp.broadcast_to(v[:, place : place + 1], (1, 2 * LANES)) for v in chosen)
+
+        over, under = of_peer(to_right, 0), of_peer(to_left, LANES - 1)
+        (up0, down0), (up1, down1) = weights
+        for q in range(2):
+            upward = jnp.where(lower, over[q] * up0 + over[2 + q] * up1, weights[q][0])
+            downward = jnp.where(lower, weights[q][1], under[q] * down0 + under[2 + q] * down1)
+            stack.append(jnp.where(me < 2, upward, downward))
+    else:
+        stack = []
+        for k in range(1, partners + 1):
+            upward = jnp.bitwise_xor(me, k) > me
+            stack += [jnp.where(upward, w[0], w[1]) for w in weights]
     while len(stack) % 8:
         stack.append(jnp.zeros((1, 2 * LANES), jnp.float32))
     count = len(stack)
@@ -293,11 +300,18 @@
     first = stack.astype(jnp.bfloat16).astype(jnp.float32)
     both = jnp.concatenate([first, stack - first], axis=0).astype(jnp.bfloat16)
     across = (((1,), (1,)), ((), ()))
-    on_high = matmul(both, high[...], across)
-    on_low = matmul(both, low[...], across)
-    moments = (on_high[:count] + on_high[count:]) + on_low[:count]
-    for k in range(partners):
-        messages[k][...] = moments[2 * k : 2 * k + 2]
+    total = high.shape[0]
+    size = planes_x * wy
+    for begin in range(0, total, size):
+        rows = slice(begin, min(begin + size, total))
+        on_high = matmul(both, high[rows, :], across)
+        on_low = matmul(both, low[rows, :], across)
+        moments = (on_high[:count] + on_high[count:]) + on_low[:count]
+        if paired:
+            messages[0][:, rows] = moments[0:4]
+        else:
+            for k in range(partners):
+                messages[k][:, rows] = moments[2 * k : 2 * k + 2]
 
 
 def dense_inverse(columns, start, width, stack):
@@ -372,9 +386,8 @@
 def stage_plan(count):
     plan, stride = [], 1
     while stride < count:
-        radix = 4 if count // stride >= 4 else 2
-        plan.append((stride, radix))
-        stride *= radix
+        plan.append((stride, 2))
+        stride *= 2
     return plan
 
 
@@ -407,7 +420,7 @@
     return jnp.where(condition, 1.0, 0.0)
 
 
-def second_kernel(ny, nz, count_z, wy, partners, chains, factors, matrix, entering, weights_y, *scratch):
+def second_kernel(ny, nz, count_z, wy, partners, paired, chains, factors, matrix, entering, weights_y, *scratch):
     columns, stacked, rows_ref = scratch
     me_z, me_y = lax.axis_index("gz"), lax.axis_index("gy")
 
@@ -427,20 +440,27 @@
     matrix[2 * LANES : 4 * LANES, :] = second
     matrix[4 * LANES : 6 * LANES, :] = first
 
-    others = [jnp.bitwise_xor(me_z, k) for k in range(1, partners + 1)]
-    always = [1.0] * partners
+    if paired:
+        pair = me_z // 2 * 2
+        begins, ends = [me_z, pair], [me_z + 1, pair + 2]
+        lowers = [me_z % 2 == 1, pair > 0]
+    else:
+        others = [jnp.bitwise_xor(me_z, k) for k in range(1, partners + 1)]
+        begins, ends = [other + 1 for other in others], others
+        lowers = [other < me_z for other in others]
+    size = len(begins)
     up = chain_products(
-        chains, 0, lambda b: (ny + b, 0), count_z, [o + 1 for o in others], [me_z] * partners, always, False
+        chains, 0, lambda b: (ny + b, 0), count_z, begins, [me_z] * size, [1.0] * size, False
     )
     down = chain_products(
-        chains, 4, lambda b: (ny + b, LANES - 1), count_z, [me_z + 1] * partners, others, always, True
+        chains, 4, lambda b: (ny + b, LANES - 1), count_z, [me_z + 1] * size, ends, [1.0] * size, True
     )
     stack = []
-    for k, other in enumerate(others):
+    for k, lower in enumerate(lowers):
         for p in range(2):
             from_low = up[2 * p][k : k + 1] * head0 + up[2 * p + 1][k : k + 1] * head1
             from_high = down[2 * p][k : k + 1] * tail0 + down[2 * p + 1][k : k + 1] * tail1
-            stack.append(jnp.where(other < me_z, from_low, from_high))
+            stack.append(jnp.where(lower, from_low, from_high))
     while len(stack) % 8:
         stack.append(jnp.zeros((1, LANES), jnp.float32))
     stack = jnp.concatenate(stack, axis=0)
@@ -519,10 +539,14 @@
             coefs[base + k] = value[k]
 
 
+def pair_kernel(own, received, total):
+    total[...] = own[2:4] + received[2:4]
+
+
 def third_kernel(partners, wy, weights_y, high, low, matrix, entering, *refs):
     messages, (solved, carried) = refs[:partners], refs[partners:]
     planes = carried.shape[1]
-    received = [m[...] for m in messages]
+    received = [m[0:2] for m in messages]
     padding = entering.shape[0] // 3 - 2 * partners
     if padding:
         received.append(jnp.zeros((padding, received[0].shape[1]), jnp.float32))
@@ -553,7 +577,7 @@
             carried[number, part * 8 : (part + 1) * 8, :] = jnp.concatenate(lines, axis=0)
 
 
-def local_y_kernel(wy, solved, inverse_y, out):
+def local_y_kernel(wy, solved, inverse_y, unused, out):
     planes = out.shape[0]
     first, second = halves(inverse_y[:, 0 : wy + EXTRA])
     left = jnp.concatenate([first, second, first], axis=1)
@@ -660,14 +684,16 @@
     planes = fields * planes_x
     rows = planes * (wy + EXTRA)
     partners = count_z - 1
-    entering_rows = -(-2 * partners // 8) * 8
+    paired = count_z == 4
+    arrivals = 2 if paired else partners
+    entering_rows = -(-2 * arrivals // 8) * 8
     half = jax.ShapeDtypeStruct((rows, 2 * LANES), jnp.bfloat16)
     outputs = pl.pallas_call(
-        functools.partial(first_kernel, ny, nz, partners),
+        functools.partial(first_kernel, ny, nz, partners, paired),
         out_shape=[half, half, array(28, ny + nz, LANES), array(8, ny + nz, LANES)]
-        + [array(2, rows)] * partners,
+        + ([array(4, rows)] if paired else [array(2, rows)] * partners),
         in_specs=[HBM] * 4,
-        out_specs=[VMEM] * (4 + partners),
+        out_specs=[VMEM] * (5 if paired else 4 + partners),
         scratch_shapes=[
             pltpu.VMEM(flow.shape, jnp.float32),
             pltpu.VMEM(speed.shape, jnp.float32),
@@ -687,11 +713,23 @@
             received.append(lax.ppermute(value, axis, pairs))
         return received
 
-    received = exchange(outputs[4:], "gz", count_z, 1, count_z)
+    if paired:
+        near = exchange(outputs[4:], "gz", count_z, 1, 2)
+        total = pl.pallas_call(
+            pair_kernel,
+            out_shape=array(2, rows),
+            in_specs=[VMEM] * 2,
+            out_specs=VMEM,
+            compiler_params=PARAMS,
+            name="join_pair",
+        )(outputs[4], near[0])
+        received = near + exchange([total], "gz", count_z, 2, 2)
+    else:
+        received = exchange(outputs[4:], "gz", count_z, 1, count_z)
     plan = stage_plan(count_y)
     work = [pltpu.VMEM((LANES + 16, LANES), jnp.float32)] * 2
     matrix, entering, weights_y = pl.pallas_call(
-        functools.partial(second_kernel, ny, nz, count_z, wy, partners),
+        functools.partial(second_kernel, ny, nz, count_z, wy, partners, paired),
         out_shape=[
             jax.ShapeDtypeStruct((6 * LANES, LANES), jnp.bfloat16),
             array(3 * entering_rows, LANES),
@@ -705,9 +743,9 @@
         name="inverse_z",
     )(chains, factors)
     solved, carried = pl.pallas_call(
-        functools.partial(third_kernel, partners, wy),
+        functools.partial(third_kernel, arrivals, wy),
         out_shape=[array(rows, LANES), array(4, planes, LANES)],
-        in_specs=[VMEM] * (5 + partners),
+        in_specs=[VMEM] * (5 + arrivals),
         out_specs=[VMEM] * 2,
         compiler_params=PARAMS,
         name="finish_z",
@@ -729,15 +767,6 @@
                 cost_estimate=cost(2 * rows * 128 * 128 * 6, 4 * rows * 256),
                 name="inverse_y",
             )(chains, factors, carried)
-            result = pl.pallas_call(
-                functools.partial(local_y_kernel, wy),
-                out_shape=array(planes, wy, LANES),
-                in_specs=[VMEM] * 2,
-                out_specs=VMEM,
-                compiler_params=PARAMS,
-                cost_estimate=cost(2 * rows * 128 * 128 * 6, 4 * rows * 256),
-                name="local_y",
-            )(solved, inverse_y)
         if number + 1 < len(plan):
             slim = narrow and number + 2 == len(plan)
             inputs = [carried] + received + ([entered] if entered is not None else [])
@@ -750,9 +779,17 @@
                 name="join_groups",
             )(coefs, *inputs)
             base += 2 * radix - 1
+            if number == 0:
+                result = pl.pallas_call(
+                    functools.partial(local_y_kernel, wy),
+                    out_shape=array(planes, wy, LANES),
+                    in_specs=[VMEM] * 2 + [HBM],
+                    out_specs=VMEM,
+                    compiler_params=PARAMS,
+                    cost_estimate=cost(2 * rows * 128 * 128 * 6, 4 * rows * 256),
+                    name="local_y",
+                )(solved, inverse_y, entered)
         else:
-            if entered is None:
-                entered = jnp.zeros((4, planes, LANES), jnp.float32)
             return pl.pallas_call(
                 functools.partial(last_kernel, base, radix, narrow, wy),
                 out_shape=array(fields, planes_x, wy, wz),

time: 28.3 us -> 28.8 us (1.018)
  starting transfers between devices: 9.36 us -> 10.9 us
  Pallas kernels: 14.2 us -> 12.9 us
    ppermute x7 -> x5, starting transfers between devices: 9.36 us -> 10.9 us  [exchange(): received.append(lax.ppermute(value, axis, pairs))]
    pallas_call x2 -> x3, Pallas kernels: 7.68 us -> 6.35 us  [the longest x1 4.52 us: on_device(): pl.pallas_call(functools.partial(first_kernel, ny, nz, partners, paired),...]
    ppermute x7 -> x5, waiting for transfers between devices: 4.56 us -> 4.81 us  [exchange(): received.append(lax.ppermute(value, axis, pairs))]
  transfers between devices with their start and end apart: 7 -> 5, of which waited for: 5 -> 4; matrix products, arithmetic and copies ran while one was open for 0% -> 0% of each run, Pallas kernels for 17% -> 17%
where the time goes in v3:
time: 28.8 us; the launch traced here: 28.6 us
  Pallas kernels  12.9 us (45%)
  starting transfers between devices  10.9 us (38%)
  waiting for transfers between devices  4.81 us (17%)
    ppermute x5, starting transfers between devices, exchange(): received.append(lax.ppermute(value, axis, pairs))  10.9 us
    ppermute x5, waiting for transfers between devices, exchange(): received.append(lax.ppermute(value, axis, pairs))  4.81 us
    pallas_call x1, Pallas kernels, on_device(): pl.pallas_call(functools.partial(first_kernel, ny, nz, partners, paired),...  4.52 us
    pallas_call x1, Pallas kernels, on_device(): pl.pallas_call(functools.partial(second_kernel, ny, nz, count_z, wy, part...  1.87 us
    pallas_call x1, Pallas kernels, on_device(): pl.pallas_call(functools.partial(third_kernel, arrivals, wy), out_shape=[...  1.82 us
    pallas_call x1, Pallas kernels, on_device(): pl.pallas_call(functools.partial(last_kernel, base, radix, narrow, wy), o...  1.59 us
    pallas_call x1, Pallas kernels, on_device(): pl.pallas_call(functools.partial(local_y_kernel, wy), out_shape=array(pla...  1.55 us
    pallas_call x1, Pallas kernels, on_device(): pl.pallas_call(functools.partial(y_kernel, count_y, wy), out_shape=[array...  1.42 us
  transfers between devices with their start and end apart: 5, of which 4 were waited for; matrix products, arithmetic and copies ran while one was open for 0% of the time, Pallas kernels for 17%

profile of v3, /device:TPU:0, one launch (start us, length us, event | category | flops | bytes accessed | tf_op | source)
XLA Modules:
  0.0 28.6 jit_solution(15342113148024731696)
XLA Ops:
  0.0 4.5 %forcing_and_factor.1 = (bf16[2880,256]{1,0:T(8,128)(2,1)S(1)}, bf16[2880,256]{1,0:T(8,128)(2,1)S(1)}, f32[28,8,128]{2,1,0:T(8,128)S(1)}, f32[8,8,128]{2,1,0:T(8,128)S(1)}, f32[4,2880]{1,0:T(4,128)S(1)}) custom-call(f32[5,8,64,128]{3,2,1,0:T(8,128)} %flow_hbm.1, f32[8,64,128]{2,1,0:T(8,128)} %speed_hbm.1, f32[4,128]{1,0:T(4,128)} %bitcast.2, f32[4,128]{1,0:T(4,128)} %bitcast.3), custom_call_target="tpu_custom_call" | custom-call | tf_op jit(solution)/shard_map/forcing_and_factor/pallas_call | solution.py:691
  4.5 0.5 %collective-permute-start = (f32[4,2880]{1,0:T(4,128)S(1)}, f32[4,2880]{1,0:T(4,128)S(1)}, u32[]{:S(2)}, u32[]{:S(2)}) collective-permute-start(f32[4,2880]{1,0:T(4,128)S(1)} %get-tuple-element.28.own), channel_id=1, source_target_pairs={{0,8},{8,0},{16,24},{24,16},{1,9},{9,1},{17,25},{25,17},{2,10},{10... | collective-permute-start | bytes 138248 | tf_op jit(solution)/shard_map/ppermute | solution.py:713
  5.0 0.9 %collective-permute-done.received.refs_0_ = f32[4,2880]{1,0:T(4,128)S(1)} collective-permute-done((f32[4,2880]{1,0:T(4,128)S(1)}, f32[4,2880]{1,0:T(4,128)S(1)}, u32[]{:S(2)}, u32[]{:S(2)}) %collective-permute-start) | collective-permute-done | bytes 46112 | tf_op jit(solution)/shard_map/ppermute | solution.py:713
  5.9 2.9 %collective-permute-start.1 = (f32[2,2880]{1,0:T(2,128)S(1)}, f32[2,2880]{1,0:T(2,128)S(1)}, u32[]{:S(2)}, u32[]{:S(2)}) collective-permute-start(f32[2,2880]{1,0:T(2,128)S(1)} %join_pair.1), channel_id=1, source_target_pairs={{0,16},{8,24},{16,0},{24,8},{1,17},{9,25},{17,1},{25,9},{2,18},{10... | collective-permute-start | bytes 69128 | tf_op jit(solution)/shard_map/ppermute | solution.py:713
  8.8 1.9 %inverse_z.1 = (bf16[768,128]{1,0:T(8,128)(2,1)S(1)}, f32[24,128]{1,0:T(8,128)S(1)}, f32[4,72,128]{2,1,0:T(8,128)S(1)}) custom-call(f32[8,8,128]{2,1,0:T(8,128)S(1)} %get-tuple-element.21.chains, f32[28,8,128]{2,1,0:T(8,128)S(1)} %get-tuple-element.22.factors), custom_call_target="tpu_custom_call" | custom-call | flops 1132462080 | bytes 4423680 | tf_op jit(solution)/shard_map/inverse_z/pallas_call | solution.py:731
  10.7 0.0 collective-permute-done.1.refs_1_
  10.7 1.8 %finish_z.1 = (f32[2880,128]{1,0:T(8,128)S(1)}, f32[4,40,128]{2,1,0:T(8,128)S(1)}) custom-call(f32[4,72,128]{2,1,0:T(8,128)S(1)} %get-tuple-element.23.weights_y, bf16[2880,256]{1,0:T(8,128)(2,1)S(1)} %get-tuple-element.24.high, bf16[2880,256]{1,0:T(8,128)(2,1)S(1)} %get-tuple-element.25.low, bf16[768,128]{1,0:T(8,128)(2,1)S(1)} %get-tuple-element.26.matrix, ...), custom_call_target="tpu_custom_call" | custom-call | tf_op jit(solution)/shard_map/finish_z/pallas_call | solution.py:745
  12.6 2.0 %collective-permute-start.2 = (f32[4,40,128]{2,1,0:T(8,128)S(1)}, f32[4,40,128]{2,1,0:T(8,128)S(1)}, u32[]{:S(2)}, u32[]{:S(2)}) collective-permute-start(f32[4,40,128]{2,1,0:T(8,128)S(1)} %get-tuple-element.29.unused.refs_0_), channel_id=1, source_target_pairs={{0,1},{1,0},{2,3},{3,2},{4,5},{5,4},{6,7},{7,6},{8,9},{9,8},{10,11... | collective-permute-start | bytes 245768 | tf_op jit(solution)/shard_map/ppermute | solution.py:713
  14.6 1.4 %inverse_y.1 = (f32[64,128]{1,0:T(8,128)S(1)}, f32[8,8,128]{2,1,0:T(8,128)S(1)}) custom-call(f32[8,8,128]{2,1,0:T(8,128)S(1)} %get-tuple-element.21.chains, f32[28,8,128]{2,1,0:T(8,128)S(1)} %get-tuple-element.22.factors, f32[4,40,128]{2,1,0:T(8,128)S(1)} %get-tuple-element.29.unused.refs_0_), custom_call_target="tpu_custom_call" | custom-call | flops 566231040 | bytes 2949120 | tf_op jit(solution)/shard_map/inverse_y/pallas_call | solution.py:760
  16.0 1.1 %collective-permute-done.2.refs_1_ = f32[4,40,128]{2,1,0:T(8,128)S(1)} collective-permute-done((f32[4,40,128]{2,1,0:T(8,128)S(1)}, f32[4,40,128]{2,1,0:T(8,128)S(1)}, u32[]{:S(2)}, u32[]{:S(2)}) %collective-permute-start.2) | collective-permute-done | bytes 81952 | tf_op jit(solution)/shard_map/ppermute | solution.py:713
  17.1 2.1 %collective-permute-start.3 = (f32[4,40,128]{2,1,0:T(8,128)S(1)}, f32[4,40,128]{2,1,0:T(8,128)S(1)}, u32[]{:S(2)}, u32[]{:S(2)}) collective-permute-start(f32[4,40,128]{2,1,0:T(8,128)S(1)} %get-tuple-element.34.refs_0_), channel_id=1, source_target_pairs={{0,2},{1,3},{2,0},{3,1},{4,6},{5,7},{6,4},{7,5},{8,10},{9,11},{10,... | collective-permute-start | bytes 245768 | tf_op jit(solution)/shard_map/ppermute | solution.py:713
  19.2 2.4 %collective-permute-done.3.refs_1_ = f32[4,40,128]{2,1,0:T(8,128)S(1)} collective-permute-done((f32[4,40,128]{2,1,0:T(8,128)S(1)}, f32[4,40,128]{2,1,0:T(8,128)S(1)}, u32[]{:S(2)}, u32[]{:S(2)}) %collective-permute-start.3) | collective-permute-done | bytes 81952 | tf_op jit(solution)/shard_map/ppermute | solution.py:713
  21.6 3.4 %collective-permute-start.4 = (f32[2,40,128]{2,1,0:T(8,128)S(1)}, f32[2,40,128]{2,1,0:T(8,128)S(1)}, u32[]{:S(2)}, u32[]{:S(2)}) collective-permute-start(f32[2,40,128]{2,1,0:T(8,128)S(1)} %get-tuple-element.36), channel_id=1, source_target_pairs={{0,4},{1,5},{2,6},{3,7},{4,0},{5,1},{6,2},{7,3},{8,12},{9,13},{10,... | collective-permute-start | bytes 122888 | tf_op jit(solution)/shard_map/ppermute | solution.py:713
  25.1 1.5 %local_y.1.local = f32[40,64,128]{2,1,0:T(8,128)S(1)} custom-call(f32[2880,128]{1,0:T(8,128)S(1)} %get-tuple-element.31.solved, f32[64,128]{1,0:T(8,128)S(1)} %get-tuple-element.32.inverse_y, f32[4,40,128]{2,1,0:T(8,128)S(1)} %get-tuple-element.33.unused.refs_2_), custom_call_target="tpu_custom_call" | custom-call | flops 566231040 | bytes 2949120 | tf_op jit(solution)/shard_map/local_y/pallas_call | solution.py:783
  26.6 0.4 %collective-permute-done.4.refs_0_ = f32[2,40,128]{2,1,0:T(8,128)S(1)} collective-permute-done((f32[2,40,128]{2,1,0:T(8,128)S(1)}, f32[2,40,128]{2,1,0:T(8,128)S(1)}, u32[]{:S(2)}, u32[]{:S(2)}) %collective-permute-start.4) | collective-permute-done | bytes 40992 | tf_op jit(solution)/shard_map/ppermute | solution.py:713
  27.0 1.6 %finish_y.1 = f32[5,8,64,128]{3,2,1,0:T(8,128)} custom-call(f32[8,8,128]{2,1,0:T(8,128)S(1)} %get-tuple-element.30.coefs, f32[40,64,128]{2,1,0:T(8,128)S(1)} %local_y.1.local, f32[64,128]{1,0:T(8,128)S(1)} %get-tuple-element.32.inverse_y, f32[4,40,128]{2,1,0:T(8,128)S(1)} %get-tuple-element.35.entered, f32[2,40,128]{2,1,0:T(8,128)S(1)} %collective-permute-done.4.refs_0_), custom_call_target="tpu_custom_call" | custom-call | tf_op jit(solution)/shard_map/finish_y/pallas_call | solution.py:793
  (3 shorter events, 0.1 us)
Async XLA Ops:
  4.5 1.4 %collective-permute-start = (f32[4,2880]{1,0:T(4,128)S(1)}, f32[4,2880]{1,0:T(4,128)S(1)}, u32[]{:S(2)}, u32[]{:S(2)}) collective-permute-start(f32[4,2880]{1,0:T(4,128)S(1)} %get-tuple-element.28.own), channel_id=1, source_target_pairs={{0,8},{8,0},{16,24},{24,16},{1,9},{9,1},{17,25},{25,17},{2,10},{10... | collective-permute-start | bytes 138248 | tf_op jit(solution)/shard_map/ppermute | solution.py:713
  5.9 4.8 %collective-permute-start.1 = (f32[2,2880]{1,0:T(2,128)S(1)}, f32[2,2880]{1,0:T(2,128)S(1)}, u32[]{:S(2)}, u32[]{:S(2)}) collective-permute-start(f32[2,2880]{1,0:T(2,128)S(1)} %join_pair.1), channel_id=1, source_target_pairs={{0,16},{8,24},{16,0},{24,8},{1,17},{9,25},{17,1},{25,9},{2,18},{10... | collective-permute-start | bytes 69128 | tf_op jit(solution)/shard_map/ppermute | solution.py:713
  12.6 4.5 %collective-permute-start.2 = (f32[4,40,128]{2,1,0:T(8,128)S(1)}, f32[4,40,128]{2,1,0:T(8,128)S(1)}, u32[]{:S(2)}, u32[]{:S(2)}) collective-permute-start(f32[4,40,128]{2,1,0:T(8,128)S(1)} %get-tuple-element.29.unused.refs_0_), channel_id=1, source_target_pairs={{0,1},{1,0},{2,3},{3,2},{4,5},{5,4},{6,7},{7,6},{8,9},{9,8},{10,11... | collective-permute-start | bytes 245768 | tf_op jit(solution)/shard_map/ppermute | solution.py:713
  17.1 4.5 %collective-permute-start.3 = (f32[4,40,128]{2,1,0:T(8,128)S(1)}, f32[4,40,128]{2,1,0:T(8,128)S(1)}, u32[]{:S(2)}, u32[]{:S(2)}) collective-permute-start(f32[4,40,128]{2,1,0:T(8,128)S(1)} %get-tuple-element.34.refs_0_), channel_id=1, source_target_pairs={{0,2},{1,3},{2,0},{3,1},{4,6},{5,7},{6,4},{7,5},{8,10},{9,11},{10,... | collective-permute-start | bytes 245768 | tf_op jit(solution)/shard_map/ppermute | solution.py:713
  21.6 5.4 %collective-permute-start.4 = (f32[2,40,128]{2,1,0:T(8,128)S(1)}, f32[2,40,128]{2,1,0:T(8,128)S(1)}, u32[]{:S(2)}, u32[]{:S(2)}) collective-permute-start(f32[2,40,128]{2,1,0:T(8,128)S(1)} %get-tuple-element.36), channel_id=1, source_target_pairs={{0,4},{1,5},{2,6},{3,7},{4,0},{5,1},{6,2},{7,3},{8,12},{9,13},{10,... | collective-permute-start | bytes 122888 | tf_op jit(solution)/shard_map/ppermute | solution.py:713

commit v4 on v3

--- a/solution.py
+++ b/solution.py
@@ -386,8 +386,9 @@
 def stage_plan(count):
     plan, stride = [], 1
     while stride < count:
-        plan.append((stride, 2))
-        stride *= 2
+        radix = 4 if count // stride >= 4 else 2
+        plan.append((stride, radix))
+        stride *= radix
     return plan
 
 

time: 28.8 us -> 27.3 us (0.948)
  starting transfers between devices: 10.9 us -> 9.75 us
  waiting for transfers between devices: 4.81 us -> 4.47 us
    ppermute x5 -> x6, starting transfers between devices: 10.9 us -> 9.75 us  [exchange(): received.append(lax.ppermute(value, axis, pairs))]
    ppermute x5 -> x6, waiting for transfers between devices: 4.81 us -> 4.47 us  [exchange(): received.append(lax.ppermute(value, axis, pairs))]
  transfers between devices with their start and end apart: 5 -> 6, of which waited for: 4 -> 5; matrix products, arithmetic and copies ran while one was open for 0% -> 0% of each run, Pallas kernels for 17% -> 18%
where the time goes in v4:
time: 27.3 us; the launch traced here: 27.1 us
  Pallas kernels  12.9 us (47%)
  starting transfers between devices  9.75 us (36%)
  waiting for transfers between devices  4.47 us (16%)
    ppermute x6, starting transfers between devices, exchange(): received.append(lax.ppermute(value, axis, pairs))  9.75 us
    pallas_call x1, Pallas kernels, on_device(): pl.pallas_call(functools.partial(first_kernel, ny, nz, partners, paired),...  4.52 us
    ppermute x6, waiting for transfers between devices, exchange(): received.append(lax.ppermute(value, axis, pairs))  4.47 us
    pallas_call x1, Pallas kernels, on_device(): pl.pallas_call(functools.partial(second_kernel, ny, nz, count_z, wy, part...  1.87 us
    pallas_call x1, Pallas kernels, on_device(): pl.pallas_call(functools.partial(third_kernel, arrivals, wy), out_shape=[...  1.82 us
    pallas_call x1, Pallas kernels, on_device(): pl.pallas_call(functools.partial(last_kernel, base, radix, narrow, wy), o...  1.59 us
    pallas_call x1, Pallas kernels, on_device(): pl.pallas_call(functools.partial(local_y_kernel, wy), out_shape=array(pla...  1.54 us
    pallas_call x1, Pallas kernels, on_device(): pl.pallas_call(functools.partial(y_kernel, count_y, wy), out_shape=[array...  1.42 us
  transfers between devices with their start and end apart: 6, of which 5 were waited for; matrix products, arithmetic and copies ran while one was open for 0% of the time, Pallas kernels for 18%

profile of v4, /device:TPU:0, one launch (start us, length us, event | category | flops | bytes accessed | tf_op | source)
XLA Modules:
  0.0 27.1 jit_solution(6932797475074350993)
XLA Ops:
  0.0 4.5 %forcing_and_factor.1 = (bf16[2880,256]{1,0:T(8,128)(2,1)S(1)}, bf16[2880,256]{1,0:T(8,128)(2,1)S(1)}, f32[28,8,128]{2,1,0:T(8,128)S(1)}, f32[8,8,128]{2,1,0:T(8,128)S(1)}, f32[4,2880]{1,0:T(4,128)S(1)}) custom-call(f32[5,8,64,128]{3,2,1,0:T(8,128)} %flow_hbm.1, f32[8,64,128]{2,1,0:T(8,128)} %speed_hbm.1, f32[4,128]{1,0:T(4,128)} %bitcast.2, f32[4,128]{1,0:T(4,128)} %bitcast.3), custom_call_target="tpu_custom_call" | custom-call | tf_op jit(solution)/shard_map/forcing_and_factor/pallas_call | solution.py:692
  4.5 0.5 %collective-permute-start = (f32[4,2880]{1,0:T(4,128)S(1)}, f32[4,2880]{1,0:T(4,128)S(1)}, u32[]{:S(2)}, u32[]{:S(2)}) collective-permute-start(f32[4,2880]{1,0:T(4,128)S(1)} %get-tuple-element.26.own), channel_id=1, source_target_pairs={{0,8},{8,0},{16,24},{24,16},{1,9},{9,1},{17,25},{25,17},{2,10},{10... | collective-permute-start | bytes 138248 | tf_op jit(solution)/shard_map/ppermute | solution.py:714
  5.0 0.9 %collective-permute-done.received.refs_0_ = f32[4,2880]{1,0:T(4,128)S(1)} collective-permute-done((f32[4,2880]{1,0:T(4,128)S(1)}, f32[4,2880]{1,0:T(4,128)S(1)}, u32[]{:S(2)}, u32[]{:S(2)}) %collective-permute-start) | collective-permute-done | bytes 46112 | tf_op jit(solution)/shard_map/ppermute | solution.py:714
  5.9 2.9 %collective-permute-start.1 = (f32[2,2880]{1,0:T(2,128)S(1)}, f32[2,2880]{1,0:T(2,128)S(1)}, u32[]{:S(2)}, u32[]{:S(2)}) collective-permute-start(f32[2,2880]{1,0:T(2,128)S(1)} %join_pair.1), channel_id=1, source_target_pairs={{0,16},{8,24},{16,0},{24,8},{1,17},{9,25},{17,1},{25,9},{2,18},{10... | collective-permute-start | bytes 69128 | tf_op jit(solution)/shard_map/ppermute | solution.py:714
  8.8 1.9 %inverse_z.1 = (bf16[768,128]{1,0:T(8,128)(2,1)S(1)}, f32[24,128]{1,0:T(8,128)S(1)}, f32[4,72,128]{2,1,0:T(8,128)S(1)}) custom-call(f32[8,8,128]{2,1,0:T(8,128)S(1)} %get-tuple-element.19.chains, f32[28,8,128]{2,1,0:T(8,128)S(1)} %get-tuple-element.20.factors), custom_call_target="tpu_custom_call" | custom-call | flops 1132462080 | bytes 4423680 | tf_op jit(solution)/shard_map/inverse_z/pallas_call | solution.py:732
  10.7 0.0 collective-permute-done.1.refs_1_
  10.7 1.8 %finish_z.1 = (f32[2880,128]{1,0:T(8,128)S(1)}, f32[4,40,128]{2,1,0:T(8,128)S(1)}) custom-call(f32[4,72,128]{2,1,0:T(8,128)S(1)} %get-tuple-element.21.weights_y, bf16[2880,256]{1,0:T(8,128)(2,1)S(1)} %get-tuple-element.22.high, bf16[2880,256]{1,0:T(8,128)(2,1)S(1)} %get-tuple-element.23.low, bf16[768,128]{1,0:T(8,128)(2,1)S(1)} %get-tuple-element.24.matrix, ...), custom_call_target="tpu_custom_call" | custom-call | tf_op jit(solution)/shard_map/finish_z/pallas_call | solution.py:746
  12.6 3.0 %collective-permute-start.4 = (f32[4,40,128]{2,1,0:T(8,128)S(1)}, f32[4,40,128]{2,1,0:T(8,128)S(1)}, u32[]{:S(2)}, u32[]{:S(2)}) collective-permute-start(f32[4,40,128]{2,1,0:T(8,128)S(1)} %get-tuple-element.27.unused.refs_0_), channel_id=1, source_target_pairs={{0,3},{1,2},{2,1},{3,0},{4,7},{5,6},{6,5},{7,4},{8,11},{9,10},{10,... | collective-permute-start | bytes 245768 | tf_op jit(solution)/shard_map/ppermute | solution.py:714
  15.6 0.4 %collective-permute-start.3 = (f32[4,40,128]{2,1,0:T(8,128)S(1)}, f32[4,40,128]{2,1,0:T(8,128)S(1)}, u32[]{:S(2)}, u32[]{:S(2)}) collective-permute-start(f32[4,40,128]{2,1,0:T(8,128)S(1)} %get-tuple-element.27.unused.refs_0_), channel_id=1, source_target_pairs={{0,2},{1,3},{2,0},{3,1},{4,6},{5,7},{6,4},{7,5},{8,10},{9,11},{10,... | collective-permute-start | bytes 245768 | tf_op jit(solution)/shard_map/ppermute | solution.py:714
  16.0 0.2 collective-permute-start.2
  16.2 1.4 %inverse_y.1 = (f32[64,128]{1,0:T(8,128)S(1)}, f32[8,8,128]{2,1,0:T(8,128)S(1)}) custom-call(f32[8,8,128]{2,1,0:T(8,128)S(1)} %get-tuple-element.19.chains, f32[28,8,128]{2,1,0:T(8,128)S(1)} %get-tuple-element.20.factors, f32[4,40,128]{2,1,0:T(8,128)S(1)} %get-tuple-element.27.unused.refs_0_), custom_call_target="tpu_custom_call" | custom-call | flops 566231040 | bytes 2949120 | tf_op jit(solution)/shard_map/inverse_y/pallas_call | solution.py:761
  17.7 1.1 %collective-permute-done.4.refs_3_ = f32[4,40,128]{2,1,0:T(8,128)S(1)} collective-permute-done((f32[4,40,128]{2,1,0:T(8,128)S(1)}, f32[4,40,128]{2,1,0:T(8,128)S(1)}, u32[]{:S(2)}, u32[]{:S(2)}) %collective-permute-start.4) | collective-permute-done | bytes 81952 | tf_op jit(solution)/shard_map/ppermute | solution.py:714
  18.7 1.3 %collective-permute-done.3.refs_2_ = f32[4,40,128]{2,1,0:T(8,128)S(1)} collective-permute-done((f32[4,40,128]{2,1,0:T(8,128)S(1)}, f32[4,40,128]{2,1,0:T(8,128)S(1)}, u32[]{:S(2)}, u32[]{:S(2)}) %collective-permute-start.3) | collective-permute-done | bytes 81952 | tf_op jit(solution)/shard_map/ppermute | solution.py:714
  20.0 0.4 %collective-permute-done.2.refs_1_ = f32[4,40,128]{2,1,0:T(8,128)S(1)} collective-permute-done((f32[4,40,128]{2,1,0:T(8,128)S(1)}, f32[4,40,128]{2,1,0:T(8,128)S(1)}, u32[]{:S(2)}, u32[]{:S(2)}) %collective-permute-start.2) | collective-permute-done | bytes 81952 | tf_op jit(solution)/shard_map/ppermute | solution.py:714
  20.5 0.1 join_groups.1
  20.6 2.7 %collective-permute-start.5 = (f32[2,40,128]{2,1,0:T(8,128)S(1)}, f32[2,40,128]{2,1,0:T(8,128)S(1)}, u32[]{:S(2)}, u32[]{:S(2)}) collective-permute-start(f32[2,40,128]{2,1,0:T(8,128)S(1)} %get-tuple-element.32), channel_id=1, source_target_pairs={{0,4},{1,5},{2,6},{3,7},{4,0},{5,1},{6,2},{7,3},{8,12},{9,13},{10,... | collective-permute-start | bytes 122888 | tf_op jit(solution)/shard_map/ppermute | solution.py:714
  23.2 1.5 %local_y.1.local = f32[40,64,128]{2,1,0:T(8,128)S(1)} custom-call(f32[2880,128]{1,0:T(8,128)S(1)} %get-tuple-element.29.solved, f32[64,128]{1,0:T(8,128)S(1)} %get-tuple-element.30.inverse_y, f32[4,40,128]{2,1,0:T(8,128)S(1)} %get-tuple-element.31.unused.entered), custom_call_target="tpu_custom_call" | custom-call | flops 566231040 | bytes 2949120 | tf_op jit(solution)/shard_map/local_y/pallas_call | solution.py:784
  24.8 0.8 %collective-permute-done.5.refs_0_ = f32[2,40,128]{2,1,0:T(8,128)S(1)} collective-permute-done((f32[2,40,128]{2,1,0:T(8,128)S(1)}, f32[2,40,128]{2,1,0:T(8,128)S(1)}, u32[]{:S(2)}, u32[]{:S(2)}) %collective-permute-start.5) | collective-permute-done | bytes 40992 | tf_op jit(solution)/shard_map/ppermute | solution.py:714
  25.5 1.6 %finish_y.1 = f32[5,8,64,128]{3,2,1,0:T(8,128)} custom-call(f32[8,8,128]{2,1,0:T(8,128)S(1)} %get-tuple-element.28.coefs, f32[40,64,128]{2,1,0:T(8,128)S(1)} %local_y.1.local, f32[64,128]{1,0:T(8,128)S(1)} %get-tuple-element.30.inverse_y, f32[4,40,128]{2,1,0:T(8,128)S(1)} %get-tuple-element.31.unused.entered, f32[2,40,128]{2,1,0:T(8,128)S(1)} %collective-permute-done.5.refs_0_), custom_call_target="tpu_custom_call" | custom-call | tf_op jit(solution)/shard_map/finish_y/pallas_call | solution.py:794
  (1 shorter events, 0.0 us)
Async XLA Ops:
  4.5 1.4 %collective-permute-start = (f32[4,2880]{1,0:T(4,128)S(1)}, f32[4,2880]{1,0:T(4,128)S(1)}, u32[]{:S(2)}, u32[]{:S(2)}) collective-permute-start(f32[4,2880]{1,0:T(4,128)S(1)} %get-tuple-element.26.own), channel_id=1, source_target_pairs={{0,8},{8,0},{16,24},{24,16},{1,9},{9,1},{17,25},{25,17},{2,10},{10... | collective-permute-start | bytes 138248 | tf_op jit(solution)/shard_map/ppermute | solution.py:714
  5.9 4.8 %collective-permute-start.1 = (f32[2,2880]{1,0:T(2,128)S(1)}, f32[2,2880]{1,0:T(2,128)S(1)}, u32[]{:S(2)}, u32[]{:S(2)}) collective-permute-start(f32[2,2880]{1,0:T(2,128)S(1)} %join_pair.1), channel_id=1, source_target_pairs={{0,16},{8,24},{16,0},{24,8},{1,17},{9,25},{17,1},{25,9},{2,18},{10... | collective-permute-start | bytes 69128 | tf_op jit(solution)/shard_map/ppermute | solution.py:714
  12.6 6.2 %collective-permute-start.4 = (f32[4,40,128]{2,1,0:T(8,128)S(1)}, f32[4,40,128]{2,1,0:T(8,128)S(1)}, u32[]{:S(2)}, u32[]{:S(2)}) collective-permute-start(f32[4,40,128]{2,1,0:T(8,128)S(1)} %get-tuple-element.27.unused.refs_0_), channel_id=1, source_target_pairs={{0,3},{1,2},{2,1},{3,0},{4,7},{5,6},{6,5},{7,4},{8,11},{9,10},{10,... | collective-permute-start | bytes 245768 | tf_op jit(solution)/shard_map/ppermute | solution.py:714
  15.6 4.4 %collective-permute-start.3 = (f32[4,40,128]{2,1,0:T(8,128)S(1)}, f32[4,40,128]{2,1,0:T(8,128)S(1)}, u32[]{:S(2)}, u32[]{:S(2)}) collective-permute-start(f32[4,40,128]{2,1,0:T(8,128)S(1)} %get-tuple-element.27.unused.refs_0_), channel_id=1, source_target_pairs={{0,2},{1,3},{2,0},{3,1},{4,6},{5,7},{6,4},{7,5},{8,10},{9,11},{10,... | collective-permute-start | bytes 245768 | tf_op jit(solution)/shard_map/ppermute | solution.py:714
  16.0 4.4 %collective-permute-start.2 = (f32[4,40,128]{2,1,0:T(8,128)S(1)}, f32[4,40,128]{2,1,0:T(8,128)S(1)}, u32[]{:S(2)}, u32[]{:S(2)}) collective-permute-start(f32[4,40,128]{2,1,0:T(8,128)S(1)} %get-tuple-element.27.unused.refs_0_), channel_id=1, source_target_pairs={{0,1},{1,0},{2,3},{3,2},{4,5},{5,4},{6,7},{7,6},{8,9},{9,8},{10,11... | collective-permute-start | bytes 245768 | tf_op jit(solution)/shard_map/ppermute | solution.py:714
  20.6 5.0 %collective-permute-start.5 = (f32[2,40,128]{2,1,0:T(8,128)S(1)}, f32[2,40,128]{2,1,0:T(8,128)S(1)}, u32[]{:S(2)}, u32[]{:S(2)}) collective-permute-start(f32[2,40,128]{2,1,0:T(8,128)S(1)} %get-tuple-element.32), channel_id=1, source_target_pairs={{0,4},{1,5},{2,6},{3,7},{4,0},{5,1},{6,2},{7,3},{8,12},{9,13},{10,... | collective-permute-start | bytes 122888 | tf_op jit(solution)/shard_map/ppermute | solution.py:714

commit v5 on v4

--- a/solution.py
+++ b/solution.py
@@ -174,7 +174,7 @@
 
     lane = lax.broadcasted_iota(jnp.int32, (wy, LANES), 1)
     extra_row = lax.broadcasted_iota(jnp.int32, (EXTRA, LANES), 0)
-    for slot in range(2):
+    for slot in range(planes_x):
         for part in range(3):
             spread[slot, part, 0:8, :] = jnp.zeros((8, LANES), jnp.float32)
             spread[slot, part, wy + 8 : wy + 16, :] = jnp.zeros((8, LANES), jnp.float32)
@@ -193,7 +193,7 @@
         fluxes = [half * (values[x] * speed[x]) for x in range(planes_x)]
         extras = []
         for x in range(planes_x):
-            u, flux, slot = values[x], fluxes[x], x % 2
+            u, flux, slot = values[x], fluxes[x], x
             total = centre * u
             for other, sign in ((x + 1, -1), (x - 1, 1)):
                 if 0 <= other < planes_x:
@@ -421,10 +421,8 @@
     return jnp.where(condition, 1.0, 0.0)
 
 
-def second_kernel(ny, nz, count_z, wy, partners, paired, chains, factors, matrix, entering, weights_y, *scratch):
-    columns, stacked, rows_ref = scratch
-    me_z, me_y = lax.axis_index("gz"), lax.axis_index("gy")
-
+def inverse_z_kernel(ny, factors, matrix, columns, stacked, rows_ref):
+    me_z = lax.axis_index("gz")
     columns[0:LANES, 0:32] = transposed(factors, ny + me_z)
     inverse = dense_inverse(columns, 0, LANES, stacked)
     rows_ref[0:LANES, :] = inverse
@@ -437,9 +435,25 @@
         rows_ref[LANES + q : LANES + q + 1, :] = past[2 * q] * tail0 + past[2 * q + 1] * tail1
         rows_ref[2 * LANES - 2 + q : 2 * LANES - 1 + q, :] = ahead[2 * q] * head0 + ahead[2 * q + 1] * head1
     first, second = halves(rows_ref[...])
-    matrix[0 : 2 * LANES, :] = first
-    matrix[2 * LANES : 4 * LANES, :] = second
-    matrix[4 * LANES : 6 * LANES, :] = first
+    matrix[:, 0:LANES] = first
+    matrix[:, LANES : 2 * LANES] = second
+
+
+def whole_rows(matrix, row):
+    start = row // 16 * 16
+    both = matrix[start : start + 16, :].astype(jnp.float32)
+    value = both[:, 0:LANES] + both[:, LANES : 2 * LANES]
+    return value[row - start : row - start + 1]
+
+
+def second_kernel(
+    ny, nz, count_z, wy, partners, paired, chains, factors, matrix, high, low, local, moments, entering, spread_high, spread_low, *scratch
+):
+    columns, weights_y = scratch
+    me_z, me_y = lax.axis_index("gz"), lax.axis_index("gy")
+    planes = moments.shape[0] // 4
+    head0, head1 = whole_rows(matrix, 0), whole_rows(matrix, 1)
+    tail0, tail1 = whole_rows(matrix, LANES - 2), whole_rows(matrix, LANES - 1)
 
     if paired:
         pair = me_z // 2 * 2
@@ -496,6 +510,78 @@
                 value = jnp.where(extra_row == r, v, value)
             weights_y[output, wy : wy + EXTRA, :] = value
 
+    total = planes * (wy + EXTRA)
+
+    def solve(begin, size):
+        rows = slice(begin, begin + size)
+        both = matmul(high[rows, :], matrix[...])
+        value = both[:, 0:LANES] + (both[:, LANES : 2 * LANES] + matmul(low[rows, :], matrix[:, 0:LANES]))
+        local[rows, :] = value
+        return value
+
+    extra = solve(planes * wy, planes * EXTRA)
+    for part in range(planes // 8):
+        core = solve(part * 8 * wy, 8 * wy)
+        for number in range(4):
+            lines = []
+            for k in range(8):
+                index = part * 8 + k
+                value = jnp.sum(core[k * wy : (k + 1) * wy] * weights_y[number, 0:wy, :], axis=0, keepdims=True)
+                past = extra[index * EXTRA : (index + 1) * EXTRA] * weights_y[number, wy : wy + EXTRA, :]
+                lines.append(value + jnp.sum(past, axis=0, keepdims=True))
+            start = number * planes + part * 8
+            moments[start : start + 8, :] = jnp.concatenate(lines, axis=0)
+
+    row = cell // LANES
+    lane = lax.broadcasted_iota(jnp.int32, (1, LANES), 1)
+    even = (lane & 1) == 0
+
+    def chain(number):
+        return tuple(factors[number + k, pl.ds(row, 1), :] for k in range(4))
+
+    def turned(x, by):
+        return pltpu.roll(x, lax.rem(by + 2 * LANES, LANES), 1)
+
+    def tiled(x, period):
+        x = jnp.where(lane < period, x, 0.0)
+        while period < LANES:
+            x = x + lane_roll(x, period)
+            period *= 2
+        return x
+
+    up, down, before, after = chain(12), chain(16), chain(20), chain(24)
+    past_up, past_down = mm(before, up), mm(after, down)
+    plane_row = lax.broadcasted_iota(jnp.int32, (planes, LANES), 0)
+    wide_lane = lax.broadcasted_iota(jnp.int32, (planes, LANES), 1)
+    for column in range(2):
+        same = jnp.where(even, unit[column], unit[2 + column])
+        for number, inside, early, late in (
+            (column, up, turned(cell_weights(past_up, column, even), -start_y(cell)), same),
+            (
+                2 + column,
+                down,
+                same,
+                turned(cell_weights(past_down, column, even), 4 - wy - start_y(cell)),
+            ),
+        ):
+            inside = tiled(turned(cell_weights(inside, column, even), -start_y(cell)), wy)
+            past = jnp.where(lane < 2, early, jnp.where(lane < 4, late, 0.0))
+            past = tiled(past, EXTRA)
+            rows = slice(number * planes, (number + 1) * planes)
+            for begin in range(0, total, LANES):
+                if begin < planes * wy:
+                    owner, value = (begin + wide_lane) // wy, inside
+                else:
+                    owner, value = (begin - planes * wy + wide_lane) // EXTRA, past
+                size = min(LANES, total - begin)
+                first, second = halves(jnp.where(plane_row == owner, value, 0.0))
+                spread_high[rows, begin : begin + size] = first[:, 0:size]
+                spread_low[rows, begin : begin + size] = second[:, 0:size]
+
+
+def start_y(cell):
+    return lax.rem(cell, LANES)
+
 
 def y_kernel(count_y, wy, chains, factors, unused, inverse_y, coefs, columns, stacked):
     me_y = lax.axis_index("gy")
@@ -540,46 +626,48 @@
             coefs[base + k] = value[k]
 
 
-def pair_kernel(own, received, total):
+def pair_kernel(own, received, unused, total):
     total[...] = own[2:4] + received[2:4]
 
 
-def third_kernel(partners, wy, weights_y, high, low, matrix, entering, *refs):
-    messages, (solved, carried) = refs[:partners], refs[partners:]
+def arrived_rows(messages, count):
+    rows = [m[0:2] for m in messages]
+    if count > 2 * len(messages):
+        rows.append(jnp.zeros((count - 2 * len(messages), rows[0].shape[1]), jnp.float32))
+    return jnp.concatenate(rows, axis=0)
+
+
+def third_kernel(moments, spread_high, spread_low, entering, *refs):
+    messages, carried = refs[:-1], refs[-1]
+    count = entering.shape[0] // 3
+    received = arrived_rows(messages, count)
+    first = received.astype(jnp.bfloat16).astype(jnp.float32)
+    both = jnp.concatenate([first, received - first], axis=0).astype(jnp.bfloat16)
+    top = jnp.concatenate([first, jnp.zeros_like(first)], axis=0).astype(jnp.bfloat16)
+    across = (((1,), (1,)), ((), ()))
+    corner = matmul(spread_high[...], both, across) + matmul(spread_low[...], top, across)
+    values = entering[0:count, :] + entering[count : 2 * count, :]
+    added = lax.dot_general(
+        corner,
+        jnp.concatenate([values, values], axis=0),
+        (((1,), (0,)), ((), ())),
+        precision=lax.Precision.HIGHEST,
+        preferred_element_type=jnp.float32,
+    )
     planes = carried.shape[1]
-    received = [m[0:2] for m in messages]
-    padding = entering.shape[0] // 3 - 2 * partners
-    if padding:
-        received.append(jnp.zeros((padding, received[0].shape[1]), jnp.float32))
-    received = jnp.concatenate(received, axis=0)
+    for number in range(4):
+        rows = slice(number * planes, (number + 1) * planes)
+        carried[number] = moments[rows, :] + added[rows]
+
+
+def local_y_kernel(wy, local, entering, inverse_y, unused, *refs):
+    messages, (out, solved) = refs[:-2], refs[-2:]
+    planes = out.shape[0]
+    count = entering.shape[0] // 3
+    received = arrived_rows(messages, count)
     first = received.astype(jnp.bfloat16).astype(jnp.float32)
     received = jnp.concatenate([first, first, received - first], axis=0).T.astype(jnp.bfloat16)
-    entered = entering[...].astype(jnp.bfloat16)
-    parts = planes // 8
-    total = planes * (wy + EXTRA)
-
-    def solve(begin, size):
-        rows = slice(begin, begin + size)
-        left = jnp.concatenate([high[rows, :], high[rows, :], low[rows, :]], axis=1)
-        return matmul(left, matrix[...]) + matmul(received[rows], entered)
-
-    extra = solve(planes * wy, planes * EXTRA)
-    solved[planes * wy : total, :] = extra
-    for part in range(parts):
-        core = solve(part * 8 * wy, 8 * wy)
-        solved[part * 8 * wy : (part + 1) * 8 * wy, :] = core
-        for number in range(4):
-            lines = []
-            for k in range(8):
-                index = part * 8 + k
-                value = jnp.sum(core[k * wy : (k + 1) * wy] * weights_y[number, 0:wy, :], axis=0, keepdims=True)
-                past = extra[index * EXTRA : (index + 1) * EXTRA] * weights_y[number, wy : wy + EXTRA, :]
-                lines.append(value + jnp.sum(past, axis=0, keepdims=True))
-            carried[number, part * 8 : (part + 1) * 8, :] = jnp.concatenate(lines, axis=0)
-
-
-def local_y_kernel(wy, solved, inverse_y, unused, out):
-    planes = out.shape[0]
+    solved[...] = local[...] + matmul(received, entering[...].astype(jnp.bfloat16))
     first, second = halves(inverse_y[:, 0 : wy + EXTRA])
     left = jnp.concatenate([first, second, first], axis=1)
 
@@ -652,9 +740,11 @@
             for number in range(4):
                 value = value + sides[number] * st[number][index : index + 1]
             out[field, x] = value
-        copy = pltpu.make_async_copy(out.at[field], out_hbm.at[field], sent.at[field])
-        copy.start()
-        copies.append(copy)
+            if (x + 1) % 4 == 0:
+                part = (field, pl.ds(x - 3, 4))
+                copy = pltpu.make_async_copy(out.at[part], out_hbm.at[part], sent.at[len(copies)])
+                copy.start()
+                copies.append(copy)
     for copy in copies:
         copy.wait()
 
@@ -699,7 +789,7 @@
             pltpu.VMEM(flow.shape, jnp.float32),
             pltpu.VMEM(speed.shape, jnp.float32),
             pltpu.VMEM((ny + nz, LANES), jnp.float32),
-            pltpu.VMEM((2, 3, wy + 16, LANES), jnp.float32),
+            pltpu.VMEM((planes_x, 3, wy + 16, LANES), jnp.float32),
             pltpu.SemaphoreType.DMA((fields + 3,)),
         ],
         compiler_params=PARAMS,
@@ -714,43 +804,60 @@
             received.append(lax.ppermute(value, axis, pairs))
         return received
 
+    plan = stage_plan(count_y)
+    work = [pltpu.VMEM((LANES + 16, LANES), jnp.float32)] * 2
+    matrix = pl.pallas_call(
+        functools.partial(inverse_z_kernel, ny),
+        out_shape=jax.ShapeDtypeStruct((2 * LANES, 2 * LANES), jnp.bfloat16),
+        in_specs=[VMEM],
+        out_specs=VMEM,
+        scratch_shapes=work + [pltpu.VMEM((2 * LANES, LANES), jnp.float32)],
+        compiler_params=PARAMS,
+        cost_estimate=cost(rows * 1024, 4 * rows * 64),
+        name="inverse_z",
+    )(factors)
     if paired:
         near = exchange(outputs[4:], "gz", count_z, 1, 2)
         total = pl.pallas_call(
             pair_kernel,
             out_shape=array(2, rows),
-            in_specs=[VMEM] * 2,
+            in_specs=[VMEM] * 2 + [HBM],
             out_specs=VMEM,
             compiler_params=PARAMS,
             name="join_pair",
-        )(outputs[4], near[0])
+        )(outputs[4], near[0], matrix)
         received = near + exchange([total], "gz", count_z, 2, 2)
     else:
         received = exchange(outputs[4:], "gz", count_z, 1, count_z)
-    plan = stage_plan(count_y)
-    work = [pltpu.VMEM((LANES + 16, LANES), jnp.float32)] * 2
-    matrix, entering, weights_y = pl.pallas_call(
+    spread = jax.ShapeDtypeStruct((4 * planes, rows), jnp.bfloat16)
+    local, moments, entering, spread_high, spread_low = pl.pallas_call(
         functools.partial(second_kernel, ny, nz, count_z, wy, partners, paired),
         out_shape=[
-            jax.ShapeDtypeStruct((6 * LANES, LANES), jnp.bfloat16),
+            array(rows, LANES),
+            array(4 * planes, LANES),
             array(3 * entering_rows, LANES),
-            array(4, wy + EXTRA, LANES),
+            spread,
+            spread,
         ],
-        in_specs=[SMEM, VMEM],
-        out_specs=[VMEM] * 3,
-        scratch_shapes=work + [pltpu.VMEM((2 * LANES, LANES), jnp.float32)],
+        in_specs=[SMEM] + [VMEM] * 4,
+        out_specs=[VMEM] * 5,
+        scratch_shapes=[
+            pltpu.VMEM((LANES + 16, LANES), jnp.float32),
+            pltpu.VMEM((4, wy + EXTRA, LANES), jnp.float32),
+        ],
         compiler_params=PARAMS,
         cost_estimate=cost(2 * rows * 256 * 128 * 6, 4 * rows * 384),
-        name="inverse_z",
-    )(chains, factors)
-    solved, carried = pl.pallas_call(
-        functools.partial(third_kernel, arrivals, wy),
-        out_shape=[array(rows, LANES), array(4, planes, LANES)],
-        in_specs=[VMEM] * (5 + arrivals),
-        out_specs=[VMEM] * 2,
+        name="local_z",
+    )(chains, factors, matrix, high, low)
+    carried = pl.pallas_call(
+        third_kernel,
+        out_shape=array(4, planes, LANES),
+        in_specs=[VMEM] * (4 + arrivals),
+        out_specs=VMEM,
         compiler_params=PARAMS,
-        name="finish_z",
-    )(weights_y, high, low, matrix, entering, *received)
+        name="carried_y",
+    )(moments, spread_high, spread_low, entering, *received)
+    arrived = received
 
     narrow = plan[-1][1] == 2 and len(plan) > 1
     base, entered, result = 0, None, None
@@ -784,12 +891,13 @@
                 result = pl.pallas_call(
                     functools.partial(local_y_kernel, wy),
                     out_shape=array(planes, wy, LANES),
-                    in_specs=[VMEM] * 2 + [HBM],
+                    in_specs=[VMEM] * 3 + [HBM] + [VMEM] * arrivals,
                     out_specs=VMEM,
+                    scratch_shapes=[pltpu.VMEM((rows, LANES), jnp.float32)],
                     compiler_params=PARAMS,
                     cost_estimate=cost(2 * rows * 128 * 128 * 6, 4 * rows * 256),
                     name="local_y",
-                )(solved, inverse_y, entered)
+                )(local, entering, inverse_y, entered, *arrived)
         else:
             return pl.pallas_call(
                 functools.partial(last_kernel, base, radix, narrow, wy),
@@ -798,7 +906,7 @@
                 out_specs=HBM,
                 scratch_shapes=[
                     pltpu.VMEM(flow.shape, jnp.float32),
-                    pltpu.SemaphoreType.DMA((fields,)),
+                    pltpu.SemaphoreType.DMA((planes // 4,)),
                 ],
                 compiler_params=PARAMS,
                 name="finish_y",

time: 27.3 us -> 27.4 us (level)
  waiting for transfers between devices: 4.47 us -> 4.81 us
    pallas_call x1, Pallas kernels: 1.87 us -> 2.54 us  [on_device(): pl.pallas_call(functools.partial(second_kernel, ny, nz, count_z, wy, part...]
    pallas_call x1 -> x2, Pallas kernels: 1.82 us -> 1.38 us  [the longest x1 0.93 us: on_device(): pl.pallas_call(third_kernel, out_shape=array(4, planes, LANES), in_specs=...]
    pallas_call x1, Pallas kernels: 4.52 us -> 4.1 us  [on_device(): pl.pallas_call(functools.partial(first_kernel, ny, nz, partners, paired),...]
    ppermute x6, waiting for transfers between devices: 4.47 us -> 4.81 us  [exchange(): received.append(lax.ppermute(value, axis, pairs))]
    pallas_call x1, Pallas kernels: 1.54 us -> 1.86 us  [on_device(): pl.pallas_call(functools.partial(local_y_kernel, wy), out_shape=array(pla...]
  transfers between devices with their start and end apart: 6 -> 6, of which waited for: 5 -> 4; matrix products, arithmetic and copies ran while one was open for 0% -> 0% of each run, Pallas kernels for 18% -> 23%
where the time goes in v5:
time: 27.4 us; the launch traced here: 27.3 us
  Pallas kernels  12.8 us (47%)
  starting transfers between devices  9.63 us (35%)
  waiting for transfers between devices  4.81 us (18%)
    ppermute x6, starting transfers between devices, exchange(): received.append(lax.ppermute(value, axis, pairs))  9.63 us
    ppermute x6, waiting for transfers between devices, exchange(): received.append(lax.ppermute(value, axis, pairs))  4.81 us
    pallas_call x1, Pallas kernels, on_device(): pl.pallas_call(functools.partial(first_kernel, ny, nz, partners, paired),...  4.1 us
    pallas_call x1, Pallas kernels, on_device(): pl.pallas_call(functools.partial(second_kernel, ny, nz, count_z, wy, part...  2.54 us
    pallas_call x1, Pallas kernels, on_device(): pl.pallas_call(functools.partial(local_y_kernel, wy), out_shape=array(pla...  1.86 us
    pallas_call x1, Pallas kernels, on_device(): pl.pallas_call(functools.partial(y_kernel, count_y, wy), out_shape=[array...  1.42 us
    pallas_call x1, Pallas kernels, on_device(): pl.pallas_call(functools.partial(last_kernel, base, radix, narrow, wy), o...  1.35 us
    pallas_call x1, Pallas kernels, on_device(): pl.pallas_call(third_kernel, out_shape=array(4, planes, LANES), in_specs=...  0.93 us
  transfers between devices with their start and end apart: 6, of which 4 were waited for; matrix products, arithmetic and copies ran while one was open for 0% of the time, Pallas kernels for 23%

profile of v5, /device:TPU:0, one launch (start us, length us, event | category | flops | bytes accessed | tf_op | source)
XLA Modules:
  0.0 27.3 jit_solution(6787889226727878471)
XLA Ops:
  0.0 4.1 %forcing_and_factor.1 = (bf16[2880,256]{1,0:T(8,128)(2,1)S(1)}, bf16[2880,256]{1,0:T(8,128)(2,1)S(1)}, f32[28,8,128]{2,1,0:T(8,128)S(1)}, f32[8,8,128]{2,1,0:T(8,128)S(1)}, f32[4,2880]{1,0:T(4,128)S(1)}) custom-call(f32[5,8,64,128]{3,2,1,0:T(8,128)} %flow_hbm.1, f32[8,64,128]{2,1,0:T(8,128)} %speed_hbm.1, f32[4,128]{1,0:T(4,128)} %bitcast.2, f32[4,128]{1,0:T(4,128)} %bitcast.3), custom_call_target="tpu_custom_call" | custom-call | tf_op jit(solution)/shard_map/forcing_and_factor/pallas_call | solution.py:782
  4.1 0.5 %collective-permute-start = (f32[4,2880]{1,0:T(4,128)S(1)}, f32[4,2880]{1,0:T(4,128)S(1)}, u32[]{:S(2)}, u32[]{:S(2)}) collective-permute-start(f32[4,2880]{1,0:T(4,128)S(1)} %get-tuple-element.27.own), channel_id=1, source_target_pairs={{0,8},{8,0},{16,24},{24,16},{1,9},{9,1},{17,25},{25,17},{2,10},{10... | collective-permute-start | bytes 138248 | tf_op jit(solution)/shard_map/ppermute | solution.py:804
  4.6 0.5 %inverse_z.1.matrix.unused = bf16[256,256]{1,0:T(8,128)(2,1)S(1)} custom-call(f32[28,8,128]{2,1,0:T(8,128)S(1)} %get-tuple-element.20.factors), custom_call_target="tpu_custom_call" | custom-call | flops 2949120 | bytes 737280 | tf_op jit(solution)/shard_map/inverse_z/pallas_call | solution.py:809
  5.1 0.4 %collective-permute-done.received.refs_0_ = f32[4,2880]{1,0:T(4,128)S(1)} collective-permute-done((f32[4,2880]{1,0:T(4,128)S(1)}, f32[4,2880]{1,0:T(4,128)S(1)}, u32[]{:S(2)}, u32[]{:S(2)}) %collective-permute-start) | collective-permute-done | bytes 46112 | tf_op jit(solution)/shard_map/ppermute | solution.py:804
  5.5 2.9 %collective-permute-start.1 = (f32[2,2880]{1,0:T(2,128)S(1)}, f32[2,2880]{1,0:T(2,128)S(1)}, u32[]{:S(2)}, u32[]{:S(2)}) collective-permute-start(f32[2,2880]{1,0:T(2,128)S(1)} %join_pair.1), channel_id=1, source_target_pairs={{0,16},{8,24},{16,0},{24,8},{1,17},{9,25},{17,1},{25,9},{2,18},{10... | collective-permute-start | bytes 69128 | tf_op jit(solution)/shard_map/ppermute | solution.py:804
  8.4 2.5 %local_z.1 = (f32[2880,128]{1,0:T(8,128)S(1)}, f32[160,128]{1,0:T(8,128)S(1)}, f32[24,128]{1,0:T(8,128)S(1)}, bf16[160,2880]{1,0:T(8,128)(2,1)S(1)}, bf16[160,2880]{1,0:T(8,128)(2,1)S(1)}) custom-call(f32[8,8,128]{2,1,0:T(8,128)S(1)} %get-tuple-element.19.chains, f32[28,8,128]{2,1,0:T(8,128)S(1)} %get-tuple-element.20.factors, ...), custom_call_target="tpu_custom_call" | custom-call | flops 1132462080 | bytes 4423680 | tf_op jit(solution)/shard_map/local_z/pallas_call | solution.py:833
  11.0 0.0 collective-permute-done.1.refs_1_
  11.0 0.9 %carried_y.1.unused.refs_0_ = f32[4,40,128]{2,1,0:T(8,128)S(1)} custom-call(f32[160,128]{1,0:T(8,128)S(1)} %get-tuple-element.23.moments, bf16[160,2880]{1,0:T(8,128)(2,1)S(1)} %get-tuple-element.24.spread_high, bf16[160,2880]{1,0:T(8,128)(2,1)S(1)} %get-tuple-element.25.spread_low, f32[24,128]{1,0:T(8,128)S(1)} %get-tuple-element.26.entering, ...), custom_call_target="tpu_custom_call" | custom-call | tf_op jit(solution)/shard_map/carried_y/pallas_call | solution.py:852
  11.9 1.6 %collective-permute-start.2 = (f32[4,40,128]{2,1,0:T(8,128)S(1)}, f32[4,40,128]{2,1,0:T(8,128)S(1)}, u32[]{:S(2)}, u32[]{:S(2)}) collective-permute-start(f32[4,40,128]{2,1,0:T(8,128)S(1)} %carried_y.1.unused.refs_0_), channel_id=1, source_target_pairs={{0,1},{1,0},{2,3},{3,2},{4,5},{5,4},{6,7},{7,6},{8,9},{9,8},{10,11... | collective-permute-start | bytes 245768 | tf_op jit(solution)/shard_map/ppermute | solution.py:804
  13.5 1.6 %collective-permute-start.3 = (f32[4,40,128]{2,1,0:T(8,128)S(1)}, f32[4,40,128]{2,1,0:T(8,128)S(1)}, u32[]{:S(2)}, u32[]{:S(2)}) collective-permute-start(f32[4,40,128]{2,1,0:T(8,128)S(1)} %carried_y.1.unused.refs_0_), channel_id=1, source_target_pairs={{0,2},{1,3},{2,0},{3,1},{4,6},{5,7},{6,4},{7,5},{8,10},{9,11},{10,... | collective-permute-start | bytes 245768 | tf_op jit(solution)/shard_map/ppermute | solution.py:804
  15.1 0.4 %collective-permute-start.4 = (f32[4,40,128]{2,1,0:T(8,128)S(1)}, f32[4,40,128]{2,1,0:T(8,128)S(1)}, u32[]{:S(2)}, u32[]{:S(2)}) collective-permute-start(f32[4,40,128]{2,1,0:T(8,128)S(1)} %carried_y.1.unused.refs_0_), channel_id=1, source_target_pairs={{0,3},{1,2},{2,1},{3,0},{4,7},{5,6},{6,5},{7,4},{8,11},{9,10},{10,... | collective-permute-start | bytes 245768 | tf_op jit(solution)/shard_map/ppermute | solution.py:804
  15.5 1.4 %inverse_y.1 = (f32[64,128]{1,0:T(8,128)S(1)}, f32[8,8,128]{2,1,0:T(8,128)S(1)}) custom-call(f32[8,8,128]{2,1,0:T(8,128)S(1)} %get-tuple-element.19.chains, f32[28,8,128]{2,1,0:T(8,128)S(1)} %get-tuple-element.20.factors, f32[4,40,128]{2,1,0:T(8,128)S(1)} %carried_y.1.unused.refs_0_), custom_call_target="tpu_custom_call" | custom-call | flops 566231040 | bytes 2949120 | tf_op jit(solution)/shard_map/inverse_y/pallas_call | solution.py:868
  16.9 0.0 collective-permute-done.2.refs_1_
  16.9 1.8 %collective-permute-done.3.refs_2_ = f32[4,40,128]{2,1,0:T(8,128)S(1)} collective-permute-done((f32[4,40,128]{2,1,0:T(8,128)S(1)}, f32[4,40,128]{2,1,0:T(8,128)S(1)}, u32[]{:S(2)}, u32[]{:S(2)}) %collective-permute-start.3) | collective-permute-done | bytes 81952 | tf_op jit(solution)/shard_map/ppermute | solution.py:804
  18.7 1.7 %collective-permute-done.4.refs_3_ = f32[4,40,128]{2,1,0:T(8,128)S(1)} collective-permute-done((f32[4,40,128]{2,1,0:T(8,128)S(1)}, f32[4,40,128]{2,1,0:T(8,128)S(1)}, u32[]{:S(2)}, u32[]{:S(2)}) %collective-permute-start.4) | collective-permute-done | bytes 81952 | tf_op jit(solution)/shard_map/ppermute | solution.py:804
  20.4 0.1 join_groups.1
  20.5 2.7 %collective-permute-start.5 = (f32[2,40,128]{2,1,0:T(8,128)S(1)}, f32[2,40,128]{2,1,0:T(8,128)S(1)}, u32[]{:S(2)}, u32[]{:S(2)}) collective-permute-start(f32[2,40,128]{2,1,0:T(8,128)S(1)} %get-tuple-element.32), channel_id=1, source_target_pairs={{0,4},{1,5},{2,6},{3,7},{4,0},{5,1},{6,2},{7,3},{8,12},{9,13},{10,... | collective-permute-start | bytes 122888 | tf_op jit(solution)/shard_map/ppermute | solution.py:804
  23.2 1.9 %local_y.1.local = f32[40,64,128]{2,1,0:T(8,128)S(1)} custom-call(f32[2880,128]{1,0:T(8,128)S(1)} %get-tuple-element.29.local, f32[24,128]{1,0:T(8,128)S(1)} %get-tuple-element.26.entering, f32[64,128]{1,0:T(8,128)S(1)} %get-tuple-element.30.inverse_y, f32[4,40,128]{2,1,0:T(8,128)S(1)} %get-tuple-element.31.unused.entered, ...), custom_call_target="tpu_custom_call" | custom-call | flops 566231040 | bytes 2949120 | tf_op jit(solution)/shard_map/local_y/pallas_call | solution.py:891
  25.0 0.9 %collective-permute-done.5.refs_0_ = f32[2,40,128]{2,1,0:T(8,128)S(1)} collective-permute-done((f32[2,40,128]{2,1,0:T(8,128)S(1)}, f32[2,40,128]{2,1,0:T(8,128)S(1)}, u32[]{:S(2)}, u32[]{:S(2)}) %collective-permute-start.5) | collective-permute-done | bytes 40992 | tf_op jit(solution)/shard_map/ppermute | solution.py:804
  25.9 1.4 %finish_y.1 = f32[5,8,64,128]{3,2,1,0:T(8,128)} custom-call(f32[8,8,128]{2,1,0:T(8,128)S(1)} %get-tuple-element.28.coefs, f32[40,64,128]{2,1,0:T(8,128)S(1)} %local_y.1.local, f32[64,128]{1,0:T(8,128)S(1)} %get-tuple-element.30.inverse_y, f32[4,40,128]{2,1,0:T(8,128)S(1)} %get-tuple-element.31.unused.entered, f32[2,40,128]{2,1,0:T(8,128)S(1)} %collective-permute-done.5.refs_0_), custom_call_target="tpu_custom_call" | custom-call | tf_op jit(solution)/shard_map/finish_y/pallas_call | solution.py:902
  (1 shorter events, 0.0 us)
Async XLA Ops:
  4.1 1.4 %collective-permute-start = (f32[4,2880]{1,0:T(4,128)S(1)}, f32[4,2880]{1,0:T(4,128)S(1)}, u32[]{:S(2)}, u32[]{:S(2)}) collective-permute-start(f32[4,2880]{1,0:T(4,128)S(1)} %get-tuple-element.27.own), channel_id=1, source_target_pairs={{0,8},{8,0},{16,24},{24,16},{1,9},{9,1},{17,25},{25,17},{2,10},{10... | collective-permute-start | bytes 138248 | tf_op jit(solution)/shard_map/ppermute | solution.py:804
  5.5 5.4 %collective-permute-start.1 = (f32[2,2880]{1,0:T(2,128)S(1)}, f32[2,2880]{1,0:T(2,128)S(1)}, u32[]{:S(2)}, u32[]{:S(2)}) collective-permute-start(f32[2,2880]{1,0:T(2,128)S(1)} %join_pair.1), channel_id=1, source_target_pairs={{0,16},{8,24},{16,0},{24,8},{1,17},{9,25},{17,1},{25,9},{2,18},{10... | collective-permute-start | bytes 69128 | tf_op jit(solution)/shard_map/ppermute | solution.py:804
  11.9 5.0 %collective-permute-start.2 = (f32[4,40,128]{2,1,0:T(8,128)S(1)}, f32[4,40,128]{2,1,0:T(8,128)S(1)}, u32[]{:S(2)}, u32[]{:S(2)}) collective-permute-start(f32[4,40,128]{2,1,0:T(8,128)S(1)} %carried_y.1.unused.refs_0_), channel_id=1, source_target_pairs={{0,1},{1,0},{2,3},{3,2},{4,5},{5,4},{6,7},{7,6},{8,9},{9,8},{10,11... | collective-permute-start | bytes 245768 | tf_op jit(solution)/shard_map/ppermute | solution.py:804
  13.5 5.2 %collective-permute-start.3 = (f32[4,40,128]{2,1,0:T(8,128)S(1)}, f32[4,40,128]{2,1,0:T(8,128)S(1)}, u32[]{:S(2)}, u32[]{:S(2)}) collective-permute-start(f32[4,40,128]{2,1,0:T(8,128)S(1)} %carried_y.1.unused.refs_0_), channel_id=1, source_target_pairs={{0,2},{1,3},{2,0},{3,1},{4,6},{5,7},{6,4},{7,5},{8,10},{9,11},{10,... | collective-permute-start | bytes 245768 | tf_op jit(solution)/shard_map/ppermute | solution.py:804
  15.1 5.3 %collective-permute-start.4 = (f32[4,40,128]{2,1,0:T(8,128)S(1)}, f32[4,40,128]{2,1,0:T(8,128)S(1)}, u32[]{:S(2)}, u32[]{:S(2)}) collective-permute-start(f32[4,40,128]{2,1,0:T(8,128)S(1)} %carried_y.1.unused.refs_0_), channel_id=1, source_target_pairs={{0,3},{1,2},{2,1},{3,0},{4,7},{5,6},{6,5},{7,4},{8,11},{9,10},{10,... | collective-permute-start | bytes 245768 | tf_op jit(solution)/shard_map/ppermute | solution.py:804
  20.5 5.4 %collective-permute-start.5 = (f32[2,40,128]{2,1,0:T(8,128)S(1)}, f32[2,40,128]{2,1,0:T(8,128)S(1)}, u32[]{:S(2)}, u32[]{:S(2)}) collective-permute-start(f32[2,40,128]{2,1,0:T(8,128)S(1)} %get-tuple-element.32), channel_id=1, source_target_pairs={{0,4},{1,5},{2,6},{3,7},{4,0},{5,1},{6,2},{7,3},{8,12},{9,13},{10,... | collective-permute-start | bytes 122888 | tf_op jit(solution)/shard_map/ppermute | solution.py:804

commit v6 on v5

--- a/solution.py
+++ b/solution.py
@@ -421,7 +421,7 @@
     return jnp.where(condition, 1.0, 0.0)
 
 
-def inverse_z_kernel(ny, factors, matrix, columns, stacked, rows_ref):
+def inverse_z_kernel(ny, planes, wy, factors, matrix, spread_high, spread_low, columns, stacked, rows_ref):
     me_z = lax.axis_index("gz")
     columns[0:LANES, 0:32] = transposed(factors, ny + me_z)
     inverse = dense_inverse(columns, 0, LANES, stacked)
@@ -438,101 +438,10 @@
     matrix[:, 0:LANES] = first
     matrix[:, LANES : 2 * LANES] = second
 
-
-def whole_rows(matrix, row):
-    start = row // 16 * 16
-    both = matrix[start : start + 16, :].astype(jnp.float32)
-    value = both[:, 0:LANES] + both[:, LANES : 2 * LANES]
-    return value[row - start : row - start + 1]
-
-
-def second_kernel(
-    ny, nz, count_z, wy, partners, paired, chains, factors, matrix, high, low, local, moments, entering, spread_high, spread_low, *scratch
-):
-    columns, weights_y = scratch
-    me_z, me_y = lax.axis_index("gz"), lax.axis_index("gy")
-    planes = moments.shape[0] // 4
-    head0, head1 = whole_rows(matrix, 0), whole_rows(matrix, 1)
-    tail0, tail1 = whole_rows(matrix, LANES - 2), whole_rows(matrix, LANES - 1)
-
-    if paired:
-        pair = me_z // 2 * 2
-        begins, ends = [me_z, pair], [me_z + 1, pair + 2]
-        lowers = [me_z % 2 == 1, pair > 0]
-    else:
-        others = [jnp.bitwise_xor(me_z, k) for k in range(1, partners + 1)]
-        begins, ends = [other + 1 for other in others], others
-        lowers = [other < me_z for other in others]
-    size = len(begins)
-    up = chain_products(
-        chains, 0, lambda b: (ny + b, 0), count_z, begins, [me_z] * size, [1.0] * size, False
-    )
-    down = chain_products(
-        chains, 4, lambda b: (ny + b, LANES - 1), count_z, [me_z + 1] * size, ends, [1.0] * size, True
-    )
-    stack = []
-    for k, lower in enumerate(lowers):
-        for p in range(2):
-            from_low = up[2 * p][k : k + 1] * head0 + up[2 * p + 1][k : k + 1] * head1
-            from_high = down[2 * p][k : k + 1] * tail0 + down[2 * p + 1][k : k + 1] * tail1
-            stack.append(jnp.where(lower, from_low, from_high))
-    while len(stack) % 8:
-        stack.append(jnp.zeros((1, LANES), jnp.float32))
-    stack = jnp.concatenate(stack, axis=0)
-    first = stack.astype(jnp.bfloat16).astype(jnp.float32)
-    entering[...] = jnp.concatenate([first, stack - first, first], axis=0)
-
-    cell = me_y * wy
-    columns[0:LANES, 0:32] = transposed(factors, cell // LANES)
-    start = lax.rem(cell, LANES)
-    row = lax.broadcasted_iota(jnp.int32, (wy, LANES), 0)
-    extra_row = lax.broadcasted_iota(jnp.int32, (EXTRA, LANES), 0)
+    cell = lax.axis_index("gy") * wy
+    row = cell // LANES
+    total = planes * (wy + EXTRA)
     unit = (1.0, 0.0, 0.0, 1.0)
-
-    def head(number):
-        return tuple(columns[pl.ds(start, 1), number + k : number + k + 1] for k in range(4))
-
-    def tail(number):
-        return tuple(columns[pl.ds(start + wy - 1, 1), number + k : number + k + 1] for k in range(4))
-
-    past_up, past_down = mm(head(12), head(20)), mm(tail(16), tail(24))
-    for column in range(2):
-        for output, number in ((column, 20), (2 + column, 24)):
-            even = columns[pl.ds(start, wy), number + column : number + column + 1]
-            odd = columns[pl.ds(start, wy), number + 2 + column : number + 3 + column]
-            weights_y[output, 0:wy, :] = jnp.where((row & 1) == 0, even, odd)
-        for output, early, late in (
-            (column, (past_up[column], past_up[2 + column]), (unit[column], unit[2 + column])),
-            (2 + column, (unit[column], unit[2 + column]), (past_down[column], past_down[2 + column])),
-        ):
-            value = jnp.zeros((EXTRA, LANES), jnp.float32)
-            for r, v in enumerate(early + late):
-                value = jnp.where(extra_row == r, v, value)
-            weights_y[output, wy : wy + EXTRA, :] = value
-
-    total = planes * (wy + EXTRA)
-
-    def solve(begin, size):
-        rows = slice(begin, begin + size)
-        both = matmul(high[rows, :], matrix[...])
-        value = both[:, 0:LANES] + (both[:, LANES : 2 * LANES] + matmul(low[rows, :], matrix[:, 0:LANES]))
-        local[rows, :] = value
-        return value
-
-    extra = solve(planes * wy, planes * EXTRA)
-    for part in range(planes // 8):
-        core = solve(part * 8 * wy, 8 * wy)
-        for number in range(4):
-            lines = []
-            for k in range(8):
-                index = part * 8 + k
-                value = jnp.sum(core[k * wy : (k + 1) * wy] * weights_y[number, 0:wy, :], axis=0, keepdims=True)
-                past = extra[index * EXTRA : (index + 1) * EXTRA] * weights_y[number, wy : wy + EXTRA, :]
-                lines.append(value + jnp.sum(past, axis=0, keepdims=True))
-            start = number * planes + part * 8
-            moments[start : start + 8, :] = jnp.concatenate(lines, axis=0)
-
-    row = cell // LANES
     lane = lax.broadcasted_iota(jnp.int32, (1, LANES), 1)
     even = (lane & 1) == 0
 
@@ -579,6 +488,100 @@
                 spread_low[rows, begin : begin + size] = second[:, 0:size]
 
 
+def whole_rows(matrix, row):
+    start = row // 16 * 16
+    both = matrix[start : start + 16, :].astype(jnp.float32)
+    value = both[:, 0:LANES] + both[:, LANES : 2 * LANES]
+    return value[row - start : row - start + 1]
+
+
+def second_kernel(
+    ny, nz, count_z, wy, partners, paired, chains, factors, matrix, high, low, local, moments, entering, *scratch
+):
+    columns, weights_y = scratch
+    me_z, me_y = lax.axis_index("gz"), lax.axis_index("gy")
+    planes = moments.shape[0] // 4
+    head0, head1 = whole_rows(matrix, 0), whole_rows(matrix, 1)
+    tail0, tail1 = whole_rows(matrix, LANES - 2), whole_rows(matrix, LANES - 1)
+
+    if paired:
+        pair = me_z // 2 * 2
+        begins, ends = [me_z, pair], [me_z + 1, pair + 2]
+        lowers = [me_z % 2 == 1, pair > 0]
+    else:
+        others = [jnp.bitwise_xor(me_z, k) for k in range(1, partners + 1)]
+        begins, ends = [other + 1 for other in others], others
+        lowers = [other < me_z for other in others]
+    size = len(begins)
+    up = chain_products(
+        chains, 0, lambda b: (ny + b, 0), count_z, begins, [me_z] * size, [1.0] * size, False
+    )
+    down = chain_products(
+        chains, 4, lambda b: (ny + b, LANES - 1), count_z, [me_z + 1] * size, ends, [1.0] * size, True
+    )
+    stack = []
+    for k, lower in enumerate(lowers):
+        for p in range(2):
+            from_low = up[2 * p][k : k + 1] * head0 + up[2 * p + 1][k : k + 1] * head1
+            from_high = down[2 * p][k : k + 1] * tail0 + down[2 * p + 1][k : k + 1] * tail1
+            stack.append(jnp.where(lower, from_low, from_high))
+    while len(stack) % 8:
+        stack.append(jnp.zeros((1, LANES), jnp.float32))
+    stack = jnp.concatenate(stack, axis=0)
+    first = stack.astype(jnp.bfloat16).astype(jnp.float32)
+    entering[...] = jnp.concatenate([first, stack - first, first], axis=0)
+
+    cell = me_y * wy
+    columns[0:LANES, 0:32] = transposed(factors, cell // LANES)
+    start = lax.rem(cell, LANES)
+    row = lax.broadcasted_iota(jnp.int32, (wy, LANES), 0)
+    extra_row = lax.broadcasted_iota(jnp.int32, (EXTRA, LANES), 0)
+    unit = (1.0, 0.0, 0.0, 1.0)
+
+    def head(number):
+        return tuple(columns[pl.ds(start, 1), number + k : number + k + 1] for k in range(4))
+
+    def tail(number):
+        return tuple(columns[pl.ds(start + wy - 1, 1), number + k : number + k + 1] for k in range(4))
+
+    past_up, past_down = mm(head(12), head(20)), mm(tail(16), tail(24))
+    for column in range(2):
+        for output, number in ((column, 20), (2 + column, 24)):
+            even = columns[pl.ds(start, wy), number + column : number + column + 1]
+            odd = columns[pl.ds(start, wy), number + 2 + column : number + 3 + column]
+            weights_y[output, 0:wy, :] = jnp.where((row & 1) == 0, even, odd)
+        for output, early, late in (
+            (column, (past_up[column], past_up[2 + column]), (unit[column], unit[2 + column])),
+            (2 + column, (unit[column], unit[2 + column]), (past_down[column], past_down[2 + column])),
+        ):
+            value = jnp.zeros((EXTRA, LANES), jnp.float32)
+            for r, v in enumerate(early + late):
+                value = jnp.where(extra_row == r, v, value)
+            weights_y[output, wy : wy + EXTRA, :] = value
+
+    total = planes * (wy + EXTRA)
+
+    def solve(begin, size):
+        rows = slice(begin, begin + size)
+        both = matmul(high[rows, :], matrix[...])
+        value = both[:, 0:LANES] + (both[:, LANES : 2 * LANES] + matmul(low[rows, :], matrix[:, 0:LANES]))
+        local[rows, :] = value
+        return value
+
+    extra = solve(planes * wy, planes * EXTRA)
+    for part in range(planes // 8):
+        core = solve(part * 8 * wy, 8 * wy)
+        for number in range(4):
+            lines = []
+            for k in range(8):
+                index = part * 8 + k
+                value = jnp.sum(core[k * wy : (k + 1) * wy] * weights_y[number, 0:wy, :], axis=0, keepdims=True)
+                past = extra[index * EXTRA : (index + 1) * EXTRA] * weights_y[number, wy : wy + EXTRA, :]
+                lines.append(value + jnp.sum(past, axis=0, keepdims=True))
+            start = number * planes + part * 8
+            moments[start : start + 8, :] = jnp.concatenate(lines, axis=0)
+
+
 def start_y(cell):
     return lax.rem(cell, LANES)
 
@@ -697,7 +700,7 @@
 
 
 def stage_kernel(base, stride, radix, narrow, has_entered, coefs, *refs):
-    values = refs[:radix]
+    values = (refs[0],) + tuple(refs[1:radix][::-1])
     position = radix
     entered = None
     if has_entered:
@@ -798,19 +801,20 @@
     high, low, factors, chains = outputs[:4]
 
     def exchange(values, axis, count, stride, radix):
-        received = []
-        for k, value in zip(range(1, radix), values):
+        received = {}
+        for k in reversed(range(1, radix)):
             pairs = [(i, i ^ (k * stride)) for i in range(count)]
-            received.append(lax.ppermute(value, axis, pairs))
-        return received
+            received[k] = lax.ppermute(values[k - 1], axis, pairs)
+        return [received[k] for k in range(1, radix)]
 
     plan = stage_plan(count_y)
     work = [pltpu.VMEM((LANES + 16, LANES), jnp.float32)] * 2
-    matrix = pl.pallas_call(
-        functools.partial(inverse_z_kernel, ny),
-        out_shape=jax.ShapeDtypeStruct((2 * LANES, 2 * LANES), jnp.bfloat16),
+    spread = jax.ShapeDtypeStruct((4 * planes, rows), jnp.bfloat16)
+    matrix, spread_high, spread_low = pl.pallas_call(
+        functools.partial(inverse_z_kernel, ny, planes, wy),
+        out_shape=[jax.ShapeDtypeStruct((2 * LANES, 2 * LANES), jnp.bfloat16), spread, spread],
         in_specs=[VMEM],
-        out_specs=VMEM,
+        out_specs=[VMEM] * 3,
         scratch_shapes=work + [pltpu.VMEM((2 * LANES, LANES), jnp.float32)],
         compiler_params=PARAMS,
         cost_estimate=cost(rows * 1024, 4 * rows * 64),
@@ -829,18 +833,15 @@
         received = near + exchange([total], "gz", count_z, 2, 2)
     else:
         received = exchange(outputs[4:], "gz", count_z, 1, count_z)
-    spread = jax.ShapeDtypeStruct((4 * planes, rows), jnp.bfloat16)
-    local, moments, entering, spread_high, spread_low = pl.pallas_call(
+    local, moments, entering = pl.pallas_call(
         functools.partial(second_kernel, ny, nz, count_z, wy, partners, paired),
         out_shape=[
             array(rows, LANES),
             array(4 * planes, LANES),
             array(3 * entering_rows, LANES),
-            spread,
-            spread,
         ],
         in_specs=[SMEM] + [VMEM] * 4,
-        out_specs=[VMEM] * 5,
+        out_specs=[VMEM] * 3,
         scratch_shapes=[
             pltpu.VMEM((LANES + 16, LANES), jnp.float32),
             pltpu.VMEM((4, wy + EXTRA, LANES), jnp.float32),
@@ -877,7 +878,7 @@
             )(chains, factors, carried)
         if number + 1 < len(plan):
             slim = narrow and number + 2 == len(plan)
-            inputs = [carried] + received + ([entered] if entered is not None else [])
+            inputs = [carried] + received[::-1] + ([entered] if entered is not None else [])
             carried, entered = pl.pallas_call(
                 functools.partial(stage_kernel, base, stride, radix, slim, entered is not None),
                 out_shape=[array(2 if slim else 4, planes, LANES), array(4, planes, LANES)],

time: 27.4 us -> 25.7 us (0.938)
  waiting for transfers between devices: 4.81 us -> 3.14 us
    ppermute x6, waiting for transfers between devices: 4.81 us -> 3.14 us  [exchange(): received[k] = lax.ppermute(values[k - 1], axis, pairs)]
    pallas_call x1, Pallas kernels: 2.54 us -> 2.22 us  [on_device(): pl.pallas_call(functools.partial(second_kernel, ny, nz, count_z, wy, part...]
    pallas_call x1, Pallas kernels: 0.45 us -> 0.76 us  [on_device(): pl.pallas_call(functools.partial(inverse_z_kernel, ny, planes, wy), out_s...]
  transfers between devices with their start and end apart: 6 -> 6, of which waited for: 4 -> 5; matrix products, arithmetic and copies ran while one was open for 0% -> 0% of each run, Pallas kernels for 23% -> 24%
where the time goes in v6:
time: 25.7 us; the launch traced here: 25.6 us
  Pallas kernels  12.7 us (49%)
  starting transfers between devices  9.64 us (38%)
  waiting for transfers between devices  3.14 us (12%)
    ppermute x6, starting transfers between devices, exchange(): received[k] = lax.ppermute(values[k - 1], axis, pairs)  9.64 us
    pallas_call x1, Pallas kernels, on_device(): pl.pallas_call(functools.partial(first_kernel, ny, nz, partners, paired),...  4.1 us
    ppermute x6, waiting for transfers between devices, exchange(): received[k] = lax.ppermute(values[k - 1], axis, pairs)  3.14 us
    pallas_call x1, Pallas kernels, on_device(): pl.pallas_call(functools.partial(second_kernel, ny, nz, count_z, wy, part...  2.22 us
    pallas_call x1, Pallas kernels, on_device(): pl.pallas_call(functools.partial(local_y_kernel, wy), out_shape=array(pla...  1.86 us
    pallas_call x1, Pallas kernels, on_device(): pl.pallas_call(functools.partial(y_kernel, count_y, wy), out_shape=[array...  1.42 us
    pallas_call x1, Pallas kernels, on_device(): pl.pallas_call(functools.partial(last_kernel, base, radix, narrow, wy), o...  1.35 us
    pallas_call x1, Pallas kernels, on_device(): pl.pallas_call(third_kernel, out_shape=array(4, planes, LANES), in_specs=...  0.93 us
  transfers between devices with their start and end apart: 6, of which 5 were waited for; matrix products, arithmetic and copies ran while one was open for 0% of the time, Pallas kernels for 24%

profile of v6, /device:TPU:0, one launch (start us, length us, event | category | flops | bytes accessed | tf_op | source)
XLA Modules:
  0.0 25.6 jit_solution(16287827561529416380)
XLA Ops:
  0.0 4.1 %forcing_and_factor.1 = (bf16[2880,256]{1,0:T(8,128)(2,1)S(1)}, bf16[2880,256]{1,0:T(8,128)(2,1)S(1)}, f32[28,8,128]{2,1,0:T(8,128)S(1)}, f32[8,8,128]{2,1,0:T(8,128)S(1)}, f32[4,2880]{1,0:T(4,128)S(1)}) custom-call(f32[5,8,64,128]{3,2,1,0:T(8,128)} %flow_hbm.1, f32[8,64,128]{2,1,0:T(8,128)} %speed_hbm.1, f32[4,128]{1,0:T(4,128)} %bitcast.2, f32[4,128]{1,0:T(4,128)} %bitcast.3), custom_call_target="tpu_custom_call" | custom-call | tf_op jit(solution)/shard_map/forcing_and_factor/pallas_call | solution.py:785
  4.1 0.5 %collective-permute-start = (f32[4,2880]{1,0:T(4,128)S(1)}, f32[4,2880]{1,0:T(4,128)S(1)}, u32[]{:S(2)}, u32[]{:S(2)}) collective-permute-start(f32[4,2880]{1,0:T(4,128)S(1)} %get-tuple-element.29.own), channel_id=1, source_target_pairs={{0,8},{8,0},{16,24},{24,16},{1,9},{9,1},{17,25},{25,17},{2,10},{10... | collective-permute-start | bytes 138248 | tf_op jit(solution)/shard_map/ppermute | solution.py:807
  4.6 0.8 %inverse_z.1 = (bf16[256,256]{1,0:T(8,128)(2,1)S(1)}, bf16[160,2880]{1,0:T(8,128)(2,1)S(1)}, bf16[160,2880]{1,0:T(8,128)(2,1)S(1)}) custom-call(f32[28,8,128]{2,1,0:T(8,128)S(1)} %get-tuple-element.21.factors), custom_call_target="tpu_custom_call" | custom-call | flops 2949120 | bytes 737280 | tf_op jit(solution)/shard_map/inverse_z/pallas_call | solution.py:813
  5.4 0.1 collective-permute-done.received.refs_0_
  5.5 2.9 %collective-permute-start.1 = (f32[2,2880]{1,0:T(2,128)S(1)}, f32[2,2880]{1,0:T(2,128)S(1)}, u32[]{:S(2)}, u32[]{:S(2)}) collective-permute-start(f32[2,2880]{1,0:T(2,128)S(1)} %join_pair.1), channel_id=1, source_target_pairs={{0,16},{8,24},{16,0},{24,8},{1,17},{9,25},{17,1},{25,9},{2,18},{10... | collective-permute-start | bytes 69128 | tf_op jit(solution)/shard_map/ppermute | solution.py:807
  8.4 2.2 %local_z.1 = (f32[2880,128]{1,0:T(8,128)S(1)}, f32[160,128]{1,0:T(8,128)S(1)}, f32[24,128]{1,0:T(8,128)S(1)}) custom-call(f32[8,8,128]{2,1,0:T(8,128)S(1)} %get-tuple-element.20.chains, f32[28,8,128]{2,1,0:T(8,128)S(1)} %get-tuple-element.21.factors, bf16[256,256]{1,0:T(8,128)(2,1)S(1)} %get-tuple-element.22.matrix.unused, ...), custom_call_target="tpu_custom_call" | custom-call | flops 1132462080 | bytes 4423680 | tf_op jit(solution)/shard_map/local_z/pallas_call | solution.py:836
  10.6 0.0 collective-permute-done.1.refs_1_
  10.7 0.9 %carried_y.1.unused.refs_0_ = f32[4,40,128]{2,1,0:T(8,128)S(1)} custom-call(f32[160,128]{1,0:T(8,128)S(1)} %get-tuple-element.25.moments, bf16[160,2880]{1,0:T(8,128)(2,1)S(1)} %get-tuple-element.26.spread_high, bf16[160,2880]{1,0:T(8,128)(2,1)S(1)} %get-tuple-element.27.spread_low, f32[24,128]{1,0:T(8,128)S(1)} %get-tuple-element.28.entering, ...), custom_call_target="tpu_custom_call" | custom-call | tf_op jit(solution)/shard_map/carried_y/pallas_call | solution.py:853
  11.6 2.7 %collective-permute-start.2 = (f32[4,40,128]{2,1,0:T(8,128)S(1)}, f32[4,40,128]{2,1,0:T(8,128)S(1)}, u32[]{:S(2)}, u32[]{:S(2)}) collective-permute-start(f32[4,40,128]{2,1,0:T(8,128)S(1)} %carried_y.1.unused.refs_0_), channel_id=1, source_target_pairs={{0,3},{1,2},{2,1},{3,0},{4,7},{5,6},{6,5},{7,4},{8,11},{9,10},{10,... | collective-permute-start | bytes 245768 | tf_op jit(solution)/shard_map/ppermute | solution.py:807
  14.3 0.4 %collective-permute-start.3 = (f32[4,40,128]{2,1,0:T(8,128)S(1)}, f32[4,40,128]{2,1,0:T(8,128)S(1)}, u32[]{:S(2)}, u32[]{:S(2)}) collective-permute-start(f32[4,40,128]{2,1,0:T(8,128)S(1)} %carried_y.1.unused.refs_0_), channel_id=1, source_target_pairs={{0,2},{1,3},{2,0},{3,1},{4,6},{5,7},{6,4},{7,5},{8,10},{9,11},{10,... | collective-permute-start | bytes 245768 | tf_op jit(solution)/shard_map/ppermute | solution.py:807
  14.7 0.4 %collective-permute-start.4 = (f32[4,40,128]{2,1,0:T(8,128)S(1)}, f32[4,40,128]{2,1,0:T(8,128)S(1)}, u32[]{:S(2)}, u32[]{:S(2)}) collective-permute-start(f32[4,40,128]{2,1,0:T(8,128)S(1)} %carried_y.1.unused.refs_0_), channel_id=1, source_target_pairs={{0,1},{1,0},{2,3},{3,2},{4,5},{5,4},{6,7},{7,6},{8,9},{9,8},{10,11... | collective-permute-start | bytes 245768 | tf_op jit(solution)/shard_map/ppermute | solution.py:807
  15.1 1.4 %inverse_y.1 = (f32[64,128]{1,0:T(8,128)S(1)}, f32[8,8,128]{2,1,0:T(8,128)S(1)}) custom-call(f32[8,8,128]{2,1,0:T(8,128)S(1)} %get-tuple-element.20.chains, f32[28,8,128]{2,1,0:T(8,128)S(1)} %get-tuple-element.21.factors, f32[4,40,128]{2,1,0:T(8,128)S(1)} %carried_y.1.unused.refs_0_), custom_call_target="tpu_custom_call" | custom-call | flops 566231040 | bytes 2949120 | tf_op jit(solution)/shard_map/inverse_y/pallas_call | solution.py:869
  16.6 1.1 %collective-permute-done.2.refs_1_ = f32[4,40,128]{2,1,0:T(8,128)S(1)} collective-permute-done((f32[4,40,128]{2,1,0:T(8,128)S(1)}, f32[4,40,128]{2,1,0:T(8,128)S(1)}, u32[]{:S(2)}, u32[]{:S(2)}) %collective-permute-start.2) | collective-permute-done | bytes 81952 | tf_op jit(solution)/shard_map/ppermute | solution.py:807
  17.7 1.2 %collective-permute-done.3.refs_2_ = f32[4,40,128]{2,1,0:T(8,128)S(1)} collective-permute-done((f32[4,40,128]{2,1,0:T(8,128)S(1)}, f32[4,40,128]{2,1,0:T(8,128)S(1)}, u32[]{:S(2)}, u32[]{:S(2)}) %collective-permute-start.3) | collective-permute-done | bytes 81952 | tf_op jit(solution)/shard_map/ppermute | solution.py:807
  18.9 0.3 %collective-permute-done.4.refs_3_ = f32[4,40,128]{2,1,0:T(8,128)S(1)} collective-permute-done((f32[4,40,128]{2,1,0:T(8,128)S(1)}, f32[4,40,128]{2,1,0:T(8,128)S(1)}, u32[]{:S(2)}, u32[]{:S(2)}) %collective-permute-start.4) | collective-permute-done | bytes 81952 | tf_op jit(solution)/shard_map/ppermute | solution.py:807
  19.2 0.1 join_groups.1
  19.3 2.7 %collective-permute-start.5 = (f32[2,40,128]{2,1,0:T(8,128)S(1)}, f32[2,40,128]{2,1,0:T(8,128)S(1)}, u32[]{:S(2)}, u32[]{:S(2)}) collective-permute-start(f32[2,40,128]{2,1,0:T(8,128)S(1)} %get-tuple-element.34), channel_id=1, source_target_pairs={{0,4},{1,5},{2,6},{3,7},{4,0},{5,1},{6,2},{7,3},{8,12},{9,13},{10,... | collective-permute-start | bytes 122888 | tf_op jit(solution)/shard_map/ppermute | solution.py:807
  21.9 1.9 %local_y.1.local = f32[40,64,128]{2,1,0:T(8,128)S(1)} custom-call(f32[2880,128]{1,0:T(8,128)S(1)} %get-tuple-element.31.local, f32[24,128]{1,0:T(8,128)S(1)} %get-tuple-element.28.entering, f32[64,128]{1,0:T(8,128)S(1)} %get-tuple-element.32.inverse_y, f32[4,40,128]{2,1,0:T(8,128)S(1)} %get-tuple-element.33.unused.entered, ...), custom_call_target="tpu_custom_call" | custom-call | flops 566231040 | bytes 2949120 | tf_op jit(solution)/shard_map/local_y/pallas_call | solution.py:892
  23.8 0.4 %collective-permute-done.5.refs_0_ = f32[2,40,128]{2,1,0:T(8,128)S(1)} collective-permute-done((f32[2,40,128]{2,1,0:T(8,128)S(1)}, f32[2,40,128]{2,1,0:T(8,128)S(1)}, u32[]{:S(2)}, u32[]{:S(2)}) %collective-permute-start.5) | collective-permute-done | bytes 40992 | tf_op jit(solution)/shard_map/ppermute | solution.py:807
  24.2 1.4 %finish_y.1 = f32[5,8,64,128]{3,2,1,0:T(8,128)} custom-call(f32[8,8,128]{2,1,0:T(8,128)S(1)} %get-tuple-element.30.coefs, f32[40,64,128]{2,1,0:T(8,128)S(1)} %local_y.1.local, f32[64,128]{1,0:T(8,128)S(1)} %get-tuple-element.32.inverse_y, f32[4,40,128]{2,1,0:T(8,128)S(1)} %get-tuple-element.33.unused.entered, f32[2,40,128]{2,1,0:T(8,128)S(1)} %collective-permute-done.5.refs_0_), custom_call_target="tpu_custom_call" | custom-call | tf_op jit(solution)/shard_map/finish_y/pallas_call | solution.py:903
  (1 shorter events, 0.0 us)
Async XLA Ops:
  4.1 1.4 %collective-permute-start = (f32[4,2880]{1,0:T(4,128)S(1)}, f32[4,2880]{1,0:T(4,128)S(1)}, u32[]{:S(2)}, u32[]{:S(2)}) collective-permute-start(f32[4,2880]{1,0:T(4,128)S(1)} %get-tuple-element.29.own), channel_id=1, source_target_pairs={{0,8},{8,0},{16,24},{24,16},{1,9},{9,1},{17,25},{25,17},{2,10},{10... | collective-permute-start | bytes 138248 | tf_op jit(solution)/shard_map/ppermute | solution.py:807
  5.5 5.1 %collective-permute-start.1 = (f32[2,2880]{1,0:T(2,128)S(1)}, f32[2,2880]{1,0:T(2,128)S(1)}, u32[]{:S(2)}, u32[]{:S(2)}) collective-permute-start(f32[2,2880]{1,0:T(2,128)S(1)} %join_pair.1), channel_id=1, source_target_pairs={{0,16},{8,24},{16,0},{24,8},{1,17},{9,25},{17,1},{25,9},{2,18},{10... | collective-permute-start | bytes 69128 | tf_op jit(solution)/shard_map/ppermute | solution.py:807
  11.6 6.1 %collective-permute-start.2 = (f32[4,40,128]{2,1,0:T(8,128)S(1)}, f32[4,40,128]{2,1,0:T(8,128)S(1)}, u32[]{:S(2)}, u32[]{:S(2)}) collective-permute-start(f32[4,40,128]{2,1,0:T(8,128)S(1)} %carried_y.1.unused.refs_0_), channel_id=1, source_target_pairs={{0,3},{1,2},{2,1},{3,0},{4,7},{5,6},{6,5},{7,4},{8,11},{9,10},{10,... | collective-permute-start | bytes 245768 | tf_op jit(solution)/shard_map/ppermute | solution.py:807
  14.3 4.6 %collective-permute-start.3 = (f32[4,40,128]{2,1,0:T(8,128)S(1)}, f32[4,40,128]{2,1,0:T(8,128)S(1)}, u32[]{:S(2)}, u32[]{:S(2)}) collective-permute-start(f32[4,40,128]{2,1,0:T(8,128)S(1)} %carried_y.1.unused.refs_0_), channel_id=1, source_target_pairs={{0,2},{1,3},{2,0},{3,1},{4,6},{5,7},{6,4},{7,5},{8,10},{9,11},{10,... | collective-permute-start | bytes 245768 | tf_op jit(solution)/shard_map/ppermute | solution.py:807
  14.7 4.4 %collective-permute-start.4 = (f32[4,40,128]{2,1,0:T(8,128)S(1)}, f32[4,40,128]{2,1,0:T(8,128)S(1)}, u32[]{:S(2)}, u32[]{:S(2)}) collective-permute-start(f32[4,40,128]{2,1,0:T(8,128)S(1)} %carried_y.1.unused.refs_0_), channel_id=1, source_target_pairs={{0,1},{1,0},{2,3},{3,2},{4,5},{5,4},{6,7},{7,6},{8,9},{9,8},{10,11... | collective-permute-start | bytes 245768 | tf_op jit(solution)/shard_map/ppermute | solution.py:807
  19.3 5.0 %collective-permute-start.5 = (f32[2,40,128]{2,1,0:T(8,128)S(1)}, f32[2,40,128]{2,1,0:T(8,128)S(1)}, u32[]{:S(2)}, u32[]{:S(2)}) collective-permute-start(f32[2,40,128]{2,1,0:T(8,128)S(1)} %get-tuple-element.34), channel_id=1, source_target_pairs={{0,4},{1,5},{2,6},{3,7},{4,0},{5,1},{6,2},{7,3},{8,12},{9,13},{10,... | collective-permute-start | bytes 122888 | tf_op jit(solution)/shard_map/ppermute | solution.py:807

commit v7 on v6

--- a/solution.py
+++ b/solution.py
@@ -41,6 +41,22 @@
 
 def matmul(a, b, dims=(((1,), (0,)), ((), ()))):
     return lax.dot_general(a, b, dims, preferred_element_type=jnp.float32)
+
+
+def scan(m, ahead, count, step, shift, product):
+    unit = (1.0, 0.0, 0.0, 1.0)
+
+    def moved(by):
+        return tuple(jnp.where(ahead >= by, shift(x, by), u) for x, u in zip(m, unit))
+
+    while step < count:
+        if 2 * step < count:
+            m = product(product(m, moved(step)), product(moved(2 * step), moved(3 * step)))
+            step *= 4
+        else:
+            m = product(m, moved(step))
+            step *= 2
+    return m
 
 
 def lane_roll(x, by):
@@ -96,19 +112,13 @@
         eps_in = back(eps, 1)
         scale = 1.0 / (face_in + 2.0 * eps_in)
         m = ((mass + face_in) * scale, mass - eps_in * eps_in * scale, scale, jnp.ones_like(scale))
-        step = 1
-        while step < LANES:
-            inside = (self.lane >= step) if sign > 0 else (self.lane < LANES - step)
-            m = pick(inside, mm(m, tuple(lane_roll(x, sign * step) for x in m)), m)
-            step *= 2
+        ahead = self.lane if sign > 0 else LANES - 1 - self.lane
+        m = scan(m, ahead, LANES, 1, lambda x, by: lane_roll(x, sign * by), mm)
         edge = LANES - 1 if sign > 0 else 0
         total = tuple(jnp.broadcast_to(x[:, edge : edge + 1], (rows, LANES)) for x in m)
-        step = 1
-        while step < max(self.ny, self.nz):
-            total = pick(
-                place >= step, mm(total, tuple(row_roll(x, sign * step) for x in total)), total
-            )
-            step *= 2
+        total = scan(
+            total, place, max(self.ny, self.nz), 1, lambda x, by: row_roll(x, sign * by), mm
+        )
         top = jnp.where(place >= 1, row_roll(total[0], sign), 1.0)
         low = jnp.where(place >= 1, row_roll(total[2], sign), 0.0)
         eta = (m[0] * top + m[1] * low) / (m[2] * top + m[3] * low)
@@ -140,12 +150,8 @@
         diagonal = mm(inverse_of_one_minus(mm(from_right, from_left_after)), left_inverse)
         width = jnp.where(self.row < self.ny, self.wy, LANES)
         place = lane & (width - 1)
-        right, left = from_right, from_left
-        step = 2
-        while step < LANES:
-            right = pick(place + step < width, mm(right, tuple(lane_roll(x, -step) for x in right)), right)
-            left = pick(place >= step, mm(left, tuple(lane_roll(x, step) for x in left)), left)
-            step *= 2
+        right = scan(from_right, width - 1 - place, LANES, 2, lambda x, by: lane_roll(x, -by), mm)
+        left = scan(from_left, place, LANES, 2, lane_roll, mm)
         return from_right, from_left, diagonal, right, left, from_right_before, from_left_after
 
 
@@ -190,15 +196,16 @@
 
     def one_field(field):
         values = [flow[field, x] for x in range(planes_x)]
-        fluxes = [half * (values[x] * speed[x]) for x in range(planes_x)]
+        fluxes = [values[x] * speed[x] for x in range(planes_x)]
+        aside = [(time_step * viscous) * u for u in values]
         extras = []
         for x in range(planes_x):
             u, flux, slot = values[x], fluxes[x], x
             total = centre * u
-            for other, sign in ((x + 1, -1), (x - 1, 1)):
-                if 0 <= other < planes_x:
-                    total = total + (time_step * viscous) * values[other]
-                    total = total + fluxes[other] if sign > 0 else total - fluxes[other]
+            if x + 1 < planes_x:
+                total = total + (aside[x + 1] - fluxes[x + 1])
+            if x > 0:
+                total = total + (aside[x - 1] + fluxes[x - 1])
             scaled = side * u
             onward, backward, far = scaled + flux, scaled - flux, fourth * u
             spread[slot, 0, 8 : wy + 8, :] = onward
@@ -208,11 +215,12 @@
             total = total + (spread[slot, 2, 6 : wy + 6, :] + spread[slot, 2, 10 : wy + 10, :])
             a, b = lane_roll(onward, 1), lane_roll(backward, -1)
             c, d = lane_roll(far, 2), lane_roll(far, -2)
-            ends = jnp.where(lane < 2, c + jnp.where(lane < 1, a, 0.0), 0.0)
-            ends = jnp.where(lane >= LANES - 2, d + jnp.where(lane >= LANES - 1, b, 0.0), ends)
+            from_low, from_high = a + c, b + d
+            ends = jnp.where(lane == 0, from_low, jnp.where(lane == 1, c, 0.0))
+            ends = jnp.where(lane == LANES - 1, from_high, jnp.where(lane == LANES - 2, d, ends))
             index = field * planes_x + x
             start = index * wy
-            store(start, 0, total + ((a + b) + (c + d) - ends))
+            store(start, 0, total + (from_low + from_high))
             store(start, LANES, ends)
             above = spread[slot, 1, 7:15, :] + spread[slot, 2, 8:16, :]
             below = spread[slot, 0, wy + 5 : wy + 13, :] + spread[slot, 2, wy + 4 : wy + 12, :]
@@ -233,6 +241,8 @@
     guess_l, guess_r = factor.guess(1), factor.guess(-1)
     left, right = factor.sweep(1, *guess_l[:2]), factor.sweep(-1, *guess_r[:2])
     copies[2].wait()
+    for x in range(planes_x):
+        speed[x] = half * speed[x]
     for field in range(fields):
         pltpu.make_async_copy(flow_hbm.at[field], flow.at[field], arrived.at[field]).wait()
     left, right = factor.sweep(1, *left[:2]), factor.sweep(-1, *right[:2])
@@ -265,8 +275,10 @@
         inside_down = cell_weights(down, column, even)
         past_up = lane_roll(cell_weights(up_past, column, even), -2)
         past_down = lane_roll(cell_weights(down_past, column, even), 2)
-        ends_up = jnp.where(lane < 2, same, jnp.where(lane >= LANES - 2, past_up, 0.0))
-        ends_down = jnp.where(lane < 2, past_down, jnp.where(lane >= LANES - 2, same, 0.0))
+        ends_up = jnp.where(lane < 2, same, past_up) - inside_up
+        ends_down = jnp.where(lane < 2, past_down, same) - inside_down
+        at_end = (lane < 2) | (lane >= LANES - 2)
+        ends_up, ends_down = jnp.where(at_end, ends_up, 0.0), jnp.where(at_end, ends_down, 0.0)
         weights.append(
             (
                 jnp.concatenate([inside_up, ends_up], axis=1),
@@ -432,8 +444,10 @@
     head0, head1 = rows_ref[0:1, :], rows_ref[1:2, :]
     tail0, tail1 = rows_ref[LANES - 2 : LANES - 1, :], rows_ref[LANES - 1 : LANES, :]
     for q in range(2):
-        rows_ref[LANES + q : LANES + q + 1, :] = past[2 * q] * tail0 + past[2 * q + 1] * tail1
-        rows_ref[2 * LANES - 2 + q : 2 * LANES - 1 + q, :] = ahead[2 * q] * head0 + ahead[2 * q + 1] * head1
+        beyond = past[2 * q] * tail0 + past[2 * q + 1] * tail1
+        rows_ref[LANES + q : LANES + q + 1, :] = beyond - (head0, head1)[q]
+        beyond = ahead[2 * q] * head0 + ahead[2 * q + 1] * head1
+        rows_ref[2 * LANES - 2 + q : 2 * LANES - 1 + q, :] = beyond - (tail0, tail1)[q]
     first, second = halves(rows_ref[...])
     matrix[:, 0:LANES] = first
     matrix[:, LANES : 2 * LANES] = second

time: 25.7 us -> 25.4 us (0.988)
  Pallas kernels: 12.7 us -> 12.4 us
    pallas_call x1, Pallas kernels: 4.1 us -> 3.75 us  [on_device(): pl.pallas_call(functools.partial(first_kernel, ny, nz, partners, paired),...]
  transfers between devices with their start and end apart: 6 -> 6, of which waited for: 5 -> 5; matrix products, arithmetic and copies ran while one was open for 0% -> 0% of each run, Pallas kernels for 24% -> 25%
where the time goes in v7:
time: 25.4 us; the launch traced here: 25.2 us
  Pallas kernels  12.4 us (49%)
  starting transfers between devices  9.63 us (38%)
  waiting for transfers between devices  3.15 us (12%)
    ppermute x6, starting transfers between devices, exchange(): received[k] = lax.ppermute(values[k - 1], axis, pairs)  9.63 us
    pallas_call x1, Pallas kernels, on_device(): pl.pallas_call(functools.partial(first_kernel, ny, nz, partners, paired),...  3.75 us
    ppermute x6, waiting for transfers between devices, exchange(): received[k] = lax.ppermute(values[k - 1], axis, pairs)  3.15 us
    pallas_call x1, Pallas kernels, on_device(): pl.pallas_call(functools.partial(second_kernel, ny, nz, count_z, wy, part...  2.23 us
    pallas_call x1, Pallas kernels, on_device(): pl.pallas_call(functools.partial(local_y_kernel, wy), out_shape=array(pla...  1.86 us
    pallas_call x1, Pallas kernels, on_device(): pl.pallas_call(functools.partial(y_kernel, count_y, wy), out_shape=[array...  1.42 us
    pallas_call x1, Pallas kernels, on_device(): pl.pallas_call(functools.partial(last_kernel, base, radix, narrow, wy), o...  1.35 us
    pallas_call x1, Pallas kernels, on_device(): pl.pallas_call(third_kernel, out_shape=array(4, planes, LANES), in_specs=...  0.93 us
  transfers between devices with their start and end apart: 6, of which 5 were waited for; matrix products, arithmetic and copies ran while one was open for 0% of the time, Pallas kernels for 25%

profile of v7, /device:TPU:0, one launch (start us, length us, event | category | flops | bytes accessed | tf_op | source)
XLA Modules:
  0.0 25.2 jit_solution(16244195689829845757)
XLA Ops:
  0.0 3.8 %forcing_and_factor.1 = (bf16[2880,256]{1,0:T(8,128)(2,1)S(1)}, bf16[2880,256]{1,0:T(8,128)(2,1)S(1)}, f32[28,8,128]{2,1,0:T(8,128)S(1)}, f32[8,8,128]{2,1,0:T(8,128)S(1)}, f32[4,2880]{1,0:T(4,128)S(1)}) custom-call(f32[5,8,64,128]{3,2,1,0:T(8,128)} %flow_hbm.1, f32[8,64,128]{2,1,0:T(8,128)} %speed_hbm.1, f32[4,128]{1,0:T(4,128)} %bitcast.2, f32[4,128]{1,0:T(4,128)} %bitcast.3), custom_call_target="tpu_custom_call" | custom-call | tf_op jit(solution)/shard_map/forcing_and_factor/pallas_call | solution.py:799
  3.8 0.5 %collective-permute-start = (f32[4,2880]{1,0:T(4,128)S(1)}, f32[4,2880]{1,0:T(4,128)S(1)}, u32[]{:S(2)}, u32[]{:S(2)}) collective-permute-start(f32[4,2880]{1,0:T(4,128)S(1)} %get-tuple-element.29.own), channel_id=1, source_target_pairs={{0,8},{8,0},{16,24},{24,16},{1,9},{9,1},{17,25},{25,17},{2,10},{10... | collective-permute-start | bytes 138248 | tf_op jit(solution)/shard_map/ppermute | solution.py:821
  4.3 0.8 %inverse_z.1 = (bf16[256,256]{1,0:T(8,128)(2,1)S(1)}, bf16[160,2880]{1,0:T(8,128)(2,1)S(1)}, bf16[160,2880]{1,0:T(8,128)(2,1)S(1)}) custom-call(f32[28,8,128]{2,1,0:T(8,128)S(1)} %get-tuple-element.21.factors), custom_call_target="tpu_custom_call" | custom-call | flops 2949120 | bytes 737280 | tf_op jit(solution)/shard_map/inverse_z/pallas_call | solution.py:827
  5.0 0.1 collective-permute-done.received.refs_0_
  5.2 2.9 %collective-permute-start.1 = (f32[2,2880]{1,0:T(2,128)S(1)}, f32[2,2880]{1,0:T(2,128)S(1)}, u32[]{:S(2)}, u32[]{:S(2)}) collective-permute-start(f32[2,2880]{1,0:T(2,128)S(1)} %join_pair.1), channel_id=1, source_target_pairs={{0,16},{8,24},{16,0},{24,8},{1,17},{9,25},{17,1},{25,9},{2,18},{10... | collective-permute-start | bytes 69128 | tf_op jit(solution)/shard_map/ppermute | solution.py:821
  8.1 2.2 %local_z.1 = (f32[2880,128]{1,0:T(8,128)S(1)}, f32[160,128]{1,0:T(8,128)S(1)}, f32[24,128]{1,0:T(8,128)S(1)}) custom-call(f32[8,8,128]{2,1,0:T(8,128)S(1)} %get-tuple-element.20.chains, f32[28,8,128]{2,1,0:T(8,128)S(1)} %get-tuple-element.21.factors, bf16[256,256]{1,0:T(8,128)(2,1)S(1)} %get-tuple-element.22.matrix.unused, ...), custom_call_target="tpu_custom_call" | custom-call | flops 1132462080 | bytes 4423680 | tf_op jit(solution)/shard_map/local_z/pallas_call | solution.py:850
  10.3 0.0 collective-permute-done.1.refs_1_
  10.3 0.9 %carried_y.1.unused.refs_0_ = f32[4,40,128]{2,1,0:T(8,128)S(1)} custom-call(f32[160,128]{1,0:T(8,128)S(1)} %get-tuple-element.25.moments, bf16[160,2880]{1,0:T(8,128)(2,1)S(1)} %get-tuple-element.26.spread_high, bf16[160,2880]{1,0:T(8,128)(2,1)S(1)} %get-tuple-element.27.spread_low, f32[24,128]{1,0:T(8,128)S(1)} %get-tuple-element.28.entering, ...), custom_call_target="tpu_custom_call" | custom-call | tf_op jit(solution)/shard_map/carried_y/pallas_call | solution.py:867
  11.3 2.7 %collective-permute-start.2 = (f32[4,40,128]{2,1,0:T(8,128)S(1)}, f32[4,40,128]{2,1,0:T(8,128)S(1)}, u32[]{:S(2)}, u32[]{:S(2)}) collective-permute-start(f32[4,40,128]{2,1,0:T(8,128)S(1)} %carried_y.1.unused.refs_0_), channel_id=1, source_target_pairs={{0,3},{1,2},{2,1},{3,0},{4,7},{5,6},{6,5},{7,4},{8,11},{9,10},{10,... | collective-permute-start | bytes 245768 | tf_op jit(solution)/shard_map/ppermute | solution.py:821
  13.9 0.4 %collective-permute-start.3 = (f32[4,40,128]{2,1,0:T(8,128)S(1)}, f32[4,40,128]{2,1,0:T(8,128)S(1)}, u32[]{:S(2)}, u32[]{:S(2)}) collective-permute-start(f32[4,40,128]{2,1,0:T(8,128)S(1)} %carried_y.1.unused.refs_0_), channel_id=1, source_target_pairs={{0,2},{1,3},{2,0},{3,1},{4,6},{5,7},{6,4},{7,5},{8,10},{9,11},{10,... | collective-permute-start | bytes 245768 | tf_op jit(solution)/shard_map/ppermute | solution.py:821
  14.4 0.4 %collective-permute-start.4 = (f32[4,40,128]{2,1,0:T(8,128)S(1)}, f32[4,40,128]{2,1,0:T(8,128)S(1)}, u32[]{:S(2)}, u32[]{:S(2)}) collective-permute-start(f32[4,40,128]{2,1,0:T(8,128)S(1)} %carried_y.1.unused.refs_0_), channel_id=1, source_target_pairs={{0,1},{1,0},{2,3},{3,2},{4,5},{5,4},{6,7},{7,6},{8,9},{9,8},{10,11... | collective-permute-start | bytes 245768 | tf_op jit(solution)/shard_map/ppermute | solution.py:821
  14.8 1.4 %inverse_y.1 = (f32[64,128]{1,0:T(8,128)S(1)}, f32[8,8,128]{2,1,0:T(8,128)S(1)}) custom-call(f32[8,8,128]{2,1,0:T(8,128)S(1)} %get-tuple-element.20.chains, f32[28,8,128]{2,1,0:T(8,128)S(1)} %get-tuple-element.21.factors, f32[4,40,128]{2,1,0:T(8,128)S(1)} %carried_y.1.unused.refs_0_), custom_call_target="tpu_custom_call" | custom-call | flops 566231040 | bytes 2949120 | tf_op jit(solution)/shard_map/inverse_y/pallas_call | solution.py:883
  16.2 1.1 %collective-permute-done.2.refs_1_ = f32[4,40,128]{2,1,0:T(8,128)S(1)} collective-permute-done((f32[4,40,128]{2,1,0:T(8,128)S(1)}, f32[4,40,128]{2,1,0:T(8,128)S(1)}, u32[]{:S(2)}, u32[]{:S(2)}) %collective-permute-start.2) | collective-permute-done | bytes 81952 | tf_op jit(solution)/shard_map/ppermute | solution.py:821
  17.3 1.2 %collective-permute-done.3.refs_2_ = f32[4,40,128]{2,1,0:T(8,128)S(1)} collective-permute-done((f32[4,40,128]{2,1,0:T(8,128)S(1)}, f32[4,40,128]{2,1,0:T(8,128)S(1)}, u32[]{:S(2)}, u32[]{:S(2)}) %collective-permute-start.3) | collective-permute-done | bytes 81952 | tf_op jit(solution)/shard_map/ppermute | solution.py:821
  18.6 0.3 %collective-permute-done.4.refs_3_ = f32[4,40,128]{2,1,0:T(8,128)S(1)} collective-permute-done((f32[4,40,128]{2,1,0:T(8,128)S(1)}, f32[4,40,128]{2,1,0:T(8,128)S(1)}, u32[]{:S(2)}, u32[]{:S(2)}) %collective-permute-start.4) | collective-permute-done | bytes 81952 | tf_op jit(solution)/shard_map/ppermute | solution.py:821
  18.8 0.1 join_groups.1
  18.9 2.7 %collective-permute-start.5 = (f32[2,40,128]{2,1,0:T(8,128)S(1)}, f32[2,40,128]{2,1,0:T(8,128)S(1)}, u32[]{:S(2)}, u32[]{:S(2)}) collective-permute-start(f32[2,40,128]{2,1,0:T(8,128)S(1)} %get-tuple-element.34), channel_id=1, source_target_pairs={{0,4},{1,5},{2,6},{3,7},{4,0},{5,1},{6,2},{7,3},{8,12},{9,13},{10,... | collective-permute-start | bytes 122888 | tf_op jit(solution)/shard_map/ppermute | solution.py:821
  21.6 1.9 %local_y.1.local = f32[40,64,128]{2,1,0:T(8,128)S(1)} custom-call(f32[2880,128]{1,0:T(8,128)S(1)} %get-tuple-element.31.local, f32[24,128]{1,0:T(8,128)S(1)} %get-tuple-element.28.entering, f32[64,128]{1,0:T(8,128)S(1)} %get-tuple-element.32.inverse_y, f32[4,40,128]{2,1,0:T(8,128)S(1)} %get-tuple-element.33.unused.entered, ...), custom_call_target="tpu_custom_call" | custom-call | flops 566231040 | bytes 2949120 | tf_op jit(solution)/shard_map/local_y/pallas_call | solution.py:906
  23.4 0.4 %collective-permute-done.5.refs_0_ = f32[2,40,128]{2,1,0:T(8,128)S(1)} collective-permute-done((f32[2,40,128]{2,1,0:T(8,128)S(1)}, f32[2,40,128]{2,1,0:T(8,128)S(1)}, u32[]{:S(2)}, u32[]{:S(2)}) %collective-permute-start.5) | collective-permute-done | bytes 40992 | tf_op jit(solution)/shard_map/ppermute | solution.py:821
  23.9 1.4 %finish_y.1 = f32[5,8,64,128]{3,2,1,0:T(8,128)} custom-call(f32[8,8,128]{2,1,0:T(8,128)S(1)} %get-tuple-element.30.coefs, f32[40,64,128]{2,1,0:T(8,128)S(1)} %local_y.1.local, f32[64,128]{1,0:T(8,128)S(1)} %get-tuple-element.32.inverse_y, f32[4,40,128]{2,1,0:T(8,128)S(1)} %get-tuple-element.33.unused.entered, f32[2,40,128]{2,1,0:T(8,128)S(1)} %collective-permute-done.5.refs_0_), custom_call_target="tpu_custom_call" | custom-call | tf_op jit(solution)/shard_map/finish_y/pallas_call | solution.py:917
  (1 shorter events, 0.0 us)
Async XLA Ops:
  3.8 1.4 %collective-permute-start = (f32[4,2880]{1,0:T(4,128)S(1)}, f32[4,2880]{1,0:T(4,128)S(1)}, u32[]{:S(2)}, u32[]{:S(2)}) collective-permute-start(f32[4,2880]{1,0:T(4,128)S(1)} %get-tuple-element.29.own), channel_id=1, source_target_pairs={{0,8},{8,0},{16,24},{24,16},{1,9},{9,1},{17,25},{25,17},{2,10},{10... | collective-permute-start | bytes 138248 | tf_op jit(solution)/shard_map/ppermute | solution.py:821
  5.2 5.1 %collective-permute-start.1 = (f32[2,2880]{1,0:T(2,128)S(1)}, f32[2,2880]{1,0:T(2,128)S(1)}, u32[]{:S(2)}, u32[]{:S(2)}) collective-permute-start(f32[2,2880]{1,0:T(2,128)S(1)} %join_pair.1), channel_id=1, source_target_pairs={{0,16},{8,24},{16,0},{24,8},{1,17},{9,25},{17,1},{25,9},{2,18},{10... | collective-permute-start | bytes 69128 | tf_op jit(solution)/shard_map/ppermute | solution.py:821
  11.3 6.1 %collective-permute-start.2 = (f32[4,40,128]{2,1,0:T(8,128)S(1)}, f32[4,40,128]{2,1,0:T(8,128)S(1)}, u32[]{:S(2)}, u32[]{:S(2)}) collective-permute-start(f32[4,40,128]{2,1,0:T(8,128)S(1)} %carried_y.1.unused.refs_0_), channel_id=1, source_target_pairs={{0,3},{1,2},{2,1},{3,0},{4,7},{5,6},{6,5},{7,4},{8,11},{9,10},{10,... | collective-permute-start | bytes 245768 | tf_op jit(solution)/shard_map/ppermute | solution.py:821
  13.9 4.6 %collective-permute-start.3 = (f32[4,40,128]{2,1,0:T(8,128)S(1)}, f32[4,40,128]{2,1,0:T(8,128)S(1)}, u32[]{:S(2)}, u32[]{:S(2)}) collective-permute-start(f32[4,40,128]{2,1,0:T(8,128)S(1)} %carried_y.1.unused.refs_0_), channel_id=1, source_target_pairs={{0,2},{1,3},{2,0},{3,1},{4,6},{5,7},{6,4},{7,5},{8,10},{9,11},{10,... | collective-permute-start | bytes 245768 | tf_op jit(solution)/shard_map/ppermute | solution.py:821
  14.4 4.4 %collective-permute-start.4 = (f32[4,40,128]{2,1,0:T(8,128)S(1)}, f32[4,40,128]{2,1,0:T(8,128)S(1)}, u32[]{:S(2)}, u32[]{:S(2)}) collective-permute-start(f32[4,40,128]{2,1,0:T(8,128)S(1)} %carried_y.1.unused.refs_0_), channel_id=1, source_target_pairs={{0,1},{1,0},{2,3},{3,2},{4,5},{5,4},{6,7},{7,6},{8,9},{9,8},{10,11... | collective-permute-start | bytes 245768 | tf_op jit(solution)/shard_map/ppermute | solution.py:821
  18.9 5.0 %collective-permute-start.5 = (f32[2,40,128]{2,1,0:T(8,128)S(1)}, f32[2,40,128]{2,1,0:T(8,128)S(1)}, u32[]{:S(2)}, u32[]{:S(2)}) collective-permute-start(f32[2,40,128]{2,1,0:T(8,128)S(1)} %get-tuple-element.34), channel_id=1, source_target_pairs={{0,4},{1,5},{2,6},{3,7},{4,0},{5,1},{6,2},{7,3},{8,12},{9,13},{10,... | collective-permute-start | bytes 122888 | tf_op jit(solution)/shard_map/ppermute | solution.py:821

commit v8 on v7

--- a/solution.py
+++ b/solution.py
@@ -713,14 +713,14 @@
     return out
 
 
-def stage_kernel(base, stride, radix, narrow, has_entered, coefs, *refs):
+def stage_kernel(base, stride, radix, narrow, has_entered, split, coefs, *refs):
     values = (refs[0],) + tuple(refs[1:radix][::-1])
     position = radix
     entered = None
     if has_entered:
         entered = refs[position]
         position += 1
-    message, entering = refs[position : position + 2]
+    entering, messages = refs[position], refs[position + 1 :]
     below = combine(coefs, 0, base, values[1:])
     above = combine(coefs, 4, base, values[1:])
     for row, value in enumerate(below + above):
@@ -730,36 +730,40 @@
     if narrow:
         group = lax.axis_index("gy") // (stride * radix)
         sends_up = lax.rem(group, 2) == 0
-        for row in range(2):
-            message[row] = jnp.where(sends_up, upward[row], downward[row])
+        values = [jnp.where(sends_up, upward[row], downward[row]) for row in range(2)]
     else:
-        for row, value in enumerate(upward + downward):
-            message[row] = value
-
-
-def last_kernel(base, radix, narrow, wy, coefs, local, inverse_y, entered, *refs):
-    messages, (out_hbm, out, sent) = refs[: radix - 1], refs[radix - 1 :]
+        values = upward + downward
+    for row, value in enumerate(values):
+        for message, (begin, end) in zip(messages, split):
+            message[row] = value[begin:end]
+
+
+def last_kernel(base, radix, narrow, wy, begin, end, has_out, coefs, local, inverse_y, entered, *refs):
+    messages, (out_hbm, out, sent) = refs[: radix - 1], refs[radix - 1 + has_out :]
+    planes_x = out.shape[1]
+    rows = slice(begin * planes_x, end * planes_x)
     values = list(messages)
     if narrow:
         values = [(m[0], m[1], m[0], m[1]) for m in values]
     below = combine(coefs, 0, base, values)
     above = combine(coefs, 4, base, values)
-    st = [value + entered[row] for row, value in enumerate(below + above)]
+    st = [value + entered[row, rows] for row, value in enumerate(below + above)]
     sides = [
         jnp.broadcast_to(inverse_y[:, c : c + 1], (wy, LANES)) for c in (0, 1, wy - 2, wy - 1)
     ]
-    fields, planes_x = out.shape[:2]
     copies = []
-    for field in range(fields):
+    for field in range(begin, end):
         for x in range(planes_x):
-            index = field * planes_x + x
-            value = local[index]
+            index = (field - begin) * planes_x + x
+            value = local[field * planes_x + x]
             for number in range(4):
                 value = value + sides[number] * st[number][index : index + 1]
-            out[field, x] = value
+            out[field - begin, x] = value
             if (x + 1) % 4 == 0:
-                part = (field, pl.ds(x - 3, 4))
-                copy = pltpu.make_async_copy(out.at[part], out_hbm.at[part], sent.at[len(copies)])
+                part = pl.ds(x - 3, 4)
+                copy = pltpu.make_async_copy(
+                    out.at[field - begin, part], out_hbm.at[field, part], sent.at[len(copies)]
+                )
                 copy.start()
                 copies.append(copy)
     for copy in copies:
@@ -875,8 +879,32 @@
     arrived = received
 
     narrow = plan[-1][1] == 2 and len(plan) > 1
+    cut = (fields + 1) // 2
+    ranges = [(0, cut), (cut, fields)]
     base, entered, result = 0, None, None
     for number, (stride, radix) in enumerate(plan):
+        if number + 1 == len(plan):
+            parts = carried if number else [carried[:, b * planes_x : e * planes_x] for b, e in ranges]
+            received = [exchange([part] * (radix - 1), "gy", count_y, stride, radix) for part in parts]
+            out = None
+            for (begin, end), messages in zip(ranges, received):
+                inputs = [coefs, result, inverse_y, entered, *messages]
+                out = pl.pallas_call(
+                    functools.partial(
+                        last_kernel, base, radix, narrow, wy, begin, end, int(out is not None)
+                    ),
+                    out_shape=array(fields, planes_x, wy, wz),
+                    in_specs=[VMEM] * len(inputs) + ([HBM] if out is not None else []),
+                    out_specs=HBM,
+                    scratch_shapes=[
+                        pltpu.VMEM((end - begin, planes_x, wy, wz), jnp.float32),
+                        pltpu.SemaphoreType.DMA(((end - begin) * planes_x // 4,)),
+                    ],
+                    input_output_aliases={len(inputs): 0} if out is not None else {},
+                    compiler_params=PARAMS,
+                    name="finish_y",
+                )(*inputs, *([out] if out is not None else []))
+            return out
         received = exchange([carried] * (radix - 1), "gy", count_y, stride, radix)
         if number == 0:
             entries = sum(2 * radix - 1 for _, radix in plan[:-1]) + plan[-1][1] - 1
@@ -890,42 +918,32 @@
                 cost_estimate=cost(2 * rows * 128 * 128 * 6, 4 * rows * 256),
                 name="inverse_y",
             )(chains, factors, carried)
-        if number + 1 < len(plan):
-            slim = narrow and number + 2 == len(plan)
-            inputs = [carried] + received[::-1] + ([entered] if entered is not None else [])
-            carried, entered = pl.pallas_call(
-                functools.partial(stage_kernel, base, stride, radix, slim, entered is not None),
-                out_shape=[array(2 if slim else 4, planes, LANES), array(4, planes, LANES)],
-                in_specs=[VMEM] * (1 + len(inputs)),
-                out_specs=[VMEM] * 2,
+        before_last = number + 2 == len(plan)
+        slim = narrow and before_last
+        split = [(b * planes_x, e * planes_x) for b, e in ranges] if before_last else [(0, planes)]
+        inputs = [carried] + received[::-1] + ([entered] if entered is not None else [])
+        entered, *carried = pl.pallas_call(
+            functools.partial(stage_kernel, base, stride, radix, slim, entered is not None, split),
+            out_shape=[array(4, planes, LANES)]
+            + [array(2 if slim else 4, end - begin, LANES) for begin, end in split],
+            in_specs=[VMEM] * (1 + len(inputs)),
+            out_specs=[VMEM] * (1 + len(split)),
+            compiler_params=PARAMS,
+            name="join_groups",
+        )(coefs, *inputs)
+        carried = carried if before_last else carried[0]
+        base += 2 * radix - 1
+        if number == 0:
+            result = pl.pallas_call(
+                functools.partial(local_y_kernel, wy),
+                out_shape=array(planes, wy, LANES),
+                in_specs=[VMEM] * 3 + [HBM] + [VMEM] * arrivals,
+                out_specs=VMEM,
+                scratch_shapes=[pltpu.VMEM((rows, LANES), jnp.float32)],
                 compiler_params=PARAMS,
-                name="join_groups",
-            )(coefs, *inputs)
-            base += 2 * radix - 1
-            if number == 0:
-                result = pl.pallas_call(
-                    functools.partial(local_y_kernel, wy),
-                    out_shape=array(planes, wy, LANES),
-                    in_specs=[VMEM] * 3 + [HBM] + [VMEM] * arrivals,
-                    out_specs=VMEM,
-                    scratch_shapes=[pltpu.VMEM((rows, LANES), jnp.float32)],
-                    compiler_params=PARAMS,
-                    cost_estimate=cost(2 * rows * 128 * 128 * 6, 4 * rows * 256),
-                    name="local_y",
-                )(local, entering, inverse_y, entered, *arrived)
-        else:
-            return pl.pallas_call(
-                functools.partial(last_kernel, base, radix, narrow, wy),
-                out_shape=array(fields, planes_x, wy, wz),
-                in_specs=[VMEM] * (4 + len(received)),
-                out_specs=HBM,
-                scratch_shapes=[
-                    pltpu.VMEM(flow.shape, jnp.float32),
-                    pltpu.SemaphoreType.DMA((planes // 4,)),
-                ],
-                compiler_params=PARAMS,
-                name="finish_y",
-            )(coefs, result, inverse_y, entered, *received)
+                cost_estimate=cost(2 * rows * 128 * 128 * 6, 4 * rows * 256),
+                name="local_y",
+            )(local, entering, inverse_y, entered, *arrived)
 
 
 def solution(mesh):

time: 25.4 us -> 27.4 us (1.079)
  Pallas kernels: 12.4 us -> 13.3 us
  waiting for transfers between devices: 3.15 us -> 3.89 us
  starting transfers between devices: 9.63 us -> 9.96 us
    pallas_call x1 -> x2, Pallas kernels: 1.35 us -> 2.28 us  [on_device(): pl.pallas_call(functools.partial(last_kernel, base, radix, narrow, wy, be...]
    ppermute x6 -> x7, waiting for transfers between devices: 3.15 us -> 3.89 us  [exchange(): received[k] = lax.ppermute(values[k - 1], axis, pairs)]
    ppermute x6 -> x7, starting transfers between devices: 9.63 us -> 9.96 us  [exchange(): received[k] = lax.ppermute(values[k - 1], axis, pairs)]
  transfers between devices with their start and end apart: 6 -> 7, of which waited for: 5 -> 5; matrix products, arithmetic and copies ran while one was open for 0% -> 0% of each run, Pallas kernels for 25% -> 27%
where the time goes in v8:
time: 27.4 us; the launch traced here: 27.3 us
  Pallas kernels  13.3 us (49%)
  starting transfers between devices  9.96 us (36%)
  waiting for transfers between devices  3.89 us (14%)
    ppermute x7, starting transfers between devices, exchange(): received[k] = lax.ppermute(values[k - 1], axis, pairs)  9.96 us
    ppermute x7, waiting for transfers between devices, exchange(): received[k] = lax.ppermute(values[k - 1], axis, pairs)  3.89 us
    pallas_call x1, Pallas kernels, on_device(): pl.pallas_call(functools.partial(first_kernel, ny, nz, partners, paired),...  3.75 us
    pallas_call x2, Pallas kernels, on_device(): pl.pallas_call(functools.partial(last_kernel, base, radix, narrow, wy, be...  2.28 us
    pallas_call x1, Pallas kernels, on_device(): pl.pallas_call(functools.partial(second_kernel, ny, nz, count_z, wy, part...  2.23 us
    pallas_call x1, Pallas kernels, on_device(): pl.pallas_call(functools.partial(local_y_kernel, wy), out_shape=array(pla...  1.86 us
    pallas_call x1, Pallas kernels, on_device(): pl.pallas_call(functools.partial(y_kernel, count_y, wy), out_shape=[array...  1.42 us
    pallas_call x1, Pallas kernels, on_device(): pl.pallas_call(third_kernel, out_shape=array(4, planes, LANES), in_specs=...  0.93 us
  transfers between devices with their start and end apart: 7, of which 5 were waited for; matrix products, arithmetic and copies ran while one was open for 0% of the time, Pallas kernels for 27%

profile of v8, /device:TPU:0, one launch (start us, length us, event | category | flops | bytes accessed | tf_op | source)
XLA Modules:
  0.0 27.3 jit_solution(17795855496778931462)
XLA Ops:
  0.0 3.8 %forcing_and_factor.1 = (bf16[2880,256]{1,0:T(8,128)(2,1)S(1)}, bf16[2880,256]{1,0:T(8,128)(2,1)S(1)}, f32[28,8,128]{2,1,0:T(8,128)S(1)}, f32[8,8,128]{2,1,0:T(8,128)S(1)}, f32[4,2880]{1,0:T(4,128)S(1)}) custom-call(f32[5,8,64,128]{3,2,1,0:T(8,128)} %flow_hbm.1, f32[8,64,128]{2,1,0:T(8,128)} %speed_hbm.1, f32[4,128]{1,0:T(4,128)} %bitcast.2, f32[4,128]{1,0:T(4,128)} %bitcast.3), custom_call_target="tpu_custom_call" | custom-call | tf_op jit(solution)/shard_map/forcing_and_factor/pallas_call | solution.py:803
  3.8 0.5 %collective-permute-start = (f32[4,2880]{1,0:T(4,128)S(1)}, f32[4,2880]{1,0:T(4,128)S(1)}, u32[]{:S(2)}, u32[]{:S(2)}) collective-permute-start(f32[4,2880]{1,0:T(4,128)S(1)} %get-tuple-element.30.own), channel_id=1, source_target_pairs={{0,8},{8,0},{16,24},{24,16},{1,9},{9,1},{17,25},{25,17},{2,10},{10... | collective-permute-start | bytes 138248 | tf_op jit(solution)/shard_map/ppermute | solution.py:825
  4.3 0.8 %inverse_z.1 = (bf16[256,256]{1,0:T(8,128)(2,1)S(1)}, bf16[160,2880]{1,0:T(8,128)(2,1)S(1)}, bf16[160,2880]{1,0:T(8,128)(2,1)S(1)}) custom-call(f32[28,8,128]{2,1,0:T(8,128)S(1)} %get-tuple-element.22.factors), custom_call_target="tpu_custom_call" | custom-call | flops 2949120 | bytes 737280 | tf_op jit(solution)/shard_map/inverse_z/pallas_call | solution.py:831
  5.0 0.1 collective-permute-done.received.refs_0_
  5.2 2.9 %collective-permute-start.1 = (f32[2,2880]{1,0:T(2,128)S(1)}, f32[2,2880]{1,0:T(2,128)S(1)}, u32[]{:S(2)}, u32[]{:S(2)}) collective-permute-start(f32[2,2880]{1,0:T(2,128)S(1)} %join_pair.1), channel_id=1, source_target_pairs={{0,16},{8,24},{16,0},{24,8},{1,17},{9,25},{17,1},{25,9},{2,18},{10... | collective-permute-start | bytes 69128 | tf_op jit(solution)/shard_map/ppermute | solution.py:825
  8.1 2.2 %local_z.1 = (f32[2880,128]{1,0:T(8,128)S(1)}, f32[160,128]{1,0:T(8,128)S(1)}, f32[24,128]{1,0:T(8,128)S(1)}) custom-call(f32[8,8,128]{2,1,0:T(8,128)S(1)} %get-tuple-element.21.chains, f32[28,8,128]{2,1,0:T(8,128)S(1)} %get-tuple-element.22.factors, bf16[256,256]{1,0:T(8,128)(2,1)S(1)} %get-tuple-element.23.matrix.unused, ...), custom_call_target="tpu_custom_call" | custom-call | flops 1132462080 | bytes 4423680 | tf_op jit(solution)/shard_map/local_z/pallas_call | solution.py:854
  10.3 0.0 collective-permute-done.1.refs_1_
  10.3 0.9 %carried_y.1.unused.refs_0_ = f32[4,40,128]{2,1,0:T(8,128)S(1)} custom-call(f32[160,128]{1,0:T(8,128)S(1)} %get-tuple-element.26.moments, bf16[160,2880]{1,0:T(8,128)(2,1)S(1)} %get-tuple-element.27.spread_high, bf16[160,2880]{1,0:T(8,128)(2,1)S(1)} %get-tuple-element.28.spread_low, f32[24,128]{1,0:T(8,128)S(1)} %get-tuple-element.29.entering, ...), custom_call_target="tpu_custom_call" | custom-call | tf_op jit(solution)/shard_map/carried_y/pallas_call | solution.py:871
  11.3 2.7 %collective-permute-start.2 = (f32[4,40,128]{2,1,0:T(8,128)S(1)}, f32[4,40,128]{2,1,0:T(8,128)S(1)}, u32[]{:S(2)}, u32[]{:S(2)}) collective-permute-start(f32[4,40,128]{2,1,0:T(8,128)S(1)} %carried_y.1.unused.refs_0_), channel_id=1, source_target_pairs={{0,3},{1,2},{2,1},{3,0},{4,7},{5,6},{6,5},{7,4},{8,11},{9,10},{10,... | collective-permute-start | bytes 245768 | tf_op jit(solution)/shard_map/ppermute | solution.py:825
  13.9 0.4 %collective-permute-start.3 = (f32[4,40,128]{2,1,0:T(8,128)S(1)}, f32[4,40,128]{2,1,0:T(8,128)S(1)}, u32[]{:S(2)}, u32[]{:S(2)}) collective-permute-start(f32[4,40,128]{2,1,0:T(8,128)S(1)} %carried_y.1.unused.refs_0_), channel_id=1, source_target_pairs={{0,2},{1,3},{2,0},{3,1},{4,6},{5,7},{6,4},{7,5},{8,10},{9,11},{10,... | collective-permute-start | bytes 245768 | tf_op jit(solution)/shard_map/ppermute | solution.py:825
  14.4 0.4 %collective-permute-start.4 = (f32[4,40,128]{2,1,0:T(8,128)S(1)}, f32[4,40,128]{2,1,0:T(8,128)S(1)}, u32[]{:S(2)}, u32[]{:S(2)}) collective-permute-start(f32[4,40,128]{2,1,0:T(8,128)S(1)} %carried_y.1.unused.refs_0_), channel_id=1, source_target_pairs={{0,1},{1,0},{2,3},{3,2},{4,5},{5,4},{6,7},{7,6},{8,9},{9,8},{10,11... | collective-permute-start | bytes 245768 | tf_op jit(solution)/shard_map/ppermute | solution.py:825
  14.8 1.4 %inverse_y.1 = (f32[64,128]{1,0:T(8,128)S(1)}, f32[8,8,128]{2,1,0:T(8,128)S(1)}) custom-call(f32[8,8,128]{2,1,0:T(8,128)S(1)} %get-tuple-element.21.chains, f32[28,8,128]{2,1,0:T(8,128)S(1)} %get-tuple-element.22.factors, f32[4,40,128]{2,1,0:T(8,128)S(1)} %carried_y.1.unused.refs_0_), custom_call_target="tpu_custom_call" | custom-call | flops 566231040 | bytes 2949120 | tf_op jit(solution)/shard_map/inverse_y/pallas_call | solution.py:911
  16.2 1.1 %collective-permute-done.2.refs_1_ = f32[4,40,128]{2,1,0:T(8,128)S(1)} collective-permute-done((f32[4,40,128]{2,1,0:T(8,128)S(1)}, f32[4,40,128]{2,1,0:T(8,128)S(1)}, u32[]{:S(2)}, u32[]{:S(2)}) %collective-permute-start.2) | collective-permute-done | bytes 81952 | tf_op jit(solution)/shard_map/ppermute | solution.py:825
  17.3 1.2 %collective-permute-done.3.refs_2_ = f32[4,40,128]{2,1,0:T(8,128)S(1)} collective-permute-done((f32[4,40,128]{2,1,0:T(8,128)S(1)}, f32[4,40,128]{2,1,0:T(8,128)S(1)}, u32[]{:S(2)}, u32[]{:S(2)}) %collective-permute-start.3) | collective-permute-done | bytes 81952 | tf_op jit(solution)/shard_map/ppermute | solution.py:825
  18.6 0.3 collective-permute-done.4.refs_3_
  18.8 0.1 join_groups.1
  18.9 2.7 %collective-permute-start.6 = (f32[2,24,128]{2,1,0:T(8,128)S(1)}, f32[2,24,128]{2,1,0:T(8,128)S(1)}, u32[]{:S(2)}, u32[]{:S(2)}) collective-permute-start(f32[2,24,128]{2,1,0:T(8,128)S(1)} %get-tuple-element.36), channel_id=1, source_target_pairs={{0,4},{1,5},{2,6},{3,7},{4,0},{5,1},{6,2},{7,3},{8,12},{9,13},{10,... | collective-permute-start | bytes 73736 | tf_op jit(solution)/shard_map/ppermute | solution.py:825
  21.6 0.3 %collective-permute-start.5 = (f32[2,16,128]{2,1,0:T(8,128)S(1)}, f32[2,16,128]{2,1,0:T(8,128)S(1)}, u32[]{:S(2)}, u32[]{:S(2)}) collective-permute-start(f32[2,16,128]{2,1,0:T(8,128)S(1)} %get-tuple-element.35), channel_id=1, source_target_pairs={{0,4},{1,5},{2,6},{3,7},{4,0},{5,1},{6,2},{7,3},{8,12},{9,13},{10,... | collective-permute-start | bytes 49160 | tf_op jit(solution)/shard_map/ppermute | solution.py:825
  21.9 1.9 %local_y.1.local = f32[40,64,128]{2,1,0:T(8,128)S(1)} custom-call(f32[2880,128]{1,0:T(8,128)S(1)} %get-tuple-element.32.local, f32[24,128]{1,0:T(8,128)S(1)} %get-tuple-element.29.entering, f32[64,128]{1,0:T(8,128)S(1)} %get-tuple-element.33.inverse_y, f32[4,40,128]{2,1,0:T(8,128)S(1)} %get-tuple-element.34.unused.entered, ...), custom_call_target="tpu_custom_call" | custom-call | flops 566231040 | bytes 2949120 | tf_op jit(solution)/shard_map/local_y/pallas_call | solution.py:937
  23.8 0.0 collective-permute-done.6.refs_0_
  23.8 1.2 %finish_y.2.refs_1_ = f32[5,8,64,128]{3,2,1,0:T(8,128)} custom-call(f32[8,8,128]{2,1,0:T(8,128)S(1)} %get-tuple-element.31.coefs, f32[40,64,128]{2,1,0:T(8,128)S(1)} %local_y.1.local, f32[64,128]{1,0:T(8,128)S(1)} %get-tuple-element.33.inverse_y, f32[4,40,128]{2,1,0:T(8,128)S(1)} %get-tuple-element.34.unused.entered, ...), custom_call_target="tpu_custom_call" | custom-call | tf_op jit(solution)/shard_map/finish_y/pallas_call | solution.py:892
  25.0 1.2 %collective-permute-done.5.refs_0_ = f32[2,16,128]{2,1,0:T(8,128)S(1)} collective-permute-done((f32[2,16,128]{2,1,0:T(8,128)S(1)}, f32[2,16,128]{2,1,0:T(8,128)S(1)}, u32[]{:S(2)}, u32[]{:S(2)}) %collective-permute-start.5) | collective-permute-done | bytes 16416 | tf_op jit(solution)/shard_map/ppermute | solution.py:825
  26.2 1.0 %finish_y.3 = f32[5,8,64,128]{3,2,1,0:T(8,128)} custom-call(f32[8,8,128]{2,1,0:T(8,128)S(1)} %get-tuple-element.31.coefs, f32[40,64,128]{2,1,0:T(8,128)S(1)} %local_y.1.local, f32[64,128]{1,0:T(8,128)S(1)} %get-tuple-element.33.inverse_y, f32[4,40,128]{2,1,0:T(8,128)S(1)} %get-tuple-element.34.unused.entered, ...), custom_call_target="tpu_custom_call", output_to_operand_aliasing={{}: (5, {})} | custom-call | tf_op jit(solution)/shard_map/finish_y/pallas_call | solution.py:892
  (1 shorter events, 0.0 us)
Async XLA Ops:
  3.8 1.4 %collective-permute-start = (f32[4,2880]{1,0:T(4,128)S(1)}, f32[4,2880]{1,0:T(4,128)S(1)}, u32[]{:S(2)}, u32[]{:S(2)}) collective-permute-start(f32[4,2880]{1,0:T(4,128)S(1)} %get-tuple-element.30.own), channel_id=1, source_target_pairs={{0,8},{8,0},{16,24},{24,16},{1,9},{9,1},{17,25},{25,17},{2,10},{10... | collective-permute-start | bytes 138248 | tf_op jit(solution)/shard_map/ppermute | solution.py:825
  5.2 5.1 %collective-permute-start.1 = (f32[2,2880]{1,0:T(2,128)S(1)}, f32[2,2880]{1,0:T(2,128)S(1)}, u32[]{:S(2)}, u32[]{:S(2)}) collective-permute-start(f32[2,2880]{1,0:T(2,128)S(1)} %join_pair.1), channel_id=1, source_target_pairs={{0,16},{8,24},{16,0},{24,8},{1,17},{9,25},{17,1},{25,9},{2,18},{10... | collective-permute-start | bytes 69128 | tf_op jit(solution)/shard_map/ppermute | solution.py:825
  11.3 6.1 %collective-permute-start.2 = (f32[4,40,128]{2,1,0:T(8,128)S(1)}, f32[4,40,128]{2,1,0:T(8,128)S(1)}, u32[]{:S(2)}, u32[]{:S(2)}) collective-permute-start(f32[4,40,128]{2,1,0:T(8,128)S(1)} %carried_y.1.unused.refs_0_), channel_id=1, source_target_pairs={{0,3},{1,2},{2,1},{3,0},{4,7},{5,6},{6,5},{7,4},{8,11},{9,10},{10,... | collective-permute-start | bytes 245768 | tf_op jit(solution)/shard_map/ppermute | solution.py:825
  13.9 4.6 %collective-permute-start.3 = (f32[4,40,128]{2,1,0:T(8,128)S(1)}, f32[4,40,128]{2,1,0:T(8,128)S(1)}, u32[]{:S(2)}, u32[]{:S(2)}) collective-permute-start(f32[4,40,128]{2,1,0:T(8,128)S(1)} %carried_y.1.unused.refs_0_), channel_id=1, source_target_pairs={{0,2},{1,3},{2,0},{3,1},{4,6},{5,7},{6,4},{7,5},{8,10},{9,11},{10,... | collective-permute-start | bytes 245768 | tf_op jit(solution)/shard_map/ppermute | solution.py:825
  14.4 4.4 %collective-permute-start.4 = (f32[4,40,128]{2,1,0:T(8,128)S(1)}, f32[4,40,128]{2,1,0:T(8,128)S(1)}, u32[]{:S(2)}, u32[]{:S(2)}) collective-permute-start(f32[4,40,128]{2,1,0:T(8,128)S(1)} %carried_y.1.unused.refs_0_), channel_id=1, source_target_pairs={{0,1},{1,0},{2,3},{3,2},{4,5},{5,4},{6,7},{7,6},{8,9},{9,8},{10,11... | collective-permute-start | bytes 245768 | tf_op jit(solution)/shard_map/ppermute | solution.py:825
  18.9 4.9 %collective-permute-start.6 = (f32[2,24,128]{2,1,0:T(8,128)S(1)}, f32[2,24,128]{2,1,0:T(8,128)S(1)}, u32[]{:S(2)}, u32[]{:S(2)}) collective-permute-start(f32[2,24,128]{2,1,0:T(8,128)S(1)} %get-tuple-element.36), channel_id=1, source_target_pairs={{0,4},{1,5},{2,6},{3,7},{4,0},{5,1},{6,2},{7,3},{8,12},{9,13},{10,... | collective-permute-start | bytes 73736 | tf_op jit(solution)/shard_map/ppermute | solution.py:825
  21.6 4.6 %collective-permute-start.5 = (f32[2,16,128]{2,1,0:T(8,128)S(1)}, f32[2,16,128]{2,1,0:T(8,128)S(1)}, u32[]{:S(2)}, u32[]{:S(2)}) collective-permute-start(f32[2,16,128]{2,1,0:T(8,128)S(1)} %get-tuple-element.35), channel_id=1, source_target_pairs={{0,4},{1,5},{2,6},{3,7},{4,0},{5,1},{6,2},{7,3},{8,12},{9,13},{10,... | collective-permute-start | bytes 49160 | tf_op jit(solution)/shard_map/ppermute | solution.py:825

commit v9 on v7

--- a/solution.py
+++ b/solution.py
@@ -655,7 +655,7 @@
 
 
 def third_kernel(moments, spread_high, spread_low, entering, *refs):
-    messages, carried = refs[:-1], refs[-1]
+    messages, carried = refs[:-1][::-1], refs[-1]
     count = entering.shape[0] // 3
     received = arrived_rows(messages, count)
     first = received.astype(jnp.bfloat16).astype(jnp.float32)
@@ -792,7 +792,7 @@
     planes = fields * planes_x
     rows = planes * (wy + EXTRA)
     partners = count_z - 1
-    paired = count_z == 4
+    paired = False
     arrivals = 2 if paired else partners
     entering_rows = -(-2 * arrivals // 8) * 8
     half = jax.ShapeDtypeStruct((rows, 2 * LANES), jnp.bfloat16)
@@ -871,7 +871,7 @@
         out_specs=VMEM,
         compiler_params=PARAMS,
         name="carried_y",
-    )(moments, spread_high, spread_low, entering, *received)
+    )(moments, spread_high, spread_low, entering, *received[::-1])
     arrived = received
 
     narrow = plan[-1][1] == 2 and len(plan) > 1

time: 25.4 us -> 26.6 us (1.047)
  waiting for transfers between devices: 3.15 us -> 4.67 us
  starting transfers between devices: 9.63 us -> 9.34 us
    ppermute x6 -> x7, waiting for transfers between devices: 3.15 us -> 4.67 us  [exchange(): received[k] = lax.ppermute(values[k - 1], axis, pairs)]
    ppermute x6 -> x7, starting transfers between devices: 9.63 us -> 9.34 us  [exchange(): received[k] = lax.ppermute(values[k - 1], axis, pairs)]
  transfers between devices with their start and end apart: 6 -> 7, of which waited for: 5 -> 4; matrix products, arithmetic and copies ran while one was open for 0% -> 0% of each run, Pallas kernels for 25% -> 24%
where the time goes in v9:
time: 26.6 us; the launch traced here: 26.5 us
  Pallas kernels  12.4 us (47%)
  starting transfers between devices  9.34 us (35%)
  waiting for transfers between devices  4.67 us (18%)
    ppermute x7, starting transfers between devices, exchange(): received[k] = lax.ppermute(values[k - 1], axis, pairs)  9.34 us
    ppermute x7, waiting for transfers between devices, exchange(): received[k] = lax.ppermute(values[k - 1], axis, pairs)  4.67 us
    pallas_call x1, Pallas kernels, on_device(): pl.pallas_call(functools.partial(first_kernel, ny, nz, partners, paired),...  3.78 us
    pallas_call x1, Pallas kernels, on_device(): pl.pallas_call(functools.partial(second_kernel, ny, nz, count_z, wy, part...  2.24 us
    pallas_call x1, Pallas kernels, on_device(): pl.pallas_call(functools.partial(local_y_kernel, wy), out_shape=array(pla...  1.86 us
    pallas_call x1, Pallas kernels, on_device(): pl.pallas_call(functools.partial(y_kernel, count_y, wy), out_shape=[array...  1.42 us
    pallas_call x1, Pallas kernels, on_device(): pl.pallas_call(functools.partial(last_kernel, base, radix, narrow, wy), o...  1.35 us
    pallas_call x1, Pallas kernels, on_device(): pl.pallas_call(third_kernel, out_shape=array(4, planes, LANES), in_specs=...  0.92 us
  transfers between devices with their start and end apart: 7, of which 4 were waited for; matrix products, arithmetic and copies ran while one was open for 0% of the time, Pallas kernels for 24%

profile of v9, /device:TPU:0, one launch (start us, length us, event | category | flops | bytes accessed | tf_op | source)
XLA Modules:
  0.0 26.5 jit_solution(1128564563805917205)
XLA Ops:
  0.0 3.8 %forcing_and_factor.1 = (bf16[2880,256]{1,0:T(8,128)(2,1)S(1)}, bf16[2880,256]{1,0:T(8,128)(2,1)S(1)}, f32[28,8,128]{2,1,0:T(8,128)S(1)}, f32[8,8,128]{2,1,0:T(8...) custom-call(f32[5,8,64,128]{3,2,1,0:T(8,128)} %flow_hbm.1, ...), custom_call_target="tpu_custom_call" | custom-call | tf_op jit(solution)/shard_map/forcing_and_factor/pallas_call | solution.py:799
  3.8 2.4 %collective-permute-start = (f32[2,2880]{1,0:T(2,128)S(1)}, f32[2,2880]{1,0:T(2,128)S(1)}, u32[]{:S(2)}, u32[]{:S(2)}) collective-permute-start(f32[2,2880]{1,0:T(2,128)S(1)} %get-tuple-element.31), channel_id=1, source_target_pairs={{0,24},{8,16},{16,8},{24,0},{1,25},{9,17},{17,9},{25,1},{2,26},{10... | collective-permute-start | bytes 69128 | tf_op jit(solution)/shard_map/ppermute | solution.py:821
  6.2 0.6 %collective-permute-start.1 = (f32[2,2880]{1,0:T(2,128)S(1)}, f32[2,2880]{1,0:T(2,128)S(1)}, u32[]{:S(2)}, u32[]{:S(2)}) collective-permute-start(f32[2,2880]{1,0:T(2,128)S(1)} %get-tuple-element.32), channel_id=1, source_target_pairs={{0,16},{8,24},{16,0},{24,8},{1,17},{9,25},{17,1},{25,9},{2,18},{10... | collective-permute-start | bytes 69128 | tf_op jit(solution)/shard_map/ppermute | solution.py:821
  6.9 0.0 collective-permute-start.2
  6.9 0.8 %inverse_z.1 = (bf16[256,256]{1,0:T(8,128)(2,1)S(1)}, bf16[160,2880]{1,0:T(8,128)(2,1)S(1)}, bf16[160,2880]{1,0:T(8,128)(2,1)S(1)}) custom-call(f32[28,8,128]{2,1,0:T(8,128)S(1)} %get-tuple-element.23.factors), custom_call_target="tpu_custom_call" | custom-call | flops 2949120 | bytes 737280 | tf_op jit(solution)/shard_map/inverse_z/pallas_call | solution.py:827
  7.7 2.2 %local_z.1 = (f32[2880,128]{1,0:T(8,128)S(1)}, f32[160,128]{1,0:T(8,128)S(1)}, f32[24,128]{1,0:T(8,128)S(1)}) custom-call(f32[8,8,128]{2,1,0:T(8,128)S(1)} %get-tuple-element.22.chains, f32[28,8,128]{2,1,0:T(8,128)S(1)} %get-tuple-element.23.factors, bf16[256,256]{1,0:T(8,128)(2,1)S(1)} %get-tuple-element.24.matrix, ...), custom_call_target="tpu_custom_call" | custom-call | flops 1132462080 | bytes 4423680 | tf_op jit(solution)/shard_map/local_z/pallas_call | solution.py:850
  9.9 0.0 collective-permute-done.refs_0_.refs_2_
  9.9 0.1 collective-permute-done.1.refs_1_
  10.0 0.0 collective-permute-done.2.refs_2_.refs_0_
  10.0 0.9 %carried_y.1.unused.refs_0_ = f32[4,40,128]{2,1,0:T(8,128)S(1)} custom-call(f32[160,128]{1,0:T(8,128)S(1)} %get-tuple-element.27.moments, bf16[160,2880]{1,0:T(8,128)(2,1)S(1)} %get-tuple-element.28.spread_high, bf16[160,2880]{1,0:T(8,128)(2,1)S(1)} %get-tuple-element.29.spread_low, f32[24,128]{1,0:T(8,128)S(1)} %get-tuple-element.30.entering, ...), custom_call_target="tpu_custom_call" | custom-call | tf_op jit(solution)/shard_map/carried_y/pallas_call | solution.py:867
  11.0 1.7 %collective-permute-start.5 = (f32[4,40,128]{2,1,0:T(8,128)S(1)}, f32[4,40,128]{2,1,0:T(8,128)S(1)}, u32[]{:S(2)}, u32[]{:S(2)}) collective-permute-start(f32[4,40,128]{2,1,0:T(8,128)S(1)} %carried_y.1.unused.refs_0_), channel_id=1, source_target_pairs={{0,1},{1,0},{2,3},{3,2},{4,5},{5,4},{6,7},{7,6},{8,9},{9,8},{10,11... | collective-permute-start | bytes 245768 | tf_op jit(solution)/shard_map/ppermute | solution.py:821
  12.7 1.6 %collective-permute-start.4 = (f32[4,40,128]{2,1,0:T(8,128)S(1)}, f32[4,40,128]{2,1,0:T(8,128)S(1)}, u32[]{:S(2)}, u32[]{:S(2)}) collective-permute-start(f32[4,40,128]{2,1,0:T(8,128)S(1)} %carried_y.1.unused.refs_0_), channel_id=1, source_target_pairs={{0,2},{1,3},{2,0},{3,1},{4,6},{5,7},{6,4},{7,5},{8,10},{9,11},{10,... | collective-permute-start | bytes 245768 | tf_op jit(solution)/shard_map/ppermute | solution.py:821
  14.3 0.3 collective-permute-start.3
  14.5 1.4 %inverse_y.1 = (f32[64,128]{1,0:T(8,128)S(1)}, f32[8,8,128]{2,1,0:T(8,128)S(1)}) custom-call(f32[8,8,128]{2,1,0:T(8,128)S(1)} %get-tuple-element.22.chains, f32[28,8,128]{2,1,0:T(8,128)S(1)} %get-tuple-element.23.factors, f32[4,40,128]{2,1,0:T(8,128)S(1)} %carried_y.1.unused.refs_0_), custom_call_target="tpu_custom_call" | custom-call | flops 566231040 | bytes 2949120 | tf_op jit(solution)/shard_map/inverse_y/pallas_call | solution.py:883
  16.0 0.0 collective-permute-done.5.refs_3_
  16.0 1.8 %collective-permute-done.4.refs_2_ = f32[4,40,128]{2,1,0:T(8,128)S(1)} collective-permute-done((f32[4,40,128]{2,1,0:T(8,128)S(1)}, f32[4,40,128]{2,1,0:T(8,128)S(1)}, u32[]{:S(2)}, u32[]{:S(2)}) %collective-permute-start.4) | collective-permute-done | bytes 81952 | tf_op jit(solution)/shard_map/ppermute | solution.py:821
  17.8 1.8 %collective-permute-done.3.refs_1_ = f32[4,40,128]{2,1,0:T(8,128)S(1)} collective-permute-done((f32[4,40,128]{2,1,0:T(8,128)S(1)}, f32[4,40,128]{2,1,0:T(8,128)S(1)}, u32[]{:S(2)}, u32[]{:S(2)}) %collective-permute-start.3) | collective-permute-done | bytes 81952 | tf_op jit(solution)/shard_map/ppermute | solution.py:821
  19.6 0.1 join_groups.1
  19.7 2.6 %collective-permute-start.6 = (f32[2,40,128]{2,1,0:T(8,128)S(1)}, f32[2,40,128]{2,1,0:T(8,128)S(1)}, u32[]{:S(2)}, u32[]{:S(2)}) collective-permute-start(f32[2,40,128]{2,1,0:T(8,128)S(1)} %get-tuple-element.38), channel_id=1, source_target_pairs={{0,4},{1,5},{2,6},{3,7},{4,0},{5,1},{6,2},{7,3},{8,12},{9,13},{10,... | collective-permute-start | bytes 122888 | tf_op jit(solution)/shard_map/ppermute | solution.py:821
  22.4 1.9 %local_y.1.local = f32[40,64,128]{2,1,0:T(8,128)S(1)} custom-call(f32[2880,128]{1,0:T(8,128)S(1)} %get-tuple-element.35.local, f32[24,128]{1,0:T(8,128)S(1)} %get-tuple-element.30.entering, f32[64,128]{1,0:T(8,128)S(1)} %get-tuple-element.36.inverse_y, f32[4,40,128]{2,1,0:T(8,128)S(1)} %get-tuple-element.37.unused.entered, ...), custom_call_target="tpu_custom_call" | custom-call | flops 566231040 | bytes 2949120 | tf_op jit(solution)/shard_map/local_y/pallas_call | solution.py:906
  24.2 0.9 %collective-permute-done.6.refs_0_ = f32[2,40,128]{2,1,0:T(8,128)S(1)} collective-permute-done((f32[2,40,128]{2,1,0:T(8,128)S(1)}, f32[2,40,128]{2,1,0:T(8,128)S(1)}, u32[]{:S(2)}, u32[]{:S(2)}) %collective-permute-start.6) | collective-permute-done | bytes 40992 | tf_op jit(solution)/shard_map/ppermute | solution.py:821
  25.1 1.4 %finish_y.1 = f32[5,8,64,128]{3,2,1,0:T(8,128)} custom-call(f32[8,8,128]{2,1,0:T(8,128)S(1)} %get-tuple-element.34.coefs, f32[40,64,128]{2,1,0:T(8,128)S(1)} %local_y.1.local, f32[64,128]{1,0:T(8,128)S(1)} %get-tuple-element.36.inverse_y, f32[4,40,128]{2,1,0:T(8,128)S(1)} %get-tuple-element.37.unused.entered, f32[2,40,128]{2,1,0:T(8,128)S(1)} %collective-permute-done.6.refs_0_), custom_call_target="tpu_custom_call" | custom-call | tf_op jit(solution)/shard_map/finish_y/pallas_call | solution.py:917
Async XLA Ops:
  3.8 6.1 %collective-permute-start = (f32[2,2880]{1,0:T(2,128)S(1)}, f32[2,2880]{1,0:T(2,128)S(1)}, u32[]{:S(2)}, u32[]{:S(2)}) collective-permute-start(f32[2,2880]{1,0:T(2,128)S(1)} %get-tuple-element.31), channel_id=1, source_target_pairs={{0,24},{8,16},{16,8},{24,0},{1,25},{9,17},{17,9},{25,1},{2,26},{10... | collective-permute-start | bytes 69128 | tf_op jit(solution)/shard_map/ppermute | solution.py:821
  6.2 3.8 %collective-permute-start.1 = (f32[2,2880]{1,0:T(2,128)S(1)}, f32[2,2880]{1,0:T(2,128)S(1)}, u32[]{:S(2)}, u32[]{:S(2)}) collective-permute-start(f32[2,2880]{1,0:T(2,128)S(1)} %get-tuple-element.32), channel_id=1, source_target_pairs={{0,16},{8,24},{16,0},{24,8},{1,17},{9,25},{17,1},{25,9},{2,18},{10... | collective-permute-start | bytes 69128 | tf_op jit(solution)/shard_map/ppermute | solution.py:821
  6.9 3.2 %collective-permute-start.2 = (f32[2,2880]{1,0:T(2,128)S(1)}, f32[2,2880]{1,0:T(2,128)S(1)}, u32[]{:S(2)}, u32[]{:S(2)}) collective-permute-start(f32[2,2880]{1,0:T(2,128)S(1)} %get-tuple-element.33), channel_id=1, source_target_pairs={{0,8},{8,0},{16,24},{24,16},{1,9},{9,1},{17,25},{25,17},{2,10},{10... | collective-permute-start | bytes 69128 | tf_op jit(solution)/shard_map/ppermute | solution.py:821
  11.0 5.0 %collective-permute-start.5 = (f32[4,40,128]{2,1,0:T(8,128)S(1)}, f32[4,40,128]{2,1,0:T(8,128)S(1)}, u32[]{:S(2)}, u32[]{:S(2)}) collective-permute-start(f32[4,40,128]{2,1,0:T(8,128)S(1)} %carried_y.1.unused.refs_0_), channel_id=1, source_target_pairs={{0,1},{1,0},{2,3},{3,2},{4,5},{5,4},{6,7},{7,6},{8,9},{9,8},{10,11... | collective-permute-start | bytes 245768 | tf_op jit(solution)/shard_map/ppermute | solution.py:821
  12.7 5.1 %collective-permute-start.4 = (f32[4,40,128]{2,1,0:T(8,128)S(1)}, f32[4,40,128]{2,1,0:T(8,128)S(1)}, u32[]{:S(2)}, u32[]{:S(2)}) collective-permute-start(f32[4,40,128]{2,1,0:T(8,128)S(1)} %carried_y.1.unused.refs_0_), channel_id=1, source_target_pairs={{0,2},{1,3},{2,0},{3,1},{4,6},{5,7},{6,4},{7,5},{8,10},{9,11},{10,... | collective-permute-start | bytes 245768 | tf_op jit(solution)/shard_map/ppermute | solution.py:821
  14.3 5.3 %collective-permute-start.3 = (f32[4,40,128]{2,1,0:T(8,128)S(1)}, f32[4,40,128]{2,1,0:T(8,128)S(1)}, u32[]{:S(2)}, u32[]{:S(2)}) collective-permute-start(f32[4,40,128]{2,1,0:T(8,128)S(1)} %carried_y.1.unused.refs_0_), channel_id=1, source_target_pairs={{0,3},{1,2},{2,1},{3,0},{4,7},{5,6},{6,5},{7,4},{8,11},{9,10},{10,... | collective-permute-start | bytes 245768 | tf_op jit(solution)/shard_map/ppermute | solution.py:821
  19.7 5.4 %collective-permute-start.6 = (f32[2,40,128]{2,1,0:T(8,128)S(1)}, f32[2,40,128]{2,1,0:T(8,128)S(1)}, u32[]{:S(2)}, u32[]{:S(2)}) collective-permute-start(f32[2,40,128]{2,1,0:T(8,128)S(1)} %get-tuple-element.38), channel_id=1, source_target_pairs={{0,4},{1,5},{2,6},{3,7},{4,0},{5,1},{6,2},{7,3},{8,12},{9,13},{10,... | collective-permute-start | bytes 122888 | tf_op jit(solution)/shard_map/ppermute | solution.py:821

commit v10 on v9

--- a/solution.py
+++ b/solution.py
@@ -714,7 +714,7 @@
 
 
 def stage_kernel(base, stride, radix, narrow, has_entered, coefs, *refs):
-    values = (refs[0],) + tuple(refs[1:radix][::-1])
+    values = refs[:radix]
     position = radix
     entered = None
     if has_entered:
@@ -892,7 +892,7 @@
             )(chains, factors, carried)
         if number + 1 < len(plan):
             slim = narrow and number + 2 == len(plan)
-            inputs = [carried] + received[::-1] + ([entered] if entered is not None else [])
+            inputs = [carried] + received + ([entered] if entered is not None else [])
             carried, entered = pl.pallas_call(
                 functools.partial(stage_kernel, base, stride, radix, slim, entered is not None),
                 out_shape=[array(2 if slim else 4, planes, LANES), array(4, planes, LANES)],

time: 26.6 us -> 25.2 us (0.947)
  waiting for transfers between devices: 4.67 us -> 3.22 us
    ppermute x7, waiting for transfers between devices: 4.67 us -> 3.22 us  [exchange(): received[k] = lax.ppermute(values[k - 1], axis, pairs)]
  transfers between devices with their start and end apart: 7 -> 7, of which waited for: 4 -> 5; matrix products, arithmetic and copies ran while one was open for 0% -> 0% of each run, Pallas kernels for 24% -> 25%
where the time goes in v10:
time: 25.2 us; the launch traced here: 25 us
  Pallas kernels  12.4 us (49%)
  starting transfers between devices  9.34 us (37%)
  waiting for transfers between devices  3.22 us (13%)
    ppermute x7, starting transfers between devices, exchange(): received[k] = lax.ppermute(values[k - 1], axis, pairs)  9.34 us
    pallas_call x1, Pallas kernels, on_device(): pl.pallas_call(functools.partial(first_kernel, ny, nz, partners, paired),...  3.78 us
    ppermute x7, waiting for transfers between devices, exchange(): received[k] = lax.ppermute(values[k - 1], axis, pairs)  3.22 us
    pallas_call x1, Pallas kernels, on_device(): pl.pallas_call(functools.partial(second_kernel, ny, nz, count_z, wy, part...  2.24 us
    pallas_call x1, Pallas kernels, on_device(): pl.pallas_call(functools.partial(local_y_kernel, wy), out_shape=array(pla...  1.86 us
    pallas_call x1, Pallas kernels, on_device(): pl.pallas_call(functools.partial(y_kernel, count_y, wy), out_shape=[array...  1.42 us
    pallas_call x1, Pallas kernels, on_device(): pl.pallas_call(functools.partial(last_kernel, base, radix, narrow, wy), o...  1.35 us
    pallas_call x1, Pallas kernels, on_device(): pl.pallas_call(third_kernel, out_shape=array(4, planes, LANES), in_specs=...  0.92 us
  transfers between devices with their start and end apart: 7, of which 5 were waited for; matrix products, arithmetic and copies ran while one was open for 0% of the time, Pallas kernels for 25%

profile of v10, /device:TPU:0, one launch (start us, length us, event | category | flops | bytes accessed | tf_op | source)
XLA Modules:
  0.0 25.0 jit_solution(15672481822456468106)
XLA Ops:
  0.0 3.8 %forcing_and_factor.1 = (bf16[2880,256]{1,0:T(8,128)(2,1)S(1)}, bf16[2880,256]{1,0:T(8,128)(2,1)S(1)}, f32[28,8,128]{2,1,0:T(8,128)S(1)}, f32[8,8,128]{2,1,0:T(8...) custom-call(f32[5,8,64,128]{3,2,1,0:T(8,128)} %flow_hbm.1, ...), custom_call_target="tpu_custom_call" | custom-call | tf_op jit(solution)/shard_map/forcing_and_factor/pallas_call | solution.py:799
  3.8 2.4 %collective-permute-start = (f32[2,2880]{1,0:T(2,128)S(1)}, f32[2,2880]{1,0:T(2,128)S(1)}, u32[]{:S(2)}, u32[]{:S(2)}) collective-permute-start(f32[2,2880]{1,0:T(2,128)S(1)} %get-tuple-element.31), channel_id=1, source_target_pairs={{0,24},{8,16},{16,8},{24,0},{1,25},{9,17},{17,9},{25,1},{2,26},{10... | collective-permute-start | bytes 69128 | tf_op jit(solution)/shard_map/ppermute | solution.py:821
  6.2 0.6 %collective-permute-start.1 = (f32[2,2880]{1,0:T(2,128)S(1)}, f32[2,2880]{1,0:T(2,128)S(1)}, u32[]{:S(2)}, u32[]{:S(2)}) collective-permute-start(f32[2,2880]{1,0:T(2,128)S(1)} %get-tuple-element.32), channel_id=1, source_target_pairs={{0,16},{8,24},{16,0},{24,8},{1,17},{9,25},{17,1},{25,9},{2,18},{10... | collective-permute-start | bytes 69128 | tf_op jit(solution)/shard_map/ppermute | solution.py:821
  6.9 0.0 collective-permute-start.2
  6.9 0.8 %inverse_z.1 = (bf16[256,256]{1,0:T(8,128)(2,1)S(1)}, bf16[160,2880]{1,0:T(8,128)(2,1)S(1)}, bf16[160,2880]{1,0:T(8,128)(2,1)S(1)}) custom-call(f32[28,8,128]{2,1,0:T(8,128)S(1)} %get-tuple-element.23.factors), custom_call_target="tpu_custom_call" | custom-call | flops 2949120 | bytes 737280 | tf_op jit(solution)/shard_map/inverse_z/pallas_call | solution.py:827
  7.7 2.2 %local_z.1 = (f32[2880,128]{1,0:T(8,128)S(1)}, f32[160,128]{1,0:T(8,128)S(1)}, f32[24,128]{1,0:T(8,128)S(1)}) custom-call(f32[8,8,128]{2,1,0:T(8,128)S(1)} %get-tuple-element.22.chains, f32[28,8,128]{2,1,0:T(8,128)S(1)} %get-tuple-element.23.factors, bf16[256,256]{1,0:T(8,128)(2,1)S(1)} %get-tuple-element.24.matrix, ...), custom_call_target="tpu_custom_call" | custom-call | flops 1132462080 | bytes 4423680 | tf_op jit(solution)/shard_map/local_z/pallas_call | solution.py:850
  9.9 0.0 collective-permute-done.refs_0_.refs_2_
  9.9 0.1 collective-permute-done.1.refs_1_
  10.0 0.0 collective-permute-done.2.refs_2_.refs_0_
  10.0 0.9 %carried_y.1.unused.refs_0_ = f32[4,40,128]{2,1,0:T(8,128)S(1)} custom-call(f32[160,128]{1,0:T(8,128)S(1)} %get-tuple-element.27.moments, bf16[160,2880]{1,0:T(8,128)(2,1)S(1)} %get-tuple-element.28.spread_high, bf16[160,2880]{1,0:T(8,128)(2,1)S(1)} %get-tuple-element.29.spread_low, f32[24,128]{1,0:T(8,128)S(1)} %get-tuple-element.30.entering, ...), custom_call_target="tpu_custom_call" | custom-call | tf_op jit(solution)/shard_map/carried_y/pallas_call | solution.py:867
  11.0 2.7 %collective-permute-start.5 = (f32[4,40,128]{2,1,0:T(8,128)S(1)}, f32[4,40,128]{2,1,0:T(8,128)S(1)}, u32[]{:S(2)}, u32[]{:S(2)}) collective-permute-start(f32[4,40,128]{2,1,0:T(8,128)S(1)} %carried_y.1.unused.refs_0_), channel_id=1, source_target_pairs={{0,3},{1,2},{2,1},{3,0},{4,7},{5,6},{6,5},{7,4},{8,11},{9,10},{10,... | collective-permute-start | bytes 245768 | tf_op jit(solution)/shard_map/ppermute | solution.py:821
  13.7 0.4 %collective-permute-start.4 = (f32[4,40,128]{2,1,0:T(8,128)S(1)}, f32[4,40,128]{2,1,0:T(8,128)S(1)}, u32[]{:S(2)}, u32[]{:S(2)}) collective-permute-start(f32[4,40,128]{2,1,0:T(8,128)S(1)} %carried_y.1.unused.refs_0_), channel_id=1, source_target_pairs={{0,2},{1,3},{2,0},{3,1},{4,6},{5,7},{6,4},{7,5},{8,10},{9,11},{10,... | collective-permute-start | bytes 245768 | tf_op jit(solution)/shard_map/ppermute | solution.py:821
  14.2 0.4 %collective-permute-start.3 = (f32[4,40,128]{2,1,0:T(8,128)S(1)}, f32[4,40,128]{2,1,0:T(8,128)S(1)}, u32[]{:S(2)}, u32[]{:S(2)}) collective-permute-start(f32[4,40,128]{2,1,0:T(8,128)S(1)} %carried_y.1.unused.refs_0_), channel_id=1, source_target_pairs={{0,1},{1,0},{2,3},{3,2},{4,5},{5,4},{6,7},{7,6},{8,9},{9,8},{10,11... | collective-permute-start | bytes 245768 | tf_op jit(solution)/shard_map/ppermute | solution.py:821
  14.6 1.4 %inverse_y.1 = (f32[64,128]{1,0:T(8,128)S(1)}, f32[8,8,128]{2,1,0:T(8,128)S(1)}) custom-call(f32[8,8,128]{2,1,0:T(8,128)S(1)} %get-tuple-element.22.chains, f32[28,8,128]{2,1,0:T(8,128)S(1)} %get-tuple-element.23.factors, f32[4,40,128]{2,1,0:T(8,128)S(1)} %carried_y.1.unused.refs_0_), custom_call_target="tpu_custom_call" | custom-call | flops 566231040 | bytes 2949120 | tf_op jit(solution)/shard_map/inverse_y/pallas_call | solution.py:883
  16.0 1.2 %collective-permute-done.5.refs_3_ = f32[4,40,128]{2,1,0:T(8,128)S(1)} collective-permute-done((f32[4,40,128]{2,1,0:T(8,128)S(1)}, f32[4,40,128]{2,1,0:T(8,128)S(1)}, u32[]{:S(2)}, u32[]{:S(2)}) %collective-permute-start.5) | collective-permute-done | bytes 81952 | tf_op jit(solution)/shard_map/ppermute | solution.py:821
  17.2 1.3 %collective-permute-done.4.refs_2_ = f32[4,40,128]{2,1,0:T(8,128)S(1)} collective-permute-done((f32[4,40,128]{2,1,0:T(8,128)S(1)}, f32[4,40,128]{2,1,0:T(8,128)S(1)}, u32[]{:S(2)}, u32[]{:S(2)}) %collective-permute-start.4) | collective-permute-done | bytes 81952 | tf_op jit(solution)/shard_map/ppermute | solution.py:821
  18.5 0.1 collective-permute-done.3.refs_1_
  18.6 0.1 join_groups.1
  18.7 2.7 %collective-permute-start.6 = (f32[2,40,128]{2,1,0:T(8,128)S(1)}, f32[2,40,128]{2,1,0:T(8,128)S(1)}, u32[]{:S(2)}, u32[]{:S(2)}) collective-permute-start(f32[2,40,128]{2,1,0:T(8,128)S(1)} %get-tuple-element.38), channel_id=1, source_target_pairs={{0,4},{1,5},{2,6},{3,7},{4,0},{5,1},{6,2},{7,3},{8,12},{9,13},{10,... | collective-permute-start | bytes 122888 | tf_op jit(solution)/shard_map/ppermute | solution.py:821
  21.4 1.9 %local_y.1.local = f32[40,64,128]{2,1,0:T(8,128)S(1)} custom-call(f32[2880,128]{1,0:T(8,128)S(1)} %get-tuple-element.35.local, f32[24,128]{1,0:T(8,128)S(1)} %get-tuple-element.30.entering, f32[64,128]{1,0:T(8,128)S(1)} %get-tuple-element.36.inverse_y, f32[4,40,128]{2,1,0:T(8,128)S(1)} %get-tuple-element.37.unused.entered, ...), custom_call_target="tpu_custom_call" | custom-call | flops 566231040 | bytes 2949120 | tf_op jit(solution)/shard_map/local_y/pallas_call | solution.py:906
  23.2 0.5 %collective-permute-done.6.refs_0_ = f32[2,40,128]{2,1,0:T(8,128)S(1)} collective-permute-done((f32[2,40,128]{2,1,0:T(8,128)S(1)}, f32[2,40,128]{2,1,0:T(8,128)S(1)}, u32[]{:S(2)}, u32[]{:S(2)}) %collective-permute-start.6) | collective-permute-done | bytes 40992 | tf_op jit(solution)/shard_map/ppermute | solution.py:821
  23.7 1.4 %finish_y.1 = f32[5,8,64,128]{3,2,1,0:T(8,128)} custom-call(f32[8,8,128]{2,1,0:T(8,128)S(1)} %get-tuple-element.34.coefs, f32[40,64,128]{2,1,0:T(8,128)S(1)} %local_y.1.local, f32[64,128]{1,0:T(8,128)S(1)} %get-tuple-element.36.inverse_y, f32[4,40,128]{2,1,0:T(8,128)S(1)} %get-tuple-element.37.unused.entered, f32[2,40,128]{2,1,0:T(8,128)S(1)} %collective-permute-done.6.refs_0_), custom_call_target="tpu_custom_call" | custom-call | tf_op jit(solution)/shard_map/finish_y/pallas_call | solution.py:917
Async XLA Ops:
  3.8 6.1 %collective-permute-start = (f32[2,2880]{1,0:T(2,128)S(1)}, f32[2,2880]{1,0:T(2,128)S(1)}, u32[]{:S(2)}, u32[]{:S(2)}) collective-permute-start(f32[2,2880]{1,0:T(2,128)S(1)} %get-tuple-element.31), channel_id=1, source_target_pairs={{0,24},{8,16},{16,8},{24,0},{1,25},{9,17},{17,9},{25,1},{2,26},{10... | collective-permute-start | bytes 69128 | tf_op jit(solution)/shard_map/ppermute | solution.py:821
  6.2 3.8 %collective-permute-start.1 = (f32[2,2880]{1,0:T(2,128)S(1)}, f32[2,2880]{1,0:T(2,128)S(1)}, u32[]{:S(2)}, u32[]{:S(2)}) collective-permute-start(f32[2,2880]{1,0:T(2,128)S(1)} %get-tuple-element.32), channel_id=1, source_target_pairs={{0,16},{8,24},{16,0},{24,8},{1,17},{9,25},{17,1},{25,9},{2,18},{10... | collective-permute-start | bytes 69128 | tf_op jit(solution)/shard_map/ppermute | solution.py:821
  6.9 3.2 %collective-permute-start.2 = (f32[2,2880]{1,0:T(2,128)S(1)}, f32[2,2880]{1,0:T(2,128)S(1)}, u32[]{:S(2)}, u32[]{:S(2)}) collective-permute-start(f32[2,2880]{1,0:T(2,128)S(1)} %get-tuple-element.33), channel_id=1, source_target_pairs={{0,8},{8,0},{16,24},{24,16},{1,9},{9,1},{17,25},{25,17},{2,10},{10... | collective-permute-start | bytes 69128 | tf_op jit(solution)/shard_map/ppermute | solution.py:821
  11.0 6.2 %collective-permute-start.5 = (f32[4,40,128]{2,1,0:T(8,128)S(1)}, f32[4,40,128]{2,1,0:T(8,128)S(1)}, u32[]{:S(2)}, u32[]{:S(2)}) collective-permute-start(f32[4,40,128]{2,1,0:T(8,128)S(1)} %carried_y.1.unused.refs_0_), channel_id=1, source_target_pairs={{0,3},{1,2},{2,1},{3,0},{4,7},{5,6},{6,5},{7,4},{8,11},{9,10},{10,... | collective-permute-start | bytes 245768 | tf_op jit(solution)/shard_map/ppermute | solution.py:821
  13.7 4.7 %collective-permute-start.4 = (f32[4,40,128]{2,1,0:T(8,128)S(1)}, f32[4,40,128]{2,1,0:T(8,128)S(1)}, u32[]{:S(2)}, u32[]{:S(2)}) collective-permute-start(f32[4,40,128]{2,1,0:T(8,128)S(1)} %carried_y.1.unused.refs_0_), channel_id=1, source_target_pairs={{0,2},{1,3},{2,0},{3,1},{4,6},{5,7},{6,4},{7,5},{8,10},{9,11},{10,... | collective-permute-start | bytes 245768 | tf_op jit(solution)/shard_map/ppermute | solution.py:821
  14.2 4.4 %collective-permute-start.3 = (f32[4,40,128]{2,1,0:T(8,128)S(1)}, f32[4,40,128]{2,1,0:T(8,128)S(1)}, u32[]{:S(2)}, u32[]{:S(2)}) collective-permute-start(f32[4,40,128]{2,1,0:T(8,128)S(1)} %carried_y.1.unused.refs_0_), channel_id=1, source_target_pairs={{0,1},{1,0},{2,3},{3,2},{4,5},{5,4},{6,7},{7,6},{8,9},{9,8},{10,11... | collective-permute-start | bytes 245768 | tf_op jit(solution)/shard_map/ppermute | solution.py:821
  18.7 5.0 %collective-permute-start.6 = (f32[2,40,128]{2,1,0:T(8,128)S(1)}, f32[2,40,128]{2,1,0:T(8,128)S(1)}, u32[]{:S(2)}, u32[]{:S(2)}) collective-permute-start(f32[2,40,128]{2,1,0:T(8,128)S(1)} %get-tuple-element.38), channel_id=1, source_target_pairs={{0,4},{1,5},{2,6},{3,7},{4,0},{5,1},{6,2},{7,3},{8,12},{9,13},{10,... | collective-permute-start | bytes 122888 | tf_op jit(solution)/shard_map/ppermute | solution.py:821

commit v11 on v10

--- a/solution.py
+++ b/solution.py
@@ -159,11 +159,10 @@
     return jnp.where(even, chain[column], chain[2 + column])
 
 
-def first_kernel(ny, nz, partners, paired, flow_hbm, speed_hbm, metric_y, metric_z, *refs):
+def first_kernel(ny, nz, partners, flow_hbm, speed_hbm, metric_y, metric_z, *refs):
     high, low, factors, chains = refs[:4]
-    count = 1 if paired else partners
-    messages = refs[4 : 4 + count]
-    flow, speed, metric, spread, arrived = refs[4 + count :]
+    messages = refs[4 : 4 + partners]
+    flow, speed, metric, spread, arrived = refs[4 + partners :]
     fields, planes_x, wy, _ = flow.shape
     rows = ny + nz
     core_rows = fields * planes_x * wy
@@ -285,26 +284,10 @@
                 jnp.concatenate([inside_down, ends_down], axis=1),
             )
         )
-    if paired:
-        lower = (me & 1) == 0
-        stack = [jnp.where(lower, w[0], w[1]) for w in weights]
-        peer = lax.broadcasted_iota(jnp.int32, (rows, LANES), 0) == ny + jnp.bitwise_xor(me, 1)
-
-        def of_peer(values, place):
-            chosen = tuple(jnp.sum(jnp.where(peer, v, 0.0), axis=0, keepdims=True) for v in values)
-            return tuple(jnp.broadcast_to(v[:, place : place + 1], (1, 2 * LANES)) for v in chosen)
-
-        over, under = of_peer(to_right, 0), of_peer(to_left, LANES - 1)
-        (up0, down0), (up1, down1) = weights
-        for q in range(2):
-            upward = jnp.where(lower, over[q] * up0 + over[2 + q] * up1, weights[q][0])
-            downward = jnp.where(lower, weights[q][1], under[q] * down0 + under[2 + q] * down1)
-            stack.append(jnp.where(me < 2, upward, downward))
-    else:
-        stack = []
-        for k in range(1, partners + 1):
-            upward = jnp.bitwise_xor(me, k) > me
-            stack += [jnp.where(upward, w[0], w[1]) for w in weights]
+    stack = []
+    for k in range(1, partners + 1):
+        upward = jnp.bitwise_xor(me, k) > me
+        stack += [jnp.where(upward, w[0], w[1]) for w in weights]
     while len(stack) % 8:
         stack.append(jnp.zeros((1, 2 * LANES), jnp.float32))
     count = len(stack)
@@ -319,11 +302,8 @@
         on_high = matmul(both, high[rows, :], across)
         on_low = matmul(both, low[rows, :], across)
         moments = (on_high[:count] + on_high[count:]) + on_low[:count]
-        if paired:
-            messages[0][:, rows] = moments[0:4]
-        else:
-            for k in range(partners):
-                messages[k][:, rows] = moments[2 * k : 2 * k + 2]
+        for k in range(partners):
+            messages[k][:, rows] = moments[2 * k : 2 * k + 2]
 
 
 def dense_inverse(columns, start, width, stack):
@@ -433,8 +413,12 @@
     return jnp.where(condition, 1.0, 0.0)
 
 
-def inverse_z_kernel(ny, planes, wy, factors, matrix, spread_high, spread_low, columns, stacked, rows_ref):
-    me_z = lax.axis_index("gz")
+def second_kernel(
+    ny, nz, count_z, wy, partners, chains, factors, high, low, local, moments, entering, spread_core, spread_extra, *scratch
+):
+    columns, stacked, rows_ref, matrix, weights_y = scratch
+    planes = (moments.shape[0] - 8) // 4
+    me_z, me_y = lax.axis_index("gz"), lax.axis_index("gy")
     columns[0:LANES, 0:32] = transposed(factors, ny + me_z)
     inverse = dense_inverse(columns, 0, LANES, stacked)
     rows_ref[0:LANES, :] = inverse
@@ -452,9 +436,9 @@
     matrix[:, 0:LANES] = first
     matrix[:, LANES : 2 * LANES] = second
 
-    cell = lax.axis_index("gy") * wy
+    cell = me_y * wy
+    start = lax.rem(cell, LANES)
     row = cell // LANES
-    total = planes * (wy + EXTRA)
     unit = (1.0, 0.0, 0.0, 1.0)
     lane = lax.broadcasted_iota(jnp.int32, (1, LANES), 1)
     even = (lane & 1) == 0
@@ -474,58 +458,26 @@
 
     up, down, before, after = chain(12), chain(16), chain(20), chain(24)
     past_up, past_down = mm(before, up), mm(after, down)
-    plane_row = lax.broadcasted_iota(jnp.int32, (planes, LANES), 0)
-    wide_lane = lax.broadcasted_iota(jnp.int32, (planes, LANES), 1)
+    core_rows, extra_rows = [], []
     for column in range(2):
         same = jnp.where(even, unit[column], unit[2 + column])
-        for number, inside, early, late in (
-            (column, up, turned(cell_weights(past_up, column, even), -start_y(cell)), same),
-            (
-                2 + column,
-                down,
-                same,
-                turned(cell_weights(past_down, column, even), 4 - wy - start_y(cell)),
-            ),
-        ):
-            inside = tiled(turned(cell_weights(inside, column, even), -start_y(cell)), wy)
-            past = jnp.where(lane < 2, early, jnp.where(lane < 4, late, 0.0))
-            past = tiled(past, EXTRA)
-            rows = slice(number * planes, (number + 1) * planes)
-            for begin in range(0, total, LANES):
-                if begin < planes * wy:
-                    owner, value = (begin + wide_lane) // wy, inside
-                else:
-                    owner, value = (begin - planes * wy + wide_lane) // EXTRA, past
-                size = min(LANES, total - begin)
-                first, second = halves(jnp.where(plane_row == owner, value, 0.0))
-                spread_high[rows, begin : begin + size] = first[:, 0:size]
-                spread_low[rows, begin : begin + size] = second[:, 0:size]
-
-
-def whole_rows(matrix, row):
-    start = row // 16 * 16
-    both = matrix[start : start + 16, :].astype(jnp.float32)
-    value = both[:, 0:LANES] + both[:, LANES : 2 * LANES]
-    return value[row - start : row - start + 1]
-
-
-def second_kernel(
-    ny, nz, count_z, wy, partners, paired, chains, factors, matrix, high, low, local, moments, entering, *scratch
-):
-    columns, weights_y = scratch
-    me_z, me_y = lax.axis_index("gz"), lax.axis_index("gy")
-    planes = moments.shape[0] // 4
-    head0, head1 = whole_rows(matrix, 0), whole_rows(matrix, 1)
-    tail0, tail1 = whole_rows(matrix, LANES - 2), whole_rows(matrix, LANES - 1)
-
-    if paired:
-        pair = me_z // 2 * 2
-        begins, ends = [me_z, pair], [me_z + 1, pair + 2]
-        lowers = [me_z % 2 == 1, pair > 0]
-    else:
-        others = [jnp.bitwise_xor(me_z, k) for k in range(1, partners + 1)]
-        begins, ends = [other + 1 for other in others], others
-        lowers = [other < me_z for other in others]
+        early = turned(cell_weights(past_up, column, even), -start)
+        late = turned(cell_weights(past_down, column, even), 4 - wy - start)
+        for inside, first, second in ((up, early, same), (down, same, late)):
+            core_rows.append(tiled(turned(cell_weights(inside, column, even), -start), wy))
+            past = jnp.where(lane < 2, first, jnp.where(lane < 4, second, 0.0))
+            extra_rows.append(tiled(past, EXTRA))
+    for number, source in enumerate((0, 2, 1, 3)):
+        for rows, out, width in ((core_rows, spread_core, wy), (extra_rows, spread_extra, EXTRA)):
+            per = LANES // width
+            owner = lax.broadcasted_iota(jnp.int32, (per, LANES), 0)
+            wide_lane = lax.broadcasted_iota(jnp.int32, (per, LANES), 1)
+            value = jnp.where(owner == wide_lane // width, rows[source], 0.0)
+            out[number * per : (number + 1) * per, :] = value
+
+    others = [jnp.bitwise_xor(me_z, k) for k in range(1, partners + 1)]
+    begins, ends = [other + 1 for other in others], others
+    lowers = [other < me_z for other in others]
     size = len(begins)
     up = chain_products(
         chains, 0, lambda b: (ny + b, 0), count_z, begins, [me_z] * size, [1.0] * size, False
@@ -545,9 +497,7 @@
     first = stack.astype(jnp.bfloat16).astype(jnp.float32)
     entering[...] = jnp.concatenate([first, stack - first, first], axis=0)
 
-    cell = me_y * wy
     columns[0:LANES, 0:32] = transposed(factors, cell // LANES)
-    start = lax.rem(cell, LANES)
     row = lax.broadcasted_iota(jnp.int32, (wy, LANES), 0)
     extra_row = lax.broadcasted_iota(jnp.int32, (EXTRA, LANES), 0)
     unit = (1.0, 0.0, 0.0, 1.0)
@@ -594,10 +544,6 @@
                 lines.append(value + jnp.sum(past, axis=0, keepdims=True))
             start = number * planes + part * 8
             moments[start : start + 8, :] = jnp.concatenate(lines, axis=0)
-
-
-def start_y(cell):
-    return lax.rem(cell, LANES)
 
 
 def y_kernel(count_y, wy, chains, factors, unused, inverse_y, coefs, columns, stacked):
@@ -643,10 +589,6 @@
             coefs[base + k] = value[k]
 
 
-def pair_kernel(own, received, unused, total):
-    total[...] = own[2:4] + received[2:4]
-
-
 def arrived_rows(messages, count):
     rows = [m[0:2] for m in messages]
     if count > 2 * len(messages):
@@ -654,27 +596,55 @@
     return jnp.concatenate(rows, axis=0)
 
 
-def third_kernel(moments, spread_high, spread_low, entering, *refs):
-    messages, carried = refs[:-1][::-1], refs[-1]
+def third_kernel(wy, moments, spread_core, spread_extra, entering, *refs):
+    messages, (carried, held, result) = refs[:-3][::-1], refs[-3:]
+    planes = carried.shape[1]
     count = entering.shape[0] // 3
     received = arrived_rows(messages, count)
     first = received.astype(jnp.bfloat16).astype(jnp.float32)
-    both = jnp.concatenate([first, received - first], axis=0).astype(jnp.bfloat16)
-    top = jnp.concatenate([first, jnp.zeros_like(first)], axis=0).astype(jnp.bfloat16)
+    both = jnp.concatenate([first, received - first], axis=0)
+    values = entering[0:count, :] + entering[count : 2 * count, :]
     across = (((1,), (1,)), ((), ()))
-    corner = matmul(spread_high[...], both, across) + matmul(spread_low[...], top, across)
-    values = entering[0:count, :] + entering[count : 2 * count, :]
-    added = lax.dot_general(
-        corner,
-        jnp.concatenate([values, values], axis=0),
-        (((1,), (0,)), ((), ())),
-        precision=lax.Precision.HIGHEST,
-        preferred_element_type=jnp.float32,
-    )
-    planes = carried.shape[1]
-    for number in range(4):
-        rows = slice(number * planes, (number + 1) * planes)
-        carried[number] = moments[rows, :] + added[rows]
+    used = 2 * len(messages)
+
+    def chunks(begin, end):
+        parts = [both[:, at : min(at + LANES, end)] for at in range(begin, end, LANES)]
+        if parts[-1].shape[1] < LANES:
+            missing = jnp.zeros((2 * count, LANES - parts[-1].shape[1]), jnp.float32)
+            parts[-1] = jnp.concatenate([parts[-1], missing], axis=1)
+        return jnp.concatenate(parts, axis=0).astype(jnp.bfloat16), len(parts)
+
+    per = LANES // wy
+    stack, number = chunks(0, planes * wy)
+    top, rest = halves(spread_core[...])
+    held[0 : number * 2 * count, 0 : 4 * per] = matmul(stack, top, across) + matmul(stack, rest, across)
+    columns = [
+        held[pl.ds(r, number, stride=2 * count), :] + held[pl.ds(count + r, number, stride=2 * count), :]
+        for r in range(used)
+    ]
+    for m in range(4):
+        for p in range(per):
+            lane = m * per + p
+            value = moments[pl.ds(m * planes + p, number, stride=per), :]
+            for r in range(used):
+                value = value + columns[r][:, lane : lane + 1] * values[r : r + 1]
+            result[pl.ds(m * planes + p, number, stride=per), :] = value
+
+    per = LANES // EXTRA
+    stack, number = chunks(planes * wy, planes * (wy + EXTRA))
+    top, rest = halves(spread_extra[...])
+    corner = matmul(top, stack, across) + matmul(rest, stack, across)
+    for m in range(4):
+        for chunk in range(number):
+            size = min(per, planes - chunk * per)
+            rows = slice(chunk * per, chunk * per + size)
+            value = result[m * planes + chunk * per : m * planes + chunk * per + size, :]
+            for r in range(used):
+                lane = chunk * 2 * count + r
+                part = corner[m * per : m * per + size]
+                column = part[:, lane : lane + 1] + part[:, lane + count : lane + count + 1]
+                value = value + column * values[r : r + 1]
+            carried[m, rows, :] = value
 
 
 def local_y_kernel(wy, local, entering, inverse_y, unused, *refs):
@@ -792,16 +762,15 @@
     planes = fields * planes_x
     rows = planes * (wy + EXTRA)
     partners = count_z - 1
-    paired = False
-    arrivals = 2 if paired else partners
+    arrivals = partners
     entering_rows = -(-2 * arrivals // 8) * 8
     half = jax.ShapeDtypeStruct((rows, 2 * LANES), jnp.bfloat16)
     outputs = pl.pallas_call(
-        functools.partial(first_kernel, ny, nz, partners, paired),
+        functools.partial(first_kernel, ny, nz, partners),
         out_shape=[half, half, array(28, ny + nz, LANES), array(8, ny + nz, LANES)]
-        + ([array(4, rows)] if paired else [array(2, rows)] * partners),
+        + [array(2, rows)] * partners,
         in_specs=[HBM] * 4,
-        out_specs=[VMEM] * (5 if paired else 4 + partners),
+        out_specs=[VMEM] * (4 + partners),
         scratch_shapes=[
             pltpu.VMEM(flow.shape, jnp.float32),
             pltpu.VMEM(speed.shape, jnp.float32),
@@ -823,55 +792,40 @@
 
     plan = stage_plan(count_y)
     work = [pltpu.VMEM((LANES + 16, LANES), jnp.float32)] * 2
-    spread = jax.ShapeDtypeStruct((4 * planes, rows), jnp.bfloat16)
-    matrix, spread_high, spread_low = pl.pallas_call(
-        functools.partial(inverse_z_kernel, ny, planes, wy),
-        out_shape=[jax.ShapeDtypeStruct((2 * LANES, 2 * LANES), jnp.bfloat16), spread, spread],
-        in_specs=[VMEM],
-        out_specs=[VMEM] * 3,
-        scratch_shapes=work + [pltpu.VMEM((2 * LANES, LANES), jnp.float32)],
-        compiler_params=PARAMS,
-        cost_estimate=cost(rows * 1024, 4 * rows * 64),
-        name="inverse_z",
-    )(factors)
-    if paired:
-        near = exchange(outputs[4:], "gz", count_z, 1, 2)
-        total = pl.pallas_call(
-            pair_kernel,
-            out_shape=array(2, rows),
-            in_specs=[VMEM] * 2 + [HBM],
-            out_specs=VMEM,
-            compiler_params=PARAMS,
-            name="join_pair",
-        )(outputs[4], near[0], matrix)
-        received = near + exchange([total], "gz", count_z, 2, 2)
-    else:
-        received = exchange(outputs[4:], "gz", count_z, 1, count_z)
-    local, moments, entering = pl.pallas_call(
-        functools.partial(second_kernel, ny, nz, count_z, wy, partners, paired),
+    received = exchange(outputs[4:], "gz", count_z, 1, count_z)
+    local, moments, entering, spread_core, spread_extra = pl.pallas_call(
+        functools.partial(second_kernel, ny, nz, count_z, wy, partners),
         out_shape=[
             array(rows, LANES),
-            array(4 * planes, LANES),
+            array(4 * planes + 8, LANES),
             array(3 * entering_rows, LANES),
+            array(4 * (LANES // wy), LANES),
+            array(4 * (LANES // EXTRA), LANES),
         ],
-        in_specs=[SMEM] + [VMEM] * 4,
-        out_specs=[VMEM] * 3,
-        scratch_shapes=[
-            pltpu.VMEM((LANES + 16, LANES), jnp.float32),
+        in_specs=[SMEM] + [VMEM] * 3,
+        out_specs=[VMEM] * 5,
+        scratch_shapes=work
+        + [
+            pltpu.VMEM((2 * LANES, LANES), jnp.float32),
+            pltpu.VMEM((2 * LANES, 2 * LANES), jnp.bfloat16),
             pltpu.VMEM((4, wy + EXTRA, LANES), jnp.float32),
         ],
         compiler_params=PARAMS,
         cost_estimate=cost(2 * rows * 256 * 128 * 6, 4 * rows * 384),
         name="local_z",
-    )(chains, factors, matrix, high, low)
+    )(chains, factors, high, low)
     carried = pl.pallas_call(
-        third_kernel,
+        functools.partial(third_kernel, wy),
         out_shape=array(4, planes, LANES),
         in_specs=[VMEM] * (4 + arrivals),
         out_specs=VMEM,
+        scratch_shapes=[
+            pltpu.VMEM((planes * wy // LANES * 2 * entering_rows + 2 * entering_rows, LANES), jnp.float32),
+            pltpu.VMEM((4 * planes + 8, LANES), jnp.float32),
+        ],
         compiler_params=PARAMS,
         name="carried_y",
-    )(moments, spread_high, spread_low, entering, *received[::-1])
+    )(moments, spread_core, spread_extra, entering, *received[::-1])
     arrived = received
 
     narrow = plan[-1][1] == 2 and len(plan) > 1

time: 25.2 us -> 25.2 us (level)
    pallas_call x3 -> x2, Pallas kernels: 5.45 us -> 4.57 us  [the longest x1 3.74 us: on_device(): pl.pallas_call(functools.partial(first_kernel, ny, nz, partners), out_sha...]
    pallas_call x1, Pallas kernels: 2.24 us -> 3.09 us  [on_device(): pl.pallas_call(functools.partial(second_kernel, ny, nz, count_z, wy, part...]
  transfers between devices with their start and end apart: 7 -> 7, of which waited for: 5 -> 4; matrix products, arithmetic and copies ran while one was open for 0% -> 0% of each run, Pallas kernels for 25% -> 26%
where the time goes in v11:
time: 25.2 us; the launch traced here: 25 us
  Pallas kernels  12.4 us (49%)
  starting transfers between devices  9.33 us (37%)
  waiting for transfers between devices  3.23 us (13%)
    ppermute x7, starting transfers between devices, exchange(): received[k] = lax.ppermute(values[k - 1], axis, pairs)  9.33 us
    pallas_call x1, Pallas kernels, on_device(): pl.pallas_call(functools.partial(first_kernel, ny, nz, partners), out_sha...  3.74 us
    ppermute x7, waiting for transfers between devices, exchange(): received[k] = lax.ppermute(values[k - 1], axis, pairs)  3.23 us
    pallas_call x1, Pallas kernels, on_device(): pl.pallas_call(functools.partial(second_kernel, ny, nz, count_z, wy, part...  3.09 us
    pallas_call x1, Pallas kernels, on_device(): pl.pallas_call(functools.partial(local_y_kernel, wy), out_shape=array(pla...  1.86 us
    pallas_call x1, Pallas kernels, on_device(): pl.pallas_call(functools.partial(y_kernel, count_y, wy), out_shape=[array...  1.42 us
    pallas_call x1, Pallas kernels, on_device(): pl.pallas_call(functools.partial(last_kernel, base, radix, narrow, wy), o...  1.35 us
    pallas_call x1, Pallas kernels, on_device(): pl.pallas_call(functools.partial(third_kernel, wy), out_shape=array(4, pl...  0.83 us
  transfers between devices with their start and end apart: 7, of which 4 were waited for; matrix products, arithmetic and copies ran while one was open for 0% of the time, Pallas kernels for 26%

profile of v11, /device:TPU:0, one launch (start us, length us, event | category | flops | bytes accessed | tf_op | source)
XLA Modules:
  0.0 25.0 jit_solution(188843211517162047)
XLA Ops:
  0.0 3.7 %forcing_and_factor.1 = (bf16[2880,256]{1,0:T(8,128)(2,1)S(1)}, bf16[2880,256]{1,0:T(8,128)(2,1)S(1)}, f32[28,8,128]{2,1,0:T(8,128)S(1)}, f32[8,8,128]{2,1,0:T(8...) custom-call(f32[5,8,64,128]{3,2,1,0:T(8,128)} %flow_hbm.1, ...), custom_call_target="tpu_custom_call" | custom-call | tf_op jit(solution)/shard_map/forcing_and_factor/pallas_call | solution.py:768
  3.7 2.4 %collective-permute-start = (f32[2,2880]{1,0:T(2,128)S(1)}, f32[2,2880]{1,0:T(2,128)S(1)}, u32[]{:S(2)}, u32[]{:S(2)}) collective-permute-start(f32[2,2880]{1,0:T(2,128)S(1)} %get-tuple-element.29), channel_id=1, source_target_pairs={{0,24},{8,16},{16,8},{24,0},{1,25},{9,17},{17,9},{25,1},{2,26},{10... | collective-permute-start | bytes 69128 | tf_op jit(solution)/shard_map/ppermute | solution.py:790
  6.2 0.6 %collective-permute-start.1 = (f32[2,2880]{1,0:T(2,128)S(1)}, f32[2,2880]{1,0:T(2,128)S(1)}, u32[]{:S(2)}, u32[]{:S(2)}) collective-permute-start(f32[2,2880]{1,0:T(2,128)S(1)} %get-tuple-element.30), channel_id=1, source_target_pairs={{0,16},{8,24},{16,0},{24,8},{1,17},{9,25},{17,1},{25,9},{2,18},{10... | collective-permute-start | bytes 69128 | tf_op jit(solution)/shard_map/ppermute | solution.py:790
  6.8 0.0 collective-permute-start.2
  6.9 3.1 %local_z.1 = (f32[2880,128]{1,0:T(8,128)S(1)}, f32[168,128]{1,0:T(8,128)S(1)}, f32[24,128]{1,0:T(8,128)S(1)}, f32[8,128]{1,0:T(8,128)S(1)}, f32[64,128]{1,0:T(8,128)S(1)}) custom-call(f32[8,8,128]{2,1,0:T(8,128)S(1)} %get-tuple-element.21.chains, f32[28,8,128]{2,1,0:T(8,128)S(1)} %get-tuple-element.22.factors, bf16[2880,256]{1,0:T(8,128)(2,1)S(1)} %get-tuple-element.23.high, ...), custom_call_target="tpu_custom_call" | custom-call | flops 1132462080 | bytes 4423680 | tf_op jit(solution)/shard_map/local_z/pallas_call | solution.py:796
  10.0 0.0 collective-permute-done.refs_0_.refs_2_
  10.0 0.0 collective-permute-done.1.refs_1_
  10.0 0.0 collective-permute-done.2.refs_2_.refs_0_
  10.0 0.8 %carried_y.1.unused.refs_0_ = f32[4,40,128]{2,1,0:T(8,128)S(1)} custom-call(f32[168,128]{1,0:T(8,128)S(1)} %get-tuple-element.25.moments, f32[8,128]{1,0:T(8,128)S(1)} %get-tuple-element.26.spread_core, f32[64,128]{1,0:T(8,128)S(1)} %get-tuple-element.27.spread_extra, f32[24,128]{1,0:T(8,128)S(1)} %get-tuple-element.28.entering, ...), custom_call_target="tpu_custom_call" | custom-call | tf_op jit(solution)/shard_map/carried_y/pallas_call | solution.py:817
  10.8 2.8 %collective-permute-start.5 = (f32[4,40,128]{2,1,0:T(8,128)S(1)}, f32[4,40,128]{2,1,0:T(8,128)S(1)}, u32[]{:S(2)}, u32[]{:S(2)}) collective-permute-start(f32[4,40,128]{2,1,0:T(8,128)S(1)} %carried_y.1.unused.refs_0_), channel_id=1, source_target_pairs={{0,3},{1,2},{2,1},{3,0},{4,7},{5,6},{6,5},{7,4},{8,11},{9,10},{10,... | collective-permute-start | bytes 245768 | tf_op jit(solution)/shard_map/ppermute | solution.py:790
  13.7 0.5 %collective-permute-start.4 = (f32[4,40,128]{2,1,0:T(8,128)S(1)}, f32[4,40,128]{2,1,0:T(8,128)S(1)}, u32[]{:S(2)}, u32[]{:S(2)}) collective-permute-start(f32[4,40,128]{2,1,0:T(8,128)S(1)} %carried_y.1.unused.refs_0_), channel_id=1, source_target_pairs={{0,2},{1,3},{2,0},{3,1},{4,6},{5,7},{6,4},{7,5},{8,10},{9,11},{10,... | collective-permute-start | bytes 245768 | tf_op jit(solution)/shard_map/ppermute | solution.py:790
  14.1 0.3 %collective-permute-start.3 = (f32[4,40,128]{2,1,0:T(8,128)S(1)}, f32[4,40,128]{2,1,0:T(8,128)S(1)}, u32[]{:S(2)}, u32[]{:S(2)}) collective-permute-start(f32[4,40,128]{2,1,0:T(8,128)S(1)} %carried_y.1.unused.refs_0_), channel_id=1, source_target_pairs={{0,1},{1,0},{2,3},{3,2},{4,5},{5,4},{6,7},{7,6},{8,9},{9,8},{10,11... | collective-permute-start | bytes 245768 | tf_op jit(solution)/shard_map/ppermute | solution.py:790
  14.4 1.4 %inverse_y.1 = (f32[64,128]{1,0:T(8,128)S(1)}, f32[8,8,128]{2,1,0:T(8,128)S(1)}) custom-call(f32[8,8,128]{2,1,0:T(8,128)S(1)} %get-tuple-element.21.chains, f32[28,8,128]{2,1,0:T(8,128)S(1)} %get-tuple-element.22.factors, f32[4,40,128]{2,1,0:T(8,128)S(1)} %carried_y.1.unused.refs_0_), custom_call_target="tpu_custom_call" | custom-call | flops 566231040 | bytes 2949120 | tf_op jit(solution)/shard_map/inverse_y/pallas_call | solution.py:837
  15.8 1.2 %collective-permute-done.5.refs_3_ = f32[4,40,128]{2,1,0:T(8,128)S(1)} collective-permute-done((f32[4,40,128]{2,1,0:T(8,128)S(1)}, f32[4,40,128]{2,1,0:T(8,128)S(1)}, u32[]{:S(2)}, u32[]{:S(2)}) %collective-permute-start.5) | collective-permute-done | bytes 81952 | tf_op jit(solution)/shard_map/ppermute | solution.py:790
  17.1 1.4 %collective-permute-done.4.refs_2_ = f32[4,40,128]{2,1,0:T(8,128)S(1)} collective-permute-done((f32[4,40,128]{2,1,0:T(8,128)S(1)}, f32[4,40,128]{2,1,0:T(8,128)S(1)}, u32[]{:S(2)}, u32[]{:S(2)}) %collective-permute-start.4) | collective-permute-done | bytes 81952 | tf_op jit(solution)/shard_map/ppermute | solution.py:790
  18.4 0.1 collective-permute-done.3.refs_1_
  18.6 0.1 join_groups.1
  18.7 2.7 %collective-permute-start.6 = (f32[2,40,128]{2,1,0:T(8,128)S(1)}, f32[2,40,128]{2,1,0:T(8,128)S(1)}, u32[]{:S(2)}, u32[]{:S(2)}) collective-permute-start(f32[2,40,128]{2,1,0:T(8,128)S(1)} %get-tuple-element.36), channel_id=1, source_target_pairs={{0,4},{1,5},{2,6},{3,7},{4,0},{5,1},{6,2},{7,3},{8,12},{9,13},{10,... | collective-permute-start | bytes 122888 | tf_op jit(solution)/shard_map/ppermute | solution.py:790
  21.3 1.9 %local_y.1.local = f32[40,64,128]{2,1,0:T(8,128)S(1)} custom-call(f32[2880,128]{1,0:T(8,128)S(1)} %get-tuple-element.33.local, f32[24,128]{1,0:T(8,128)S(1)} %get-tuple-element.28.entering, f32[64,128]{1,0:T(8,128)S(1)} %get-tuple-element.34.inverse_y, f32[4,40,128]{2,1,0:T(8,128)S(1)} %get-tuple-element.35.unused.entered, ...), custom_call_target="tpu_custom_call" | custom-call | flops 566231040 | bytes 2949120 | tf_op jit(solution)/shard_map/local_y/pallas_call | solution.py:860
  23.2 0.4 %collective-permute-done.6.refs_0_ = f32[2,40,128]{2,1,0:T(8,128)S(1)} collective-permute-done((f32[2,40,128]{2,1,0:T(8,128)S(1)}, f32[2,40,128]{2,1,0:T(8,128)S(1)}, u32[]{:S(2)}, u32[]{:S(2)}) %collective-permute-start.6) | collective-permute-done | bytes 40992 | tf_op jit(solution)/shard_map/ppermute | solution.py:790
  23.6 1.4 %finish_y.1 = f32[5,8,64,128]{3,2,1,0:T(8,128)} custom-call(f32[8,8,128]{2,1,0:T(8,128)S(1)} %get-tuple-element.32.coefs, f32[40,64,128]{2,1,0:T(8,128)S(1)} %local_y.1.local, f32[64,128]{1,0:T(8,128)S(1)} %get-tuple-element.34.inverse_y, f32[4,40,128]{2,1,0:T(8,128)S(1)} %get-tuple-element.35.unused.entered, f32[2,40,128]{2,1,0:T(8,128)S(1)} %collective-permute-done.6.refs_0_), custom_call_target="tpu_custom_call" | custom-call | tf_op jit(solution)/shard_map/finish_y/pallas_call | solution.py:871
Async XLA Ops:
  3.7 6.2 %collective-permute-start = (f32[2,2880]{1,0:T(2,128)S(1)}, f32[2,2880]{1,0:T(2,128)S(1)}, u32[]{:S(2)}, u32[]{:S(2)}) collective-permute-start(f32[2,2880]{1,0:T(2,128)S(1)} %get-tuple-element.29), channel_id=1, source_target_pairs={{0,24},{8,16},{16,8},{24,0},{1,25},{9,17},{17,9},{25,1},{2,26},{10... | collective-permute-start | bytes 69128 | tf_op jit(solution)/shard_map/ppermute | solution.py:790
  6.2 3.8 %collective-permute-start.1 = (f32[2,2880]{1,0:T(2,128)S(1)}, f32[2,2880]{1,0:T(2,128)S(1)}, u32[]{:S(2)}, u32[]{:S(2)}) collective-permute-start(f32[2,2880]{1,0:T(2,128)S(1)} %get-tuple-element.30), channel_id=1, source_target_pairs={{0,16},{8,24},{16,0},{24,8},{1,17},{9,25},{17,1},{25,9},{2,18},{10... | collective-permute-start | bytes 69128 | tf_op jit(solution)/shard_map/ppermute | solution.py:790
  6.8 3.2 %collective-permute-start.2 = (f32[2,2880]{1,0:T(2,128)S(1)}, f32[2,2880]{1,0:T(2,128)S(1)}, u32[]{:S(2)}, u32[]{:S(2)}) collective-permute-start(f32[2,2880]{1,0:T(2,128)S(1)} %get-tuple-element.31), channel_id=1, source_target_pairs={{0,8},{8,0},{16,24},{24,16},{1,9},{9,1},{17,25},{25,17},{2,10},{10... | collective-permute-start | bytes 69128 | tf_op jit(solution)/shard_map/ppermute | solution.py:790
  10.8 6.2 %collective-permute-start.5 = (f32[4,40,128]{2,1,0:T(8,128)S(1)}, f32[4,40,128]{2,1,0:T(8,128)S(1)}, u32[]{:S(2)}, u32[]{:S(2)}) collective-permute-start(f32[4,40,128]{2,1,0:T(8,128)S(1)} %carried_y.1.unused.refs_0_), channel_id=1, source_target_pairs={{0,3},{1,2},{2,1},{3,0},{4,7},{5,6},{6,5},{7,4},{8,11},{9,10},{10,... | collective-permute-start | bytes 245768 | tf_op jit(solution)/shard_map/ppermute | solution.py:790
  13.7 4.7 %collective-permute-start.4 = (f32[4,40,128]{2,1,0:T(8,128)S(1)}, f32[4,40,128]{2,1,0:T(8,128)S(1)}, u32[]{:S(2)}, u32[]{:S(2)}) collective-permute-start(f32[4,40,128]{2,1,0:T(8,128)S(1)} %carried_y.1.unused.refs_0_), channel_id=1, source_target_pairs={{0,2},{1,3},{2,0},{3,1},{4,6},{5,7},{6,4},{7,5},{8,10},{9,11},{10,... | collective-permute-start | bytes 245768 | tf_op jit(solution)/shard_map/ppermute | solution.py:790
  14.1 4.4 %collective-permute-start.3 = (f32[4,40,128]{2,1,0:T(8,128)S(1)}, f32[4,40,128]{2,1,0:T(8,128)S(1)}, u32[]{:S(2)}, u32[]{:S(2)}) collective-permute-start(f32[4,40,128]{2,1,0:T(8,128)S(1)} %carried_y.1.unused.refs_0_), channel_id=1, source_target_pairs={{0,1},{1,0},{2,3},{3,2},{4,5},{5,4},{6,7},{7,6},{8,9},{9,8},{10,11... | collective-permute-start | bytes 245768 | tf_op jit(solution)/shard_map/ppermute | solution.py:790
  18.7 5.0 %collective-permute-start.6 = (f32[2,40,128]{2,1,0:T(8,128)S(1)}, f32[2,40,128]{2,1,0:T(8,128)S(1)}, u32[]{:S(2)}, u32[]{:S(2)}) collective-permute-start(f32[2,40,128]{2,1,0:T(8,128)S(1)} %get-tuple-element.36), channel_id=1, source_target_pairs={{0,4},{1,5},{2,6},{3,7},{4,0},{5,1},{6,2},{7,3},{8,12},{9,13},{10,... | collective-permute-start | bytes 122888 | tf_op jit(solution)/shard_map/ppermute | solution.py:790

commit v12 on v11

--- a/solution.py
+++ b/solution.py
@@ -160,9 +160,9 @@
 
 
 def first_kernel(ny, nz, partners, flow_hbm, speed_hbm, metric_y, metric_z, *refs):
-    high, low, factors, chains = refs[:4]
-    messages = refs[4 : 4 + partners]
-    flow, speed, metric, spread, arrived = refs[4 + partners :]
+    high, low, factors = refs[:3]
+    messages = refs[3 : 3 + partners]
+    flow, speed, metric, spread, arrived = refs[3 + partners :]
     fields, planes_x, wy, _ = flow.shape
     rows = ny + nz
     core_rows = fields * planes_x * wy
@@ -251,8 +251,6 @@
     from_right, from_left, diagonal, to_right, to_left, before, after = parts
     for number, value in enumerate(v for part in parts for v in part):
         factors[number] = value
-    for number, value in enumerate(to_right + to_left):
-        chains[number] = value
     for field in range(fields // 2, fields):
         one_field(field)
 
@@ -392,7 +390,7 @@
     return jnp.concatenate(rows, axis=0).T
 
 
-def chain_products(chains, number, place, blocks, begins, ends, masks, reverse):
+def chain_products(factors, number, place, blocks, begins, ends, masks, reverse):
     count = -(-len(begins) // 8) * 8
     row = lax.broadcasted_iota(jnp.int32, (count, LANES), 0)
     begin = jnp.zeros((count, LANES), jnp.int32)
@@ -404,7 +402,8 @@
     product = (one, zero, zero, one)
     for block in range(blocks - 1, -1, -1) if reverse else range(blocks):
         where = place(block)
-        value = tuple(chains[number + k, where[0], where[1]] for k in range(4))
+        at = (slice(where[0], where[0] + 1), slice(where[1], where[1] + 1))
+        value = tuple(factors[(number + k, *at)] for k in range(4))
         product = pick((begin <= block) & (block < end), mm(product, value), product)
     return tuple(x * mask for x in product)
 
@@ -414,7 +413,7 @@
 
 
 def second_kernel(
-    ny, nz, count_z, wy, partners, chains, factors, high, low, local, moments, entering, spread_core, spread_extra, *scratch
+    ny, nz, count_z, wy, partners, factors, high, low, local, moments, entering, spread_core, spread_extra, *scratch
 ):
     columns, stacked, rows_ref, matrix, weights_y = scratch
     planes = (moments.shape[0] - 8) // 4
@@ -480,10 +479,10 @@
     lowers = [other < me_z for other in others]
     size = len(begins)
     up = chain_products(
-        chains, 0, lambda b: (ny + b, 0), count_z, begins, [me_z] * size, [1.0] * size, False
+        factors, 12, lambda b: (ny + b, 0), count_z, begins, [me_z] * size, [1.0] * size, False
     )
     down = chain_products(
-        chains, 4, lambda b: (ny + b, LANES - 1), count_z, [me_z + 1] * size, ends, [1.0] * size, True
+        factors, 16, lambda b: (ny + b, LANES - 1), count_z, [me_z + 1] * size, ends, [1.0] * size, True
     )
     stack = []
     for k, lower in enumerate(lowers):
@@ -546,7 +545,7 @@
             moments[start : start + 8, :] = jnp.concatenate(lines, axis=0)
 
 
-def y_kernel(count_y, wy, chains, factors, unused, inverse_y, coefs, columns, stacked):
+def y_kernel(count_y, wy, factors, unused, inverse_y, coefs, columns, stacked):
     me_y = lax.axis_index("gy")
     cell = me_y * wy
     columns[0:LANES, 0:32] = transposed(factors, cell // LANES)
@@ -582,8 +581,8 @@
         return place(block)[0], place(block)[1] + wy - 1
 
     for base, value in (
-        (0, chain_products(chains, 0, place, count_y, *up, False)),
-        (4, chain_products(chains, 4, place_end, count_y, *down, True)),
+        (0, chain_products(factors, 12, place, count_y, *up, False)),
+        (4, chain_products(factors, 16, place_end, count_y, *down, True)),
     ):
         for k in range(4):
             coefs[base + k] = value[k]
@@ -634,6 +633,9 @@
     stack, number = chunks(planes * wy, planes * (wy + EXTRA))
     top, rest = halves(spread_extra[...])
     corner = matmul(top, stack, across) + matmul(rest, stack, across)
+    spare = jnp.zeros((corner.shape[0], -corner.shape[1] % LANES), jnp.float32)
+    corner = jnp.concatenate([corner, spare], axis=1)
+    corner = corner + pltpu.roll(corner, corner.shape[1] - count, 1)
     for m in range(4):
         for chunk in range(number):
             size = min(per, planes - chunk * per)
@@ -642,8 +644,7 @@
             for r in range(used):
                 lane = chunk * 2 * count + r
                 part = corner[m * per : m * per + size]
-                column = part[:, lane : lane + 1] + part[:, lane + count : lane + count + 1]
-                value = value + column * values[r : r + 1]
+                value = value + part[:, lane : lane + 1] * values[r : r + 1]
             carried[m, rows, :] = value
 
 
@@ -738,7 +739,6 @@
 
 VMEM = pl.BlockSpec(memory_space=pltpu.VMEM)
 HBM = pl.BlockSpec(memory_space=pltpu.HBM)
-SMEM = pl.BlockSpec(memory_space=pltpu.SMEM)
 PARAMS = pltpu.CompilerParams(vmem_limit_bytes=40 * 1024 * 1024)
 
 
@@ -767,10 +767,10 @@
     half = jax.ShapeDtypeStruct((rows, 2 * LANES), jnp.bfloat16)
     outputs = pl.pallas_call(
         functools.partial(first_kernel, ny, nz, partners),
-        out_shape=[half, half, array(28, ny + nz, LANES), array(8, ny + nz, LANES)]
+        out_shape=[half, half, array(28, ny + nz, LANES)]
         + [array(2, rows)] * partners,
         in_specs=[HBM] * 4,
-        out_specs=[VMEM] * (4 + partners),
+        out_specs=[VMEM] * (3 + partners),
         scratch_shapes=[
             pltpu.VMEM(flow.shape, jnp.float32),
             pltpu.VMEM(speed.shape, jnp.float32),
@@ -781,7 +781,7 @@
         compiler_params=PARAMS,
         name="forcing_and_factor",
     )(*(in_hbm(x) for x in (flow, speed, metric_y.reshape(ny, LANES), metric_z.reshape(nz, LANES))))
-    high, low, factors, chains = outputs[:4]
+    high, low, factors = outputs[:3]
 
     def exchange(values, axis, count, stride, radix):
         received = {}
@@ -792,7 +792,7 @@
 
     plan = stage_plan(count_y)
     work = [pltpu.VMEM((LANES + 16, LANES), jnp.float32)] * 2
-    received = exchange(outputs[4:], "gz", count_z, 1, count_z)
+    received = exchange(outputs[3:], "gz", count_z, 1, count_z)
     local, moments, entering, spread_core, spread_extra = pl.pallas_call(
         functools.partial(second_kernel, ny, nz, count_z, wy, partners),
         out_shape=[
@@ -802,7 +802,7 @@
             array(4 * (LANES // wy), LANES),
             array(4 * (LANES // EXTRA), LANES),
         ],
-        in_specs=[SMEM] + [VMEM] * 3,
+        in_specs=[VMEM] * 3,
         out_specs=[VMEM] * 5,
         scratch_shapes=work
         + [
@@ -813,7 +813,7 @@
         compiler_params=PARAMS,
         cost_estimate=cost(2 * rows * 256 * 128 * 6, 4 * rows * 384),
         name="local_z",
-    )(chains, factors, high, low)
+    )(factors, high, low)
     carried = pl.pallas_call(
         functools.partial(third_kernel, wy),
         out_shape=array(4, planes, LANES),
@@ -837,13 +837,13 @@
             inverse_y, coefs = pl.pallas_call(
                 functools.partial(y_kernel, count_y, wy),
                 out_shape=[array(wy, LANES), array(8, -(-entries // 8) * 8, LANES)],
-                in_specs=[SMEM, VMEM, HBM],
+                in_specs=[VMEM, HBM],
                 out_specs=[VMEM] * 2,
                 scratch_shapes=work,
                 compiler_params=PARAMS,
                 cost_estimate=cost(2 * rows * 128 * 128 * 6, 4 * rows * 256),
                 name="inverse_y",
-            )(chains, factors, carried)
+            )(factors, carried)
         if number + 1 < len(plan):
             slim = narrow and number + 2 == len(plan)
             inputs = [carried] + received + ([entered] if entered is not None else [])

time: 25.2 us -> 24.7 us (0.980)
  Pallas kernels: 12.4 us -> 10.1 us
  waiting for transfers between devices: 3.23 us -> 5.11 us
    ppermute x7, waiting for transfers between devices: 3.23 us -> 5.11 us  [exchange(): received[k] = lax.ppermute(values[k - 1], axis, pairs)]
    pallas_call x1, Pallas kernels: 3.09 us -> 1.97 us  [on_device(): pl.pallas_call(functools.partial(second_kernel, ny, nz, count_z, wy, part...]
    pallas_call x1, Pallas kernels: 1.42 us -> 0.43 us  [on_device(): pl.pallas_call(functools.partial(y_kernel, count_y, wy), out_shape=[array...]
  transfers between devices with their start and end apart: 7 -> 7, of which waited for: 4 -> 5; matrix products, arithmetic and copies ran while one was open for 0% -> 0% of each run, Pallas kernels for 26% -> 17%
where the time goes in v12:
time: 24.7 us; the launch traced here: 24.5 us
  Pallas kernels  10.1 us (41%)
  starting transfers between devices  9.33 us (38%)
  waiting for transfers between devices  5.11 us (21%)
    ppermute x7, starting transfers between devices, exchange(): received[k] = lax.ppermute(values[k - 1], axis, pairs)  9.33 us
    ppermute x7, waiting for transfers between devices, exchange(): received[k] = lax.ppermute(values[k - 1], axis, pairs)  5.11 us
    pallas_call x1, Pallas kernels, on_device(): pl.pallas_call(functools.partial(first_kernel, ny, nz, partners), out_sha...  3.74 us
    pallas_call x1, Pallas kernels, on_device(): pl.pallas_call(functools.partial(second_kernel, ny, nz, count_z, wy, part...  1.97 us
    pallas_call x1, Pallas kernels, on_device(): pl.pallas_call(functools.partial(local_y_kernel, wy), out_shape=array(pla...  1.86 us
    pallas_call x1, Pallas kernels, on_device(): pl.pallas_call(functools.partial(last_kernel, base, radix, narrow, wy), o...  1.35 us
    pallas_call x1, Pallas kernels, on_device(): pl.pallas_call(functools.partial(third_kernel, wy), out_shape=array(4, pl...  0.63 us
  transfers between devices with their start and end apart: 7, of which 5 were waited for; matrix products, arithmetic and copies ran while one was open for 0% of the time, Pallas kernels for 17%

profile of v12, /device:TPU:0, one launch (start us, length us, event | category | flops | bytes accessed | tf_op | source)
XLA Modules:
  0.0 24.5 jit_solution(908558415815175644)
XLA Ops:
  0.0 3.7 %forcing_and_factor.1 = (bf16[2880,256]{1,0:T(8,128)(2,1)S(1)}, bf16[2880,256]{1,0:T(8,128)(2,1)S(1)}, f32[28,8,128]{2,1,0:T(8,128)S(1)}, f32[2,2880]{1,0:T(2,12...) custom-call(f32[5,8,64,128]{3,2,1,0:T(8,128)} %flow_hbm.1, f32[8,64,128]{2,1,0:T(8,128)} %speed_hbm.1, ...), custom_call_target="tpu_custom_call" | custom-call | tf_op jit(solution)/shard_map/forcing_and_factor/pallas_call | solution.py:768
  3.7 2.4 %collective-permute-start = (f32[2,2880]{1,0:T(2,128)S(1)}, f32[2,2880]{1,0:T(2,128)S(1)}, u32[]{:S(2)}, u32[]{:S(2)}) collective-permute-start(f32[2,2880]{1,0:T(2,128)S(1)} %get-tuple-element.27), channel_id=1, source_target_pairs={{0,24},{8,16},{16,8},{24,0},{1,25},{9,17},{17,9},{25,1},{2,26},{10... | collective-permute-start | bytes 69128 | tf_op jit(solution)/shard_map/ppermute | solution.py:790
  6.2 0.6 %collective-permute-start.1 = (f32[2,2880]{1,0:T(2,128)S(1)}, f32[2,2880]{1,0:T(2,128)S(1)}, u32[]{:S(2)}, u32[]{:S(2)}) collective-permute-start(f32[2,2880]{1,0:T(2,128)S(1)} %get-tuple-element.28), channel_id=1, source_target_pairs={{0,16},{8,24},{16,0},{24,8},{1,17},{9,25},{17,1},{25,9},{2,18},{10... | collective-permute-start | bytes 69128 | tf_op jit(solution)/shard_map/ppermute | solution.py:790
  6.8 0.0 collective-permute-start.2
  6.9 2.0 %local_z.1 = (f32[2880,128]{1,0:T(8,128)S(1)}, f32[168,128]{1,0:T(8,128)S(1)}, f32[24,128]{1,0:T(8,128)S(1)}, f32[8,128]{1,0:T(8,128)S(1)}, f32[64,128]{1,0:T(8,128)S(1)}) custom-call(f32[28,8,128]{2,1,0:T(8,128)S(1)} %get-tuple-element.20.factors, bf16[2880,256]{1,0:T(8,128)(2,1)S(1)} %get-tuple-element.21.high, bf16[2880,256]{1,0:T(8,128)(2,1)S(1)} %get-tuple-element.22.low), custom_call_target="tpu_custom_call" | custom-call | flops 1132462080 | bytes 4423680 | tf_op jit(solution)/shard_map/local_z/pallas_call | solution.py:796
  8.8 0.0 collective-permute-done.refs_0_.refs_2_
  8.9 1.2 %collective-permute-done.1.refs_1_ = f32[2,2880]{1,0:T(2,128)S(1)} collective-permute-done((f32[2,2880]{1,0:T(2,128)S(1)}, f32[2,2880]{1,0:T(2,128)S(1)}, u32[]{:S(2)}, u32[]{:S(2)}) %collective-permute-start.1) | collective-permute-done | bytes 23072 | tf_op jit(solution)/shard_map/ppermute | solution.py:790
  10.0 0.0 collective-permute-done.2.refs_2_.refs_0_
  10.0 0.6 %carried_y.1.unused.refs_0_ = f32[4,40,128]{2,1,0:T(8,128)S(1)} custom-call(f32[168,128]{1,0:T(8,128)S(1)} %get-tuple-element.23.moments, f32[8,128]{1,0:T(8,128)S(1)} %get-tuple-element.24.spread_core, f32[64,128]{1,0:T(8,128)S(1)} %get-tuple-element.25.spread_extra, f32[24,128]{1,0:T(8,128)S(1)} %get-tuple-element.26.entering, ...), custom_call_target="tpu_custom_call" | custom-call | tf_op jit(solution)/shard_map/carried_y/pallas_call | solution.py:817
  10.6 2.6 %collective-permute-start.5 = (f32[4,40,128]{2,1,0:T(8,128)S(1)}, f32[4,40,128]{2,1,0:T(8,128)S(1)}, u32[]{:S(2)}, u32[]{:S(2)}) collective-permute-start(f32[4,40,128]{2,1,0:T(8,128)S(1)} %carried_y.1.unused.refs_0_), channel_id=1, source_target_pairs={{0,3},{1,2},{2,1},{3,0},{4,7},{5,6},{6,5},{7,4},{8,11},{9,10},{10,... | collective-permute-start | bytes 245768 | tf_op jit(solution)/shard_map/ppermute | solution.py:790
  13.2 0.4 %collective-permute-start.4 = (f32[4,40,128]{2,1,0:T(8,128)S(1)}, f32[4,40,128]{2,1,0:T(8,128)S(1)}, u32[]{:S(2)}, u32[]{:S(2)}) collective-permute-start(f32[4,40,128]{2,1,0:T(8,128)S(1)} %carried_y.1.unused.refs_0_), channel_id=1, source_target_pairs={{0,2},{1,3},{2,0},{3,1},{4,6},{5,7},{6,4},{7,5},{8,10},{9,11},{10,... | collective-permute-start | bytes 245768 | tf_op jit(solution)/shard_map/ppermute | solution.py:790
  13.7 0.5 %collective-permute-start.3 = (f32[4,40,128]{2,1,0:T(8,128)S(1)}, f32[4,40,128]{2,1,0:T(8,128)S(1)}, u32[]{:S(2)}, u32[]{:S(2)}) collective-permute-start(f32[4,40,128]{2,1,0:T(8,128)S(1)} %carried_y.1.unused.refs_0_), channel_id=1, source_target_pairs={{0,1},{1,0},{2,3},{3,2},{4,5},{5,4},{6,7},{7,6},{8,9},{9,8},{10,11... | collective-permute-start | bytes 245768 | tf_op jit(solution)/shard_map/ppermute | solution.py:790
  14.2 0.4 %inverse_y.1 = (f32[64,128]{1,0:T(8,128)S(1)}, f32[8,8,128]{2,1,0:T(8,128)S(1)}) custom-call(f32[28,8,128]{2,1,0:T(8,128)S(1)} %get-tuple-element.20.factors, f32[4,40,128]{2,1,0:T(8,128)S(1)} %carried_y.1.unused.refs_0_), custom_call_target="tpu_custom_call" | custom-call | flops 566231040 | bytes 2949120 | tf_op jit(solution)/shard_map/inverse_y/pallas_call | solution.py:837
  14.6 2.2 %collective-permute-done.5.refs_3_ = f32[4,40,128]{2,1,0:T(8,128)S(1)} collective-permute-done((f32[4,40,128]{2,1,0:T(8,128)S(1)}, f32[4,40,128]{2,1,0:T(8,128)S(1)}, u32[]{:S(2)}, u32[]{:S(2)}) %collective-permute-start.5) | collective-permute-done | bytes 81952 | tf_op jit(solution)/shard_map/ppermute | solution.py:790
  16.9 0.8 %collective-permute-done.4.refs_2_ = f32[4,40,128]{2,1,0:T(8,128)S(1)} collective-permute-done((f32[4,40,128]{2,1,0:T(8,128)S(1)}, f32[4,40,128]{2,1,0:T(8,128)S(1)}, u32[]{:S(2)}, u32[]{:S(2)}) %collective-permute-start.4) | collective-permute-done | bytes 81952 | tf_op jit(solution)/shard_map/ppermute | solution.py:790
  17.7 0.4 %collective-permute-done.3.refs_1_ = f32[4,40,128]{2,1,0:T(8,128)S(1)} collective-permute-done((f32[4,40,128]{2,1,0:T(8,128)S(1)}, f32[4,40,128]{2,1,0:T(8,128)S(1)}, u32[]{:S(2)}, u32[]{:S(2)}) %collective-permute-start.3) | collective-permute-done | bytes 81952 | tf_op jit(solution)/shard_map/ppermute | solution.py:790
  18.1 0.1 join_groups.1
  18.2 2.7 %collective-permute-start.6 = (f32[2,40,128]{2,1,0:T(8,128)S(1)}, f32[2,40,128]{2,1,0:T(8,128)S(1)}, u32[]{:S(2)}, u32[]{:S(2)}) collective-permute-start(f32[2,40,128]{2,1,0:T(8,128)S(1)} %get-tuple-element.34), channel_id=1, source_target_pairs={{0,4},{1,5},{2,6},{3,7},{4,0},{5,1},{6,2},{7,3},{8,12},{9,13},{10,... | collective-permute-start | bytes 122888 | tf_op jit(solution)/shard_map/ppermute | solution.py:790
  20.9 1.9 %local_y.1.local = f32[40,64,128]{2,1,0:T(8,128)S(1)} custom-call(f32[2880,128]{1,0:T(8,128)S(1)} %get-tuple-element.31.local, f32[24,128]{1,0:T(8,128)S(1)} %get-tuple-element.26.entering, f32[64,128]{1,0:T(8,128)S(1)} %get-tuple-element.32.inverse_y, f32[4,40,128]{2,1,0:T(8,128)S(1)} %get-tuple-element.33.unused.entered, ...), custom_call_target="tpu_custom_call" | custom-call | flops 566231040 | bytes 2949120 | tf_op jit(solution)/shard_map/local_y/pallas_call | solution.py:860
  22.7 0.5 %collective-permute-done.6.refs_0_ = f32[2,40,128]{2,1,0:T(8,128)S(1)} collective-permute-done((f32[2,40,128]{2,1,0:T(8,128)S(1)}, f32[2,40,128]{2,1,0:T(8,128)S(1)}, u32[]{:S(2)}, u32[]{:S(2)}) %collective-permute-start.6) | collective-permute-done | bytes 40992 | tf_op jit(solution)/shard_map/ppermute | solution.py:790
  23.2 1.4 %finish_y.1 = f32[5,8,64,128]{3,2,1,0:T(8,128)} custom-call(f32[8,8,128]{2,1,0:T(8,128)S(1)} %get-tuple-element.30.coefs, f32[40,64,128]{2,1,0:T(8,128)S(1)} %local_y.1.local, f32[64,128]{1,0:T(8,128)S(1)} %get-tuple-element.32.inverse_y, f32[4,40,128]{2,1,0:T(8,128)S(1)} %get-tuple-element.33.unused.entered, f32[2,40,128]{2,1,0:T(8,128)S(1)} %collective-permute-done.6.refs_0_), custom_call_target="tpu_custom_call" | custom-call | tf_op jit(solution)/shard_map/finish_y/pallas_call | solution.py:871
Async XLA Ops:
  3.7 5.1 %collective-permute-start = (f32[2,2880]{1,0:T(2,128)S(1)}, f32[2,2880]{1,0:T(2,128)S(1)}, u32[]{:S(2)}, u32[]{:S(2)}) collective-permute-start(f32[2,2880]{1,0:T(2,128)S(1)} %get-tuple-element.27), channel_id=1, source_target_pairs={{0,24},{8,16},{16,8},{24,0},{1,25},{9,17},{17,9},{25,1},{2,26},{10... | collective-permute-start | bytes 69128 | tf_op jit(solution)/shard_map/ppermute | solution.py:790
  6.2 3.8 %collective-permute-start.1 = (f32[2,2880]{1,0:T(2,128)S(1)}, f32[2,2880]{1,0:T(2,128)S(1)}, u32[]{:S(2)}, u32[]{:S(2)}) collective-permute-start(f32[2,2880]{1,0:T(2,128)S(1)} %get-tuple-element.28), channel_id=1, source_target_pairs={{0,16},{8,24},{16,0},{24,8},{1,17},{9,25},{17,1},{25,9},{2,18},{10... | collective-permute-start | bytes 69128 | tf_op jit(solution)/shard_map/ppermute | solution.py:790
  6.8 3.2 %collective-permute-start.2 = (f32[2,2880]{1,0:T(2,128)S(1)}, f32[2,2880]{1,0:T(2,128)S(1)}, u32[]{:S(2)}, u32[]{:S(2)}) collective-permute-start(f32[2,2880]{1,0:T(2,128)S(1)} %get-tuple-element.29), channel_id=1, source_target_pairs={{0,8},{8,0},{16,24},{24,16},{1,9},{9,1},{17,25},{25,17},{2,10},{10... | collective-permute-start | bytes 69128 | tf_op jit(solution)/shard_map/ppermute | solution.py:790
  10.6 6.2 %collective-permute-start.5 = (f32[4,40,128]{2,1,0:T(8,128)S(1)}, f32[4,40,128]{2,1,0:T(8,128)S(1)}, u32[]{:S(2)}, u32[]{:S(2)}) collective-permute-start(f32[4,40,128]{2,1,0:T(8,128)S(1)} %carried_y.1.unused.refs_0_), channel_id=1, source_target_pairs={{0,3},{1,2},{2,1},{3,0},{4,7},{5,6},{6,5},{7,4},{8,11},{9,10},{10,... | collective-permute-start | bytes 245768 | tf_op jit(solution)/shard_map/ppermute | solution.py:790
  13.2 4.5 %collective-permute-start.4 = (f32[4,40,128]{2,1,0:T(8,128)S(1)}, f32[4,40,128]{2,1,0:T(8,128)S(1)}, u32[]{:S(2)}, u32[]{:S(2)}) collective-permute-start(f32[4,40,128]{2,1,0:T(8,128)S(1)} %carried_y.1.unused.refs_0_), channel_id=1, source_target_pairs={{0,2},{1,3},{2,0},{3,1},{4,6},{5,7},{6,4},{7,5},{8,10},{9,11},{10,... | collective-permute-start | bytes 245768 | tf_op jit(solution)/shard_map/ppermute | solution.py:790
  13.7 4.4 %collective-permute-start.3 = (f32[4,40,128]{2,1,0:T(8,128)S(1)}, f32[4,40,128]{2,1,0:T(8,128)S(1)}, u32[]{:S(2)}, u32[]{:S(2)}) collective-permute-start(f32[4,40,128]{2,1,0:T(8,128)S(1)} %carried_y.1.unused.refs_0_), channel_id=1, source_target_pairs={{0,1},{1,0},{2,3},{3,2},{4,5},{5,4},{6,7},{7,6},{8,9},{9,8},{10,11... | collective-permute-start | bytes 245768 | tf_op jit(solution)/shard_map/ppermute | solution.py:790
  18.2 5.0 %collective-permute-start.6 = (f32[2,40,128]{2,1,0:T(8,128)S(1)}, f32[2,40,128]{2,1,0:T(8,128)S(1)}, u32[]{:S(2)}, u32[]{:S(2)}) collective-permute-start(f32[2,40,128]{2,1,0:T(8,128)S(1)} %get-tuple-element.34), channel_id=1, source_target_pairs={{0,4},{1,5},{2,6},{3,7},{4,0},{5,1},{6,2},{7,3},{8,12},{9,13},{10,... | collective-permute-start | bytes 122888 | tf_op jit(solution)/shard_map/ppermute | solution.py:790

commit v13 on v12

--- a/solution.py
+++ b/solution.py
@@ -595,14 +595,15 @@
     return jnp.concatenate(rows, axis=0)
 
 
-def third_kernel(wy, moments, spread_core, spread_extra, entering, *refs):
+def third_kernel(planes, wy, chosen, moments, spread_core, spread_extra, entering, *refs):
     messages, (carried, held, result) = refs[:-3][::-1], refs[-3:]
-    planes = carried.shape[1]
-    count = entering.shape[0] // 3
+    count = -(-2 * len(messages) // 8) * 8
+    total = entering.shape[0] // 3
     received = arrived_rows(messages, count)
     first = received.astype(jnp.bfloat16).astype(jnp.float32)
     both = jnp.concatenate([first, received - first], axis=0)
-    values = entering[0:count, :] + entering[count : 2 * count, :]
+    values = entering[0:total, :] + entering[total : 2 * total, :]
+    values = [values[2 * (k - 1) + p : 2 * k - 1 + p] for k in chosen for p in range(2)]
     across = (((1,), (1,)), ((), ()))
     used = 2 * len(messages)
 
@@ -626,7 +627,7 @@
             lane = m * per + p
             value = moments[pl.ds(m * planes + p, number, stride=per), :]
             for r in range(used):
-                value = value + columns[r][:, lane : lane + 1] * values[r : r + 1]
+                value = value + columns[r][:, lane : lane + 1] * values[r]
             result[pl.ds(m * planes + p, number, stride=per), :] = value
 
     per = LANES // EXTRA
@@ -644,8 +645,11 @@
             for r in range(used):
                 lane = chunk * 2 * count + r
                 part = corner[m * per : m * per + size]
-                value = value + part[:, lane : lane + 1] * values[r : r + 1]
-            carried[m, rows, :] = value
+                value = value + part[:, lane : lane + 1] * values[r]
+            if len(carried.shape) == 3:
+                carried[m, rows, :] = value
+            else:
+                carried[m * planes + rows.start : m * planes + rows.stop, :] = value
 
 
 def local_y_kernel(wy, local, entering, inverse_y, unused, *refs):
@@ -814,18 +818,23 @@
         cost_estimate=cost(2 * rows * 256 * 128 * 6, 4 * rows * 384),
         name="local_z",
     )(factors, high, low)
-    carried = pl.pallas_call(
-        functools.partial(third_kernel, wy),
-        out_shape=array(4, planes, LANES),
-        in_specs=[VMEM] * (4 + arrivals),
-        out_specs=VMEM,
-        scratch_shapes=[
-            pltpu.VMEM((planes * wy // LANES * 2 * entering_rows + 2 * entering_rows, LANES), jnp.float32),
-            pltpu.VMEM((4 * planes + 8, LANES), jnp.float32),
-        ],
-        compiler_params=PARAMS,
-        name="carried_y",
-    )(moments, spread_core, spread_extra, entering, *received[::-1])
+    early = [k for k in range(1, partners + 1) if k > 2]
+    late = [k for k in range(1, partners + 1) if k <= 2]
+    carried = moments
+    for chosen, shape in ((early, (4 * planes + 8, LANES)), (late, (4, planes, LANES))):
+        room = 2 * (-(-2 * len(chosen) // 8) * 8)
+        carried = pl.pallas_call(
+            functools.partial(third_kernel, planes, wy, chosen),
+            out_shape=array(*shape),
+            in_specs=[VMEM] * (4 + len(chosen)),
+            out_specs=VMEM,
+            scratch_shapes=[
+                pltpu.VMEM((planes * wy // LANES * room + room, LANES), jnp.float32),
+                pltpu.VMEM((4 * planes + 8, LANES), jnp.float32),
+            ],
+            compiler_params=PARAMS,
+            name="carried_y",
+        )(carried, spread_core, spread_extra, entering, *[received[k - 1] for k in chosen[::-1]])
     arrived = received
 
     narrow = plan[-1][1] == 2 and len(plan) > 1

time: 24.7 us -> 24.6 us (level)
  waiting for transfers between devices: 5.11 us -> 4.69 us
  Pallas kernels: 10.1 us -> 10.4 us
    ppermute x7, waiting for transfers between devices: 5.11 us -> 4.69 us  [exchange(): received[k] = lax.ppermute(values[k - 1], axis, pairs)]
    pallas_call x1 -> x2, Pallas kernels: 0.63 us -> 0.93 us  [on_device(): pl.pallas_call(functools.partial(third_kernel, planes, wy, chosen), out_s...]
  transfers between devices with their start and end apart: 7 -> 7, of which waited for: 5 -> 5; matrix products, arithmetic and copies ran while one was open for 0% -> 0% of each run, Pallas kernels for 17% -> 19%
where the time goes in v13:
time: 24.6 us; the launch traced here: 24.4 us
  Pallas kernels  10.4 us (42%)
  starting transfers between devices  9.33 us (38%)
  waiting for transfers between devices  4.69 us (19%)
    ppermute x7, starting transfers between devices, exchange(): received[k] = lax.ppermute(values[k - 1], axis, pairs)  9.33 us
    ppermute x7, waiting for transfers between devices, exchange(): received[k] = lax.ppermute(values[k - 1], axis, pairs)  4.69 us
    pallas_call x1, Pallas kernels, on_device(): pl.pallas_call(functools.partial(first_kernel, ny, nz, partners), out_sha...  3.74 us
    pallas_call x1, Pallas kernels, on_device(): pl.pallas_call(functools.partial(second_kernel, ny, nz, count_z, wy, part...  1.97 us
    pallas_call x1, Pallas kernels, on_device(): pl.pallas_call(functools.partial(local_y_kernel, wy), out_shape=array(pla...  1.86 us
    pallas_call x1, Pallas kernels, on_device(): pl.pallas_call(functools.partial(last_kernel, base, radix, narrow, wy), o...  1.35 us
    pallas_call x2, Pallas kernels, on_device(): pl.pallas_call(functools.partial(third_kernel, planes, wy, chosen), out_s...  0.93 us
  transfers between devices with their start and end apart: 7, of which 5 were waited for; matrix products, arithmetic and copies ran while one was open for 0% of the time, Pallas kernels for 19%

profile of v13, /device:TPU:0, one launch (start us, length us, event | category | flops | bytes accessed | tf_op | source)
XLA Modules:
  0.0 24.4 jit_solution(2590371655698285872)
XLA Ops:
  0.0 3.7 %forcing_and_factor.1 = (bf16[2880,256]{1,0:T(8,128)(2,1)S(1)}, bf16[2880,256]{1,0:T(8,128)(2,1)S(1)}, f32[28,8,128]{2,1,0:T(8,128)S(1)}, f32[2,2880]{1,0:T(2,12...) custom-call(f32[5,8,64,128]{3,2,1,0:T(8,128)} %flow_hbm.1, f32[8,64,128]{2,1,0:T(8,128)} %speed_hbm.1, ...), custom_call_target="tpu_custom_call" | custom-call | tf_op jit(solution)/shard_map/forcing_and_factor/pallas_call | solution.py:772
  3.7 2.4 %collective-permute-start = (f32[2,2880]{1,0:T(2,128)S(1)}, f32[2,2880]{1,0:T(2,128)S(1)}, u32[]{:S(2)}, u32[]{:S(2)}) collective-permute-start(f32[2,2880]{1,0:T(2,128)S(1)} %get-tuple-element.27), channel_id=1, source_target_pairs={{0,24},{8,16},{16,8},{24,0},{1,25},{9,17},{17,9},{25,1},{2,26},{10... | collective-permute-start | bytes 69128 | tf_op jit(solution)/shard_map/ppermute | solution.py:794
  6.2 0.6 %collective-permute-start.1 = (f32[2,2880]{1,0:T(2,128)S(1)}, f32[2,2880]{1,0:T(2,128)S(1)}, u32[]{:S(2)}, u32[]{:S(2)}) collective-permute-start(f32[2,2880]{1,0:T(2,128)S(1)} %get-tuple-element.28), channel_id=1, source_target_pairs={{0,16},{8,24},{16,0},{24,8},{1,17},{9,25},{17,1},{25,9},{2,18},{10... | collective-permute-start | bytes 69128 | tf_op jit(solution)/shard_map/ppermute | solution.py:794
  6.8 0.0 collective-permute-start.2
  6.9 2.0 %local_z.1 = (f32[2880,128]{1,0:T(8,128)S(1)}, f32[168,128]{1,0:T(8,128)S(1)}, f32[24,128]{1,0:T(8,128)S(1)}, f32[8,128]{1,0:T(8,128)S(1)}, f32[64,128]{1,0:T(8,128)S(1)}) custom-call(f32[28,8,128]{2,1,0:T(8,128)S(1)} %get-tuple-element.20.factors, bf16[2880,256]{1,0:T(8,128)(2,1)S(1)} %get-tuple-element.21.high, bf16[2880,256]{1,0:T(8,128)(2,1)S(1)} %get-tuple-element.22.low), custom_call_target="tpu_custom_call" | custom-call | flops 1132462080 | bytes 4423680 | tf_op jit(solution)/shard_map/local_z/pallas_call | solution.py:800
  8.8 0.0 collective-permute-done.refs_0_.refs_2_
  8.9 0.4 %carried_y.2.moments = f32[168,128]{1,0:T(8,128)S(1)} custom-call(f32[168,128]{1,0:T(8,128)S(1)} %get-tuple-element.23.moments, f32[8,128]{1,0:T(8,128)S(1)} %get-tuple-element.24.spread_core, f32[64,128]{1,0:T(8,128)S(1)} %get-tuple-element.25.spread_extra, f32[24,128]{1,0:T(8,128)S(1)} %get-tuple-element.26.entering, ...), custom_call_target="tpu_custom_call" | custom-call | tf_op jit(solution)/shard_map/carried_y/pallas_call | solution.py:826
  9.3 0.7 %collective-permute-done.1.refs_0_.refs_1_ = f32[2,2880]{1,0:T(2,128)S(1)} collective-permute-done((f32[2,2880]{1,0:T(2,128)S(1)}, f32[2,2880]{1,0:T(2,128)S(1)}, u32[]{:S(2)}, u32[]{:S(2)}) %collective-permute-start.1) | collective-permute-done | bytes 23072 | tf_op jit(solution)/shard_map/ppermute | solution.py:794
  10.0 0.0 collective-permute-done.2.refs_1_.refs_0_
  10.0 0.5 %carried_y.3.unused.refs_0_ = f32[4,40,128]{2,1,0:T(8,128)S(1)} custom-call(f32[168,128]{1,0:T(8,128)S(1)} %carried_y.2.moments, f32[8,128]{1,0:T(8,128)S(1)} %get-tuple-element.24.spread_core, f32[64,128]{1,0:T(8,128)S(1)} %get-tuple-element.25.spread_extra, f32[24,128]{1,0:T(8,128)S(1)} %get-tuple-element.26.entering, ...), custom_call_target="tpu_custom_call" | custom-call | tf_op jit(solution)/shard_map/carried_y/pallas_call | solution.py:826
  10.5 2.6 %collective-permute-start.5 = (f32[4,40,128]{2,1,0:T(8,128)S(1)}, f32[4,40,128]{2,1,0:T(8,128)S(1)}, u32[]{:S(2)}, u32[]{:S(2)}) collective-permute-start(f32[4,40,128]{2,1,0:T(8,128)S(1)} %carried_y.3.unused.refs_0_), channel_id=1, source_target_pairs={{0,3},{1,2},{2,1},{3,0},{4,7},{5,6},{6,5},{7,4},{8,11},{9,10},{10,... | collective-permute-start | bytes 245768 | tf_op jit(solution)/shard_map/ppermute | solution.py:794
  13.1 0.4 %collective-permute-start.4 = (f32[4,40,128]{2,1,0:T(8,128)S(1)}, f32[4,40,128]{2,1,0:T(8,128)S(1)}, u32[]{:S(2)}, u32[]{:S(2)}) collective-permute-start(f32[4,40,128]{2,1,0:T(8,128)S(1)} %carried_y.3.unused.refs_0_), channel_id=1, source_target_pairs={{0,2},{1,3},{2,0},{3,1},{4,6},{5,7},{6,4},{7,5},{8,10},{9,11},{10,... | collective-permute-start | bytes 245768 | tf_op jit(solution)/shard_map/ppermute | solution.py:794
  13.6 0.5 %collective-permute-start.3 = (f32[4,40,128]{2,1,0:T(8,128)S(1)}, f32[4,40,128]{2,1,0:T(8,128)S(1)}, u32[]{:S(2)}, u32[]{:S(2)}) collective-permute-start(f32[4,40,128]{2,1,0:T(8,128)S(1)} %carried_y.3.unused.refs_0_), channel_id=1, source_target_pairs={{0,1},{1,0},{2,3},{3,2},{4,5},{5,4},{6,7},{7,6},{8,9},{9,8},{10,11... | collective-permute-start | bytes 245768 | tf_op jit(solution)/shard_map/ppermute | solution.py:794
  14.1 0.4 %inverse_y.1 = (f32[64,128]{1,0:T(8,128)S(1)}, f32[8,8,128]{2,1,0:T(8,128)S(1)}) custom-call(f32[28,8,128]{2,1,0:T(8,128)S(1)} %get-tuple-element.20.factors, f32[4,40,128]{2,1,0:T(8,128)S(1)} %carried_y.3.unused.refs_0_), custom_call_target="tpu_custom_call" | custom-call | flops 566231040 | bytes 2949120 | tf_op jit(solution)/shard_map/inverse_y/pallas_call | solution.py:846
  14.5 2.2 %collective-permute-done.5.refs_3_ = f32[4,40,128]{2,1,0:T(8,128)S(1)} collective-permute-done((f32[4,40,128]{2,1,0:T(8,128)S(1)}, f32[4,40,128]{2,1,0:T(8,128)S(1)}, u32[]{:S(2)}, u32[]{:S(2)}) %collective-permute-start.5) | collective-permute-done | bytes 81952 | tf_op jit(solution)/shard_map/ppermute | solution.py:794
  16.7 1.0 %collective-permute-done.4.refs_2_ = f32[4,40,128]{2,1,0:T(8,128)S(1)} collective-permute-done((f32[4,40,128]{2,1,0:T(8,128)S(1)}, f32[4,40,128]{2,1,0:T(8,128)S(1)}, u32[]{:S(2)}, u32[]{:S(2)}) %collective-permute-start.4) | collective-permute-done | bytes 81952 | tf_op jit(solution)/shard_map/ppermute | solution.py:794
  17.8 0.3 %collective-permute-done.3.refs_1_ = f32[4,40,128]{2,1,0:T(8,128)S(1)} collective-permute-done((f32[4,40,128]{2,1,0:T(8,128)S(1)}, f32[4,40,128]{2,1,0:T(8,128)S(1)}, u32[]{:S(2)}, u32[]{:S(2)}) %collective-permute-start.3) | collective-permute-done | bytes 81952 | tf_op jit(solution)/shard_map/ppermute | solution.py:794
  18.0 0.1 join_groups.1
  18.1 2.7 %collective-permute-start.6 = (f32[2,40,128]{2,1,0:T(8,128)S(1)}, f32[2,40,128]{2,1,0:T(8,128)S(1)}, u32[]{:S(2)}, u32[]{:S(2)}) collective-permute-start(f32[2,40,128]{2,1,0:T(8,128)S(1)} %get-tuple-element.34), channel_id=1, source_target_pairs={{0,4},{1,5},{2,6},{3,7},{4,0},{5,1},{6,2},{7,3},{8,12},{9,13},{10,... | collective-permute-start | bytes 122888 | tf_op jit(solution)/shard_map/ppermute | solution.py:794
  20.8 1.9 %local_y.1.local = f32[40,64,128]{2,1,0:T(8,128)S(1)} custom-call(f32[2880,128]{1,0:T(8,128)S(1)} %get-tuple-element.31.local, f32[24,128]{1,0:T(8,128)S(1)} %get-tuple-element.26.entering, f32[64,128]{1,0:T(8,128)S(1)} %get-tuple-element.32.inverse_y, f32[4,40,128]{2,1,0:T(8,128)S(1)} %get-tuple-element.33.unused.entered, ...), custom_call_target="tpu_custom_call" | custom-call | flops 566231040 | bytes 2949120 | tf_op jit(solution)/shard_map/local_y/pallas_call | solution.py:869
  22.6 0.5 %collective-permute-done.6.refs_0_ = f32[2,40,128]{2,1,0:T(8,128)S(1)} collective-permute-done((f32[2,40,128]{2,1,0:T(8,128)S(1)}, f32[2,40,128]{2,1,0:T(8,128)S(1)}, u32[]{:S(2)}, u32[]{:S(2)}) %collective-permute-start.6) | collective-permute-done | bytes 40992 | tf_op jit(solution)/shard_map/ppermute | solution.py:794
  23.1 1.4 %finish_y.1 = f32[5,8,64,128]{3,2,1,0:T(8,128)} custom-call(f32[8,8,128]{2,1,0:T(8,128)S(1)} %get-tuple-element.30.coefs, f32[40,64,128]{2,1,0:T(8,128)S(1)} %local_y.1.local, f32[64,128]{1,0:T(8,128)S(1)} %get-tuple-element.32.inverse_y, f32[4,40,128]{2,1,0:T(8,128)S(1)} %get-tuple-element.33.unused.entered, f32[2,40,128]{2,1,0:T(8,128)S(1)} %collective-permute-done.6.refs_0_), custom_call_target="tpu_custom_call" | custom-call | tf_op jit(solution)/shard_map/finish_y/pallas_call | solution.py:880
Async XLA Ops:
  3.7 5.1 %collective-permute-start = (f32[2,2880]{1,0:T(2,128)S(1)}, f32[2,2880]{1,0:T(2,128)S(1)}, u32[]{:S(2)}, u32[]{:S(2)}) collective-permute-start(f32[2,2880]{1,0:T(2,128)S(1)} %get-tuple-element.27), channel_id=1, source_target_pairs={{0,24},{8,16},{16,8},{24,0},{1,25},{9,17},{17,9},{25,1},{2,26},{10... | collective-permute-start | bytes 69128 | tf_op jit(solution)/shard_map/ppermute | solution.py:794
  6.2 3.8 %collective-permute-start.1 = (f32[2,2880]{1,0:T(2,128)S(1)}, f32[2,2880]{1,0:T(2,128)S(1)}, u32[]{:S(2)}, u32[]{:S(2)}) collective-permute-start(f32[2,2880]{1,0:T(2,128)S(1)} %get-tuple-element.28), channel_id=1, source_target_pairs={{0,16},{8,24},{16,0},{24,8},{1,17},{9,25},{17,1},{25,9},{2,18},{10... | collective-permute-start | bytes 69128 | tf_op jit(solution)/shard_map/ppermute | solution.py:794
  6.8 3.2 %collective-permute-start.2 = (f32[2,2880]{1,0:T(2,128)S(1)}, f32[2,2880]{1,0:T(2,128)S(1)}, u32[]{:S(2)}, u32[]{:S(2)}) collective-permute-start(f32[2,2880]{1,0:T(2,128)S(1)} %get-tuple-element.29), channel_id=1, source_target_pairs={{0,8},{8,0},{16,24},{24,16},{1,9},{9,1},{17,25},{25,17},{2,10},{10... | collective-permute-start | bytes 69128 | tf_op jit(solution)/shard_map/ppermute | solution.py:794
  10.5 6.2 %collective-permute-start.5 = (f32[4,40,128]{2,1,0:T(8,128)S(1)}, f32[4,40,128]{2,1,0:T(8,128)S(1)}, u32[]{:S(2)}, u32[]{:S(2)}) collective-permute-start(f32[4,40,128]{2,1,0:T(8,128)S(1)} %carried_y.3.unused.refs_0_), channel_id=1, source_target_pairs={{0,3},{1,2},{2,1},{3,0},{4,7},{5,6},{6,5},{7,4},{8,11},{9,10},{10,... | collective-permute-start | bytes 245768 | tf_op jit(solution)/shard_map/ppermute | solution.py:794
  13.1 4.6 %collective-permute-start.4 = (f32[4,40,128]{2,1,0:T(8,128)S(1)}, f32[4,40,128]{2,1,0:T(8,128)S(1)}, u32[]{:S(2)}, u32[]{:S(2)}) collective-permute-start(f32[4,40,128]{2,1,0:T(8,128)S(1)} %carried_y.3.unused.refs_0_), channel_id=1, source_target_pairs={{0,2},{1,3},{2,0},{3,1},{4,6},{5,7},{6,4},{7,5},{8,10},{9,11},{10,... | collective-permute-start | bytes 245768 | tf_op jit(solution)/shard_map/ppermute | solution.py:794
  13.6 4.4 %collective-permute-start.3 = (f32[4,40,128]{2,1,0:T(8,128)S(1)}, f32[4,40,128]{2,1,0:T(8,128)S(1)}, u32[]{:S(2)}, u32[]{:S(2)}) collective-permute-start(f32[4,40,128]{2,1,0:T(8,128)S(1)} %carried_y.3.unused.refs_0_), channel_id=1, source_target_pairs={{0,1},{1,0},{2,3},{3,2},{4,5},{5,4},{6,7},{7,6},{8,9},{9,8},{10,11... | collective-permute-start | bytes 245768 | tf_op jit(solution)/shard_map/ppermute | solution.py:794
  18.1 5.0 %collective-permute-start.6 = (f32[2,40,128]{2,1,0:T(8,128)S(1)}, f32[2,40,128]{2,1,0:T(8,128)S(1)}, u32[]{:S(2)}, u32[]{:S(2)}) collective-permute-start(f32[2,40,128]{2,1,0:T(8,128)S(1)} %get-tuple-element.34), channel_id=1, source_target_pairs={{0,4},{1,5},{2,6},{3,7},{4,0},{5,1},{6,2},{7,3},{8,12},{9,13},{10,... | collective-permute-start | bytes 122888 | tf_op jit(solution)/shard_map/ppermute | solution.py:794

commit v14 on v13

--- a/solution.py
+++ b/solution.py
@@ -653,8 +653,10 @@
 
 
 def local_y_kernel(wy, local, entering, inverse_y, unused, *refs):
-    messages, (out, solved) = refs[:-2], refs[-2:]
+    messages, (out, sides, solved) = refs[:-3], refs[-3:]
     planes = out.shape[0]
+    for number, c in enumerate((0, 1, wy - 2, wy - 1)):
+        sides[number] = jnp.broadcast_to(inverse_y[:, c : c + 1], (wy, LANES))
     count = entering.shape[0] // 3
     received = arrived_rows(messages, count)
     first = received.astype(jnp.bfloat16).astype(jnp.float32)
@@ -712,7 +714,7 @@
             message[row] = value
 
 
-def last_kernel(base, radix, narrow, wy, coefs, local, inverse_y, entered, *refs):
+def last_kernel(base, radix, narrow, wy, coefs, local, sides, entered, *refs):
     messages, (out_hbm, out, sent) = refs[: radix - 1], refs[radix - 1 :]
     values = list(messages)
     if narrow:
@@ -720,9 +722,6 @@
     below = combine(coefs, 0, base, values)
     above = combine(coefs, 4, base, values)
     st = [value + entered[row] for row, value in enumerate(below + above)]
-    sides = [
-        jnp.broadcast_to(inverse_y[:, c : c + 1], (wy, LANES)) for c in (0, 1, wy - 2, wy - 1)
-    ]
     fields, planes_x = out.shape[:2]
     copies = []
     for field in range(fields):
@@ -866,11 +865,11 @@
             )(coefs, *inputs)
             base += 2 * radix - 1
             if number == 0:
-                result = pl.pallas_call(
+                result, sides = pl.pallas_call(
                     functools.partial(local_y_kernel, wy),
-                    out_shape=array(planes, wy, LANES),
+                    out_shape=[array(planes, wy, LANES), array(4, wy, LANES)],
                     in_specs=[VMEM] * 3 + [HBM] + [VMEM] * arrivals,
-                    out_specs=VMEM,
+                    out_specs=[VMEM] * 2,
                     scratch_shapes=[pltpu.VMEM((rows, LANES), jnp.float32)],
                     compiler_params=PARAMS,
                     cost_estimate=cost(2 * rows * 128 * 128 * 6, 4 * rows * 256),
@@ -888,7 +887,7 @@
                 ],
                 compiler_params=PARAMS,
                 name="finish_y",
-            )(coefs, result, inverse_y, entered, *received)
+            )(coefs, result, sides, entered, *received)
 
 
 def solution(mesh):

time: 24.6 us -> 24.4 us (level)
  no operation moved by 1% of the time
where the time goes in v14:
time: 24.4 us; the launch traced here: 24.3 us
  Pallas kernels  10.2 us (42%)
  starting transfers between devices  9.33 us (38%)
  waiting for transfers between devices  4.66 us (19%)
    ppermute x7, starting transfers between devices, exchange(): received[k] = lax.ppermute(values[k - 1], axis, pairs)  9.33 us
    ppermute x7, waiting for transfers between devices, exchange(): received[k] = lax.ppermute(values[k - 1], axis, pairs)  4.66 us
    pallas_call x1, Pallas kernels, on_device(): pl.pallas_call(functools.partial(first_kernel, ny, nz, partners), out_sha...  3.74 us
    pallas_call x1, Pallas kernels, on_device(): pl.pallas_call(functools.partial(second_kernel, ny, nz, count_z, wy, part...  1.99 us
    pallas_call x1, Pallas kernels, on_device(): pl.pallas_call(functools.partial(local_y_kernel, wy), out_shape=[array(pl...  1.86 us
    pallas_call x1, Pallas kernels, on_device(): pl.pallas_call(functools.partial(last_kernel, base, radix, narrow, wy), o...  1.17 us
    pallas_call x2, Pallas kernels, on_device(): pl.pallas_call(functools.partial(third_kernel, planes, wy, chosen), out_s...  0.92 us
  transfers between devices with their start and end apart: 7, of which 5 were waited for; matrix products, arithmetic and copies ran while one was open for 0% of the time, Pallas kernels for 19%

profile of v14, /device:TPU:0, one launch (start us, length us, event | category | flops | bytes accessed | tf_op | source)
XLA Modules:
  0.0 24.3 jit_solution(15947566086597224788)
XLA Ops:
  0.0 3.7 %forcing_and_factor.1 = (bf16[2880,256]{1,0:T(8,128)(2,1)S(1)}, bf16[2880,256]{1,0:T(8,128)(2,1)S(1)}, f32[28,8,128]{2,1,0:T(8,128)S(1)}, f32[2,2880]{1,0:T(2,12...) custom-call(f32[5,8,64,128]{3,2,1,0:T(8,128)} %flow_hbm.1, f32[8,64,128]{2,1,0:T(8,128)} %speed_hbm.1, ...), custom_call_target="tpu_custom_call" | custom-call | tf_op jit(solution)/shard_map/forcing_and_factor/pallas_call | solution.py:771
  3.7 2.4 %collective-permute-start = (f32[2,2880]{1,0:T(2,128)S(1)}, f32[2,2880]{1,0:T(2,128)S(1)}, u32[]{:S(2)}, u32[]{:S(2)}) collective-permute-start(f32[2,2880]{1,0:T(2,128)S(1)} %get-tuple-element.29), channel_id=1, source_target_pairs={{0,24},{8,16},{16,8},{24,0},{1,25},{9,17},{17,9},{25,1},{2,26},{10... | collective-permute-start | bytes 69128 | tf_op jit(solution)/shard_map/ppermute | solution.py:793
  6.2 0.6 %collective-permute-start.1 = (f32[2,2880]{1,0:T(2,128)S(1)}, f32[2,2880]{1,0:T(2,128)S(1)}, u32[]{:S(2)}, u32[]{:S(2)}) collective-permute-start(f32[2,2880]{1,0:T(2,128)S(1)} %get-tuple-element.30), channel_id=1, source_target_pairs={{0,16},{8,24},{16,0},{24,8},{1,17},{9,25},{17,1},{25,9},{2,18},{10... | collective-permute-start | bytes 69128 | tf_op jit(solution)/shard_map/ppermute | solution.py:793
  6.8 0.0 collective-permute-start.2
  6.9 2.0 %local_z.1 = (f32[2880,128]{1,0:T(8,128)S(1)}, f32[168,128]{1,0:T(8,128)S(1)}, f32[24,128]{1,0:T(8,128)S(1)}, f32[8,128]{1,0:T(8,128)S(1)}, f32[64,128]{1,0:T(8,128)S(1)}) custom-call(f32[28,8,128]{2,1,0:T(8,128)S(1)} %get-tuple-element.22.factors, bf16[2880,256]{1,0:T(8,128)(2,1)S(1)} %get-tuple-element.23.high, bf16[2880,256]{1,0:T(8,128)(2,1)S(1)} %get-tuple-element.24.low), custom_call_target="tpu_custom_call" | custom-call | flops 1132462080 | bytes 4423680 | tf_op jit(solution)/shard_map/local_z/pallas_call | solution.py:799
  8.9 0.0 collective-permute-done.refs_0_.refs_2_
  8.9 0.4 %carried_y.2.moments = f32[168,128]{1,0:T(8,128)S(1)} custom-call(f32[168,128]{1,0:T(8,128)S(1)} %get-tuple-element.25.moments, f32[8,128]{1,0:T(8,128)S(1)} %get-tuple-element.26.spread_core, f32[64,128]{1,0:T(8,128)S(1)} %get-tuple-element.27.spread_extra, f32[24,128]{1,0:T(8,128)S(1)} %get-tuple-element.28.entering, ...), custom_call_target="tpu_custom_call" | custom-call | tf_op jit(solution)/shard_map/carried_y/pallas_call | solution.py:825
  9.3 0.7 %collective-permute-done.1.refs_0_.refs_1_ = f32[2,2880]{1,0:T(2,128)S(1)} collective-permute-done((f32[2,2880]{1,0:T(2,128)S(1)}, f32[2,2880]{1,0:T(2,128)S(1)}, u32[]{:S(2)}, u32[]{:S(2)}) %collective-permute-start.1) | collective-permute-done | bytes 23072 | tf_op jit(solution)/shard_map/ppermute | solution.py:793
  10.0 0.0 collective-permute-done.2.refs_1_.refs_0_
  10.0 0.5 %carried_y.3.unused.refs_0_ = f32[4,40,128]{2,1,0:T(8,128)S(1)} custom-call(f32[168,128]{1,0:T(8,128)S(1)} %carried_y.2.moments, f32[8,128]{1,0:T(8,128)S(1)} %get-tuple-element.26.spread_core, f32[64,128]{1,0:T(8,128)S(1)} %get-tuple-element.27.spread_extra, f32[24,128]{1,0:T(8,128)S(1)} %get-tuple-element.28.entering, ...), custom_call_target="tpu_custom_call" | custom-call | tf_op jit(solution)/shard_map/carried_y/pallas_call | solution.py:825
  10.5 2.6 %collective-permute-start.5 = (f32[4,40,128]{2,1,0:T(8,128)S(1)}, f32[4,40,128]{2,1,0:T(8,128)S(1)}, u32[]{:S(2)}, u32[]{:S(2)}) collective-permute-start(f32[4,40,128]{2,1,0:T(8,128)S(1)} %carried_y.3.unused.refs_0_), channel_id=1, source_target_pairs={{0,3},{1,2},{2,1},{3,0},{4,7},{5,6},{6,5},{7,4},{8,11},{9,10},{10,... | collective-permute-start | bytes 245768 | tf_op jit(solution)/shard_map/ppermute | solution.py:793
  13.1 0.4 %collective-permute-start.4 = (f32[4,40,128]{2,1,0:T(8,128)S(1)}, f32[4,40,128]{2,1,0:T(8,128)S(1)}, u32[]{:S(2)}, u32[]{:S(2)}) collective-permute-start(f32[4,40,128]{2,1,0:T(8,128)S(1)} %carried_y.3.unused.refs_0_), channel_id=1, source_target_pairs={{0,2},{1,3},{2,0},{3,1},{4,6},{5,7},{6,4},{7,5},{8,10},{9,11},{10,... | collective-permute-start | bytes 245768 | tf_op jit(solution)/shard_map/ppermute | solution.py:793
  13.6 0.5 %collective-permute-start.3 = (f32[4,40,128]{2,1,0:T(8,128)S(1)}, f32[4,40,128]{2,1,0:T(8,128)S(1)}, u32[]{:S(2)}, u32[]{:S(2)}) collective-permute-start(f32[4,40,128]{2,1,0:T(8,128)S(1)} %carried_y.3.unused.refs_0_), channel_id=1, source_target_pairs={{0,1},{1,0},{2,3},{3,2},{4,5},{5,4},{6,7},{7,6},{8,9},{9,8},{10,11... | collective-permute-start | bytes 245768 | tf_op jit(solution)/shard_map/ppermute | solution.py:793
  14.1 0.4 %inverse_y.1 = (f32[64,128]{1,0:T(8,128)S(1)}, f32[8,8,128]{2,1,0:T(8,128)S(1)}) custom-call(f32[28,8,128]{2,1,0:T(8,128)S(1)} %get-tuple-element.22.factors, f32[4,40,128]{2,1,0:T(8,128)S(1)} %carried_y.3.unused.refs_0_), custom_call_target="tpu_custom_call" | custom-call | flops 566231040 | bytes 2949120 | tf_op jit(solution)/shard_map/inverse_y/pallas_call | solution.py:845
  14.5 2.2 %collective-permute-done.5.refs_3_ = f32[4,40,128]{2,1,0:T(8,128)S(1)} collective-permute-done((f32[4,40,128]{2,1,0:T(8,128)S(1)}, f32[4,40,128]{2,1,0:T(8,128)S(1)}, u32[]{:S(2)}, u32[]{:S(2)}) %collective-permute-start.5) | collective-permute-done | bytes 81952 | tf_op jit(solution)/shard_map/ppermute | solution.py:793
  16.7 1.0 %collective-permute-done.4.refs_2_ = f32[4,40,128]{2,1,0:T(8,128)S(1)} collective-permute-done((f32[4,40,128]{2,1,0:T(8,128)S(1)}, f32[4,40,128]{2,1,0:T(8,128)S(1)}, u32[]{:S(2)}, u32[]{:S(2)}) %collective-permute-start.4) | collective-permute-done | bytes 81952 | tf_op jit(solution)/shard_map/ppermute | solution.py:793
  17.7 0.3 %collective-permute-done.3.refs_1_ = f32[4,40,128]{2,1,0:T(8,128)S(1)} collective-permute-done((f32[4,40,128]{2,1,0:T(8,128)S(1)}, f32[4,40,128]{2,1,0:T(8,128)S(1)}, u32[]{:S(2)}, u32[]{:S(2)}) %collective-permute-start.3) | collective-permute-done | bytes 81952 | tf_op jit(solution)/shard_map/ppermute | solution.py:793
  18.0 0.1 join_groups.1
  18.1 2.7 %collective-permute-start.6 = (f32[2,40,128]{2,1,0:T(8,128)S(1)}, f32[2,40,128]{2,1,0:T(8,128)S(1)}, u32[]{:S(2)}, u32[]{:S(2)}) collective-permute-start(f32[2,40,128]{2,1,0:T(8,128)S(1)} %get-tuple-element.38), channel_id=1, source_target_pairs={{0,4},{1,5},{2,6},{3,7},{4,0},{5,1},{6,2},{7,3},{8,12},{9,13},{10,... | collective-permute-start | bytes 122888 | tf_op jit(solution)/shard_map/ppermute | solution.py:793
  20.8 1.9 %local_y.1 = (f32[40,64,128]{2,1,0:T(8,128)S(1)}, f32[4,64,128]{2,1,0:T(8,128)S(1)}) custom-call(f32[2880,128]{1,0:T(8,128)S(1)} %get-tuple-element.33.local, f32[24,128]{1,0:T(8,128)S(1)} %get-tuple-element.28.entering, f32[64,128]{1,0:T(8,128)S(1)} %get-tuple-element.34.inverse_y, f32[4,40,128]{2,1,0:T(8,128)S(1)} %get-tuple-element.35.unused.entered, ...), custom_call_target="tpu_custom_call" | custom-call | flops 566231040 | bytes 2949120 | tf_op jit(solution)/shard_map/local_y/pallas_call | solution.py:868
  22.6 0.4 %collective-permute-done.6.refs_0_ = f32[2,40,128]{2,1,0:T(8,128)S(1)} collective-permute-done((f32[2,40,128]{2,1,0:T(8,128)S(1)}, f32[2,40,128]{2,1,0:T(8,128)S(1)}, u32[]{:S(2)}, u32[]{:S(2)}) %collective-permute-start.6) | collective-permute-done | bytes 40992 | tf_op jit(solution)/shard_map/ppermute | solution.py:793
  23.1 1.2 %finish_y.1 = f32[5,8,64,128]{3,2,1,0:T(8,128)} custom-call(f32[8,8,128]{2,1,0:T(8,128)S(1)} %get-tuple-element.32.coefs, f32[40,64,128]{2,1,0:T(8,128)S(1)} %get-tuple-element.36.local, f32[4,64,128]{2,1,0:T(8,128)S(1)} %get-tuple-element.37.sides, f32[4,40,128]{2,1,0:T(8,128)S(1)} %get-tuple-element.35.unused.entered, ...), custom_call_target="tpu_custom_call" | custom-call | tf_op jit(solution)/shard_map/finish_y/pallas_call | solution.py:879
Async XLA Ops:
  3.7 5.1 %collective-permute-start = (f32[2,2880]{1,0:T(2,128)S(1)}, f32[2,2880]{1,0:T(2,128)S(1)}, u32[]{:S(2)}, u32[]{:S(2)}) collective-permute-start(f32[2,2880]{1,0:T(2,128)S(1)} %get-tuple-element.29), channel_id=1, source_target_pairs={{0,24},{8,16},{16,8},{24,0},{1,25},{9,17},{17,9},{25,1},{2,26},{10... | collective-permute-start | bytes 69128 | tf_op jit(solution)/shard_map/ppermute | solution.py:793
  6.2 3.8 %collective-permute-start.1 = (f32[2,2880]{1,0:T(2,128)S(1)}, f32[2,2880]{1,0:T(2,128)S(1)}, u32[]{:S(2)}, u32[]{:S(2)}) collective-permute-start(f32[2,2880]{1,0:T(2,128)S(1)} %get-tuple-element.30), channel_id=1, source_target_pairs={{0,16},{8,24},{16,0},{24,8},{1,17},{9,25},{17,1},{25,9},{2,18},{10... | collective-permute-start | bytes 69128 | tf_op jit(solution)/shard_map/ppermute | solution.py:793
  6.8 3.2 %collective-permute-start.2 = (f32[2,2880]{1,0:T(2,128)S(1)}, f32[2,2880]{1,0:T(2,128)S(1)}, u32[]{:S(2)}, u32[]{:S(2)}) collective-permute-start(f32[2,2880]{1,0:T(2,128)S(1)} %get-tuple-element.31), channel_id=1, source_target_pairs={{0,8},{8,0},{16,24},{24,16},{1,9},{9,1},{17,25},{25,17},{2,10},{10... | collective-permute-start | bytes 69128 | tf_op jit(solution)/shard_map/ppermute | solution.py:793
  10.5 6.2 %collective-permute-start.5 = (f32[4,40,128]{2,1,0:T(8,128)S(1)}, f32[4,40,128]{2,1,0:T(8,128)S(1)}, u32[]{:S(2)}, u32[]{:S(2)}) collective-permute-start(f32[4,40,128]{2,1,0:T(8,128)S(1)} %carried_y.3.unused.refs_0_), channel_id=1, source_target_pairs={{0,3},{1,2},{2,1},{3,0},{4,7},{5,6},{6,5},{7,4},{8,11},{9,10},{10,... | collective-permute-start | bytes 245768 | tf_op jit(solution)/shard_map/ppermute | solution.py:793
  13.1 4.6 %collective-permute-start.4 = (f32[4,40,128]{2,1,0:T(8,128)S(1)}, f32[4,40,128]{2,1,0:T(8,128)S(1)}, u32[]{:S(2)}, u32[]{:S(2)}) collective-permute-start(f32[4,40,128]{2,1,0:T(8,128)S(1)} %carried_y.3.unused.refs_0_), channel_id=1, source_target_pairs={{0,2},{1,3},{2,0},{3,1},{4,6},{5,7},{6,4},{7,5},{8,10},{9,11},{10,... | collective-permute-start | bytes 245768 | tf_op jit(solution)/shard_map/ppermute | solution.py:793
  13.6 4.4 %collective-permute-start.3 = (f32[4,40,128]{2,1,0:T(8,128)S(1)}, f32[4,40,128]{2,1,0:T(8,128)S(1)}, u32[]{:S(2)}, u32[]{:S(2)}) collective-permute-start(f32[4,40,128]{2,1,0:T(8,128)S(1)} %carried_y.3.unused.refs_0_), channel_id=1, source_target_pairs={{0,1},{1,0},{2,3},{3,2},{4,5},{5,4},{6,7},{7,6},{8,9},{9,8},{10,11... | collective-permute-start | bytes 245768 | tf_op jit(solution)/shard_map/ppermute | solution.py:793
  18.1 5.0 %collective-permute-start.6 = (f32[2,40,128]{2,1,0:T(8,128)S(1)}, f32[2,40,128]{2,1,0:T(8,128)S(1)}, u32[]{:S(2)}, u32[]{:S(2)}) collective-permute-start(f32[2,40,128]{2,1,0:T(8,128)S(1)} %get-tuple-element.38), channel_id=1, source_target_pairs={{0,4},{1,5},{2,6},{3,7},{4,0},{5,1},{6,2},{7,3},{8,12},{9,13},{10,... | collective-permute-start | bytes 122888 | tf_op jit(solution)/shard_map/ppermute | solution.py:793

commit v15 on v14

--- a/solution.py
+++ b/solution.py
@@ -292,14 +292,15 @@
     stack = jnp.concatenate(stack, axis=0)
     first = stack.astype(jnp.bfloat16).astype(jnp.float32)
     both = jnp.concatenate([first, stack - first], axis=0).astype(jnp.bfloat16)
+    both = jnp.concatenate([both, both], axis=1)
     across = (((1,), (1,)), ((), ()))
     total = high.shape[0]
     size = planes_x * wy
     for begin in range(0, total, size):
         rows = slice(begin, min(begin + size, total))
-        on_high = matmul(both, high[rows, :], across)
-        on_low = matmul(both, low[rows, :], across)
-        moments = (on_high[:count] + on_high[count:]) + on_low[:count]
+        sources = jnp.concatenate([high[rows, :], low[rows, :]], axis=1)
+        moments = matmul(both, sources, across)
+        moments = moments[:count] + moments[count:]
         for k in range(partners):
             messages[k][:, rows] = moments[2 * k : 2 * k + 2]
 
@@ -612,12 +613,13 @@
         if parts[-1].shape[1] < LANES:
             missing = jnp.zeros((2 * count, LANES - parts[-1].shape[1]), jnp.float32)
             parts[-1] = jnp.concatenate([parts[-1], missing], axis=1)
-        return jnp.concatenate(parts, axis=0).astype(jnp.bfloat16), len(parts)
+        stack = jnp.concatenate(parts, axis=0).astype(jnp.bfloat16)
+        return jnp.concatenate([stack, stack], axis=1), len(parts)
 
     per = LANES // wy
     stack, number = chunks(0, planes * wy)
-    top, rest = halves(spread_core[...])
-    held[0 : number * 2 * count, 0 : 4 * per] = matmul(stack, top, across) + matmul(stack, rest, across)
+    weights = jnp.concatenate(halves(spread_core[...]), axis=1)
+    held[0 : number * 2 * count, 0 : 4 * per] = matmul(stack, weights, across)
     columns = [
         held[pl.ds(r, number, stride=2 * count), :] + held[pl.ds(count + r, number, stride=2 * count), :]
         for r in range(used)
@@ -632,8 +634,8 @@
 
     per = LANES // EXTRA
     stack, number = chunks(planes * wy, planes * (wy + EXTRA))
-    top, rest = halves(spread_extra[...])
-    corner = matmul(top, stack, across) + matmul(rest, stack, across)
+    weights = jnp.concatenate(halves(spread_extra[...]), axis=1)
+    corner = matmul(weights, stack, across)
     spare = jnp.zeros((corner.shape[0], -corner.shape[1] % LANES), jnp.float32)
     corner = jnp.concatenate([corner, spare], axis=1)
     corner = corner + pltpu.roll(corner, corner.shape[1] - count, 1)

time: 24.4 us -> 24.3 us (level)
  no operation moved by 1% of the time
where the time goes in v15:
time: 24.3 us; the launch traced here: 24.2 us
  Pallas kernels  10.1 us (42%)
  starting transfers between devices  9.33 us (38%)
  waiting for transfers between devices  4.66 us (19%)
    ppermute x7, starting transfers between devices, exchange(): received[k] = lax.ppermute(values[k - 1], axis, pairs)  9.33 us
    ppermute x7, waiting for transfers between devices, exchange(): received[k] = lax.ppermute(values[k - 1], axis, pairs)  4.66 us
    pallas_call x1, Pallas kernels, on_device(): pl.pallas_call(functools.partial(first_kernel, ny, nz, partners), out_sha...  3.67 us
    pallas_call x1, Pallas kernels, on_device(): pl.pallas_call(functools.partial(second_kernel, ny, nz, count_z, wy, part...  2 us
    pallas_call x1, Pallas kernels, on_device(): pl.pallas_call(functools.partial(local_y_kernel, wy), out_shape=[array(pl...  1.86 us
    pallas_call x1, Pallas kernels, on_device(): pl.pallas_call(functools.partial(last_kernel, base, radix, narrow, wy), o...  1.17 us
    pallas_call x2, Pallas kernels, on_device(): pl.pallas_call(functools.partial(third_kernel, planes, wy, chosen), out_s...  0.92 us
  transfers between devices with their start and end apart: 7, of which 5 were waited for; matrix products, arithmetic and copies ran while one was open for 0% of the time, Pallas kernels for 19%

profile of v15, /device:TPU:0, one launch (start us, length us, event | category | flops | bytes accessed | tf_op | source)
XLA Modules:
  0.0 24.2 jit_solution(8332550944098414538)
XLA Ops:
  0.0 3.7 %forcing_and_factor.1 = (bf16[2880,256]{1,0:T(8,128)(2,1)S(1)}, bf16[2880,256]{1,0:T(8,128)(2,1)S(1)}, f32[28,8,128]{2,1,0:T(8,128)S(1)}, f32[2,2880]{1,0:T(2,12...) custom-call(f32[5,8,64,128]{3,2,1,0:T(8,128)} %flow_hbm.1, f32[8,64,128]{2,1,0:T(8,128)} %speed_hbm.1, ...), custom_call_target="tpu_custom_call" | custom-call | tf_op jit(solution)/shard_map/forcing_and_factor/pallas_call | solution.py:773
  3.7 2.4 %collective-permute-start = (f32[2,2880]{1,0:T(2,128)S(1)}, f32[2,2880]{1,0:T(2,128)S(1)}, u32[]{:S(2)}, u32[]{:S(2)}) collective-permute-start(f32[2,2880]{1,0:T(2,128)S(1)} %get-tuple-element.29), channel_id=1, source_target_pairs={{0,24},{8,16},{16,8},{24,0},{1,25},{9,17},{17,9},{25,1},{2,26},{10... | collective-permute-start | bytes 69128 | tf_op jit(solution)/shard_map/ppermute | solution.py:795
  6.1 0.6 %collective-permute-start.1 = (f32[2,2880]{1,0:T(2,128)S(1)}, f32[2,2880]{1,0:T(2,128)S(1)}, u32[]{:S(2)}, u32[]{:S(2)}) collective-permute-start(f32[2,2880]{1,0:T(2,128)S(1)} %get-tuple-element.30), channel_id=1, source_target_pairs={{0,16},{8,24},{16,0},{24,8},{1,17},{9,25},{17,1},{25,9},{2,18},{10... | collective-permute-start | bytes 69128 | tf_op jit(solution)/shard_map/ppermute | solution.py:795
  6.8 0.0 collective-permute-start.2
  6.8 2.0 %local_z.1 = (f32[2880,128]{1,0:T(8,128)S(1)}, f32[168,128]{1,0:T(8,128)S(1)}, f32[24,128]{1,0:T(8,128)S(1)}, f32[8,128]{1,0:T(8,128)S(1)}, f32[64,128]{1,0:T(8,128)S(1)}) custom-call(f32[28,8,128]{2,1,0:T(8,128)S(1)} %get-tuple-element.22.factors, bf16[2880,256]{1,0:T(8,128)(2,1)S(1)} %get-tuple-element.23.high, bf16[2880,256]{1,0:T(8,128)(2,1)S(1)} %get-tuple-element.24.low), custom_call_target="tpu_custom_call" | custom-call | flops 1132462080 | bytes 4423680 | tf_op jit(solution)/shard_map/local_z/pallas_call | solution.py:801
  8.8 0.0 collective-permute-done.refs_0_.refs_2_
  8.8 0.4 %carried_y.2.moments = f32[168,128]{1,0:T(8,128)S(1)} custom-call(f32[168,128]{1,0:T(8,128)S(1)} %get-tuple-element.25.moments, f32[8,128]{1,0:T(8,128)S(1)} %get-tuple-element.26.spread_core, f32[64,128]{1,0:T(8,128)S(1)} %get-tuple-element.27.spread_extra, f32[24,128]{1,0:T(8,128)S(1)} %get-tuple-element.28.entering, ...), custom_call_target="tpu_custom_call" | custom-call | tf_op jit(solution)/shard_map/carried_y/pallas_call | solution.py:827
  9.2 0.7 %collective-permute-done.1.refs_0_.refs_1_ = f32[2,2880]{1,0:T(2,128)S(1)} collective-permute-done((f32[2,2880]{1,0:T(2,128)S(1)}, f32[2,2880]{1,0:T(2,128)S(1)}, u32[]{:S(2)}, u32[]{:S(2)}) %collective-permute-start.1) | collective-permute-done | bytes 23072 | tf_op jit(solution)/shard_map/ppermute | solution.py:795
  9.9 0.0 collective-permute-done.2.refs_1_.refs_0_
  9.9 0.5 %carried_y.3.unused.refs_0_ = f32[4,40,128]{2,1,0:T(8,128)S(1)} custom-call(f32[168,128]{1,0:T(8,128)S(1)} %carried_y.2.moments, f32[8,128]{1,0:T(8,128)S(1)} %get-tuple-element.26.spread_core, f32[64,128]{1,0:T(8,128)S(1)} %get-tuple-element.27.spread_extra, f32[24,128]{1,0:T(8,128)S(1)} %get-tuple-element.28.entering, ...), custom_call_target="tpu_custom_call" | custom-call | tf_op jit(solution)/shard_map/carried_y/pallas_call | solution.py:827
  10.5 2.6 %collective-permute-start.5 = (f32[4,40,128]{2,1,0:T(8,128)S(1)}, f32[4,40,128]{2,1,0:T(8,128)S(1)}, u32[]{:S(2)}, u32[]{:S(2)}) collective-permute-start(f32[4,40,128]{2,1,0:T(8,128)S(1)} %carried_y.3.unused.refs_0_), channel_id=1, source_target_pairs={{0,3},{1,2},{2,1},{3,0},{4,7},{5,6},{6,5},{7,4},{8,11},{9,10},{10,... | collective-permute-start | bytes 245768 | tf_op jit(solution)/shard_map/ppermute | solution.py:795
  13.1 0.4 %collective-permute-start.4 = (f32[4,40,128]{2,1,0:T(8,128)S(1)}, f32[4,40,128]{2,1,0:T(8,128)S(1)}, u32[]{:S(2)}, u32[]{:S(2)}) collective-permute-start(f32[4,40,128]{2,1,0:T(8,128)S(1)} %carried_y.3.unused.refs_0_), channel_id=1, source_target_pairs={{0,2},{1,3},{2,0},{3,1},{4,6},{5,7},{6,4},{7,5},{8,10},{9,11},{10,... | collective-permute-start | bytes 245768 | tf_op jit(solution)/shard_map/ppermute | solution.py:795
  13.5 0.5 %collective-permute-start.3 = (f32[4,40,128]{2,1,0:T(8,128)S(1)}, f32[4,40,128]{2,1,0:T(8,128)S(1)}, u32[]{:S(2)}, u32[]{:S(2)}) collective-permute-start(f32[4,40,128]{2,1,0:T(8,128)S(1)} %carried_y.3.unused.refs_0_), channel_id=1, source_target_pairs={{0,1},{1,0},{2,3},{3,2},{4,5},{5,4},{6,7},{7,6},{8,9},{9,8},{10,11... | collective-permute-start | bytes 245768 | tf_op jit(solution)/shard_map/ppermute | solution.py:795
  14.0 0.4 %inverse_y.1 = (f32[64,128]{1,0:T(8,128)S(1)}, f32[8,8,128]{2,1,0:T(8,128)S(1)}) custom-call(f32[28,8,128]{2,1,0:T(8,128)S(1)} %get-tuple-element.22.factors, f32[4,40,128]{2,1,0:T(8,128)S(1)} %carried_y.3.unused.refs_0_), custom_call_target="tpu_custom_call" | custom-call | flops 566231040 | bytes 2949120 | tf_op jit(solution)/shard_map/inverse_y/pallas_call | solution.py:847
  14.4 2.2 %collective-permute-done.5.refs_3_ = f32[4,40,128]{2,1,0:T(8,128)S(1)} collective-permute-done((f32[4,40,128]{2,1,0:T(8,128)S(1)}, f32[4,40,128]{2,1,0:T(8,128)S(1)}, u32[]{:S(2)}, u32[]{:S(2)}) %collective-permute-start.5) | collective-permute-done | bytes 81952 | tf_op jit(solution)/shard_map/ppermute | solution.py:795
  16.6 1.0 %collective-permute-done.4.refs_2_ = f32[4,40,128]{2,1,0:T(8,128)S(1)} collective-permute-done((f32[4,40,128]{2,1,0:T(8,128)S(1)}, f32[4,40,128]{2,1,0:T(8,128)S(1)}, u32[]{:S(2)}, u32[]{:S(2)}) %collective-permute-start.4) | collective-permute-done | bytes 81952 | tf_op jit(solution)/shard_map/ppermute | solution.py:795
  17.7 0.3 %collective-permute-done.3.refs_1_ = f32[4,40,128]{2,1,0:T(8,128)S(1)} collective-permute-done((f32[4,40,128]{2,1,0:T(8,128)S(1)}, f32[4,40,128]{2,1,0:T(8,128)S(1)}, u32[]{:S(2)}, u32[]{:S(2)}) %collective-permute-start.3) | collective-permute-done | bytes 81952 | tf_op jit(solution)/shard_map/ppermute | solution.py:795
  17.9 0.1 join_groups.1
  18.0 2.7 %collective-permute-start.6 = (f32[2,40,128]{2,1,0:T(8,128)S(1)}, f32[2,40,128]{2,1,0:T(8,128)S(1)}, u32[]{:S(2)}, u32[]{:S(2)}) collective-permute-start(f32[2,40,128]{2,1,0:T(8,128)S(1)} %get-tuple-element.38), channel_id=1, source_target_pairs={{0,4},{1,5},{2,6},{3,7},{4,0},{5,1},{6,2},{7,3},{8,12},{9,13},{10,... | collective-permute-start | bytes 122888 | tf_op jit(solution)/shard_map/ppermute | solution.py:795
  20.7 1.9 %local_y.1 = (f32[40,64,128]{2,1,0:T(8,128)S(1)}, f32[4,64,128]{2,1,0:T(8,128)S(1)}) custom-call(f32[2880,128]{1,0:T(8,128)S(1)} %get-tuple-element.33.local, f32[24,128]{1,0:T(8,128)S(1)} %get-tuple-element.28.entering, f32[64,128]{1,0:T(8,128)S(1)} %get-tuple-element.34.inverse_y, f32[4,40,128]{2,1,0:T(8,128)S(1)} %get-tuple-element.35.unused.entered, ...), custom_call_target="tpu_custom_call" | custom-call | flops 566231040 | bytes 2949120 | tf_op jit(solution)/shard_map/local_y/pallas_call | solution.py:870
  22.6 0.4 %collective-permute-done.6.refs_0_ = f32[2,40,128]{2,1,0:T(8,128)S(1)} collective-permute-done((f32[2,40,128]{2,1,0:T(8,128)S(1)}, f32[2,40,128]{2,1,0:T(8,128)S(1)}, u32[]{:S(2)}, u32[]{:S(2)}) %collective-permute-start.6) | collective-permute-done | bytes 40992 | tf_op jit(solution)/shard_map/ppermute | solution.py:795
  23.0 1.2 %finish_y.1 = f32[5,8,64,128]{3,2,1,0:T(8,128)} custom-call(f32[8,8,128]{2,1,0:T(8,128)S(1)} %get-tuple-element.32.coefs, f32[40,64,128]{2,1,0:T(8,128)S(1)} %get-tuple-element.36.local, f32[4,64,128]{2,1,0:T(8,128)S(1)} %get-tuple-element.37.sides, f32[4,40,128]{2,1,0:T(8,128)S(1)} %get-tuple-element.35.unused.entered, ...), custom_call_target="tpu_custom_call" | custom-call | tf_op jit(solution)/shard_map/finish_y/pallas_call | solution.py:881
Async XLA Ops:
  3.7 5.1 %collective-permute-start = (f32[2,2880]{1,0:T(2,128)S(1)}, f32[2,2880]{1,0:T(2,128)S(1)}, u32[]{:S(2)}, u32[]{:S(2)}) collective-permute-start(f32[2,2880]{1,0:T(2,128)S(1)} %get-tuple-element.29), channel_id=1, source_target_pairs={{0,24},{8,16},{16,8},{24,0},{1,25},{9,17},{17,9},{25,1},{2,26},{10... | collective-permute-start | bytes 69128 | tf_op jit(solution)/shard_map/ppermute | solution.py:795
  6.1 3.8 %collective-permute-start.1 = (f32[2,2880]{1,0:T(2,128)S(1)}, f32[2,2880]{1,0:T(2,128)S(1)}, u32[]{:S(2)}, u32[]{:S(2)}) collective-permute-start(f32[2,2880]{1,0:T(2,128)S(1)} %get-tuple-element.30), channel_id=1, source_target_pairs={{0,16},{8,24},{16,0},{24,8},{1,17},{9,25},{17,1},{25,9},{2,18},{10... | collective-permute-start | bytes 69128 | tf_op jit(solution)/shard_map/ppermute | solution.py:795
  6.8 3.2 %collective-permute-start.2 = (f32[2,2880]{1,0:T(2,128)S(1)}, f32[2,2880]{1,0:T(2,128)S(1)}, u32[]{:S(2)}, u32[]{:S(2)}) collective-permute-start(f32[2,2880]{1,0:T(2,128)S(1)} %get-tuple-element.31), channel_id=1, source_target_pairs={{0,8},{8,0},{16,24},{24,16},{1,9},{9,1},{17,25},{25,17},{2,10},{10... | collective-permute-start | bytes 69128 | tf_op jit(solution)/shard_map/ppermute | solution.py:795
  10.5 6.2 %collective-permute-start.5 = (f32[4,40,128]{2,1,0:T(8,128)S(1)}, f32[4,40,128]{2,1,0:T(8,128)S(1)}, u32[]{:S(2)}, u32[]{:S(2)}) collective-permute-start(f32[4,40,128]{2,1,0:T(8,128)S(1)} %carried_y.3.unused.refs_0_), channel_id=1, source_target_pairs={{0,3},{1,2},{2,1},{3,0},{4,7},{5,6},{6,5},{7,4},{8,11},{9,10},{10,... | collective-permute-start | bytes 245768 | tf_op jit(solution)/shard_map/ppermute | solution.py:795
  13.1 4.6 %collective-permute-start.4 = (f32[4,40,128]{2,1,0:T(8,128)S(1)}, f32[4,40,128]{2,1,0:T(8,128)S(1)}, u32[]{:S(2)}, u32[]{:S(2)}) collective-permute-start(f32[4,40,128]{2,1,0:T(8,128)S(1)} %carried_y.3.unused.refs_0_), channel_id=1, source_target_pairs={{0,2},{1,3},{2,0},{3,1},{4,6},{5,7},{6,4},{7,5},{8,10},{9,11},{10,... | collective-permute-start | bytes 245768 | tf_op jit(solution)/shard_map/ppermute | solution.py:795
  13.5 4.4 %collective-permute-start.3 = (f32[4,40,128]{2,1,0:T(8,128)S(1)}, f32[4,40,128]{2,1,0:T(8,128)S(1)}, u32[]{:S(2)}, u32[]{:S(2)}) collective-permute-start(f32[4,40,128]{2,1,0:T(8,128)S(1)} %carried_y.3.unused.refs_0_), channel_id=1, source_target_pairs={{0,1},{1,0},{2,3},{3,2},{4,5},{5,4},{6,7},{7,6},{8,9},{9,8},{10,11... | collective-permute-start | bytes 245768 | tf_op jit(solution)/shard_map/ppermute | solution.py:795
  18.0 5.0 %collective-permute-start.6 = (f32[2,40,128]{2,1,0:T(8,128)S(1)}, f32[2,40,128]{2,1,0:T(8,128)S(1)}, u32[]{:S(2)}, u32[]{:S(2)}) collective-permute-start(f32[2,40,128]{2,1,0:T(8,128)S(1)} %get-tuple-element.38), channel_id=1, source_target_pairs={{0,4},{1,5},{2,6},{3,7},{4,0},{5,1},{6,2},{7,3},{8,12},{9,13},{10,... | collective-permute-start | bytes 122888 | tf_op jit(solution)/shard_map/ppermute | solution.py:795
